TPU v7x, 256 devices: a whole 4x4x8 slice. The times are simulated.
256 devices in a mesh: src: 32 (over z, x), tgt: 8 (over y, core).
Axes of the slice: x: 4, y: 4, z: 8, core: 2. Of those that a mesh axis runs over, the one named last changes fastest.
Arguments:
- source_embed: bfloat16 [512, 65536], P(None, 'src')
- target_embed: bfloat16 [512, 16384], P('src', 'tgt')
- source_labels: int32 [65536], P('src'), may hold values from 0 to 3, as said below
- target_labels: int32 [16384], P('tgt'), may hold values from 0 to 3, as said below
- pair_blocks: int32 [32, 8, 24, 2], P('src', 'tgt'), may hold values from 0 to 7, as said below
- pair_count: int32 [32, 8], P('src', 'tgt'), may hold values from 8 to 24, as said below
Outputs:
- source_potential: float32 [65536], P('src')
- target_potential: float32 [16384], P('tgt')
- label_cost: float32 [4, 4], replicated
Inputs may be any that keep to these rules, and one draw needn't show every extreme that they name: `source_labels`: within each device's rows of 2048 samples, the first 4 samples have labels 0, 1, ... in order. `target_labels`: within each device's rows of 2048 samples, the first 4 samples have labels 0, 1, ... in order. `pair_blocks`: each device's list holds distinct pairs; its first 8 entries are the pairs (b, b) for b = 0, 1, ... in order; entries after the count are valid pairs and are ignored. `pair_count`: some device's count equals 24.
All inputs are finite; a program needn't handle non-finite values.
Results may differ from a plain program's by a relative error of at most 0.0003.
Values may be sent and summed in bfloat16 or wider, within the bound.
No kernel may reach another device: no remote copies, remote signals or barrier semaphores. Data moves between devices by JAX's collectives and lax.ppermute only.
A program may use at most 64 MiB of HBM per device.

v0:
```python
import math

import jax
import jax.numpy as jnp
from jax import lax
from jax.sharding import PartitionSpec as P

CLASSES = 4
BLOCK = 256
ITERS = 2


EPSILON = 0.05
LOWEST = -1e30
HIGHEST = lax.Precision.HIGHEST


def joined_2(x, axis, combine):
    everything = jax.tree.map(lambda part: lax.all_gather(part, axis), x)
    leading = jax.tree.map(lambda part: part[0], everything)

    def hop(k, so_far):
        return combine(so_far, jax.tree.map(lambda part: part[k], everything))

    return lax.fori_loop(1, lax.axis_size(axis), hop, leading)


def class_onehot(labels):
    classes = jnp.arange(CLASSES, dtype=jnp.int32)
    return (labels[None, :] == classes[:, None]).astype(jnp.float32)


def local_moments(values, onehot, counts):
    sums = jnp.einsum("cr,dr->cd", onehot, values, precision=HIGHEST)
    means = sums / counts[:, None]
    centered = values - jnp.dot(means.T, onehot, precision=HIGHEST)
    spread = jnp.einsum("cr,dr->cd", onehot, centered * centered, precision=HIGHEST)
    return (means, spread)


def pairwise_combine(first, second):
    count_a, mean_a, spread_a = first
    count_b, mean_b, spread_b = second
    joined = count_a + count_b
    delta = mean_b - mean_a
    means = mean_a + delta * (count_b / joined)[:, None]
    spread = spread_a + spread_b + delta * delta * (count_a * count_b / joined)[:, None]
    return (joined, means, spread)


def class_distance(src_mean, src_var, tgt_mean, tgt_var):
    gap = src_mean[:, None, :] - tgt_mean[None, :, :]
    roots = jnp.sqrt(src_var + 1e-06)[:, None, :] - jnp.sqrt(tgt_var + 1e-06)[None, :, :]
    return jnp.sum(gap * gap + roots * roots, axis=2)


def cost_from_cross(cross, src_sq, tgt_sq, row_lab, tgt_onehot, row_block, col_block, block):
    row_start = row_block * block
    col_start = col_block * block
    lab_rows = lax.dynamic_slice_in_dim(row_lab, row_start, block, 1)
    lab_cols = lax.dynamic_slice_in_dim(tgt_onehot, col_start, block, 1)
    labels_tile = jnp.dot(lab_rows.T, lab_cols, precision=HIGHEST)
    row_sq = lax.dynamic_slice_in_dim(src_sq, row_start, block)
    col_sq = lax.dynamic_slice_in_dim(tgt_sq, col_start, block)
    return row_sq[:, None] + col_sq[None, :] - 2.0 * cross + labels_tile


def absorb(carry, scores, start, axis, block):
    maxima, totals = carry
    tile_max = jnp.max(scores, axis=axis)
    tile_sum = jnp.sum(jnp.exp(scores - jnp.expand_dims(tile_max, axis)), axis=axis)
    old_max = lax.dynamic_slice_in_dim(maxima, start, block)
    old_sum = lax.dynamic_slice_in_dim(totals, start, block)
    new_max = jnp.maximum(old_max, tile_max)
    new_sum = old_sum * jnp.exp(old_max - new_max) + tile_sum * jnp.exp(tile_max - new_max)
    maxima = lax.dynamic_update_slice_in_dim(maxima, new_max, start, 0)
    totals = lax.dynamic_update_slice_in_dim(totals, new_sum, start, 0)
    return (maxima, totals)


def on_device(source_embed, target_embed, source_labels, target_labels, pair_blocks, pair_count):
    pairs = pair_blocks[0, 0]
    count = pair_count[0, 0]
    width, rows = source_embed.shape
    src_onehot = class_onehot(source_labels)
    tgt_onehot = class_onehot(target_labels)
    src_counts = jnp.sum(src_onehot, axis=1)
    tgt_counts = jnp.sum(tgt_onehot, axis=1)
    src_values = source_embed.astype(jnp.float32)
    src_sq = jnp.sum(src_values * src_values, axis=0)
    src_mean, src_spread = local_moments(src_values, src_onehot, src_counts)
    target_full = lax.all_gather(target_embed, "src", axis=0, tiled=True)
    tgt_values = target_full.astype(jnp.float32)
    tgt_sq = jnp.sum(tgt_values * tgt_values, axis=0)
    tgt_mean, tgt_spread = local_moments(tgt_values, tgt_onehot, tgt_counts)

    def tile_cross(row_block, col_block):
        source_tile = lax.dynamic_slice_in_dim(source_embed, row_block * BLOCK, BLOCK, 1)
        target_tile = lax.dynamic_slice_in_dim(target_full, col_block * BLOCK, BLOCK, 1)
        return lax.dot_general(
            source_tile, target_tile, (((0,), (0,)), ((), ())), preferred_element_type=jnp.float32
        )

    def cross_at(row_block, col_block):
        return tile_cross(row_block, col_block)

    src_all = joined_2((src_counts, src_mean, src_spread), "src", pairwise_combine)
    tgt_all = joined_2((tgt_counts, tgt_mean, tgt_spread), "tgt", pairwise_combine)
    label_cost = class_distance(
        src_all[1], src_all[2] / src_all[0][:, None], tgt_all[1], tgt_all[2] / tgt_all[0][:, None]
    )
    row_lab = jnp.dot(label_cost.T, src_onehot, precision=HIGHEST)

    def cost_at(index):
        row_block = pairs[index, 0]
        col_block = pairs[index, 1]
        cross = cross_at(row_block, col_block)
        return (
            cost_from_cross(
                cross, src_sq, tgt_sq, row_lab, tgt_onehot, row_block, col_block, BLOCK
            ),
            row_block,
            col_block,
        )

    total_source = rows * lax.axis_size("src")
    total_target = rows * lax.axis_size("tgt")
    src_pot = jnp.zeros((rows,), jnp.float32)
    tgt_pot = jnp.zeros((rows,), jnp.float32)
    empty = (jnp.full((rows,), LOWEST, jnp.float32), jnp.zeros((rows,), jnp.float32))
    for step in range(ITERS):

        def row_step(index, carry):
            cost_tile, row_block, col_block = cost_at(index)
            column_pot = lax.dynamic_slice_in_dim(tgt_pot, col_block * BLOCK, BLOCK)
            scores = (column_pot[None, :] - cost_tile) / EPSILON
            return absorb(carry, scores, row_block * BLOCK, 1, BLOCK)

        maxima, totals = lax.fori_loop(0, count, row_step, empty)
        highest = lax.pmax(maxima, "tgt")
        totals = lax.psum(totals * jnp.exp(maxima - highest), "tgt")
        maxima = highest
        src_pot = -EPSILON * (maxima + jnp.log(totals) - math.log(total_target))

        def col_step(index, carry):
            cost_tile, row_block, col_block = cost_at(index)
            row_pot = lax.dynamic_slice_in_dim(src_pot, row_block * BLOCK, BLOCK)
            scores = (row_pot[:, None] - cost_tile) / EPSILON
            return absorb(carry, scores, col_block * BLOCK, 0, BLOCK)

        maxima, totals = lax.fori_loop(0, count, col_step, empty)
        highest = lax.pmax(maxima, "src")
        totals = lax.psum(totals * jnp.exp(maxima - highest), "src")
        maxima = highest
        tgt_pot = -EPSILON * (maxima + jnp.log(totals) - math.log(total_source))
    return (src_pot, tgt_pot, label_cost)


def solution(mesh):
    return jax.shard_map(
        on_device,
        mesh=mesh,
        in_specs=(
            P(None, "src"),
            P("src", "tgt"),
            P("src"),
            P("tgt"),
            P("src", "tgt", None, None),
            P("src", "tgt"),
        ),
        out_specs=(P("src"), P("tgt"), P()),
        check_vma=False,
    )
```

profile of v0, /device:TPU:32, one launch (start us, length us, event | category | flops | bytes accessed | tf_op | source)
XLA Modules:
  0.0 1023.0 jit_solution(14871284522659623407)
XLA Ops:
  8.7 2.2 convolution_divide_fusion.1
  11.0 1.9 fusion.61
  12.9 2.4 fusion.55
  15.3 51.3 %all-gather.7 = f32[32,4,512]{2,1,0:T(4,128)S(1)} all-gather(f32[1,4,512]{2,1,0:T(4,128)S(1)} %fusion.55), channel_id=4, replica_groups=mesh['src'=32,'tgt'=8] {'src'}, dimensions={0}, use_global_device_ids=true | all-gather | bytes 270336 | tf_op jit(solution)/shard_map/all_gather | solution.py:19
  66.6 46.9 %all-gather.6 = f32[32,4,512]{2,1,0:T(4,128)S(1)} all-gather(f32[1,4,512]{2,1,0:T(4,128)S(1)} %bitcast.105), channel_id=3, replica_groups=mesh['src'=32,'tgt'=8] {'src'}, dimensions={0}, use_global_device_ids=true | all-gather | bytes 270336 | tf_op jit(solution)/shard_map/all_gather | solution.py:19
  115.1 67.9 %all-reduce = f32[128]{0:T(128)S(1)} all-reduce(f32[128]{0:T(128)S(1)} %dynamic-update-slice), channel_id=2, replica_groups=mesh['src'=32,'tgt'=8] {'src'}, use_global_device_ids=true, to_apply=%add | all-reduce | flops 128 | bytes 1024
  183.0 3.7 while.86
  188.3 12.6 %all-reduce.1 = f32[32]{0:T(128)S(1)} all-reduce(f32[32]{0:T(128)S(1)} %dynamic-update-slice.1), channel_id=5, replica_groups=mesh['src'=32,'tgt'=8] {'tgt'}, use_global_device_ids=true, to_apply=%add.1 | all-reduce | flops 32 | bytes 256
  201.5 2.2 convolution_divide_fusion
  203.7 1.9 fusion.58
  205.6 2.3 fusion.52
  208.0 12.9 %all-gather.9 = f32[8,4,512]{2,1,0:T(4,128)S(1)} all-gather(f32[1,4,512]{2,1,0:T(4,128)S(1)} %fusion.52), channel_id=7, replica_groups=mesh['src'=32,'tgt'=8] {'tgt'}, dimensions={0}, use_global_device_ids=true | all-gather | bytes 73728 | tf_op jit(solution)/shard_map/all_gather | solution.py:19
  220.9 12.7 %all-gather.8 = f32[8,4,512]{2,1,0:T(4,128)S(1)} all-gather(f32[1,4,512]{2,1,0:T(4,128)S(1)} %bitcast.104), channel_id=6, replica_groups=mesh['src'=32,'tgt'=8] {'tgt'}, dimensions={0}, use_global_device_ids=true | all-gather | bytes 73728 | tf_op jit(solution)/shard_map/all_gather | solution.py:19
  234.8 2.0 fusion.48
  236.9 65.0 %while.88 = (s32[]{:T(128)}, f32[2048]{0:T(1024)S(1)}, f32[2048]{0:T(1024)S(1)}, s32[]{:T(128)}, s32[24,2]{0,1:T(2,128)S(1)}, /*index=5*/f32[2048]{0:T(1024)S(1)...) while((s32[]{:T(128)}, f32[2048]{0:T(1024)S(1)}, ...), condition=%wide.region_12.0_spmd, body=%wide.region_9.0_spmd.sunk | while | flops 70845456 | bytes 1596739 | solution.py:139
  239.5 1.2 fusion.107
  244.1 1.2 fusion.107
  248.7 1.2 fusion.107
  253.3 1.2 fusion.107
  262.5 1.2 fusion.107
  267.1 1.2 fusion.107
  271.7 1.2 fusion.107
  276.3 1.2 fusion.107
  280.9 1.2 fusion.107
  285.5 1.2 fusion.107
  290.1 1.2 fusion.107
  294.7 1.2 fusion.107
  299.3 1.2 fusion.107
  301.9 54.8 %pmax.28 = f32[2048]{0:T(1024)S(1)} all-reduce(f32[2048]{0:T(1024)S(1)} %get-tuple-element.616), channel_id=1, replica_groups=mesh['src'=32,'tgt'=8] {'tgt'}, use_global_device_ids=true, to_apply=%region_13.0 | all-reduce | flops 2048 | bytes 16384 | tf_op jit(solution)/shard_map/pmax | solution.py:140
  356.7 12.7 %psum.28 = f32[2048]{0:T(1024)S(1)} all-reduce(f32[2048]{0:T(1024)S(1)} %exponential_multiply_fusion.3), channel_id=1, replica_groups=mesh['src'=32,'tgt'=8] {'tgt'}, use_global_device_ids=true, to_apply=%region_14.0 | all-reduce | flops 2048 | bytes 16384 | tf_op jit(solution)/shard_map/psum | solution.py:141
  369.5 67.1 %while.89 = (s32[]{:T(128)}, f32[2048]{0:T(1024)S(1)}, f32[2048]{0:T(1024)S(1)}, s32[]{:T(128)}, s32[24,2]{0,1:T(2,128)S(1)}, /*index=5*/f32[2048]{0:T(1024)S(1)...) while((s32[]{:T(128)}, f32[2048]{0:T(1024)S(1)}, ...), condition=%wide.region_18.0_spmd, body=%wide.region_15.0_spmd.sunk | while | flops 70845456 | bytes 1599823 | solution.py:151
  386.4 1.2 fusion.111
  400.6 1.2 fusion.111
  405.4 1.2 fusion.111
  414.9 1.2 fusion.111
  419.6 1.2 fusion.111
  436.6 115.0 %pmax.29 = f32[2048]{0:T(1024)S(1)} all-reduce(f32[2048]{0:T(1024)S(1)} %get-tuple-element.618), channel_id=1, replica_groups=mesh['src'=32,'tgt'=8] {'src'}, use_global_device_ids=true, to_apply=%region_19.0 | all-reduce | flops 2048 | bytes 16384 | tf_op jit(solution)/shard_map/pmax | solution.py:152
  551.6 70.7 %psum.29 = f32[2048]{0:T(1024)S(1)} all-reduce(f32[2048]{0:T(1024)S(1)} %exponential_multiply_fusion.2), channel_id=1, replica_groups=mesh['src'=32,'tgt'=8] {'src'}, use_global_device_ids=true, to_apply=%region_20.0 | all-reduce | flops 2048 | bytes 16384 | tf_op jit(solution)/shard_map/psum | solution.py:153
  622.4 67.2 %while.90 = (s32[]{:T(128)}, f32[2048]{0:T(1024)S(1)}, f32[2048]{0:T(1024)S(1)}, s32[]{:T(128)}, s32[24,2]{0,1:T(2,128)S(1)}, /*index=5*/f32[2048]{0:T(1024)S(1)...) while((s32[]{:T(128)}, f32[2048]{0:T(1024)S(1)}, ...), condition=%wide.region_24.0_spmd, body=%wide.region_21.0_spmd.sunk | while | flops 70845456 | bytes 1599823 | solution.py:139
  625.1 1.2 fusion.115
  629.8 1.2 fusion.115
  634.6 1.2 fusion.115
  639.4 1.2 fusion.115
  644.1 1.2 fusion.115
  648.9 1.2 fusion.115
  653.6 1.2 fusion.115
  658.3 1.2 fusion.115
  663.1 1.2 fusion.115
  667.8 1.2 fusion.115
  672.6 1.2 fusion.115
  677.3 1.2 fusion.115
  682.1 1.2 fusion.115
  686.9 1.2 fusion.115
  689.6 22.7 %pmax.30 = f32[2048]{0:T(1024)S(1)} all-reduce(f32[2048]{0:T(1024)S(1)} %get-tuple-element.620), channel_id=1, replica_groups=mesh['src'=32,'tgt'=8] {'tgt'}, use_global_device_ids=true, to_apply=%region_25.0 | all-reduce | flops 2048 | bytes 16384 | tf_op jit(solution)/shard_map/pmax | solution.py:140
  712.3 12.7 %psum.30 = f32[2048]{0:T(1024)S(1)} all-reduce(f32[2048]{0:T(1024)S(1)} %exponential_multiply_fusion.1), channel_id=1, replica_groups=mesh['src'=32,'tgt'=8] {'tgt'}, use_global_device_ids=true, to_apply=%region_26.0 | all-reduce | flops 2048 | bytes 16384 | tf_op jit(solution)/shard_map/psum | solution.py:141
  725.0 67.3 %while.91 = (s32[]{:T(128)}, f32[2048]{0:T(1024)S(1)}, f32[2048]{0:T(1024)S(1)}, s32[]{:T(128)}, s32[24,2]{0,1:T(2,128)S(1)}, /*index=5*/f32[2048]{0:T(1024)S(1)...) while((s32[]{:T(128)}, f32[2048]{0:T(1024)S(1)}, ...), condition=%wide.region_30.0_spmd, body=%wide.region_27.0_spmd.sunk | while | flops 70845456 | bytes 1599823 | solution.py:151
  737.2 1.2 fusion.119
  742.0 1.2 fusion.119
  761.1 1.2 fusion.119
  770.6 1.2 fusion.119
  775.3 1.2 fusion.119
  780.1 1.2 fusion.119
  792.4 151.6 %pmax.31 = f32[2048]{0:T(1024)S(1)} all-reduce(f32[2048]{0:T(1024)S(1)} %get-tuple-element.622), channel_id=1, replica_groups=mesh['src'=32,'tgt'=8] {'src'}, use_global_device_ids=true, to_apply=%region_31.0 | all-reduce | flops 2048 | bytes 16384 | tf_op jit(solution)/shard_map/pmax | solution.py:152
  944.0 71.6 %psum.31 = f32[2048]{0:T(1024)S(1)} all-reduce(f32[2048]{0:T(1024)S(1)} %exponential_multiply_fusion), channel_id=1, replica_groups=mesh['src'=32,'tgt'=8] {'src'}, use_global_device_ids=true, to_apply=%region_32.0 | all-reduce | flops 2048 | bytes 16384 | tf_op jit(solution)/shard_map/psum | solution.py:153
  (567 shorter events, 119.8 us)
Async XLA Ops:
  7.2 3.8 copy-start.4
  7.2 194.3 %all-gather.12.cloned.1.call-start = ((), (), s32[]{:S(2)}) async-start(), calls=%async_computation | async-start | bytes 2162688 | tf_op jit(solution)/shard_map/all_gather | solution.py:92
  11.0 1.9 copy-start
  12.9 100.7 %copy-start.8 = (u32[256]{0:T(256)S(1)}, u32[256]{0:T(256)}, u32[]{:S(2)}) copy-start(u32[256]{0:T(256)} %constant.180) | copy-start | bytes 3076
  12.9 173.8 %copy-start.7 = (u32[256]{0:T(256)S(1)}, u32[256]{0:T(256)}, u32[]{:S(2)}) copy-start(u32[256]{0:T(256)} %constant.185) | copy-start | bytes 3076
  12.9 175.0 %copy-start.3 = (s32[2048]{0:T(1024)S(1)}, s32[2048]{0:T(1024)}, u32[]{:S(2)}) copy-start(s32[2048]{0:T(1024)} %param.21) | copy-start | bytes 24580
  203.7 1.9 copy-start.1
  208.0 28.9 %copy-start.2 = (s32[1,1,24,2]{2,3,1,0:T(2,128)S(1)}, s32[1,1,24,2]{2,3,1,0:T(2,128)}, u32[]{:S(2)}) copy-start(s32[1,1,24,2]{2,3,1,0:T(2,128)} %param.22) | copy-start | bytes 580
  234.6 2.3 copy-start.6
  792.4 223.8 %copy-start.5 = (f32[2048]{0:T(1024)}, f32[2048]{0:T(1024)S(1)}, u32[]{:S(2)}) copy-start(f32[2048]{0:T(1024)S(1)} %get-tuple-element.1506) | copy-start | bytes 24580
Sparse Core Ops, SparseCore 0:
  10.6 79.5 all-gather.11
where the time goes:
time: 1040 us; the launch traced here: 1020 us
  blocking collectives  716 us (69%)
  loops' own time  111 us (11%)
  matrix products  107 us (10%)
  local copies, waits for them, and re-layouts  48.1 us (5%)
  other arithmetic  25 us (2%)
  between operations  15.7 us (2%)
    pmax x2, blocking collectives, on_device(): highest = lax.pmax(maxima, 'src')  267 us
    psum x2, blocking collectives, on_device(): totals = lax.psum(totals * jnp.exp(maxima - highest), 'src')  142 us
    all_gather x4, blocking collectives, joined_2(): everything = jax.tree.map(lambda part: lax.all_gather(part, axis), x)  124 us
    unnamed x2, blocking collectives  80.4 us
    pmax x2, blocking collectives, on_device(): highest = lax.pmax(maxima, 'tgt')  77.5 us
    dot_general x56, matrix products, tile_cross(): lax.dot_general(source_tile, target_tile, (((0,), (0,)), ((), ())), prefe...  68.4 us
    another operation x2, loops' own time, on_device(): maxima, totals = lax.fori_loop(0, count, col_step, empty)  56 us
    another operation x2, loops' own time, on_device(): maxima, totals = lax.fori_loop(0, count, row_step, empty)  54.5 us
  transfers between devices with their start and end apart: 1, of which 0 were waited for; matrix products, arithmetic and copies ran while one was open for 1% of the time, Pallas kernels for 0%

commit v1 on v0

v1 whole, which is shorter than its diff:
```python
import functools
import math

import jax
import jax.numpy as jnp
import numpy as np
from jax import lax
from jax.experimental import pallas as pl
from jax.experimental.pallas import tpu as pltpu
from jax.sharding import Mesh, PartitionSpec as P

CLASSES = 4
BLOCK = 256
ROWS = 2048
BLK = ROWS // BLOCK
LANES = 128
CHUNKS = ROWS // LANES
MAXP = 24
WIDTH = 512

EPSILON = 0.05
LOWEST = -1e30
HIGHEST = lax.Precision.HIGHEST
LOG2E = 1.0 / math.log(2.0)
TO_LOG2 = LOG2E / EPSILON
TO_POT = EPSILON / LOG2E

SRC = ("z", "x")
TGT = ("y", "c")
VMEM_LIMIT = 40 * 1024 * 1024


def log2(x):
    return jnp.log(x) * LOG2E


def shared(x, axis):
    n = lax.axis_size(axis)
    return lax.all_to_all(jnp.broadcast_to(x[None], (n,) + x.shape), axis, 0, 0)


def class_onehot(labels):
    classes = jnp.arange(CLASSES, dtype=jnp.int32)
    return (labels[None, :] == classes[:, None]).astype(jnp.float32)


def local_moments(values, onehot, counts):
    sums = jnp.einsum("cr,dr->cd", onehot, values, precision=HIGHEST)
    means = sums / counts[:, None]
    centered = values - jnp.dot(means.T, onehot, precision=HIGHEST)
    spread = jnp.einsum("cr,dr->cd", onehot, centered * centered, precision=HIGHEST)
    return (means, spread)


def joined(counts, means, spreads):
    total = jnp.sum(counts, axis=0)
    share = counts / total[None]
    mean = jnp.sum(means * share[:, :, None], axis=0)
    delta = means - mean[None]
    spread = jnp.sum(spreads + delta * delta * counts[:, :, None], axis=0)
    return total, mean, spread


def class_distance(src_mean, src_var, tgt_mean, tgt_var):
    gap = src_mean[:, None, :] - tgt_mean[None, :, :]
    roots = jnp.sqrt(src_var + 1e-06)[:, None, :] - jnp.sqrt(tgt_var + 1e-06)[None, :, :]
    return jnp.sum(gap * gap + roots * roots, axis=2)


def packed(*parts):
    flat = jnp.concatenate([p.reshape(-1) for p in parts])
    rows = -(-flat.size // (8 * LANES)) * 8
    return jnp.pad(flat, (0, rows * LANES - flat.size)).reshape(rows, LANES)


def three_parts(v):
    hi = v.astype(jnp.bfloat16).astype(jnp.float32)
    rest = v - hi
    mid = rest.astype(jnp.bfloat16).astype(jnp.float32)
    return hi, mid, rest - mid


def joined_lse(g_ref):
    g = g_ref[...]
    top = jnp.max(g, axis=0)
    return top + log2(jnp.sum(jnp.exp2(g - top[None]), axis=0))


def row_finish(top, total, out_ref):
    lines = []
    for k in range(CHUNKS):
        at = pl.ds(k * LANES, LANES)
        lse = top[at, :] + log2(jnp.sum(total[at, :], axis=1, keepdims=True))
        lines.append(lse.T[0:1, :])
    line = jnp.concatenate(lines, axis=0)
    out_ref[...] = jnp.broadcast_to(line[None], out_ref.shape)


def widen_top(top):
    for k in range(CHUNKS):
        at = pl.ds(k * LANES, LANES)
        top[at, :] = jnp.broadcast_to(jnp.max(top[at, :], axis=1, keepdims=True), (LANES, LANES))


def block_at(pairs, index):
    row = pl.multiple_of(pairs[2 * index] * BLOCK, BLOCK)
    return row, pairs[2 * index + 1]


def cost_kernel(
    pairs, count, label_cost, xt, y, src_sq, src_lab, tgt_lab, tiles, out_ref, xa, ya, top, total
):
    row_id = lax.broadcasted_iota(jnp.int32, (16, 1), 0)
    part = row_id // CLASSES
    cls = row_id % CLASSES
    labels = src_lab[...]
    u = jnp.broadcast_to(src_sq[...], (16, ROWS))
    for a in range(CLASSES):
        line = jnp.zeros((16, 1), jnp.float32)
        for b in range(CLASSES):
            line = jnp.where(cls == b, label_cost[a * CLASSES + b], line)
        u = u + jnp.where(labels == a, line, 0.0)
    hi, mid, lo = three_parts(-0.5 * u)
    ones = jnp.where(row_id < 15, 1.0, 0.0)
    xa[...] = jnp.where(
        part == 0, hi, jnp.where(part == 1, mid, jnp.where(part == 2, lo, ones))
    ).astype(jnp.bfloat16)

    def square(k, acc):
        v = y[pl.ds(pl.multiple_of(k * 16, 16), 16), :].astype(jnp.float32)
        return acc + v * v

    tgt_sq = lax.fori_loop(0, WIDTH // 16, square, jnp.zeros((16, ROWS), jnp.float32))
    hi, mid, lo = three_parts(-0.5 * jnp.sum(tgt_sq, axis=0, keepdims=True))
    onehot = jnp.where(tgt_lab[...] == cls, 1.0, 0.0)
    ya[...] = jnp.where(
        part < 3,
        onehot,
        jnp.where(cls == 0, hi, jnp.where(cls == 1, mid, jnp.where(cls == 2, lo, 0.0))),
    ).astype(jnp.bfloat16)

    top[...] = jnp.full(top.shape, LOWEST, jnp.float32)
    total[...] = jnp.zeros(total.shape, jnp.float32)

    def build(index, _):
        row, col = block_at(pairs, index)
        rows = pl.ds(row, BLOCK)
        cols = pl.ds(pl.multiple_of(col * BLOCK, BLOCK), BLOCK)
        cross = jnp.dot(xt[rows, :], y[:, cols], preferred_element_type=jnp.float32)
        extra = lax.dot_general(
            xa[:, rows], ya[:, cols], (((0,), (0,)), ((), ())), preferred_element_type=jnp.float32
        )
        tile = (cross + extra) * (2.0 * TO_LOG2)
        tiles[index] = tile
        top[rows, :] = jnp.maximum(top[rows, :], jnp.maximum(tile[:, :LANES], tile[:, LANES:]))
        return 0

    lax.fori_loop(0, count[0], build, 0)
    widen_top(top)

    def add(index, _):
        row, _ = block_at(pairs, index)
        rows = pl.ds(row, BLOCK)
        high = top[rows, :]
        left = jnp.exp2(tiles[index, :, :LANES] - high)
        right = jnp.exp2(tiles[index, :, LANES:] - high)
        total[rows, :] = total[rows, :] + (left + right)
        return 0

    lax.fori_loop(0, count[0], add, 0)
    row_finish(top, total, out_ref)


def row_kernel(log_total, pairs, count, tiles, g_ref, out_ref, pot, top, total):
    pot[...] = log_total - joined_lse(g_ref)
    top[...] = jnp.full(top.shape, LOWEST, jnp.float32)
    total[...] = jnp.zeros(total.shape, jnp.float32)

    def scores(index, col):
        left = tiles[index, :, :LANES] + pot[pl.ds(2 * col, 1), :]
        right = tiles[index, :, LANES:] + pot[pl.ds(2 * col + 1, 1), :]
        return left, right

    def highest(index, _):
        row, col = block_at(pairs, index)
        rows = pl.ds(row, BLOCK)
        left, right = scores(index, col)
        top[rows, :] = jnp.maximum(top[rows, :], jnp.maximum(left, right))
        return 0

    lax.fori_loop(0, count[0], highest, 0)
    widen_top(top)

    def add(index, _):
        row, col = block_at(pairs, index)
        rows = pl.ds(row, BLOCK)
        left, right = scores(index, col)
        high = top[rows, :]
        total[rows, :] = total[rows, :] + (jnp.exp2(left - high) + jnp.exp2(right - high))
        return 0

    lax.fori_loop(0, count[0], add, 0)
    row_finish(top, total, out_ref)


def col_kernel(log_total, pairs, count, tiles, g_ref, out_ref, pot_ref, pot, top, total):
    line = log_total - joined_lse(g_ref)
    pot_ref[...] = line * TO_POT
    for k in range(CHUNKS):
        pot[pl.ds(k * LANES, LANES), :] = jnp.broadcast_to(line[k : k + 1, :], (LANES, LANES)).T
    top[...] = jnp.full(top.shape, LOWEST, jnp.float32)
    total[...] = jnp.zeros(total.shape, jnp.float32)

    def scores(index, row):
        rows = pl.ds(row, BLOCK)
        high = pot[rows, :]
        tile = tiles[index]
        return tile + jnp.concatenate([high, high], axis=1)

    def highest(index, _):
        row, col = block_at(pairs, index)
        score = scores(index, row)
        top[col] = jnp.maximum(top[col], jnp.max(score.reshape(BLOCK // 8, 8, BLOCK), axis=0))
        return 0

    lax.fori_loop(0, count[0], highest, 0)
    for k in range(BLK):
        top[k] = jnp.broadcast_to(jnp.max(top[k], axis=0, keepdims=True), (8, BLOCK))

    def add(index, _):
        row, col = block_at(pairs, index)
        score = scores(index, row).reshape(BLOCK // 8, 8, BLOCK)
        total[col] = total[col] + jnp.sum(jnp.exp2(score - top[col][None]), axis=0)
        return 0

    lax.fori_loop(0, count[0], add, 0)
    lines = []
    for k in range(BLK):
        lse = top[k][0:1] + log2(jnp.sum(total[k], axis=0, keepdims=True))
        lines += [lse[:, :LANES], lse[:, LANES:]]
    out = jnp.concatenate(lines, axis=0)
    out_ref[...] = jnp.broadcast_to(out[None], out_ref.shape)


def last_kernel(log_total, g_ref, pot_ref):
    pot_ref[...] = (log_total - joined_lse(g_ref)) * TO_POT


def smem():
    return pl.BlockSpec(memory_space=pltpu.SMEM)


def vmem():
    return pl.BlockSpec(memory_space=pltpu.VMEM)


def f32(*shape):
    return jax.ShapeDtypeStruct(shape, jnp.float32)


def params():
    return pltpu.CompilerParams(vmem_limit_bytes=VMEM_LIMIT)


def on_device(source_embed, target_embed, source_labels, target_labels, pair_blocks, pair_count):
    pairs = pair_blocks.reshape(-1)
    count = pair_count.reshape(-1)
    n_src, n_tgt = lax.axis_size(SRC), lax.axis_size(TGT)

    near = shared(target_embed, "x").reshape(-1, ROWS)
    target_full = lax.all_gather(near, "z", axis=0, tiled=True)

    src_onehot = class_onehot(source_labels)
    tgt_onehot = class_onehot(target_labels)
    src_counts = jnp.sum(src_onehot, axis=1)
    tgt_counts = jnp.sum(tgt_onehot, axis=1)
    src_values = source_embed.astype(jnp.float32)
    src_sq = jnp.sum(src_values * src_values, axis=0)
    tgt_values = target_embed.astype(jnp.float32)
    part = tgt_values.shape[0]
    tgt_mean, tgt_spread = local_moments(tgt_values, tgt_onehot, tgt_counts)
    got = shared(packed(tgt_mean, tgt_spread, tgt_counts), TGT).reshape(n_tgt, -1)
    size = CLASSES * part
    tgt_total, tgt_mean, tgt_spread = joined(
        got[:, 2 * size : 2 * size + CLASSES],
        got[:, :size].reshape(n_tgt, CLASSES, part),
        got[:, size : 2 * size].reshape(n_tgt, CLASSES, part),
    )
    tgt_slice = jnp.concatenate([tgt_mean, tgt_spread / tgt_total[:, None]], axis=0)
    src_mean, src_spread = local_moments(src_values, src_onehot, src_counts)
    full = CLASSES * WIDTH
    slices = tgt_slice[None]
    for axis in ("x", "z"):
        n = lax.axis_size(axis)
        got = shared(packed(src_mean, src_spread, slices, src_counts), axis).reshape(n, -1)
        width = slices.size
        src_counts, src_mean, src_spread = joined(
            got[:, 2 * full + width : 2 * full + width + CLASSES],
            got[:, :full].reshape(n, CLASSES, WIDTH),
            got[:, full : 2 * full].reshape(n, CLASSES, WIDTH),
        )
        slices = got[:, 2 * full : 2 * full + width].reshape(-1, 2 * CLASSES, part)
    tgt_both = slices.transpose(1, 0, 2).reshape(2 * CLASSES, WIDTH)
    label_cost = class_distance(
        src_mean, src_spread / src_counts[:, None], tgt_both[:CLASSES], tgt_both[CLASSES:]
    )

    tall = pltpu.VMEM((ROWS, LANES), jnp.float32)
    wide = pltpu.VMEM((BLK, 8, BLOCK), jnp.float32)
    log_src = math.log2(ROWS * n_src)
    log_tgt = math.log2(ROWS * n_tgt)
    tiles, sent = pl.pallas_call(
        cost_kernel,
        out_shape=(f32(MAXP, BLOCK, BLOCK), f32(n_tgt, CHUNKS, LANES)),
        in_specs=[smem(), smem(), smem(), vmem(), vmem(), vmem(), vmem(), vmem()],
        out_specs=(vmem(), vmem()),
        scratch_shapes=[
            pltpu.VMEM((16, ROWS), jnp.bfloat16),
            pltpu.VMEM((16, ROWS), jnp.bfloat16),
            tall,
            tall,
        ],
        compiler_params=params(),
        name="cost_rows",
    )(
        pairs,
        count,
        label_cost.reshape(-1),
        source_embed.T,
        target_full,
        src_sq[None],
        source_labels[None],
        target_labels[None],
    )

    def columns(got):
        return pl.pallas_call(
            functools.partial(col_kernel, log_tgt),
            out_shape=(f32(n_src, CHUNKS, LANES), f32(CHUNKS, LANES)),
            in_specs=[smem(), smem(), vmem(), vmem()],
            out_specs=(vmem(), vmem()),
            scratch_shapes=[tall, wide, wide],
            compiler_params=params(),
            name="columns",
        )(pairs, count, tiles, got)

    def rows(got):
        return pl.pallas_call(
            functools.partial(row_kernel, log_src),
            out_shape=f32(n_tgt, CHUNKS, LANES),
            in_specs=[smem(), smem(), vmem(), vmem()],
            out_specs=vmem(),
            scratch_shapes=[pltpu.VMEM((CHUNKS, LANES), jnp.float32), tall, tall],
            compiler_params=params(),
            name="rows",
        )(pairs, count, tiles, got)

    sent, _ = columns(lax.all_to_all(sent, TGT, 0, 0))
    sent = rows(lax.all_to_all(sent, SRC, 0, 0))
    sent, src_pot = columns(lax.all_to_all(sent, TGT, 0, 0))
    tgt_pot = pl.pallas_call(
        functools.partial(last_kernel, log_src),
        out_shape=f32(CHUNKS, LANES),
        in_specs=[vmem()],
        out_specs=vmem(),
        compiler_params=params(),
        name="last",
    )(lax.all_to_all(sent, SRC, 0, 0))
    return (src_pot.reshape(-1), tgt_pot.reshape(-1), label_cost)


def solution(mesh):
    fine = Mesh(np.asarray(mesh.devices).reshape(8, 4, 4, 2), SRC + TGT)
    return jax.shard_map(
        on_device,
        mesh=fine,
        in_specs=(
            P(None, SRC),
            P(SRC, TGT),
            P(SRC),
            P(TGT),
            P(SRC, TGT, None, None),
            P(SRC, TGT),
        ),
        out_specs=(P(SRC), P(TGT), P()),
        check_vma=False,
    )
```

time: 1040 us -> 162 us (0.16); the launches traced: 1020 us -> 161 us
  blocking collectives: 716 us -> 68.3 us
  loops' own time: 111 us -> 0 us
  matrix products: 107 us -> 13.5 us
  local copies, waits for them, and re-layouts: 48.1 us -> 9.56 us
  other arithmetic: 25 us -> 4.46 us
  starting transfers between devices: 0.04 us -> 17.4 us
  Pallas kernels: 0 us -> 16.1 us
  waiting for transfers between devices: 0.7 us -> 16.5 us
    pmax x4 -> x0, blocking collectives: 344 us -> none  [the longest x2 267 us: on_device(): highest = lax.pmax(maxima, 'src')]
    psum x4 -> x0, blocking collectives: 168 us -> none  [the longest x2 142 us: on_device(): totals = lax.psum(totals * jnp.exp(maxima - highest), 'src')]
    all_gather x4 -> x0, blocking collectives: 124 us -> none  [joined_2(): everything = jax.tree.map(lambda part: lax.all_gather(part, axis), x)]
    another operation x6 -> x0, loops' own time: 111 us -> none  [the longest x2 56 us: on_device(): maxima, totals = lax.fori_loop(0, count, col_step, empty)]
    dot_general x113 -> x0, matrix products: 93.8 us -> none  [the longest x56 68.4 us: tile_cross(): lax.dot_general(source_tile, target_tile, (((0,), (0,)), ((), ())), prefe...]
    unnamed x2 -> x0, blocking collectives: 80.4 us -> none
    all_to_all x0 -> x5, blocking collectives: none -> 68.3 us  [the longest x1 18.7 us: on_device(): sent = rows(lax.all_to_all(sent, SRC, 0, 0))]
    dynamic_slice x210 -> x0, local copies, waits for them, and re-layouts: 46.1 us -> none  [the longest x28 17.1 us: cost_at(): row_block = pairs[index, 0]]
  transfers between devices with their start and end apart: 1 -> 4, of which waited for: 0 -> 3; matrix products, arithmetic and copies ran while one was open for 1% -> 15% of each run, Pallas kernels for 0% -> 0%
where the time goes in v1:
time: 162 us; the launch traced here: 161 us
  blocking collectives  68.3 us (42%)
  starting transfers between devices  17.4 us (11%)
  waiting for transfers between devices  16.5 us (10%)
  Pallas kernels  16.1 us (10%)
  between operations  14.9 us (9%)
  matrix products  13.5 us (8%)
  local copies, waits for them, and re-layouts  9.56 us (6%)
  other arithmetic  4.46 us (3%)
    all_to_all x1, blocking collectives, on_device(): sent = rows(lax.all_to_all(sent, SRC, 0, 0))  18.7 us
    all_to_all x3, starting transfers between devices, shared(): return lax.all_to_all(jnp.broadcast_to(x[None], (n,) + x.shape), axis, 0, 0)  17.3 us
    all_to_all x1, blocking collectives, on_device(): lax.all_to_all(sent, SRC, 0, 0)  16.8 us
    all_to_all x1, blocking collectives, on_device(): sent, _ = columns(lax.all_to_all(sent, TGT, 0, 0))  13.5 us
    all_gather x1, waiting for transfers between devices, on_device(): target_full = lax.all_gather(near, 'z', axis=0, tiled=True)  11.3 us
    all_to_all x1, blocking collectives, shared(): return lax.all_to_all(jnp.broadcast_to(x[None], (n,) + x.shape), axis, 0, 0)  10.3 us
    all_to_all x1, blocking collectives, on_device(): sent, src_pot = columns(lax.all_to_all(sent, TGT, 0, 0))  8.96 us
    pallas_call x1, Pallas kernels, on_device(): pl.pallas_call(cost_kernel, out_shape=(f32(MAXP, BLOCK, BLOCK), f32(n_tgt...  7.11 us
  transfers between devices with their start and end apart: 4, of which 3 were waited for; matrix products, arithmetic and copies ran while one was open for 15% of the time, Pallas kernels for 0%

profile of v1, /device:TPU:32, one launch (start us, length us, event | category | flops | bytes accessed | tf_op | source)
XLA Modules:
  0.0 160.7 jit_solution(17936172151892980242)
XLA Ops:
  7.2 0.0 copy-start.1
  7.2 0.0 copy-start.2
  7.2 0.0 copy-start.3
  7.2 1.7 %broadcast_in_dim.26 = bf16[4,16,2048]{2,1,0:T(8,128)(2,1)} broadcast(bf16[16,2048]{1,0:T(8,128)(2,1)} %param.7), dimensions={1,2} | broadcast | bytes 327680 | tf_op jit(solution)/shard_map/broadcast_in_dim | solution.py:39
  8.9 4.3 %all-to-all-start.3 = ((bf16[4,16,2048]{2,1,0:T(8,128)(2,1)}), bf16[4,16,2048]{2,1,0:T(8,128)(2,1)S(1)}, u32[]{:S(2)}, u32[]{:S(2)}) async-start(bf16[4,16,2048]{2,1,0:T(8,128)(2,1)} %broadcast_in_dim.26), calls=%async_computation.3 | async-start | bytes 524288 | tf_op jit(solution)/shard_map/all_to_all | solution.py:39
  13.2 0.8 convert_reduce_fusion.1
  14.0 0.8 convert_reduce_fusion
  14.8 1.0 convolution_divide_fusion.1
  15.8 1.1 fusion.4
  17.0 2.3 %convolution_divide_fusion = f32[4,512]{1,0:T(4,128)S(1)} fusion(bf16[512,2048]{1,0:T(8,128)(2,1)} %param.6, s32[2048]{0:T(1024)} %param.8, f32[4]{0:T(128)S(1)} %convert_reduce_fusion.1), kind=kOutput, calls=%fused_computation.7 | convolution fusion | flops 8398848 | bytes 2113552 | tf_op jit(solution)/shard_map/cr,dr->cd/dot_general | solution.py:48
  19.2 4.5 %fusion.12 = f32[512,2048]{1,0:T(8,128)} fusion(f32[4,512]{1,0:T(4,128)S(1)} %convolution_divide_fusion, s32[2048]{0:T(1024)} %param.8), kind=kOutput, calls=%fused_computation.27 | convolution fusion | flops 50339840 | bytes 4210688 | tf_op jit(solution)/shard_map/dot_general | solution.py:50
  23.7 0.1 fusion.11
  23.8 0.1 reshape.139
  23.9 0.1 reshape.140
  24.0 0.1 fusion.22
  24.1 0.0 all-to-all-done.3
  24.2 0.7 broadcast_in_dim.21
  24.8 4.5 %all-to-all-start = ((f32[8,8,128]{2,1,0:T(8,128)}), f32[8,8,128]{2,1,0:T(8,128)S(1)}, u32[]{:S(2)}, u32[]{:S(2)}) async-start(f32[8,8,128]{2,1,0:T(8,128)} %broadcast_in_dim.21), calls=%async_computation | async-start | bytes 65536 | tf_op jit(solution)/shard_map/all_to_all | solution.py:39
  29.3 0.0 all-gather.2.cloned.1.call-start
  29.3 0.7 all-gather.2.cloned.1.call-update
  30.0 4.5 %fusion.5 = f32[1,4,4,128]{3,2,1,0:T(4,128)S(1)} fusion(f32[512,2048]{1,0:T(8,128)} %fusion.12, bf16[512,2048]{1,0:T(8,128)(2,1)S(1)} %copy-done.3, s32[2048]{0:T(1024)S(1)} %copy-done.1), kind=kOutput, calls=%fused_computation.8 | convolution fusion | flops 53485568 | bytes 6307840 | tf_op jit(solution)/shard_map/cr,dr->cd/dot_general | solution.py:51
  34.6 0.1 all-to-all-done
  34.8 0.1 mul.95
  34.8 0.1 mul.96
  34.9 0.1 reduce_sum.127
  35.0 0.1 mul.99
  35.1 0.1 mul.100
  35.2 0.1 fusion.21
  35.3 0.1 reduce_sum.129
  35.4 0.1 broadcast_divide_fusion.3
  35.5 0.1 reshape_broadcast_in_dim.3
  35.6 10.3 %all_to_all.40 = f32[4,40,128]{2,1,0:T(8,128)S(1)} all-to-all(f32[4,40,128]{2,1,0:T(8,128)S(1)} %broadcast_in_dim.23), channel_id=1, replica_groups=mesh['z'=8,'x'=4,'y'=4,'c'=2] {'x'}, dimensions={0} | all-to-all | bytes 163840 | tf_op jit(solution)/shard_map/all_to_all | solution.py:39
  46.0 0.1 broadcast_bitcast_fusion
  46.2 0.7 broadcast_in_dim.25
  46.9 8.6 %all-to-all-start.2 = ((f32[8,40,128]{2,1,0:T(8,128)}), f32[8,40,128]{2,1,0:T(8,128)S(1)}, u32[]{:S(2)}, u32[]{:S(2)}) async-start(f32[8,40,128]{2,1,0:T(8,128)} %broadcast_in_dim.25), calls=%async_computation.2 | async-start | bytes 327680 | tf_op jit(solution)/shard_map/all_to_all | solution.py:39
  55.4 2.9 %copy.46 = bf16[512,2048]{0,1:T(8,128)(2,1)S(1)} copy(bf16[512,2048]{1,0:T(8,128)(2,1)} %param.6) | data formatting | bytes 4194304 | tf_op args[0]
  59.0 0.1 copy.39
  59.0 0.1 reshape.135.pairs
  59.1 2.0 %fusion.3 = f32[2048]{0:T(1024)S(1)} fusion(bf16[512,2048]{1,0:T(8,128)(2,1)} %param.6), kind=kLoop, calls=%fused_computation.4 | loop fusion | flops 3143680 | bytes 2105344 | tf_op jit(solution)/shard_map/reduce_sum | solution.py:278
  61.2 4.4 %all-to-all-done.2 = f32[8,40,128]{2,1,0:T(8,128)S(1)} async-done(((f32[8,40,128]{2,1,0:T(8,128)}), f32[8,40,128]{2,1,0:T(8,128)S(1)}, u32[]{:S(2)}, u32[]{:S(2)}) %all-to-all-start.2) | async-done | bytes 163872 | tf_op jit(solution)/shard_map/all_to_all | solution.py:39
  65.6 0.1 copy.41
  65.7 0.1 copy.44
  65.8 0.1 mul.109
  65.9 0.1 mul.114
  66.0 0.1 reshape.144
  66.1 0.1 copy.42
  66.3 0.1 copy.43
  66.3 0.1 sub.71
  66.4 0.1 copy.45
  66.5 0.1 sqrt.19
  66.6 0.1 add_sqrt_fusion
  66.7 0.1 add_reduce_fusion
  66.8 0.1 reshape.145.label_cost
  66.9 11.3 %all-gather.2.cloned.1.call-done.y = bf16[512,2048]{1,0:T(8,128)(2,1)} async-done(((bf16[64,2048]{1,0:T(8,128)(2,1)}), bf16[512,2048]{1,0:T(8,128)(2,1)}) %all-gather.2.cloned.1.call-update) | async-done | bytes 2097168 | tf_op jit(solution)/shard_map/all_gather | solution.py:271
  78.2 1.6 copy-done
  79.8 7.1 %cost_rows.1 = (f32[24,256,256]{2,1,0:T(8,128)S(1)}, f32[8,16,128]{2,1,0:T(8,128)S(1)}) custom-call(s32[48]{0:T(128)S(1)} %reshape.135.pairs, s32[1]{0:T(128)} %bitcast.49.count, f32[16]{0:T(128)S(1)} %reshape.145.label_cost, bf16[2048,512]{1,0:T(8,128)(2,1)S(1)} %bitcast.53, bf16[512,2048]{1,0:T(8,128)(2,1)S(1)} %copy-done, f32[1,2048]{1,0:T(1,128)S(1)} %bitcast.56, ...), custom_call_target="tpu_custom_call" | custom-call | tf_op jit(solution)/shard_map/cost_rows/pallas_call | solution.py:312
  86.9 13.5 %all_to_all.41.g_ref = f32[8,16,128]{2,1,0:T(8,128)S(1)} all-to-all(f32[8,16,128]{2,1,0:T(8,128)S(1)} %get-tuple-element.9), channel_id=1, replica_groups=mesh['z'=8,'x'=4,'y'=4,'c'=2] {'y','c'}, dimensions={0} | all-to-all | bytes 131072 | tf_op jit(solution)/shard_map/all_to_all | solution.py:358
  100.5 2.7 %columns.2 = (f32[32,16,128]{2,1,0:T(8,128)S(1)}, f32[16,128]{1,0:T(8,128)}) custom-call(s32[48]{0:T(128)S(1)} %reshape.135.pairs, s32[1]{0:T(128)} %bitcast.50.count, f32[24,256,256]{2,1,0:T(8,128)S(1)} %get-tuple-element.8.tiles, f32[8,16,128]{2,1,0:T(8,128)S(1)} %all_to_all.41.g_ref), custom_call_target="tpu_custom_call" | custom-call | tf_op jit(solution)/shard_map/columns/pallas_call | solution.py:337
  103.2 18.7 %all_to_all.42.g_ref = f32[32,16,128]{2,1,0:T(8,128)S(1)} all-to-all(f32[32,16,128]{2,1,0:T(8,128)S(1)} %get-tuple-element.10), channel_id=1, replica_groups=mesh['z'=8,'x'=4,'y'=4,'c'=2] {'z','x'}, dimensions={0} | all-to-all | bytes 524288 | tf_op jit(solution)/shard_map/all_to_all | solution.py:359
  121.9 2.8 %rows.1 = f32[8,16,128]{2,1,0:T(8,128)S(1)} custom-call(s32[48]{0:T(128)S(1)} %reshape.135.pairs, s32[1]{0:T(128)} %bitcast.51.count, f32[24,256,256]{2,1,0:T(8,128)S(1)} %get-tuple-element.8.tiles, f32[32,16,128]{2,1,0:T(8,128)S(1)} %all_to_all.42.g_ref), custom_call_target="tpu_custom_call" | custom-call | tf_op jit(solution)/shard_map/rows/pallas_call | solution.py:348
  124.8 9.0 %all_to_all.43.g_ref = f32[8,16,128]{2,1,0:T(8,128)S(1)} all-to-all(f32[8,16,128]{2,1,0:T(8,128)S(1)} %rows.1), channel_id=1, replica_groups=mesh['z'=8,'x'=4,'y'=4,'c'=2] {'y','c'}, dimensions={0} | all-to-all | bytes 131072 | tf_op jit(solution)/shard_map/all_to_all | solution.py:360
  133.7 2.7 %columns.3 = (f32[32,16,128]{2,1,0:T(8,128)S(1)}, f32[16,128]{1,0:T(8,128)}) custom-call(s32[48]{0:T(128)S(1)} %reshape.135.pairs, s32[1]{0:T(128)} %bitcast.52.count, f32[24,256,256]{2,1,0:T(8,128)S(1)} %get-tuple-element.8.tiles, f32[8,16,128]{2,1,0:T(8,128)S(1)} %all_to_all.43.g_ref), custom_call_target="tpu_custom_call" | custom-call | tf_op jit(solution)/shard_map/columns/pallas_call | solution.py:337
  136.4 16.8 %all_to_all.44.g_ref = f32[32,16,128]{2,1,0:T(8,128)S(1)} all-to-all(f32[32,16,128]{2,1,0:T(8,128)S(1)} %get-tuple-element.12), channel_id=1, replica_groups=mesh['z'=8,'x'=4,'y'=4,'c'=2] {'z','x'}, dimensions={0} | all-to-all | bytes 524288 | tf_op jit(solution)/shard_map/all_to_all | solution.py:368
  153.2 0.7 last.1
  (37 shorter events, 0.4 us)
Async XLA Ops:
  7.2 22.9 %copy-start.1 = (s32[2048]{0:T(1024)S(1)}, s32[2048]{0:T(1024)}, u32[]{:S(2)}) copy-start(s32[2048]{0:T(1024)} %param.8) | copy-start | bytes 24580
  7.2 16.5 %copy-start.2 = (s32[2048]{0:T(1024)S(1)}, s32[2048]{0:T(1024)}, u32[]{:S(2)}) copy-start(s32[2048]{0:T(1024)} %param.9) | copy-start | bytes 24580
  7.2 22.8 %copy-start.3 = (bf16[512,2048]{1,0:T(8,128)(2,1)S(1)}, bf16[512,2048]{1,0:T(8,128)(2,1)}, u32[]{:S(2)}) copy-start(bf16[512,2048]{1,0:T(8,128)(2,1)} %param.6) | copy-start | bytes 6291460
  8.9 15.3 %all-to-all-start.3 = ((bf16[4,16,2048]{2,1,0:T(8,128)(2,1)}), bf16[4,16,2048]{2,1,0:T(8,128)(2,1)S(1)}, u32[]{:S(2)}, u32[]{:S(2)}) async-start(bf16[4,16,2048]{2,1,0:T(8,128)(2,1)} %broadcast_in_dim.26), calls=%async_computation.3 | async-start | bytes 524288 | tf_op jit(solution)/shard_map/all_to_all | solution.py:39
  24.2 5.2 %copy-start.4 = (bf16[4,16,2048]{2,1,0:T(8,128)(2,1)}, bf16[4,16,2048]{2,1,0:T(8,128)(2,1)S(1)}, u32[]{:S(2)}) copy-start(bf16[4,16,2048]{2,1,0:T(8,128)(2,1)S(1)} %all-to-all-done.3) | copy-start | bytes 786436
  24.8 9.9 %all-to-all-start = ((f32[8,8,128]{2,1,0:T(8,128)}), f32[8,8,128]{2,1,0:T(8,128)S(1)}, u32[]{:S(2)}, u32[]{:S(2)}) async-start(f32[8,8,128]{2,1,0:T(8,128)} %broadcast_in_dim.21), calls=%async_computation | async-start | bytes 65536 | tf_op jit(solution)/shard_map/all_to_all | solution.py:39
  29.3 49.0 %all-gather.2.cloned.1.call-start = ((), (), s32[]{:S(2)}) async-start(), calls=%async_computation.8 | async-start | bytes 2359296 | tf_op jit(solution)/shard_map/all_gather | solution.py:271
  34.6 24.4 %copy-start.6 = (s32[1,1,24,2]{2,3,1,0:T(2,128)S(1)}, s32[1,1,24,2]{2,3,1,0:T(2,128)}, u32[]{:S(2)}) copy-start(s32[1,1,24,2]{2,3,1,0:T(2,128)} %param.10) | copy-start | bytes 580
  46.9 18.7 %all-to-all-start.2 = ((f32[8,40,128]{2,1,0:T(8,128)}), f32[8,40,128]{2,1,0:T(8,128)S(1)}, u32[]{:S(2)}, u32[]{:S(2)}) async-start(f32[8,40,128]{2,1,0:T(8,128)} %broadcast_in_dim.25), calls=%async_computation.2 | async-start | bytes 327680 | tf_op jit(solution)/shard_map/all_to_all | solution.py:39
  66.8 36.4 %copy-start.5 = (f32[4,4]{1,0:T(4,128)}, f32[4,4]{1,0:T(4,128)S(1)}, u32[]{:S(2)}) copy-start(f32[4,4]{1,0:T(4,128)S(1)} %add_reduce_fusion) | copy-start | bytes 196
  78.2 1.6 copy-start
Sparse Core Ops, SparseCore 0:
  31.9 46.2 all-gather.1

commit v2 on v1

v2 whole, which is shorter than its diff:
```python
import functools
import math

import jax
import jax.numpy as jnp
import numpy as np
from jax import lax
from jax.experimental import pallas as pl
from jax.experimental.pallas import tpu as pltpu
from jax.sharding import Mesh, PartitionSpec as P

CLASSES = 4
BLOCK = 256
ROWS = 2048
BLK = ROWS // BLOCK
LANES = 128
CHUNKS = ROWS // LANES
MAXP = 24
UNROLL = 4
WIDTH = 512

EPSILON = 0.05
LOWEST = -1e30
LOG2E = 1.0 / math.log(2.0)
TO_LOG2 = LOG2E / EPSILON
TO_POT = EPSILON / LOG2E

SRC = ("z", "x")
TGT = ("y", "c")
VMEM_LIMIT = 40 * 1024 * 1024


def log2(x):
    return jnp.log(x) * LOG2E


def repeated_onehot(labels):
    row_id = lax.broadcasted_iota(jnp.int32, (16, 1), 0)
    return jnp.where(row_id < 12, jnp.where(labels == row_id % CLASSES, 1.0, 0.0), 0.0)


def across(onehot, values):
    return lax.dot_general(
        onehot, values, (((1,), (1,)), ((), ())), preferred_element_type=jnp.float32
    )


def class_group(values, onehot, counts):
    part = lax.broadcasted_iota(jnp.int32, (16, 1), 0) // CLASSES
    wide = values.astype(jnp.float32)
    mean = across(onehot, values) / counts
    hi, mid, lo = three_parts(mean)
    parts = jnp.where(
        part == 0, hi, jnp.where(part == 1, mid, jnp.where(part == 2, lo, 0.0))
    ).astype(jnp.bfloat16)
    center = lax.dot_general(
        parts, onehot, (((0,), (0,)), ((), ())), preferred_element_type=jnp.float32
    )
    centered = wide - center
    hi, mid, lo = three_parts(centered * centered)
    spread = sum(across(onehot, p.astype(jnp.bfloat16)) for p in (hi, mid, lo))
    return jnp.where(part == 0, mean, spread)[:8], wide


def target_group_kernel(embed, labels, out_ref):
    onehot = repeated_onehot(labels[...])
    counts = jnp.maximum(jnp.sum(onehot, axis=1, keepdims=True), 1.0)
    group, _ = class_group(embed[...], onehot.astype(jnp.bfloat16), counts)
    peers = out_ref.shape[0]
    out_ref[...] = jnp.zeros(out_ref.shape, jnp.float32)
    out_ref[:, 0:8, 0 : group.shape[1]] = jnp.broadcast_to(group[None], (peers,) + group.shape)
    out_ref[:, 8:16, :] = jnp.broadcast_to(counts[None, :8], (peers, 8, LANES))


def source_group_kernel(embed, labels, out_ref, sq_ref):
    onehot = repeated_onehot(labels[...])
    counts = jnp.maximum(jnp.sum(onehot, axis=1, keepdims=True), 1.0)
    onehot = onehot.astype(jnp.bfloat16)
    sq = jnp.zeros((1, ROWS), jnp.float32)
    for c in range(WIDTH // LANES):
        group, wide = class_group(embed[c * LANES : (c + 1) * LANES, :], onehot, counts)
        out_ref[8 * c : 8 * c + 8, :] = group
        sq = sq + jnp.sum(wide * wide, axis=0, keepdims=True)
    out_ref[32:40, :] = jnp.broadcast_to(counts[:8], (8, LANES))
    sq_ref[...] = sq


def joined_counts(counts):
    total = functools.reduce(jnp.add, counts)
    return total, [c / total for c in counts]


def joined_group(groups, counts, shares):
    row_id = lax.broadcasted_iota(jnp.int32, (8, LANES), 0)
    mean = functools.reduce(jnp.add, [g * w for g, w in zip(groups, shares)])
    between = functools.reduce(
        jnp.add, [(g - mean) * (g - mean) * c for g, c in zip(groups, counts)]
    )
    spread = functools.reduce(jnp.add, groups) + pltpu.roll(between, 4, 0)
    return jnp.where(row_id < CLASSES, mean, spread)


def near_kernel(tgt_got, src_group, out_ref):
    peers = tgt_got.shape[0]
    counts = [tgt_got[k, 8:16, :] for k in range(peers)]
    total, shares = joined_counts(counts)
    group = joined_group([tgt_got[k, 0:8, :] for k in range(peers)], counts, shares)
    row_id = lax.broadcasted_iota(jnp.int32, (8, LANES), 0)
    group = jnp.where(row_id < CLASSES, group, group / total)
    for k in range(out_ref.shape[0]):
        out_ref[k, 0:40, :] = src_group[...]
        out_ref[k, 40:48, :] = group


def source_joined(got):
    peers = got.shape[0]
    counts = [got[k, 32:40, :] for k in range(peers)]
    total, shares = joined_counts(counts)
    groups = [
        joined_group([got[k, 8 * c : 8 * c + 8, :] for k in range(peers)], counts, shares)
        for c in range(WIDTH // LANES)
    ]
    return groups, total


def middle_kernel(part, got, out_ref):
    groups, total = source_joined(got)
    tgt = got[0, 40:48, :]
    for k in range(1, got.shape[0]):
        tgt = tgt + pltpu.roll(got[k, 40:48, :], k * part, 1)
    for k in range(out_ref.shape[0]):
        for c, group in enumerate(groups):
            out_ref[k, 8 * c : 8 * c + 8, :] = group
        out_ref[k, 32:40, :] = total
        out_ref[k, 40:48, :] = tgt


def label_kernel(part, got, src_sq, src_lab, label_ref, xa_ref):
    groups, total = source_joined(got)
    row_id = lax.broadcasted_iota(jnp.int32, (8, LANES), 0)
    lane_id = lax.broadcasted_iota(jnp.int32, (8, LANES), 1)
    each = LANES // part
    sides = ([], [])
    for c, group in enumerate(groups):
        tgt = got[each * c, 40:48, :]
        for k in range(1, each):
            tgt = tgt + pltpu.roll(got[each * c + k, 40:48, :], k * part, 1)
        for side, stat in zip(sides, (jnp.where(row_id < CLASSES, group, group / total), tgt)):
            side.append(jnp.where(row_id < CLASSES, stat, jnp.sqrt(stat + 1e-06)))

    def distances(one, other):
        out = jnp.zeros((8, LANES), jnp.float32)
        for k in range(CLASSES):
            far = jnp.zeros((8, LANES), jnp.float32)
            for g, h in zip(one, other):
                gap = g - jnp.where(row_id < CLASSES, h[k : k + 1], h[CLASSES + k : CLASSES + k + 1])
                far = far + gap * gap
            far = far + pltpu.roll(far, 4, 0)
            out = jnp.where(lane_id == k, jnp.sum(far, axis=1, keepdims=True), out)
        return out

    label_ref[...] = distances(*sides)[:CLASSES, :CLASSES]
    by_target = distances(*sides[::-1])
    by_target = jnp.concatenate([by_target, by_target], axis=0)
    row_id = lax.broadcasted_iota(jnp.int32, (16, 1), 0)
    part_id = row_id // CLASSES
    labels = src_lab[...]
    u = jnp.broadcast_to(src_sq[...], (16, ROWS))
    for a in range(CLASSES):
        u = u + jnp.where(labels == a, by_target[:, a : a + 1], 0.0)
    hi, mid, lo = three_parts(-0.5 * u)
    ones = jnp.where(row_id < 15, 1.0, 0.0)
    xa_ref[...] = jnp.where(
        part_id == 0, hi, jnp.where(part_id == 1, mid, jnp.where(part_id == 2, lo, ones))
    ).astype(jnp.bfloat16)


def spread_kernel(x, out_ref):
    for k in range(out_ref.shape[0]):
        out_ref[k] = x[...]


def three_parts(v):
    hi = v.astype(jnp.bfloat16).astype(jnp.float32)
    rest = v - hi
    mid = rest.astype(jnp.bfloat16).astype(jnp.float32)
    return hi, mid, rest - mid


def joined_lse(g_ref):
    g = g_ref[...]
    top = jnp.max(g, axis=0)
    return top + log2(jnp.sum(jnp.exp2(g - top[None]), axis=0))


def row_finish(top, total, out_ref):
    lines = []
    for k in range(CHUNKS):
        at = pl.ds(k * LANES, LANES)
        lse = top[at, :] + log2(jnp.sum(total[at, :], axis=1, keepdims=True))
        lines.append(lse.T[0:1, :])
    line = jnp.concatenate(lines, axis=0)
    out_ref[...] = jnp.broadcast_to(line[None], out_ref.shape)


def widen_top(top):
    for k in range(CHUNKS):
        at = pl.ds(k * LANES, LANES)
        top[at, :] = jnp.broadcast_to(jnp.max(top[at, :], axis=1, keepdims=True), (LANES, LANES))


def over_pairs(count, body, unroll):
    def several(step, _):
        for k in range(unroll):
            body(step * unroll + k)
        return 0

    steps = (count[0] + UNROLL - 1) // UNROLL * (UNROLL // unroll)
    lax.fori_loop(0, steps, several, 0)


def block_at(pairs, index):
    row = pl.multiple_of(pairs[2 * index] * BLOCK, BLOCK)
    return row, pairs[2 * index + 1]


def cost_kernel(pairs, count, xa, xt, y, tgt_lab, tiles, out_ref, ya, top, total):
    row_id = lax.broadcasted_iota(jnp.int32, (16, 1), 0)
    part = row_id // CLASSES
    cls = row_id % CLASSES

    def square(k, acc):
        v = y[pl.ds(pl.multiple_of(k * 16, 16), 16), :].astype(jnp.float32)
        return acc + v * v

    tgt_sq = lax.fori_loop(0, WIDTH // 16, square, jnp.zeros((16, ROWS), jnp.float32))
    hi, mid, lo = three_parts(-0.5 * jnp.sum(tgt_sq, axis=0, keepdims=True))
    onehot = jnp.where(tgt_lab[...] == cls, 1.0, 0.0)
    ya[...] = jnp.where(
        part < 3,
        onehot,
        jnp.where(cls == 0, hi, jnp.where(cls == 1, mid, jnp.where(cls == 2, lo, 0.0))),
    ).astype(jnp.bfloat16)

    top[...] = jnp.full(top.shape, LOWEST, jnp.float32)
    total[...] = jnp.zeros(total.shape, jnp.float32)

    def build(index):
        row, col = block_at(pairs, index)
        rows = pl.ds(row, BLOCK)
        cols = pl.ds(pl.multiple_of(col * BLOCK, BLOCK), BLOCK)
        cross = jnp.dot(xt[rows, :], y[:, cols], preferred_element_type=jnp.float32)
        extra = lax.dot_general(
            xa[:, rows], ya[:, cols], (((0,), (0,)), ((), ())), preferred_element_type=jnp.float32
        )
        tile = (cross + extra) * (2.0 * TO_LOG2) + jnp.where(index < count[0], 0.0, LOWEST)
        tiles[index] = tile
        top[rows, :] = jnp.maximum(top[rows, :], jnp.maximum(tile[:, :LANES], tile[:, LANES:]))

    over_pairs(count, build, 2)
    widen_top(top)

    def add(index):
        row, _ = block_at(pairs, index)
        rows = pl.ds(row, BLOCK)
        high = top[rows, :]
        left = jnp.exp2(tiles[index, :, :LANES] - high)
        right = jnp.exp2(tiles[index, :, LANES:] - high)
        total[rows, :] = total[rows, :] + (left + right)

    over_pairs(count, add, 4)
    row_finish(top, total, out_ref)


def row_kernel(log_total, pairs, count, tiles, g_ref, out_ref, pot, top, total):
    pot[...] = log_total - joined_lse(g_ref)
    top[...] = jnp.full(top.shape, LOWEST, jnp.float32)
    total[...] = jnp.zeros(total.shape, jnp.float32)

    def scores(index, col):
        left = tiles[index, :, :LANES] + pot[pl.ds(2 * col, 1), :]
        right = tiles[index, :, LANES:] + pot[pl.ds(2 * col + 1, 1), :]
        return left, right

    def highest(index):
        row, col = block_at(pairs, index)
        rows = pl.ds(row, BLOCK)
        left, right = scores(index, col)
        top[rows, :] = jnp.maximum(top[rows, :], jnp.maximum(left, right))

    over_pairs(count, highest, 4)
    widen_top(top)

    def add(index):
        row, col = block_at(pairs, index)
        rows = pl.ds(row, BLOCK)
        left, right = scores(index, col)
        high = top[rows, :]
        total[rows, :] = total[rows, :] + (jnp.exp2(left - high) + jnp.exp2(right - high))

    over_pairs(count, add, 4)
    row_finish(top, total, out_ref)


def col_kernel(log_total, pairs, count, tiles, g_ref, out_ref, pot_ref, pot, top, total):
    line = log_total - joined_lse(g_ref)
    pot_ref[...] = line * TO_POT
    for k in range(CHUNKS):
        pot[pl.ds(k * LANES, LANES), :] = jnp.broadcast_to(line[k : k + 1, :], (LANES, LANES)).T
    top[...] = jnp.full(top.shape, LOWEST, jnp.float32)
    total[...] = jnp.zeros(total.shape, jnp.float32)

    def scores(index, row):
        rows = pl.ds(row, BLOCK)
        high = pot[rows, :]
        tile = tiles[index]
        return tile + jnp.concatenate([high, high], axis=1)

    def highest(index):
        row, col = block_at(pairs, index)
        score = scores(index, row)
        top[col] = jnp.maximum(top[col], jnp.max(score.reshape(BLOCK // 8, 8, BLOCK), axis=0))

    over_pairs(count, highest, 4)
    for k in range(BLK):
        top[k] = jnp.broadcast_to(jnp.max(top[k], axis=0, keepdims=True), (8, BLOCK))

    def add(index):
        row, col = block_at(pairs, index)
        score = scores(index, row).reshape(BLOCK // 8, 8, BLOCK)
        total[col] = total[col] + jnp.sum(jnp.exp2(score - top[col][None]), axis=0)

    over_pairs(count, add, 4)
    lines = []
    for k in range(BLK):
        lse = top[k][0:1] + log2(jnp.sum(total[k], axis=0, keepdims=True))
        lines += [lse[:, :LANES], lse[:, LANES:]]
    out = jnp.concatenate(lines, axis=0)
    out_ref[...] = jnp.broadcast_to(out[None], out_ref.shape)


def last_kernel(log_total, g_ref, pot_ref):
    pot_ref[...] = (log_total - joined_lse(g_ref)) * TO_POT


def smem():
    return pl.BlockSpec(memory_space=pltpu.SMEM)


def vmem():
    return pl.BlockSpec(memory_space=pltpu.VMEM)


def f32(*shape):
    return jax.ShapeDtypeStruct(shape, jnp.float32)


def params():
    return pltpu.CompilerParams(vmem_limit_bytes=VMEM_LIMIT)


def on_device(source_embed, target_embed, source_labels, target_labels, pair_blocks, pair_count):
    pairs = pair_blocks.reshape(-1)
    count = pair_count.reshape(-1)
    n_src, n_tgt = lax.axis_size(SRC), lax.axis_size(TGT)

    def call(kernel, out_shape, *args, name):
        return pl.pallas_call(
            kernel,
            out_shape=out_shape,
            in_specs=[vmem()] * len(args),
            out_specs=jax.tree.map(lambda _: vmem(), out_shape),
            compiler_params=params(),
            name=name,
        )(*args)

    n_x, n_z = lax.axis_size("x"), lax.axis_size("z")
    part = target_embed.shape[0]
    near = call(
        spread_kernel,
        jax.ShapeDtypeStruct((n_x,) + target_embed.shape, jnp.bfloat16),
        target_embed,
        name="spread",
    )
    tgt_group = call(
        target_group_kernel,
        f32(n_tgt, 16, LANES),
        target_embed,
        target_labels[None],
        name="target_group",
    )
    near = lax.all_to_all(near, "x", 0, 0)
    near, source_embed, tgt_group = lax.optimization_barrier((near, source_embed, tgt_group))
    target_full = lax.all_gather(near.reshape(-1, ROWS), "z", axis=0, tiled=True)

    tgt_got = lax.all_to_all(tgt_group, TGT, 0, 0)
    src_group, src_sq = call(
        source_group_kernel,
        (f32(40, LANES), f32(1, ROWS)),
        source_embed,
        source_labels[None],
        name="source_group",
    )
    stats = call(near_kernel, f32(n_x, 48, LANES), tgt_got, src_group, name="near")
    stats = lax.all_to_all(stats, "x", 0, 0)
    stats = call(
        functools.partial(middle_kernel, part), f32(n_z, 48, LANES), stats, name="middle"
    )
    stats = lax.all_to_all(stats, "z", 0, 0)
    label_cost, xa = call(
        functools.partial(label_kernel, part * n_x),
        (f32(CLASSES, CLASSES), jax.ShapeDtypeStruct((16, ROWS), jnp.bfloat16)),
        stats,
        src_sq,
        source_labels[None],
        name="label",
    )

    tall = pltpu.VMEM((ROWS, LANES), jnp.float32)
    wide = pltpu.VMEM((BLK, 8, BLOCK), jnp.float32)
    log_src = math.log2(ROWS * n_src)
    log_tgt = math.log2(ROWS * n_tgt)
    tiles, sent = pl.pallas_call(
        cost_kernel,
        out_shape=(f32(MAXP, BLOCK, BLOCK), f32(n_tgt, CHUNKS, LANES)),
        in_specs=[smem(), smem(), vmem(), vmem(), vmem(), vmem()],
        out_specs=(vmem(), vmem()),
        scratch_shapes=[
            pltpu.VMEM((16, ROWS), jnp.bfloat16),
            tall,
            tall,
        ],
        compiler_params=params(),
        name="cost_rows",
    )(
        pairs,
        count,
        xa,
        source_embed.T,
        target_full,
        target_labels[None],
    )

    def columns(got):
        return pl.pallas_call(
            functools.partial(col_kernel, log_tgt),
            out_shape=(f32(n_src, CHUNKS, LANES), f32(CHUNKS, LANES)),
            in_specs=[smem(), smem(), vmem(), vmem()],
            out_specs=(vmem(), vmem()),
            scratch_shapes=[tall, wide, wide],
            compiler_params=params(),
            name="columns",
        )(pairs, count, tiles, got)

    def rows(got):
        return pl.pallas_call(
            functools.partial(row_kernel, log_src),
            out_shape=f32(n_tgt, CHUNKS, LANES),
            in_specs=[smem(), smem(), vmem(), vmem()],
            out_specs=vmem(),
            scratch_shapes=[pltpu.VMEM((CHUNKS, LANES), jnp.float32), tall, tall],
            compiler_params=params(),
            name="rows",
        )(pairs, count, tiles, got)

    sent, _ = columns(lax.all_to_all(sent, TGT, 0, 0))
    sent = rows(lax.all_to_all(sent, SRC, 0, 0))
    sent, src_pot = columns(lax.all_to_all(sent, TGT, 0, 0))
    tgt_pot = pl.pallas_call(
        functools.partial(last_kernel, log_src),
        out_shape=f32(CHUNKS, LANES),
        in_specs=[vmem()],
        out_specs=vmem(),
        compiler_params=params(),
        name="last",
    )(lax.all_to_all(sent, SRC, 0, 0))
    return (src_pot.reshape(-1), tgt_pot.reshape(-1), label_cost)


def solution(mesh):
    fine = Mesh(np.asarray(mesh.devices).reshape(8, 4, 4, 2), SRC + TGT)
    return jax.shard_map(
        on_device,
        mesh=fine,
        in_specs=(
            P(None, SRC),
            P(SRC, TGT),
            P(SRC),
            P(TGT),
            P(SRC, TGT, None, None),
            P(SRC, TGT),
        ),
        out_specs=(P(SRC), P(TGT), P()),
        check_vma=False,
    )
```

time: 162 us -> 145 us (0.90)
  matrix products: 13.5 us -> 0 us
  Pallas kernels: 16.1 us -> 22.3 us
  blocking collectives: 68.3 us -> 63.8 us
  other arithmetic: 4.46 us -> 0 us
    dot_general x6 -> x0, matrix products: 13.5 us -> none  [the longest x2 5.62 us: local_moments(): centered = values - jnp.dot(means.T, onehot, precision=HIGHEST)]
    all_gather x1, waiting for transfers between devices: 11.3 us -> 3.74 us  [on_device(): lax.all_gather(near.reshape(-1, ROWS), 'z', axis=0, tiled=True)]
    all_to_all x3, waiting for transfers between devices: 4.51 us -> 11.8 us  [the longest x1 7.88 us: on_device(): stats = lax.all_to_all(stats, 'z', 0, 0)]
    pallas_call x0 -> x6, Pallas kernels: none -> 7.09 us  [call(): pl.pallas_call(kernel, out_shape=out_shape, in_specs=[vmem()] * len(args)...]
    reduce_sum x13 -> x0, other arithmetic: 4.09 us -> none  [the longest x1 2.05 us: on_device(): src_sq = jnp.sum(src_values * src_values, axis=0)]
    all_to_all x1, blocking collectives: 13.5 us -> 9.7 us  [on_device(): sent, _ = columns(lax.all_to_all(sent, TGT, 0, 0))]
    broadcast_in_dim x4 -> x0, local copies, waits for them, and re-layouts: 3.02 us -> none  [shared(): return lax.all_to_all(jnp.broadcast_to(x[None], (n,) + x.shape), axis, 0, 0)]
    optimization_barrier x0 -> x1, local copies, waits for them, and re-layouts: none -> 2.88 us  [on_device(): lax.optimization_barrier((near, source_embed, tgt_group))]
  transfers between devices with their start and end apart: 4 -> 4, of which waited for: 3 -> 3; matrix products, arithmetic and copies ran while one was open for 15% -> 2% of each run, Pallas kernels for 0% -> 4%
where the time goes in v2:
time: 145 us; the launch traced here: 144 us
  blocking collectives  63.8 us (44%)
  Pallas kernels  22.3 us (15%)
  starting transfers between devices  17.5 us (12%)
  waiting for transfers between devices  15.5 us (11%)
  between operations  14.7 us (10%)
  local copies, waits for them, and re-layouts  10 us (7%)
    all_to_all x1, blocking collectives, on_device(): sent = rows(lax.all_to_all(sent, SRC, 0, 0))  20.9 us
    all_to_all x1, blocking collectives, on_device(): lax.all_to_all(sent, SRC, 0, 0)  16.9 us
    all_to_all x1, blocking collectives, on_device(): sent, _ = columns(lax.all_to_all(sent, TGT, 0, 0))  9.7 us
    all_to_all x1, starting transfers between devices, on_device(): stats = lax.all_to_all(stats, 'z', 0, 0)  8.57 us
    all_to_all x1, blocking collectives, on_device(): stats = lax.all_to_all(stats, 'x', 0, 0)  8.24 us
    all_to_all x1, blocking collectives, on_device(): sent, src_pot = columns(lax.all_to_all(sent, TGT, 0, 0))  7.99 us
    all_to_all x1, waiting for transfers between devices, on_device(): stats = lax.all_to_all(stats, 'z', 0, 0)  7.88 us
    pallas_call x6, Pallas kernels, call(): pl.pallas_call(kernel, out_shape=out_shape, in_specs=[vmem()] * len(args)...  7.09 us
  transfers between devices with their start and end apart: 4, of which 3 were waited for; matrix products, arithmetic and copies ran while one was open for 2% of the time, Pallas kernels for 4%

profile of v2, /device:TPU:32, one launch (start us, length us, event | category | flops | bytes accessed | tf_op | source)
XLA Modules:
  0.0 143.8 jit_solution(8073651405515850791)
XLA Ops:
  7.2 0.0 copy-start.2
  7.2 0.8 copy-done.2
  8.0 0.7 spread.1
  8.7 0.0 copy-start.9
  8.7 4.4 %all-to-all-start = ((bf16[4,16,2048]{2,1,0:T(8,128)(2,1)}), bf16[4,16,2048]{2,1,0:T(8,128)(2,1)S(1)}, u32[]{:S(2)}, u32[]{:S(2)}) async-start(bf16[4,16,2048]{2,1,0:T(8,128)(2,1)} %spread.1), calls=%async_computation | async-start | bytes 524288 | tf_op jit(solution)/shard_map/all_to_all | solution.py:392
  13.1 0.0 all-gather.2.cloned.1.call-start
  13.2 0.0 copy-start.3
  13.2 0.8 copy-done.3
  14.0 0.0 copy-start.4
  14.0 0.7 copy-done.4
  14.7 1.2 target_group.1
  15.9 3.9 %all-to-all-done = bf16[4,16,2048]{2,1,0:T(8,128)(2,1)S(1)} async-done(((bf16[4,16,2048]{2,1,0:T(8,128)(2,1)}), bf16[4,16,2048]{2,1,0:T(8,128)(2,1)S(1)}, u32[]{:S(2)}, u32[]{:S(2)}) %all-to-all-start) | async-done | bytes 262176 | tf_op jit(solution)/shard_map/all_to_all | solution.py:392
  19.8 0.0 copy-start.8
  19.8 0.7 copy-done.8
  20.5 0.0 all-gather.2.cloned.1.call-update
  20.6 4.5 %all-to-all-start.1 = ((f32[8,16,128]{2,1,0:T(8,128)}), f32[8,16,128]{2,1,0:T(8,128)S(1)}, u32[]{:S(2)}, u32[]{:S(2)}) async-start(f32[8,16,128]{2,1,0:T(8,128)} %target_group.1), calls=%async_computation.1 | async-start | bytes 131072 | tf_op jit(solution)/shard_map/all_to_all | solution.py:396
  25.0 0.0 copy-start
  25.0 1.6 %copy-done = bf16[512,2048]{1,0:T(8,128)(2,1)S(1)} copy-done((bf16[512,2048]{1,0:T(8,128)(2,1)S(1)}, bf16[512,2048]{1,0:T(8,128)(2,1)}, u32[]{:S(2)}) %copy-start) | copy-done | bytes 2097176
  26.6 0.0 copy-start.6
  26.6 0.7 copy-done.6
  27.3 3.5 %source_group.1 = (f32[40,128]{1,0:T(8,128)S(1)}, f32[1,2048]{1,0:T(1,128)S(1)}) custom-call(bf16[512,2048]{1,0:T(8,128)(2,1)S(1)} %copy-done, s32[1,2048]{1,0:T(1,128)S(1)} %bitcast.16), custom_call_target="tpu_custom_call" | custom-call | tf_op jit(solution)/shard_map/source_group/pallas_call | solution.py:368
  30.8 0.0 all-to-all-done.1.tgt_got
  30.8 8.2 %all_to_all.40.got = f32[4,48,128]{2,1,0:T(8,128)S(1)} all-to-all(f32[4,48,128]{2,1,0:T(8,128)S(1)} %near.1), channel_id=1, replica_groups=mesh['z'=8,'x'=4,'y'=4,'c'=2] {'x'}, dimensions={0} | all-to-all | bytes 196608 | tf_op jit(solution)/shard_map/all_to_all | solution.py:405
  39.1 0.7 middle.1
  39.8 8.6 %all-to-all-start.3 = ((f32[8,48,128]{2,1,0:T(8,128)}), f32[8,48,128]{2,1,0:T(8,128)S(1)}, u32[]{:S(2)}, u32[]{:S(2)}) async-start(f32[8,48,128]{2,1,0:T(8,128)} %middle.1), calls=%async_computation.3 | async-start | bytes 393216 | tf_op jit(solution)/shard_map/all_to_all | solution.py:409
  49.0 0.0 copy-done.9
  49.1 0.1 copy.11
  49.1 0.1 reshape.21.pairs
  49.2 0.0 copy-start.7
  49.2 0.0 copy-start.5
  49.3 2.9 %copy.12 = bf16[512,2048]{0,1:T(8,128)(2,1)S(1)} copy(bf16[512,2048]{1,0:T(8,128)(2,1)} %embed.2) | data formatting | bytes 4194304 | tf_op jit(solution)/shard_map/optimization_barrier | solution.py:393
  52.1 7.9 %all-to-all-done.3.got = f32[8,48,128]{2,1,0:T(8,128)S(1)} async-done(((f32[8,48,128]{2,1,0:T(8,128)}), f32[8,48,128]{2,1,0:T(8,128)S(1)}, u32[]{:S(2)}, u32[]{:S(2)}) %all-to-all-start.3) | async-done | bytes 196640 | tf_op jit(solution)/shard_map/all_to_all | solution.py:409
  60.0 0.0 copy-done.7
  60.0 0.9 label.1
  60.9 3.7 %all-gather.2.cloned.1.call-done.y = bf16[512,2048]{1,0:T(8,128)(2,1)} async-done(((bf16[64,2048]{1,0:T(8,128)(2,1)}), bf16[512,2048]{1,0:T(8,128)(2,1)}) %all-gather.2.cloned.1.call-update) | async-done | bytes 2097168 | tf_op jit(solution)/shard_map/all_gather | solution.py:394
  64.7 0.0 copy-done.5
  64.7 0.0 copy-start.1
  64.7 1.6 %copy-done.1 = bf16[512,2048]{1,0:T(8,128)(2,1)S(1)} copy-done((bf16[512,2048]{1,0:T(8,128)(2,1)S(1)}, bf16[512,2048]{1,0:T(8,128)(2,1)}, u32[]{:S(2)}) %copy-start.1) | copy-done | bytes 2097176
  66.3 6.4 %cost_rows.1 = (f32[24,256,256]{2,1,0:T(8,128)S(1)}, f32[8,16,128]{2,1,0:T(8,128)S(1)}) custom-call(s32[48]{0:T(128)S(1)} %reshape.21.pairs, s32[1]{0:T(128)} %bitcast.9.count, bf16[16,2048]{1,0:T(8,128)(2,1)S(1)} %get-tuple-element.19.xa, bf16[2048,512]{1,0:T(8,128)(2,1)S(1)} %bitcast.13, bf16[512,2048]{1,0:T(8,128)(2,1)S(1)} %copy-done.1, ...), custom_call_target="tpu_custom_call" | custom-call | tf_op jit(solution)/shard_map/cost_rows/pallas_call | solution.py:423
  72.6 9.7 %all_to_all.41.g_ref = f32[8,16,128]{2,1,0:T(8,128)S(1)} all-to-all(f32[8,16,128]{2,1,0:T(8,128)S(1)} %get-tuple-element.22), channel_id=1, replica_groups=mesh['z'=8,'x'=4,'y'=4,'c'=2] {'y','c'}, dimensions={0} | all-to-all | bytes 131072 | tf_op jit(solution)/shard_map/all_to_all | solution.py:466
  82.3 2.5 %columns.2 = (f32[32,16,128]{2,1,0:T(8,128)S(1)}, f32[16,128]{1,0:T(8,128)}) custom-call(s32[48]{0:T(128)S(1)} %reshape.21.pairs, s32[1]{0:T(128)} %bitcast.10.count, f32[24,256,256]{2,1,0:T(8,128)S(1)} %get-tuple-element.21.tiles, f32[8,16,128]{2,1,0:T(8,128)S(1)} %all_to_all.41.g_ref), custom_call_target="tpu_custom_call" | custom-call | tf_op jit(solution)/shard_map/columns/pallas_call | solution.py:445
  84.8 20.9 %all_to_all.42.g_ref = f32[32,16,128]{2,1,0:T(8,128)S(1)} all-to-all(f32[32,16,128]{2,1,0:T(8,128)S(1)} %get-tuple-element.23), channel_id=1, replica_groups=mesh['z'=8,'x'=4,'y'=4,'c'=2] {'z','x'}, dimensions={0} | all-to-all | bytes 524288 | tf_op jit(solution)/shard_map/all_to_all | solution.py:467
  105.7 3.2 %rows.1 = f32[8,16,128]{2,1,0:T(8,128)S(1)} custom-call(s32[48]{0:T(128)S(1)} %reshape.21.pairs, s32[1]{0:T(128)} %bitcast.11.count, f32[24,256,256]{2,1,0:T(8,128)S(1)} %get-tuple-element.21.tiles, f32[32,16,128]{2,1,0:T(8,128)S(1)} %all_to_all.42.g_ref), custom_call_target="tpu_custom_call" | custom-call | tf_op jit(solution)/shard_map/rows/pallas_call | solution.py:456
  108.9 8.0 %all_to_all.43.g_ref = f32[8,16,128]{2,1,0:T(8,128)S(1)} all-to-all(f32[8,16,128]{2,1,0:T(8,128)S(1)} %rows.1), channel_id=1, replica_groups=mesh['z'=8,'x'=4,'y'=4,'c'=2] {'y','c'}, dimensions={0} | all-to-all | bytes 131072 | tf_op jit(solution)/shard_map/all_to_all | solution.py:468
  116.9 2.5 %columns.3 = (f32[32,16,128]{2,1,0:T(8,128)S(1)}, f32[16,128]{1,0:T(8,128)}) custom-call(s32[48]{0:T(128)S(1)} %reshape.21.pairs, s32[1]{0:T(128)} %bitcast.12.count, f32[24,256,256]{2,1,0:T(8,128)S(1)} %get-tuple-element.21.tiles, f32[8,16,128]{2,1,0:T(8,128)S(1)} %all_to_all.43.g_ref), custom_call_target="tpu_custom_call" | custom-call | tf_op jit(solution)/shard_map/columns/pallas_call | solution.py:445
  119.4 16.9 %all_to_all.44.g_ref = f32[32,16,128]{2,1,0:T(8,128)S(1)} all-to-all(f32[32,16,128]{2,1,0:T(8,128)S(1)} %get-tuple-element.25), channel_id=1, replica_groups=mesh['z'=8,'x'=4,'y'=4,'c'=2] {'z','x'}, dimensions={0} | all-to-all | bytes 524288 | tf_op jit(solution)/shard_map/all_to_all | solution.py:476
  136.3 0.7 last.1
  (1 shorter events, 0.0 us)
Async XLA Ops:
  7.2 0.8 copy-start.2
  8.7 40.3 %copy-start.9 = (s32[1,1,24,2]{2,3,1,0:T(2,128)S(1)}, s32[1,1,24,2]{2,3,1,0:T(2,128)}, u32[]{:S(2)}) copy-start(s32[1,1,24,2]{2,3,1,0:T(2,128)} %param.10) | copy-start | bytes 580
  8.7 11.1 %all-to-all-start = ((bf16[4,16,2048]{2,1,0:T(8,128)(2,1)}), bf16[4,16,2048]{2,1,0:T(8,128)(2,1)S(1)}, u32[]{:S(2)}, u32[]{:S(2)}) async-start(bf16[4,16,2048]{2,1,0:T(8,128)(2,1)} %spread.1), calls=%async_computation | async-start | bytes 524288 | tf_op jit(solution)/shard_map/all_to_all | solution.py:392
  13.1 51.5 %all-gather.2.cloned.1.call-start = ((), (), s32[]{:S(2)}) async-start(), calls=%async_computation.8 | async-start | bytes 2359296 | tf_op jit(solution)/shard_map/all_gather | solution.py:394
  13.2 0.8 copy-start.3
  14.0 0.7 copy-start.4
  19.8 0.7 copy-start.8
  20.6 10.2 %all-to-all-start.1 = ((f32[8,16,128]{2,1,0:T(8,128)}), f32[8,16,128]{2,1,0:T(8,128)S(1)}, u32[]{:S(2)}, u32[]{:S(2)}) async-start(f32[8,16,128]{2,1,0:T(8,128)} %target_group.1), calls=%async_computation.1 | async-start | bytes 131072 | tf_op jit(solution)/shard_map/all_to_all | solution.py:396
  25.0 1.6 %copy-start = (bf16[512,2048]{1,0:T(8,128)(2,1)S(1)}, bf16[512,2048]{1,0:T(8,128)(2,1)}, u32[]{:S(2)}) copy-start(bf16[512,2048]{1,0:T(8,128)(2,1)} %embed.2) | copy-start | bytes 6291460
  26.6 0.7 copy-start.6
  39.8 20.2 %all-to-all-start.3 = ((f32[8,48,128]{2,1,0:T(8,128)}), f32[8,48,128]{2,1,0:T(8,128)S(1)}, u32[]{:S(2)}, u32[]{:S(2)}) async-start(f32[8,48,128]{2,1,0:T(8,128)} %middle.1), calls=%async_computation.3 | async-start | bytes 393216 | tf_op jit(solution)/shard_map/all_to_all | solution.py:409
  49.2 10.8 %copy-start.7 = (s32[2048]{0:T(1024)S(1)}, s32[2048]{0:T(1024)}, u32[]{:S(2)}) copy-start(s32[2048]{0:T(1024)} %param.8) | copy-start | bytes 24580
  49.2 15.4 %copy-start.5 = (s32[2048]{0:T(1024)S(1)}, s32[2048]{0:T(1024)}, u32[]{:S(2)}) copy-start(s32[2048]{0:T(1024)} %param.9) | copy-start | bytes 24580
  64.7 1.6 %copy-start.1 = (bf16[512,2048]{1,0:T(8,128)(2,1)S(1)}, bf16[512,2048]{1,0:T(8,128)(2,1)}, u32[]{:S(2)}) copy-start(bf16[512,2048]{1,0:T(8,128)(2,1)} %all-gather.2.cloned.1.call-done.y) | copy-start | bytes 6291460
Sparse Core Ops, SparseCore 0:
  20.7 43.9 all-gather.1

commit v3 on v2

--- a/solution.py
+++ b/solution.py
@@ -27,7 +27,7 @@
 
 SRC = ("z", "x")
 TGT = ("y", "c")
-VMEM_LIMIT = 40 * 1024 * 1024
+VMEM_LIMIT = 24 * 1024 * 1024
 
 
 def log2(x):
@@ -123,28 +123,30 @@
     return groups, total
 
 
-def middle_kernel(part, got, out_ref):
+def middle_kernel(width, got, out_ref):
     groups, total = source_joined(got)
-    tgt = got[0, 40:48, :]
-    for k in range(1, got.shape[0]):
-        tgt = tgt + pltpu.roll(got[k, 40:48, :], k * part, 1)
+    each = LANES // width
+    for c in range(WIDTH // LANES):
+        tgt = got[each * c, 40:48, :]
+        for k in range(1, each):
+            tgt = tgt + pltpu.roll(got[each * c + k, 40:48, :], k * width, 1)
+        for k in range(out_ref.shape[0]):
+            out_ref[k, 8 * c : 8 * c + 8, :] = groups[c]
+            out_ref[k, 40 + 8 * c : 48 + 8 * c, :] = tgt
     for k in range(out_ref.shape[0]):
-        for c, group in enumerate(groups):
-            out_ref[k, 8 * c : 8 * c + 8, :] = group
         out_ref[k, 32:40, :] = total
-        out_ref[k, 40:48, :] = tgt
 
 
 def label_kernel(part, got, src_sq, src_lab, label_ref, xa_ref):
     groups, total = source_joined(got)
     row_id = lax.broadcasted_iota(jnp.int32, (8, LANES), 0)
     lane_id = lax.broadcasted_iota(jnp.int32, (8, LANES), 1)
-    each = LANES // part
     sides = ([], [])
     for c, group in enumerate(groups):
-        tgt = got[each * c, 40:48, :]
-        for k in range(1, each):
-            tgt = tgt + pltpu.roll(got[each * c + k, 40:48, :], k * part, 1)
+        at = slice(40 + 8 * c, 48 + 8 * c)
+        tgt = got[0, at, :]
+        for k in range(1, got.shape[0]):
+            tgt = tgt + pltpu.roll(got[k, at, :], k * part, 1)
         for side, stat in zip(sides, (jnp.where(row_id < CLASSES, group, group / total), tgt)):
             side.append(jnp.where(row_id < CLASSES, stat, jnp.sqrt(stat + 1e-06)))
 
@@ -224,16 +226,20 @@
     return row, pairs[2 * index + 1]
 
 
-def cost_kernel(pairs, count, xa, xt, y, tgt_lab, tiles, out_ref, ya, top, total):
+def cost_kernel(n_x, pairs, count, place, xa, xt, *args):
+    pieces, (tgt_lab, tiles, out_ref, y, ya, top, total) = args[:n_x], args[n_x:]
     row_id = lax.broadcasted_iota(jnp.int32, (16, 1), 0)
     part = row_id // CLASSES
     cls = row_id % CLASSES
 
-    def square(k, acc):
-        v = y[pl.ds(pl.multiple_of(k * 16, 16), 16), :].astype(jnp.float32)
-        return acc + v * v
-
-    tgt_sq = lax.fori_loop(0, WIDTH // 16, square, jnp.zeros((16, ROWS), jnp.float32))
+    tgt_sq = jnp.zeros((16, ROWS), jnp.float32)
+    for far, piece in enumerate(pieces):
+        at = lax.rem(place[0] + far, n_x)
+        for k in range(piece.shape[0]):
+            y[pl.ds(pl.multiple_of((k * n_x + at) * 16, 16), 16), :] = piece[k]
+            v = piece[k].astype(jnp.float32)
+            tgt_sq = tgt_sq + v * v
+
     hi, mid, lo = three_parts(-0.5 * jnp.sum(tgt_sq, axis=0, keepdims=True))
     onehot = jnp.where(tgt_lab[...] == cls, 1.0, 0.0)
     ya[...] = jnp.where(
@@ -378,7 +384,7 @@
     part = target_embed.shape[0]
     near = call(
         spread_kernel,
-        jax.ShapeDtypeStruct((n_x,) + target_embed.shape, jnp.bfloat16),
+        jax.ShapeDtypeStruct((n_z,) + target_embed.shape, jnp.bfloat16),
         target_embed,
         name="spread",
     )
@@ -389,9 +395,12 @@
         target_labels[None],
         name="target_group",
     )
-    near = lax.all_to_all(near, "x", 0, 0)
-    near, source_embed, tgt_group = lax.optimization_barrier((near, source_embed, tgt_group))
-    target_full = lax.all_gather(near.reshape(-1, ROWS), "z", axis=0, tiled=True)
+    near = lax.all_to_all(near, "z", 0, 0)
+    near, tgt_group = lax.optimization_barrier((near, tgt_group))
+    pieces = [near] + [
+        lax.ppermute(near, "x", [((i + far) % n_x, i) for i in range(n_x)])
+        for far in range(1, n_x)
+    ]
 
     tgt_got = lax.all_to_all(tgt_group, TGT, 0, 0)
     src_group, src_sq = call(
@@ -401,14 +410,14 @@
         source_labels[None],
         name="source_group",
     )
-    stats = call(near_kernel, f32(n_x, 48, LANES), tgt_got, src_group, name="near")
+    stats = call(near_kernel, f32(n_z, 48, LANES), tgt_got, src_group, name="near")
+    stats = lax.all_to_all(stats, "z", 0, 0)
+    stats = call(
+        functools.partial(middle_kernel, part * n_x), f32(n_x, 72, LANES), stats, name="middle"
+    )
     stats = lax.all_to_all(stats, "x", 0, 0)
-    stats = call(
-        functools.partial(middle_kernel, part), f32(n_z, 48, LANES), stats, name="middle"
-    )
-    stats = lax.all_to_all(stats, "z", 0, 0)
     label_cost, xa = call(
-        functools.partial(label_kernel, part * n_x),
+        functools.partial(label_kernel, part),
         (f32(CLASSES, CLASSES), jax.ShapeDtypeStruct((16, ROWS), jnp.bfloat16)),
         stats,
         src_sq,
@@ -421,11 +430,12 @@
     log_src = math.log2(ROWS * n_src)
     log_tgt = math.log2(ROWS * n_tgt)
     tiles, sent = pl.pallas_call(
-        cost_kernel,
+        functools.partial(cost_kernel, n_x),
         out_shape=(f32(MAXP, BLOCK, BLOCK), f32(n_tgt, CHUNKS, LANES)),
-        in_specs=[smem(), smem(), vmem(), vmem(), vmem(), vmem()],
+        in_specs=[smem()] * 3 + [vmem()] * (3 + n_x),
         out_specs=(vmem(), vmem()),
         scratch_shapes=[
+            pltpu.VMEM((WIDTH, ROWS), jnp.bfloat16),
             pltpu.VMEM((16, ROWS), jnp.bfloat16),
             tall,
             tall,
@@ -435,9 +445,10 @@
     )(
         pairs,
         count,
+        lax.axis_index("x").reshape(1),
         xa,
         source_embed.T,
-        target_full,
+        *pieces,
         target_labels[None],
     )
 

time: 145 us -> 137 us (0.945)
  between operations: 14.7 us -> 1.38 us
  blocking collectives: 63.8 us -> 68.4 us
  starting transfers between devices: 17.5 us -> 22 us
  local copies, waits for them, and re-layouts: 10 us -> 7.73 us
    ppermute x0 -> x3, starting transfers between devices: none -> 5.65 us  [on_device(): lax.ppermute(near, 'x', [((i + far) % n_x, i) for i in range(n_x)])]
    all_to_all x1, blocking collectives: 8.24 us -> 13.8 us  [on_device(): stats = lax.all_to_all(stats, 'z', 0, 0)]
    all_to_all x2, waiting for transfers between devices: 11.8 us -> 15.5 us  [the longest x1 13.3 us: on_device(): near = lax.all_to_all(near, 'z', 0, 0)]
    all_gather x1 -> x0, waiting for transfers between devices: 3.74 us -> none  [on_device(): lax.all_gather(near.reshape(-1, ROWS), 'z', axis=0, tiled=True)]
    optimization_barrier x1 -> x0, local copies, waits for them, and re-layouts: 2.88 us -> none  [on_device(): lax.optimization_barrier((near, source_embed, tgt_group))]
    all_to_all x1, blocking collectives: 20.9 us -> 18.4 us  [on_device(): sent = rows(lax.all_to_all(sent, SRC, 0, 0))]
    unnamed x21 -> x18, local copies, waits for them, and re-layouts: 7.05 us -> 7.63 us
  transfers between devices with their start and end apart: 4 -> 6, of which waited for: 3 -> 2; matrix products, arithmetic and copies ran while one was open for 2% -> 2% of each run, Pallas kernels for 4% -> 5%
where the time goes in v3:
time: 137 us; the launch traced here: 136 us
  blocking collectives  68.4 us (50%)
  starting transfers between devices  22 us (16%)
  Pallas kernels  21 us (15%)
  waiting for transfers between devices  15.5 us (11%)
  local copies, waits for them, and re-layouts  7.73 us (6%)
  between operations  1.38 us (1%)
    all_to_all x1, blocking collectives, on_device(): sent = rows(lax.all_to_all(sent, SRC, 0, 0))  18.4 us
    all_to_all x1, blocking collectives, on_device(): lax.all_to_all(sent, SRC, 0, 0)  17.3 us
    all_to_all x1, blocking collectives, on_device(): stats = lax.all_to_all(stats, 'z', 0, 0)  13.8 us
    all_to_all x1, waiting for transfers between devices, on_device(): near = lax.all_to_all(near, 'z', 0, 0)  13.3 us
    all_to_all x1, blocking collectives, on_device(): sent, _ = columns(lax.all_to_all(sent, TGT, 0, 0))  10.8 us
    all_to_all x1, starting transfers between devices, on_device(): near = lax.all_to_all(near, 'z', 0, 0)  8.57 us
    all_to_all x1, blocking collectives, on_device(): sent, src_pot = columns(lax.all_to_all(sent, TGT, 0, 0))  7.99 us
    unnamed x18, local copies, waits for them, and re-layouts  7.63 us
  transfers between devices with their start and end apart: 6, of which 2 were waited for; matrix products, arithmetic and copies ran while one was open for 2% of the time, Pallas kernels for 5%

profile of v3, /device:TPU:32, one launch (start us, length us, event | category | flops | bytes accessed | tf_op | source)
XLA Modules:
  0.0 136.0 jit_solution(12050784436655902219)
XLA Ops:
  0.6 0.0 copy-start.1
  0.6 0.8 copy-done.1
  1.5 0.8 spread.1
  2.3 8.6 %all-to-all-start = ((bf16[8,16,2048]{2,1,0:T(8,128)(2,1)}), bf16[8,16,2048]{2,1,0:T(8,128)(2,1)S(1)}, u32[]{:S(2)}, u32[]{:S(2)}) async-start(bf16[8,16,2048]{2,1,0:T(8,128)(2,1)} %spread.1), calls=%async_computation | async-start | bytes 1048576 | tf_op jit(solution)/shard_map/all_to_all | solution.py:398
  10.9 0.0 copy-start.2
  10.9 0.8 copy-done.2
  11.7 0.0 copy-start.5
  11.7 0.7 copy-done.5
  12.4 1.2 target_group.1
  13.7 13.3 %all-to-all-done.args_0_ = bf16[8,16,2048]{2,1,0:T(8,128)(2,1)S(1)} async-done(((bf16[8,16,2048]{2,1,0:T(8,128)(2,1)}), bf16[8,16,2048]{2,1,0:T(8,128)(2,1)S(1)}, u32[]{:S(2)}, u32[]{:S(2)}) %all-to-all-start) | async-done | bytes 524320 | tf_op jit(solution)/shard_map/all_to_all | solution.py:398
  26.9 1.5 %collective-permute-start.2 = (bf16[8,16,2048]{2,1,0:T(8,128)(2,1)S(1)}, bf16[8,16,2048]{2,1,0:T(8,128)(2,1)S(1)}, u32[]{:S(2)}, u32[]{:S(2)}) collective-permute-start(bf16[8,16,2048]{2,1,0:T(8,128)(2,1)S(1)} %all-to-all-done.args_0_), channel_id=1, source_target_pairs={{24,0},{0,8},{8,16},{16,24},{25,1},{1,9},{9,17},{17,25},{26,2},{2,... | collective-permute-start | bytes 1572872 | tf_op jit(solution)/shard_map/ppermute | solution.py:401
  28.4 2.7 %collective-permute-start.1 = (bf16[8,16,2048]{2,1,0:T(8,128)(2,1)S(1)}, bf16[8,16,2048]{2,1,0:T(8,128)(2,1)}, u32[]{:S(2)}, u32[]{:S(2)}) collective-permute-start(bf16[8,16,2048]{2,1,0:T(8,128)(2,1)S(1)} %all-to-all-done.args_0_), channel_id=1, source_target_pairs={{16,0},{24,8},{0,16},{8,24},{17,1},{25,9},{1,17},{9,25},{18,2},{26... | collective-permute-start | bytes 1572872 | tf_op jit(solution)/shard_map/ppermute | solution.py:401
  31.1 1.4 %collective-permute-start = (bf16[8,16,2048]{2,1,0:T(8,128)(2,1)S(1)}, bf16[8,16,2048]{2,1,0:T(8,128)(2,1)}, u32[]{:S(2)}, u32[]{:S(2)}) collective-permute-start(bf16[8,16,2048]{2,1,0:T(8,128)(2,1)S(1)} %all-to-all-done.args_0_), channel_id=1, source_target_pairs={{8,0},{16,8},{24,16},{0,24},{9,1},{17,9},{25,17},{1,25},{10,2},{18... | collective-permute-start | bytes 1572872 | tf_op jit(solution)/shard_map/ppermute | solution.py:401
  32.6 4.5 %all-to-all-start.1 = ((f32[8,16,128]{2,1,0:T(8,128)}), f32[8,16,128]{2,1,0:T(8,128)S(1)}, u32[]{:S(2)}, u32[]{:S(2)}) async-start(f32[8,16,128]{2,1,0:T(8,128)} %target_group.1), calls=%async_computation.1 | async-start | bytes 131072 | tf_op jit(solution)/shard_map/all_to_all | solution.py:405
  37.0 0.0 copy-start
  37.1 1.6 %copy-done = bf16[512,2048]{1,0:T(8,128)(2,1)S(1)} copy-done((bf16[512,2048]{1,0:T(8,128)(2,1)S(1)}, bf16[512,2048]{1,0:T(8,128)(2,1)}, u32[]{:S(2)}) %copy-start) | copy-done | bytes 2097176
  38.6 0.0 copy-start.3
  38.6 0.7 copy-done.3
  39.3 3.5 %source_group.1 = (f32[40,128]{1,0:T(8,128)S(1)}, f32[1,2048]{1,0:T(1,128)S(1)}) custom-call(bf16[512,2048]{1,0:T(8,128)(2,1)S(1)} %copy-done, s32[1,2048]{1,0:T(1,128)S(1)} %bitcast.14), custom_call_target="tpu_custom_call" | custom-call | tf_op jit(solution)/shard_map/source_group/pallas_call | solution.py:374
  42.8 0.0 all-to-all-done.1.tgt_got
  42.8 13.8 %all_to_all.40.got = f32[8,48,128]{2,1,0:T(8,128)S(1)} all-to-all(f32[8,48,128]{2,1,0:T(8,128)S(1)} %near.1), channel_id=1, replica_groups=mesh['z'=8,'x'=4,'y'=4,'c'=2] {'z'}, dimensions={0} | all-to-all | bytes 393216 | tf_op jit(solution)/shard_map/all_to_all | solution.py:414
  56.7 0.7 middle.1
  57.4 3.3 %all-to-all-start.3 = ((f32[4,72,128]{2,1,0:T(8,128)}), f32[4,72,128]{2,1,0:T(8,128)S(1)}, u32[]{:S(2)}, u32[]{:S(2)}) async-start(f32[4,72,128]{2,1,0:T(8,128)} %middle.1), calls=%async_computation.3 | async-start | bytes 294912 | tf_op jit(solution)/shard_map/all_to_all | solution.py:418
  60.7 0.0 copy-start.7
  60.8 0.0 copy-start.4
  60.8 0.0 copy-start.6
  60.8 2.9 %copy.12 = bf16[512,2048]{0,1:T(8,128)(2,1)S(1)} copy(bf16[512,2048]{1,0:T(8,128)(2,1)} %embed.3) | data formatting | bytes 4194304 | tf_op args[0]
  64.3 0.0 copy-done.7
  64.3 0.1 copy.11
  64.4 0.1 reshape.21.pairs
  64.5 2.3 %all-to-all-done.3.got = f32[4,72,128]{2,1,0:T(8,128)S(1)} async-done(((f32[4,72,128]{2,1,0:T(8,128)}), f32[4,72,128]{2,1,0:T(8,128)S(1)}, u32[]{:S(2)}, u32[]{:S(2)}) %all-to-all-start.3) | async-done | bytes 147488 | tf_op jit(solution)/shard_map/all_to_all | solution.py:418
  66.8 0.0 copy-done.4
  66.8 0.9 label.1
  67.7 0.0 collective-permute-done.2.args_3_
  67.7 0.0 collective-permute-done.1.args_2_
  67.7 0.0 collective-permute-done.args_1_
  67.7 0.0 copy-done.6
  67.7 5.8 %cost_rows.1 = (f32[24,256,256]{2,1,0:T(8,128)S(1)}, f32[8,16,128]{2,1,0:T(8,128)S(1)}) custom-call(s32[48]{0:T(128)S(1)} %reshape.21.pairs, s32[1]{0:T(128)} %bitcast.9.count, s32[1]{0:T(128)} %bitcast.1.place, bf16[16,2048]{1,0:T(8,128)(2,1)S(1)} %get-tuple-element.17.xa, bf16[2048,512]{1,0:T(8,128)(2,1)S(1)} %bitcast.13, ...), custom_call_target="tpu_custom_call" | custom-call | tf_op jit(solution)/shard_map/cost_rows/pallas_call | solution.py:432
  73.5 10.8 %all_to_all.41.g_ref = f32[8,16,128]{2,1,0:T(8,128)S(1)} all-to-all(f32[8,16,128]{2,1,0:T(8,128)S(1)} %get-tuple-element.20), channel_id=1, replica_groups=mesh['z'=8,'x'=4,'y'=4,'c'=2] {'y','c'}, dimensions={0} | all-to-all | bytes 131072 | tf_op jit(solution)/shard_map/all_to_all | solution.py:477
  84.3 2.2 %columns.2 = (f32[32,16,128]{2,1,0:T(8,128)S(1)}, f32[16,128]{1,0:T(8,128)}) custom-call(s32[48]{0:T(128)S(1)} %reshape.21.pairs, s32[1]{0:T(128)} %bitcast.10.count, f32[24,256,256]{2,1,0:T(8,128)S(1)} %get-tuple-element.19.tiles, f32[8,16,128]{2,1,0:T(8,128)S(1)} %all_to_all.41.g_ref), custom_call_target="tpu_custom_call" | custom-call | tf_op jit(solution)/shard_map/columns/pallas_call | solution.py:456
  86.6 18.4 %all_to_all.42.g_ref = f32[32,16,128]{2,1,0:T(8,128)S(1)} all-to-all(f32[32,16,128]{2,1,0:T(8,128)S(1)} %get-tuple-element.21), channel_id=1, replica_groups=mesh['z'=8,'x'=4,'y'=4,'c'=2] {'z','x'}, dimensions={0} | all-to-all | bytes 524288 | tf_op jit(solution)/shard_map/all_to_all | solution.py:478
  105.0 2.8 %rows.1 = f32[8,16,128]{2,1,0:T(8,128)S(1)} custom-call(s32[48]{0:T(128)S(1)} %reshape.21.pairs, s32[1]{0:T(128)} %bitcast.11.count, f32[24,256,256]{2,1,0:T(8,128)S(1)} %get-tuple-element.19.tiles, f32[32,16,128]{2,1,0:T(8,128)S(1)} %all_to_all.42.g_ref), custom_call_target="tpu_custom_call" | custom-call | tf_op jit(solution)/shard_map/rows/pallas_call | solution.py:467
  107.8 8.0 %all_to_all.43.g_ref = f32[8,16,128]{2,1,0:T(8,128)S(1)} all-to-all(f32[8,16,128]{2,1,0:T(8,128)S(1)} %rows.1), channel_id=1, replica_groups=mesh['z'=8,'x'=4,'y'=4,'c'=2] {'y','c'}, dimensions={0} | all-to-all | bytes 131072 | tf_op jit(solution)/shard_map/all_to_all | solution.py:479
  115.8 2.2 %columns.3 = (f32[32,16,128]{2,1,0:T(8,128)S(1)}, f32[16,128]{1,0:T(8,128)}) custom-call(s32[48]{0:T(128)S(1)} %reshape.21.pairs, s32[1]{0:T(128)} %bitcast.12.count, f32[24,256,256]{2,1,0:T(8,128)S(1)} %get-tuple-element.19.tiles, f32[8,16,128]{2,1,0:T(8,128)S(1)} %all_to_all.43.g_ref), custom_call_target="tpu_custom_call" | custom-call | tf_op jit(solution)/shard_map/columns/pallas_call | solution.py:456
  118.0 17.3 %all_to_all.44.g_ref = f32[32,16,128]{2,1,0:T(8,128)S(1)} all-to-all(f32[32,16,128]{2,1,0:T(8,128)S(1)} %get-tuple-element.23), channel_id=1, replica_groups=mesh['z'=8,'x'=4,'y'=4,'c'=2] {'z','x'}, dimensions={0} | all-to-all | bytes 524288 | tf_op jit(solution)/shard_map/all_to_all | solution.py:487
  135.4 0.7 last.1
  (1 shorter events, 0.0 us)
Async XLA Ops:
  0.6 0.8 copy-start.1
  2.3 24.6 %all-to-all-start = ((bf16[8,16,2048]{2,1,0:T(8,128)(2,1)}), bf16[8,16,2048]{2,1,0:T(8,128)(2,1)S(1)}, u32[]{:S(2)}, u32[]{:S(2)}) async-start(bf16[8,16,2048]{2,1,0:T(8,128)(2,1)} %spread.1), calls=%async_computation | async-start | bytes 1048576 | tf_op jit(solution)/shard_map/all_to_all | solution.py:398
  10.9 0.8 copy-start.2
  11.7 0.7 copy-start.5
  26.9 40.8 %collective-permute-start.2 = (bf16[8,16,2048]{2,1,0:T(8,128)(2,1)S(1)}, bf16[8,16,2048]{2,1,0:T(8,128)(2,1)S(1)}, u32[]{:S(2)}, u32[]{:S(2)}) collective-permute-start(bf16[8,16,2048]{2,1,0:T(8,128)(2,1)S(1)} %all-to-all-done.args_0_), channel_id=1, source_target_pairs={{24,0},{0,8},{8,16},{16,24},{25,1},{1,9},{9,17},{17,25},{26,2},{2,... | collective-permute-start | bytes 1572872 | tf_op jit(solution)/shard_map/ppermute | solution.py:401
  28.4 39.3 %collective-permute-start.1 = (bf16[8,16,2048]{2,1,0:T(8,128)(2,1)S(1)}, bf16[8,16,2048]{2,1,0:T(8,128)(2,1)}, u32[]{:S(2)}, u32[]{:S(2)}) collective-permute-start(bf16[8,16,2048]{2,1,0:T(8,128)(2,1)S(1)} %all-to-all-done.args_0_), channel_id=1, source_target_pairs={{16,0},{24,8},{0,16},{8,24},{17,1},{25,9},{1,17},{9,25},{18,2},{26... | collective-permute-start | bytes 1572872 | tf_op jit(solution)/shard_map/ppermute | solution.py:401
  31.1 36.5 %collective-permute-start = (bf16[8,16,2048]{2,1,0:T(8,128)(2,1)S(1)}, bf16[8,16,2048]{2,1,0:T(8,128)(2,1)}, u32[]{:S(2)}, u32[]{:S(2)}) collective-permute-start(bf16[8,16,2048]{2,1,0:T(8,128)(2,1)S(1)} %all-to-all-done.args_0_), channel_id=1, source_target_pairs={{8,0},{16,8},{24,16},{0,24},{9,1},{17,9},{25,17},{1,25},{10,2},{18... | collective-permute-start | bytes 1572872 | tf_op jit(solution)/shard_map/ppermute | solution.py:401
  32.6 10.2 %all-to-all-start.1 = ((f32[8,16,128]{2,1,0:T(8,128)}), f32[8,16,128]{2,1,0:T(8,128)S(1)}, u32[]{:S(2)}, u32[]{:S(2)}) async-start(f32[8,16,128]{2,1,0:T(8,128)} %target_group.1), calls=%async_computation.1 | async-start | bytes 131072 | tf_op jit(solution)/shard_map/all_to_all | solution.py:405
  37.0 1.6 %copy-start = (bf16[512,2048]{1,0:T(8,128)(2,1)S(1)}, bf16[512,2048]{1,0:T(8,128)(2,1)}, u32[]{:S(2)}) copy-start(bf16[512,2048]{1,0:T(8,128)(2,1)} %embed.3) | copy-start | bytes 6291460
  38.6 0.7 copy-start.3
  57.4 9.4 %all-to-all-start.3 = ((f32[4,72,128]{2,1,0:T(8,128)}), f32[4,72,128]{2,1,0:T(8,128)S(1)}, u32[]{:S(2)}, u32[]{:S(2)}) async-start(f32[4,72,128]{2,1,0:T(8,128)} %middle.1), calls=%async_computation.3 | async-start | bytes 294912 | tf_op jit(solution)/shard_map/all_to_all | solution.py:418
  60.7 3.6 %copy-start.7 = (s32[1,1,24,2]{2,3,1,0:T(2,128)S(1)}, s32[1,1,24,2]{2,3,1,0:T(2,128)}, u32[]{:S(2)}) copy-start(s32[1,1,24,2]{2,3,1,0:T(2,128)} %param.10) | copy-start | bytes 580
  60.8 6.0 %copy-start.4 = (s32[2048]{0:T(1024)S(1)}, s32[2048]{0:T(1024)}, u32[]{:S(2)}) copy-start(s32[2048]{0:T(1024)} %param.8) | copy-start | bytes 24580
  60.8 6.9 %copy-start.6 = (s32[2048]{0:T(1024)S(1)}, s32[2048]{0:T(1024)}, u32[]{:S(2)}) copy-start(s32[2048]{0:T(1024)} %param.9) | copy-start | bytes 24580

commit v4 on v3

--- a/solution.py
+++ b/solution.py
@@ -66,10 +66,9 @@
     onehot = repeated_onehot(labels[...])
     counts = jnp.maximum(jnp.sum(onehot, axis=1, keepdims=True), 1.0)
     group, _ = class_group(embed[...], onehot.astype(jnp.bfloat16), counts)
-    peers = out_ref.shape[0]
     out_ref[...] = jnp.zeros(out_ref.shape, jnp.float32)
-    out_ref[:, 0:8, 0 : group.shape[1]] = jnp.broadcast_to(group[None], (peers,) + group.shape)
-    out_ref[:, 8:16, :] = jnp.broadcast_to(counts[None, :8], (peers, 8, LANES))
+    out_ref[0:8, 0 : group.shape[1]] = group
+    out_ref[8:16, :] = jnp.broadcast_to(counts[:8], (8, LANES))
 
 
 def source_group_kernel(embed, labels, out_ref, sq_ref):
@@ -100,11 +99,25 @@
     return jnp.where(row_id < CLASSES, mean, spread)
 
 
-def near_kernel(tgt_got, src_group, out_ref):
-    peers = tgt_got.shape[0]
-    counts = [tgt_got[k, 8:16, :] for k in range(peers)]
+def target_joined(place, pieces, slots):
+    n = len(pieces)
+    for far, piece in enumerate(pieces):
+        slots[lax.rem(place[0] + far, n)] = piece[...]
+    counts = [slots[k, 8:16, :] for k in range(n)]
     total, shares = joined_counts(counts)
-    group = joined_group([tgt_got[k, 0:8, :] for k in range(peers)], counts, shares)
+    return joined_group([slots[k, 0:8, :] for k in range(n)], counts, shares), total
+
+
+def pair_kernel(place, *args):
+    pieces, (out_ref, slots) = args[:-2], args[-2:]
+    group, total = target_joined(place, pieces, slots)
+    out_ref[0:8, :] = group
+    out_ref[8:16, :] = total
+
+
+def near_kernel(place, *args):
+    pieces, (src_group, out_ref, slots) = args[:-3], args[-3:]
+    group, total = target_joined(place, pieces, slots)
     row_id = lax.broadcasted_iota(jnp.int32, (8, LANES), 0)
     group = jnp.where(row_id < CLASSES, group, group / total)
     for k in range(out_ref.shape[0]):
@@ -177,9 +190,14 @@
     ).astype(jnp.bfloat16)
 
 
-def spread_kernel(x, out_ref):
-    for k in range(out_ref.shape[0]):
-        out_ref[k] = x[...]
+def spread_kernel(x, out_ref, sems):
+    copies = [
+        pltpu.make_async_copy(x, out_ref.at[k], sems.at[k]) for k in range(out_ref.shape[0])
+    ]
+    for copy in copies:
+        copy.start()
+    for copy in copies:
+        copy.wait()
 
 
 def three_parts(v):
@@ -263,7 +281,7 @@
         tiles[index] = tile
         top[rows, :] = jnp.maximum(top[rows, :], jnp.maximum(tile[:, :LANES], tile[:, LANES:]))
 
-    over_pairs(count, build, 2)
+    over_pairs(count, build, 4)
     widen_top(top)
 
     def add(index):
@@ -382,27 +400,43 @@
 
     n_x, n_z = lax.axis_size("x"), lax.axis_size("z")
     part = target_embed.shape[0]
-    near = call(
+    near = pl.pallas_call(
         spread_kernel,
-        jax.ShapeDtypeStruct((n_z,) + target_embed.shape, jnp.bfloat16),
-        target_embed,
+        out_shape=jax.ShapeDtypeStruct((n_z,) + target_embed.shape, jnp.bfloat16),
+        in_specs=[pl.BlockSpec(memory_space=pl.ANY)],
+        out_specs=pl.BlockSpec(memory_space=pl.ANY),
+        scratch_shapes=[pltpu.SemaphoreType.DMA((n_z,))],
+        compiler_params=params(),
         name="spread",
-    )
+    )(target_embed)
+    near = lax.all_to_all(near, "z", 0, 0)
+
+    def around(x, axis):
+        n = lax.axis_size(axis)
+        return [x] + [
+            lax.ppermute(x, axis, [((i + far) % n, i) for i in range(n)]) for far in range(1, n)
+        ]
+
+    def join_targets(kernel, out_shape, x, axis, *more, name):
+        pieces = around(x, axis)
+        return pl.pallas_call(
+            kernel,
+            out_shape=out_shape,
+            in_specs=[smem()] + [vmem()] * (len(pieces) + len(more)),
+            out_specs=vmem(),
+            scratch_shapes=[pltpu.VMEM((len(pieces), 16, LANES), jnp.float32)],
+            compiler_params=params(),
+            name=name,
+        )(lax.axis_index(axis).reshape(1), *pieces, *more)
+
     tgt_group = call(
         target_group_kernel,
-        f32(n_tgt, 16, LANES),
+        f32(16, LANES),
         target_embed,
         target_labels[None],
         name="target_group",
     )
-    near = lax.all_to_all(near, "z", 0, 0)
-    near, tgt_group = lax.optimization_barrier((near, tgt_group))
-    pieces = [near] + [
-        lax.ppermute(near, "x", [((i + far) % n_x, i) for i in range(n_x)])
-        for far in range(1, n_x)
-    ]
-
-    tgt_got = lax.all_to_all(tgt_group, TGT, 0, 0)
+    tgt_group = join_targets(pair_kernel, f32(16, LANES), tgt_group, "c", name="pair")
     src_group, src_sq = call(
         source_group_kernel,
         (f32(40, LANES), f32(1, ROWS)),
@@ -410,7 +444,12 @@
         source_labels[None],
         name="source_group",
     )
-    stats = call(near_kernel, f32(n_z, 48, LANES), tgt_got, src_group, name="near")
+    stats = join_targets(
+        near_kernel, f32(n_z, 48, LANES), tgt_group, "y", src_group, name="near"
+    )
+    near, stats, source_tall = lax.optimization_barrier((near, stats, source_embed.T))
+
+    pieces = around(near, "x")
     stats = lax.all_to_all(stats, "z", 0, 0)
     stats = call(
         functools.partial(middle_kernel, part * n_x), f32(n_x, 72, LANES), stats, name="middle"
@@ -447,7 +486,7 @@
         count,
         lax.axis_index("x").reshape(1),
         xa,
-        source_embed.T,
+        source_tall,
         *pieces,
         target_labels[None],
     )

time: 137 us -> 128 us (0.934)
  waiting for transfers between devices: 15.5 us -> 6.41 us
  blocking collectives: 68.4 us -> 66.7 us
  starting transfers between devices: 22 us -> 23.5 us
    all_to_all x1, waiting for transfers between devices: 13.3 us -> 0.01 us  [on_device(): near = lax.all_to_all(near, 'z', 0, 0)]
    ppermute x3 -> x7, starting transfers between devices: 5.65 us -> 11.6 us  [around(): lax.ppermute(x, axis, [((i + far) % n, i) for i in range(n)])]
    all_to_all x1 -> x0, starting transfers between devices: 4.47 us -> none  [on_device(): tgt_got = lax.all_to_all(tgt_group, TGT, 0, 0)]
    all_to_all x1, waiting for transfers between devices: 2.26 us -> 5.18 us  [on_device(): stats = lax.all_to_all(stats, 'x', 0, 0)]
    all_to_all x1, blocking collectives: 10.8 us -> 7.99 us  [on_device(): sent, _ = columns(lax.all_to_all(sent, TGT, 0, 0))]
    pallas_call x6 -> x4, Pallas kernels: 7.22 us -> 5.67 us  [call(): pl.pallas_call(kernel, out_shape=out_shape, in_specs=[vmem()] * len(args)...]
    all_to_all x1, blocking collectives: 13.8 us -> 15.3 us  [on_device(): stats = lax.all_to_all(stats, 'z', 0, 0)]
    unnamed x18 -> x16, local copies, waits for them, and re-layouts: 7.63 us -> 6.93 us
  transfers between devices with their start and end apart: 6 -> 9, of which waited for: 2 -> 2; matrix products, arithmetic and copies ran while one was open for 2% -> 2% of each run, Pallas kernels for 5% -> 5%
where the time goes in v4:
time: 128 us; the launch traced here: 126 us
  blocking collectives  66.7 us (52%)
  starting transfers between devices  23.5 us (18%)
  Pallas kernels  21.4 us (17%)
  local copies, waits for them, and re-layouts  7.02 us (5%)
  waiting for transfers between devices  6.41 us (5%)
  between operations  1.4 us (1%)
    all_to_all x1, blocking collectives, on_device(): sent = rows(lax.all_to_all(sent, SRC, 0, 0))  18.7 us
    all_to_all x1, blocking collectives, on_device(): lax.all_to_all(sent, SRC, 0, 0)  16.3 us
    all_to_all x1, blocking collectives, on_device(): stats = lax.all_to_all(stats, 'z', 0, 0)  15.3 us
    ppermute x7, starting transfers between devices, around(): lax.ppermute(x, axis, [((i + far) % n, i) for i in range(n)])  11.6 us
    all_to_all x1, starting transfers between devices, on_device(): near = lax.all_to_all(near, 'z', 0, 0)  8.58 us
    all_to_all x1, blocking collectives, on_device(): sent, src_pot = columns(lax.all_to_all(sent, TGT, 0, 0))  8.43 us
    all_to_all x1, blocking collectives, on_device(): sent, _ = columns(lax.all_to_all(sent, TGT, 0, 0))  7.99 us
    unnamed x16, local copies, waits for them, and re-layouts  6.93 us
  transfers between devices with their start and end apart: 9, of which 2 were waited for; matrix products, arithmetic and copies ran while one was open for 2% of the time, Pallas kernels for 5%

profile of v4, /device:TPU:32, one launch (start us, length us, event | category | flops | bytes accessed | tf_op | source)
XLA Modules:
  0.0 126.4 jit_solution(15252239037816799236)
XLA Ops:
  0.6 0.0 copy-start.1
  0.6 0.8 copy-done.1
  1.5 0.9 spread.1
  2.4 8.6 %all-to-all-start = ((bf16[8,16,2048]{2,1,0:T(8,128)(2,1)}), bf16[8,16,2048]{2,1,0:T(8,128)(2,1)S(1)}, u32[]{:S(2)}, u32[]{:S(2)}) async-start(bf16[8,16,2048]{2,1,0:T(8,128)(2,1)} %spread.1), calls=%async_computation | async-start | bytes 1048576 | tf_op jit(solution)/shard_map/all_to_all | solution.py:412
  10.9 0.0 copy-start.2
  10.9 0.8 copy-done.2
  11.8 0.0 copy-start.4
  11.8 0.7 copy-done.4
  12.5 0.6 target_group.1.args_0_
  13.1 0.0 collective-permute-start
  13.1 1.2 collective-permute-done.args_1_
  14.3 1.6 %collective-permute-start.3 = (f32[16,128]{1,0:T(8,128)S(1)}, f32[16,128]{1,0:T(8,128)S(1)}, u32[]{:S(2)}, u32[]{:S(2)}) collective-permute-start(f32[16,128]{1,0:T(8,128)S(1)} %pair.1.args_0_), channel_id=1, source_target_pairs={{6,0},{0,2},{2,4},{4,6},{7,1},{1,3},{3,5},{5,7},{14,8},{8,10},{10,... | collective-permute-start | bytes 24584 | tf_op jit(solution)/shard_map/ppermute | solution.py:417
  15.9 2.9 %collective-permute-start.2 = (f32[16,128]{1,0:T(8,128)S(1)}, f32[16,128]{1,0:T(8,128)S(1)}, u32[]{:S(2)}, u32[]{:S(2)}) collective-permute-start(f32[16,128]{1,0:T(8,128)S(1)} %pair.1.args_0_), channel_id=1, source_target_pairs={{4,0},{6,2},{0,4},{2,6},{5,1},{7,3},{1,5},{3,7},{12,8},{14,10},{8,... | collective-permute-start | bytes 24584 | tf_op jit(solution)/shard_map/ppermute | solution.py:417
  18.8 1.3 %collective-permute-start.1 = (f32[16,128]{1,0:T(8,128)S(1)}, f32[16,128]{1,0:T(8,128)S(1)}, u32[]{:S(2)}, u32[]{:S(2)}) collective-permute-start(f32[16,128]{1,0:T(8,128)S(1)} %pair.1.args_0_), channel_id=1, source_target_pairs={{2,0},{4,2},{6,4},{0,6},{3,1},{5,3},{7,5},{1,7},{10,8},{12,10},{14... | collective-permute-start | bytes 24584 | tf_op jit(solution)/shard_map/ppermute | solution.py:417
  20.2 0.0 copy-start.3
  20.2 2.9 %copy.12 = bf16[512,2048]{0,1:T(8,128)(2,1)S(1)} copy(bf16[512,2048]{1,0:T(8,128)(2,1)} %embed.3) | data formatting | bytes 4194304 | tf_op args[0]
  23.1 0.0 copy-start.6
  23.1 0.0 copy-done.3
  23.1 0.0 copy-start
  23.1 1.6 %copy-done = bf16[512,2048]{1,0:T(8,128)(2,1)S(1)} copy-done((bf16[512,2048]{1,0:T(8,128)(2,1)S(1)}, bf16[512,2048]{1,0:T(8,128)(2,1)}, u32[]{:S(2)}) %copy-start) | copy-done | bytes 2097176
  24.7 0.0 copy-start.5
  24.7 3.5 %source_group.1 = (f32[40,128]{1,0:T(8,128)S(1)}, f32[1,2048]{1,0:T(1,128)S(1)}) custom-call(bf16[512,2048]{1,0:T(8,128)(2,1)S(1)} %copy-done, s32[1,2048]{1,0:T(1,128)S(1)} %bitcast.16), custom_call_target="tpu_custom_call" | custom-call | tf_op jit(solution)/shard_map/source_group/pallas_call | solution.py:392
  28.1 0.0 collective-permute-done.3.args_3_
  28.1 0.0 collective-permute-done.2.args_2_
  28.1 0.0 collective-permute-done.1.args_1_
  28.2 0.0 all-to-all-done.args_0_
  28.2 1.6 %collective-permute-start.6 = (bf16[8,16,2048]{2,1,0:T(8,128)(2,1)S(1)}, bf16[8,16,2048]{2,1,0:T(8,128)(2,1)S(1)}, u32[]{:S(2)}, u32[]{:S(2)}) collective-permute-start(bf16[8,16,2048]{2,1,0:T(8,128)(2,1)S(1)} %all-to-all-done.args_0_), channel_id=1, source_target_pairs={{24,0},{0,8},{8,16},{16,24},{25,1},{1,9},{9,17},{17,25},{26,2},{2,... | collective-permute-start | bytes 1572872 | tf_op jit(solution)/shard_map/ppermute | solution.py:417
  29.8 2.7 %collective-permute-start.5 = (bf16[8,16,2048]{2,1,0:T(8,128)(2,1)S(1)}, bf16[8,16,2048]{2,1,0:T(8,128)(2,1)}, u32[]{:S(2)}, u32[]{:S(2)}) collective-permute-start(bf16[8,16,2048]{2,1,0:T(8,128)(2,1)S(1)} %all-to-all-done.args_0_), channel_id=1, source_target_pairs={{16,0},{24,8},{0,16},{8,24},{17,1},{25,9},{1,17},{9,25},{18,2},{26... | collective-permute-start | bytes 1572872 | tf_op jit(solution)/shard_map/ppermute | solution.py:417
  32.5 1.4 %collective-permute-start.4 = (bf16[8,16,2048]{2,1,0:T(8,128)(2,1)S(1)}, bf16[8,16,2048]{2,1,0:T(8,128)(2,1)}, u32[]{:S(2)}, u32[]{:S(2)}) collective-permute-start(bf16[8,16,2048]{2,1,0:T(8,128)(2,1)S(1)} %all-to-all-done.args_0_), channel_id=1, source_target_pairs={{8,0},{16,8},{24,16},{0,24},{9,1},{17,9},{25,17},{1,25},{10,2},{18... | collective-permute-start | bytes 1572872 | tf_op jit(solution)/shard_map/ppermute | solution.py:417
  34.0 15.3 %all_to_all.35.got = f32[8,48,128]{2,1,0:T(8,128)S(1)} all-to-all(f32[8,48,128]{2,1,0:T(8,128)S(1)} %near.1), channel_id=1, replica_groups=mesh['z'=8,'x'=4,'y'=4,'c'=2] {'z'}, dimensions={0} | all-to-all | bytes 393216 | tf_op jit(solution)/shard_map/all_to_all | solution.py:453
  49.2 0.7 middle.1
  50.0 3.3 %all-to-all-start.2 = ((f32[4,72,128]{2,1,0:T(8,128)}), f32[4,72,128]{2,1,0:T(8,128)S(1)}, u32[]{:S(2)}, u32[]{:S(2)}) async-start(f32[4,72,128]{2,1,0:T(8,128)} %middle.1), calls=%async_computation.2 | async-start | bytes 294912 | tf_op jit(solution)/shard_map/all_to_all | solution.py:457
  54.0 0.0 copy-done.6
  54.0 0.1 copy.11
  54.1 0.1 reshape.27.pairs
  54.2 5.2 %all-to-all-done.2.got = f32[4,72,128]{2,1,0:T(8,128)S(1)} async-done(((f32[4,72,128]{2,1,0:T(8,128)}), f32[4,72,128]{2,1,0:T(8,128)S(1)}, u32[]{:S(2)}, u32[]{:S(2)}) %all-to-all-start.2) | async-done | bytes 147488 | tf_op jit(solution)/shard_map/all_to_all | solution.py:457
  59.3 0.9 label.1
  60.2 0.0 collective-permute-done.6.args_3_
  60.2 0.0 collective-permute-done.5.args_2_
  60.3 0.0 collective-permute-done.4.args_1_
  60.3 0.0 copy-done.5
  60.3 5.9 %cost_rows.1 = (f32[24,256,256]{2,1,0:T(8,128)S(1)}, f32[8,16,128]{2,1,0:T(8,128)S(1)}) custom-call(s32[48]{0:T(128)S(1)} %reshape.27.pairs, s32[1]{0:T(128)} %bitcast.11.count, s32[1]{0:T(128)} %bitcast.1.place, bf16[16,2048]{1,0:T(8,128)(2,1)S(1)} %get-tuple-element.18.xa, bf16[2048,512]{1,0:T(8,128)(2,1)S(1)} %bitcast.15, ...), custom_call_target="tpu_custom_call" | custom-call | tf_op jit(solution)/shard_map/cost_rows/pallas_call | solution.py:471
  66.2 8.0 %all_to_all.36.g_ref = f32[8,16,128]{2,1,0:T(8,128)S(1)} all-to-all(f32[8,16,128]{2,1,0:T(8,128)S(1)} %get-tuple-element.22), channel_id=1, replica_groups=mesh['z'=8,'x'=4,'y'=4,'c'=2] {'y','c'}, dimensions={0} | all-to-all | bytes 131072 | tf_op jit(solution)/shard_map/all_to_all | solution.py:516
  74.2 2.5 %columns.2 = (f32[32,16,128]{2,1,0:T(8,128)S(1)}, f32[16,128]{1,0:T(8,128)}) custom-call(s32[48]{0:T(128)S(1)} %reshape.27.pairs, s32[1]{0:T(128)} %bitcast.12.count, f32[24,256,256]{2,1,0:T(8,128)S(1)} %get-tuple-element.21.tiles, f32[8,16,128]{2,1,0:T(8,128)S(1)} %all_to_all.36.g_ref), custom_call_target="tpu_custom_call" | custom-call | tf_op jit(solution)/shard_map/columns/pallas_call | solution.py:495
  76.7 18.7 %all_to_all.37.g_ref = f32[32,16,128]{2,1,0:T(8,128)S(1)} all-to-all(f32[32,16,128]{2,1,0:T(8,128)S(1)} %get-tuple-element.23), channel_id=1, replica_groups=mesh['z'=8,'x'=4,'y'=4,'c'=2] {'z','x'}, dimensions={0} | all-to-all | bytes 524288 | tf_op jit(solution)/shard_map/all_to_all | solution.py:517
  95.3 3.2 %rows.1 = f32[8,16,128]{2,1,0:T(8,128)S(1)} custom-call(s32[48]{0:T(128)S(1)} %reshape.27.pairs, s32[1]{0:T(128)} %bitcast.13.count, f32[24,256,256]{2,1,0:T(8,128)S(1)} %get-tuple-element.21.tiles, f32[32,16,128]{2,1,0:T(8,128)S(1)} %all_to_all.37.g_ref), custom_call_target="tpu_custom_call" | custom-call | tf_op jit(solution)/shard_map/rows/pallas_call | solution.py:506
  98.5 8.4 %all_to_all.38.g_ref = f32[8,16,128]{2,1,0:T(8,128)S(1)} all-to-all(f32[8,16,128]{2,1,0:T(8,128)S(1)} %rows.1), channel_id=1, replica_groups=mesh['z'=8,'x'=4,'y'=4,'c'=2] {'y','c'}, dimensions={0} | all-to-all | bytes 131072 | tf_op jit(solution)/shard_map/all_to_all | solution.py:518
  106.9 2.5 %columns.3 = (f32[32,16,128]{2,1,0:T(8,128)S(1)}, f32[16,128]{1,0:T(8,128)}) custom-call(s32[48]{0:T(128)S(1)} %reshape.27.pairs, s32[1]{0:T(128)} %bitcast.14.count, f32[24,256,256]{2,1,0:T(8,128)S(1)} %get-tuple-element.21.tiles, f32[8,16,128]{2,1,0:T(8,128)S(1)} %all_to_all.38.g_ref), custom_call_target="tpu_custom_call" | custom-call | tf_op jit(solution)/shard_map/columns/pallas_call | solution.py:495
  109.4 16.3 %all_to_all.39.g_ref = f32[32,16,128]{2,1,0:T(8,128)S(1)} all-to-all(f32[32,16,128]{2,1,0:T(8,128)S(1)} %get-tuple-element.25), channel_id=1, replica_groups=mesh['z'=8,'x'=4,'y'=4,'c'=2] {'z','x'}, dimensions={0} | all-to-all | bytes 524288 | tf_op jit(solution)/shard_map/all_to_all | solution.py:526
  125.7 0.7 last.1
  (2 shorter events, 0.1 us)
Async XLA Ops:
  0.6 0.8 copy-start.1
  2.4 25.9 %all-to-all-start = ((bf16[8,16,2048]{2,1,0:T(8,128)(2,1)}), bf16[8,16,2048]{2,1,0:T(8,128)(2,1)S(1)}, u32[]{:S(2)}, u32[]{:S(2)}) async-start(bf16[8,16,2048]{2,1,0:T(8,128)(2,1)} %spread.1), calls=%async_computation | async-start | bytes 1048576 | tf_op jit(solution)/shard_map/all_to_all | solution.py:412
  10.9 0.8 copy-start.2
  11.8 0.7 copy-start.4
  13.1 1.2 collective-permute-start
  14.3 13.9 %collective-permute-start.3 = (f32[16,128]{1,0:T(8,128)S(1)}, f32[16,128]{1,0:T(8,128)S(1)}, u32[]{:S(2)}, u32[]{:S(2)}) collective-permute-start(f32[16,128]{1,0:T(8,128)S(1)} %pair.1.args_0_), channel_id=1, source_target_pairs={{6,0},{0,2},{2,4},{4,6},{7,1},{1,3},{3,5},{5,7},{14,8},{8,10},{10,... | collective-permute-start | bytes 24584 | tf_op jit(solution)/shard_map/ppermute | solution.py:417
  15.9 12.2 %collective-permute-start.2 = (f32[16,128]{1,0:T(8,128)S(1)}, f32[16,128]{1,0:T(8,128)S(1)}, u32[]{:S(2)}, u32[]{:S(2)}) collective-permute-start(f32[16,128]{1,0:T(8,128)S(1)} %pair.1.args_0_), channel_id=1, source_target_pairs={{4,0},{6,2},{0,4},{2,6},{5,1},{7,3},{1,5},{3,7},{12,8},{14,10},{8,... | collective-permute-start | bytes 24584 | tf_op jit(solution)/shard_map/ppermute | solution.py:417
  18.8 9.3 %collective-permute-start.1 = (f32[16,128]{1,0:T(8,128)S(1)}, f32[16,128]{1,0:T(8,128)S(1)}, u32[]{:S(2)}, u32[]{:S(2)}) collective-permute-start(f32[16,128]{1,0:T(8,128)S(1)} %pair.1.args_0_), channel_id=1, source_target_pairs={{2,0},{4,2},{6,4},{0,6},{3,1},{5,3},{7,5},{1,7},{10,8},{12,10},{14... | collective-permute-start | bytes 24584 | tf_op jit(solution)/shard_map/ppermute | solution.py:417
  20.2 2.9 %copy-start.3 = (s32[2048]{0:T(1024)S(1)}, s32[2048]{0:T(1024)}, u32[]{:S(2)}) copy-start(s32[2048]{0:T(1024)} %param.8) | copy-start | bytes 24580
  23.1 30.9 %copy-start.6 = (s32[1,1,24,2]{2,3,1,0:T(2,128)S(1)}, s32[1,1,24,2]{2,3,1,0:T(2,128)}, u32[]{:S(2)}) copy-start(s32[1,1,24,2]{2,3,1,0:T(2,128)} %param.10) | copy-start | bytes 580
  23.1 1.6 %copy-start = (bf16[512,2048]{1,0:T(8,128)(2,1)S(1)}, bf16[512,2048]{1,0:T(8,128)(2,1)}, u32[]{:S(2)}) copy-start(bf16[512,2048]{1,0:T(8,128)(2,1)} %embed.3) | copy-start | bytes 6291460
  24.7 35.6 %copy-start.5 = (s32[2048]{0:T(1024)S(1)}, s32[2048]{0:T(1024)}, u32[]{:S(2)}) copy-start(s32[2048]{0:T(1024)} %param.9) | copy-start | bytes 24580
  28.2 32.0 %collective-permute-start.6 = (bf16[8,16,2048]{2,1,0:T(8,128)(2,1)S(1)}, bf16[8,16,2048]{2,1,0:T(8,128)(2,1)S(1)}, u32[]{:S(2)}, u32[]{:S(2)}) collective-permute-start(bf16[8,16,2048]{2,1,0:T(8,128)(2,1)S(1)} %all-to-all-done.args_0_), channel_id=1, source_target_pairs={{24,0},{0,8},{8,16},{16,24},{25,1},{1,9},{9,17},{17,25},{26,2},{2,... | collective-permute-start | bytes 1572872 | tf_op jit(solution)/shard_map/ppermute | solution.py:417
  29.8 30.5 %collective-permute-start.5 = (bf16[8,16,2048]{2,1,0:T(8,128)(2,1)S(1)}, bf16[8,16,2048]{2,1,0:T(8,128)(2,1)}, u32[]{:S(2)}, u32[]{:S(2)}) collective-permute-start(bf16[8,16,2048]{2,1,0:T(8,128)(2,1)S(1)} %all-to-all-done.args_0_), channel_id=1, source_target_pairs={{16,0},{24,8},{0,16},{8,24},{17,1},{25,9},{1,17},{9,25},{18,2},{26... | collective-permute-start | bytes 1572872 | tf_op jit(solution)/shard_map/ppermute | solution.py:417
  32.5 27.7 %collective-permute-start.4 = (bf16[8,16,2048]{2,1,0:T(8,128)(2,1)S(1)}, bf16[8,16,2048]{2,1,0:T(8,128)(2,1)}, u32[]{:S(2)}, u32[]{:S(2)}) collective-permute-start(bf16[8,16,2048]{2,1,0:T(8,128)(2,1)S(1)} %all-to-all-done.args_0_), channel_id=1, source_target_pairs={{8,0},{16,8},{24,16},{0,24},{9,1},{17,9},{25,17},{1,25},{10,2},{18... | collective-permute-start | bytes 1572872 | tf_op jit(solution)/shard_map/ppermute | solution.py:417
  50.0 9.4 %all-to-all-start.2 = ((f32[4,72,128]{2,1,0:T(8,128)}), f32[4,72,128]{2,1,0:T(8,128)S(1)}, u32[]{:S(2)}, u32[]{:S(2)}) async-start(f32[4,72,128]{2,1,0:T(8,128)} %middle.1), calls=%async_computation.2 | async-start | bytes 294912 | tf_op jit(solution)/shard_map/all_to_all | solution.py:457

commit v5 on v4

--- a/solution.py
+++ b/solution.py
@@ -115,51 +115,62 @@
     out_ref[8:16, :] = total
 
 
+def lanes_of(shape):
+    return lax.broadcasted_iota(jnp.int32, shape, len(shape) - 1)
+
+
 def near_kernel(place, *args):
     pieces, (src_group, out_ref, slots) = args[:-3], args[-3:]
     group, total = target_joined(place, pieces, slots)
     row_id = lax.broadcasted_iota(jnp.int32, (8, LANES), 0)
     group = jnp.where(row_id < CLASSES, group, group / total)
-    for k in range(out_ref.shape[0]):
-        out_ref[k, 0:40, :] = src_group[...]
-        out_ref[k, 40:48, :] = group
+    out_ref[0:32, :] = src_group[0:32, :]
+    out_ref[32:40, :] = jnp.where(lanes_of((8, LANES)) < LANES // 2, group, src_group[32:40, :])
 
 
 def source_joined(got):
     peers = got.shape[0]
-    counts = [got[k, 32:40, :] for k in range(peers)]
+    half = LANES // 2
+    lower = lanes_of((8, LANES)) < half
+    last = [got[k, 32:40, :] for k in range(peers)]
+    targets = [jnp.where(lower, g, 0.0) for g in last]
+    counts = [jnp.where(lower, pltpu.roll(g, half, 1), g) for g in last]
     total, shares = joined_counts(counts)
     groups = [
         joined_group([got[k, 8 * c : 8 * c + 8, :] for k in range(peers)], counts, shares)
         for c in range(WIDTH // LANES)
     ]
-    return groups, total
-
-
-def middle_kernel(width, got, out_ref):
-    groups, total = source_joined(got)
+    return groups, total, targets
+
+
+def side_by_side(targets, width):
+    out = targets[0]
+    for k, target in enumerate(targets[1:]):
+        out = out + pltpu.roll(target, (k + 1) * width, 1)
+    return out
+
+
+def middle_kernel(part, place, *args):
+    pieces, (out_ref, slots) = args[:-2], args[-2:]
+    for far, piece in enumerate(pieces):
+        slots[lax.rem(place[0] + far, len(pieces))] = piece[...]
+    groups, total, targets = source_joined(slots)
+    target = side_by_side(targets, part)
+    target = jnp.where(lanes_of((8, LANES)) < LANES // 2, target, total)
+    for k in range(out_ref.shape[0]):
+        for c, group in enumerate(groups):
+            out_ref[k, 8 * c : 8 * c + 8, :] = group
+        out_ref[k, 32:40, :] = target
+
+
+def label_kernel(width, got, src_sq, src_lab, label_ref, xa_ref):
+    groups, total, targets = source_joined(got)
+    row_id = lax.broadcasted_iota(jnp.int32, (8, LANES), 0)
+    lane_id = lanes_of((8, LANES))
     each = LANES // width
-    for c in range(WIDTH // LANES):
-        tgt = got[each * c, 40:48, :]
-        for k in range(1, each):
-            tgt = tgt + pltpu.roll(got[each * c + k, 40:48, :], k * width, 1)
-        for k in range(out_ref.shape[0]):
-            out_ref[k, 8 * c : 8 * c + 8, :] = groups[c]
-            out_ref[k, 40 + 8 * c : 48 + 8 * c, :] = tgt
-    for k in range(out_ref.shape[0]):
-        out_ref[k, 32:40, :] = total
-
-
-def label_kernel(part, got, src_sq, src_lab, label_ref, xa_ref):
-    groups, total = source_joined(got)
-    row_id = lax.broadcasted_iota(jnp.int32, (8, LANES), 0)
-    lane_id = lax.broadcasted_iota(jnp.int32, (8, LANES), 1)
     sides = ([], [])
     for c, group in enumerate(groups):
-        at = slice(40 + 8 * c, 48 + 8 * c)
-        tgt = got[0, at, :]
-        for k in range(1, got.shape[0]):
-            tgt = tgt + pltpu.roll(got[k, at, :], k * part, 1)
+        tgt = side_by_side(targets[each * c : each * c + each], width)
         for side, stat in zip(sides, (jnp.where(row_id < CLASSES, group, group / total), tgt)):
             side.append(jnp.where(row_id < CLASSES, stat, jnp.sqrt(stat + 1e-06)))
 
@@ -417,14 +428,14 @@
             lax.ppermute(x, axis, [((i + far) % n, i) for i in range(n)]) for far in range(1, n)
         ]
 
-    def join_targets(kernel, out_shape, x, axis, *more, name):
+    def join_around(kernel, out_shape, x, axis, *more, name):
         pieces = around(x, axis)
         return pl.pallas_call(
             kernel,
             out_shape=out_shape,
             in_specs=[smem()] + [vmem()] * (len(pieces) + len(more)),
             out_specs=vmem(),
-            scratch_shapes=[pltpu.VMEM((len(pieces), 16, LANES), jnp.float32)],
+            scratch_shapes=[pltpu.VMEM((len(pieces),) + x.shape, jnp.float32)],
             compiler_params=params(),
             name=name,
         )(lax.axis_index(axis).reshape(1), *pieces, *more)
@@ -436,7 +447,7 @@
         target_labels[None],
         name="target_group",
     )
-    tgt_group = join_targets(pair_kernel, f32(16, LANES), tgt_group, "c", name="pair")
+    tgt_group = join_around(pair_kernel, f32(16, LANES), tgt_group, "c", name="pair")
     src_group, src_sq = call(
         source_group_kernel,
         (f32(40, LANES), f32(1, ROWS)),
@@ -444,19 +455,16 @@
         source_labels[None],
         name="source_group",
     )
-    stats = join_targets(
-        near_kernel, f32(n_z, 48, LANES), tgt_group, "y", src_group, name="near"
-    )
-    near, stats, source_tall = lax.optimization_barrier((near, stats, source_embed.T))
+    stats = join_around(near_kernel, f32(40, LANES), tgt_group, "y", src_group, name="near")
+    near, stats = lax.optimization_barrier((near, stats))
 
     pieces = around(near, "x")
+    stats = join_around(
+        functools.partial(middle_kernel, part), f32(n_z, 40, LANES), stats, "x", name="middle"
+    )
     stats = lax.all_to_all(stats, "z", 0, 0)
-    stats = call(
-        functools.partial(middle_kernel, part * n_x), f32(n_x, 72, LANES), stats, name="middle"
-    )
-    stats = lax.all_to_all(stats, "x", 0, 0)
     label_cost, xa = call(
-        functools.partial(label_kernel, part),
+        functools.partial(label_kernel, part * n_x),
         (f32(CLASSES, CLASSES), jax.ShapeDtypeStruct((16, ROWS), jnp.bfloat16)),
         stats,
         src_sq,
@@ -486,7 +494,7 @@
         count,
         lax.axis_index("x").reshape(1),
         xa,
-        source_tall,
+        source_embed.T,
         *pieces,
         target_labels[None],
     )

time: 128 us -> 142 us (1.11)
  waiting for transfers between devices: 6.41 us -> 24 us
  blocking collectives: 66.7 us -> 57.5 us
  starting transfers between devices: 23.5 us -> 32.5 us
  Pallas kernels: 21.4 us -> 18.4 us
    ppermute x7 -> x10, waiting for transfers between devices: 1.22 us -> 18.8 us  [around(): lax.ppermute(x, axis, [((i + far) % n, i) for i in range(n)])]
    all_to_all x1 -> x0, blocking collectives: 15.3 us -> none  [on_device(): stats = lax.all_to_all(stats, 'z', 0, 0)]
    ppermute x7 -> x10, starting transfers between devices: 11.6 us -> 16.7 us  [around(): lax.ppermute(x, axis, [((i + far) % n, i) for i in range(n)])]
    all_to_all x1, starting transfers between devices: 3.33 us -> 7.21 us  [on_device(): stats = lax.all_to_all(stats, 'z', 0, 0)]
    all_to_all x1, blocking collectives: 7.99 us -> 10.4 us  [on_device(): sent, _ = columns(lax.all_to_all(sent, TGT, 0, 0))]
    all_to_all x1, blocking collectives: 16.3 us -> 18.3 us  [on_device(): lax.all_to_all(sent, SRC, 0, 0)]
    all_to_all x1, blocking collectives: 18.7 us -> 20.2 us  [on_device(): sent = rows(lax.all_to_all(sent, SRC, 0, 0))]
    unnamed x16 -> x18, local copies, waits for them, and re-layouts: 6.93 us -> 7.65 us
  transfers between devices with their start and end apart: 9 -> 12, of which waited for: 2 -> 5; matrix products, arithmetic and copies ran while one was open for 2% -> 2% of each run, Pallas kernels for 5% -> 4%
where the time goes in v5:
time: 142 us; the launch traced here: 141 us
  blocking collectives  57.5 us (40%)
  starting transfers between devices  32.5 us (23%)
  waiting for transfers between devices  24 us (17%)
  Pallas kernels  18.4 us (13%)
  local copies, waits for them, and re-layouts  7.74 us (5%)
    all_to_all x1, blocking collectives, on_device(): sent = rows(lax.all_to_all(sent, SRC, 0, 0))  20.2 us
    ppermute x10, waiting for transfers between devices, around(): lax.ppermute(x, axis, [((i + far) % n, i) for i in range(n)])  18.8 us
    all_to_all x1, blocking collectives, on_device(): lax.all_to_all(sent, SRC, 0, 0)  18.3 us
    ppermute x10, starting transfers between devices, around(): lax.ppermute(x, axis, [((i + far) % n, i) for i in range(n)])  16.7 us
    all_to_all x1, blocking collectives, on_device(): sent, _ = columns(lax.all_to_all(sent, TGT, 0, 0))  10.4 us
    all_to_all x1, starting transfers between devices, on_device(): near = lax.all_to_all(near, 'z', 0, 0)  8.58 us
    all_to_all x1, blocking collectives, on_device(): sent, src_pot = columns(lax.all_to_all(sent, TGT, 0, 0))  8.54 us
    unnamed x18, local copies, waits for them, and re-layouts  7.65 us
  transfers between devices with their start and end apart: 12, of which 5 were waited for; matrix products, arithmetic and copies ran while one was open for 2% of the time, Pallas kernels for 4%

profile of v5, /device:TPU:32, one launch (start us, length us, event | category | flops | bytes accessed | tf_op | source)
XLA Modules:
  0.0 141.5 jit_solution(13633298307452923653)
XLA Ops:
  0.6 0.0 copy-start.1
  0.6 0.8 copy-done.1
  1.5 0.9 spread.1
  2.3 8.6 %all-to-all-start = ((bf16[8,16,2048]{2,1,0:T(8,128)(2,1)}), bf16[8,16,2048]{2,1,0:T(8,128)(2,1)S(1)}, u32[]{:S(2)}, u32[]{:S(2)}) async-start(bf16[8,16,2048]{2,1,0:T(8,128)(2,1)} %spread.1), calls=%async_computation | async-start | bytes 1048576 | tf_op jit(solution)/shard_map/all_to_all | solution.py:423
  10.9 0.0 copy-start.2
  10.9 0.8 copy-done.2
  11.8 0.0 copy-start.5
  11.8 0.7 copy-done.5
  12.5 0.6 target_group.1.args_0_
  13.0 0.0 collective-permute-start
  13.1 1.2 collective-permute-done.args_1_
  14.3 1.6 %collective-permute-start.3 = (f32[16,128]{1,0:T(8,128)S(1)}, f32[16,128]{1,0:T(8,128)S(1)}, u32[]{:S(2)}, u32[]{:S(2)}) collective-permute-start(f32[16,128]{1,0:T(8,128)S(1)} %pair.1.args_0_), channel_id=1, source_target_pairs={{6,0},{0,2},{2,4},{4,6},{7,1},{1,3},{3,5},{5,7},{14,8},{8,10},{10,... | collective-permute-start | bytes 24584 | tf_op jit(solution)/shard_map/ppermute | solution.py:428
  15.9 2.9 %collective-permute-start.2 = (f32[16,128]{1,0:T(8,128)S(1)}, f32[16,128]{1,0:T(8,128)S(1)}, u32[]{:S(2)}, u32[]{:S(2)}) collective-permute-start(f32[16,128]{1,0:T(8,128)S(1)} %pair.1.args_0_), channel_id=1, source_target_pairs={{4,0},{6,2},{0,4},{2,6},{5,1},{7,3},{1,5},{3,7},{12,8},{14,10},{8,... | collective-permute-start | bytes 24584 | tf_op jit(solution)/shard_map/ppermute | solution.py:428
  18.8 1.3 collective-permute-start.1
  20.2 0.0 copy-start
  20.2 1.6 %copy-done = bf16[512,2048]{1,0:T(8,128)(2,1)S(1)} copy-done((bf16[512,2048]{1,0:T(8,128)(2,1)S(1)}, bf16[512,2048]{1,0:T(8,128)(2,1)}, u32[]{:S(2)}) %copy-start) | copy-done | bytes 2097176
  21.8 0.0 copy-start.3
  21.8 0.7 copy-done.3
  22.5 3.5 %source_group.1 = (f32[40,128]{1,0:T(8,128)S(1)}, f32[1,2048]{1,0:T(1,128)S(1)}) custom-call(bf16[512,2048]{1,0:T(8,128)(2,1)S(1)} %copy-done, s32[1,2048]{1,0:T(1,128)S(1)} %bitcast.16), custom_call_target="tpu_custom_call" | custom-call | tf_op jit(solution)/shard_map/source_group/pallas_call | solution.py:403
  25.9 0.0 collective-permute-done.3.args_3_
  25.9 0.0 collective-permute-done.2.args_2_
  25.9 0.0 collective-permute-done.1.args_1_
  26.0 1.0 all-to-all-done.args_0_
  27.0 1.5 %collective-permute-start.9 = (bf16[8,16,2048]{2,1,0:T(8,128)(2,1)S(1)}, bf16[8,16,2048]{2,1,0:T(8,128)(2,1)S(1)}, u32[]{:S(2)}, u32[]{:S(2)}) collective-permute-start(bf16[8,16,2048]{2,1,0:T(8,128)(2,1)S(1)} %all-to-all-done.args_0_), channel_id=1, source_target_pairs={{24,0},{0,8},{8,16},{16,24},{25,1},{1,9},{9,17},{17,25},{26,2},{2,... | collective-permute-start | bytes 1572872 | tf_op jit(solution)/shard_map/ppermute | solution.py:428
  28.5 2.7 %collective-permute-start.8 = (bf16[8,16,2048]{2,1,0:T(8,128)(2,1)S(1)}, bf16[8,16,2048]{2,1,0:T(8,128)(2,1)}, u32[]{:S(2)}, u32[]{:S(2)}) collective-permute-start(bf16[8,16,2048]{2,1,0:T(8,128)(2,1)S(1)} %all-to-all-done.args_0_), channel_id=1, source_target_pairs={{16,0},{24,8},{0,16},{8,24},{17,1},{25,9},{1,17},{9,25},{18,2},{26... | collective-permute-start | bytes 1572872 | tf_op jit(solution)/shard_map/ppermute | solution.py:428
  31.2 1.4 %collective-permute-start.7 = (bf16[8,16,2048]{2,1,0:T(8,128)(2,1)S(1)}, bf16[8,16,2048]{2,1,0:T(8,128)(2,1)}, u32[]{:S(2)}, u32[]{:S(2)}) collective-permute-start(bf16[8,16,2048]{2,1,0:T(8,128)(2,1)S(1)} %all-to-all-done.args_0_), channel_id=1, source_target_pairs={{8,0},{16,8},{24,16},{0,24},{9,1},{17,9},{25,17},{1,25},{10,2},{18... | collective-permute-start | bytes 1572872 | tf_op jit(solution)/shard_map/ppermute | solution.py:428
  32.6 0.6 collective-permute-start.6
  33.2 0.9 collective-permute-start.5
  34.1 16.1 %collective-permute-done.6.args_3_ = f32[40,128]{1,0:T(8,128)S(1)} collective-permute-done((f32[40,128]{1,0:T(8,128)S(1)}, f32[40,128]{1,0:T(8,128)S(1)}, u32[]{:S(2)}, u32[]{:S(2)}) %collective-permute-start.6) | collective-permute-done | bytes 20512 | tf_op jit(solution)/shard_map/ppermute | solution.py:428
  50.2 3.7 %collective-permute-start.4 = (f32[40,128]{1,0:T(8,128)S(1)}, f32[40,128]{1,0:T(8,128)S(1)}, u32[]{:S(2)}, u32[]{:S(2)}) collective-permute-start(f32[40,128]{1,0:T(8,128)S(1)} %near.1.args_0_), channel_id=1, source_target_pairs={{8,0},{16,8},{24,16},{0,24},{9,1},{17,9},{25,17},{1,25},{10,2},{18... | collective-permute-start | bytes 61448 | tf_op jit(solution)/shard_map/ppermute | solution.py:428
  53.9 0.0 collective-permute-done.5.args_2_
  53.9 1.5 %collective-permute-done.4.args_1_ = f32[40,128]{1,0:T(8,128)S(1)} collective-permute-done((f32[40,128]{1,0:T(8,128)S(1)}, f32[40,128]{1,0:T(8,128)S(1)}, u32[]{:S(2)}, u32[]{:S(2)}) %collective-permute-start.4) | collective-permute-done | bytes 20512 | tf_op jit(solution)/shard_map/ppermute | solution.py:428
  55.4 0.8 middle.1
  56.1 7.2 %all-to-all-start.1 = ((f32[8,40,128]{2,1,0:T(8,128)}), f32[8,40,128]{2,1,0:T(8,128)S(1)}, u32[]{:S(2)}, u32[]{:S(2)}) async-start(f32[8,40,128]{2,1,0:T(8,128)} %middle.1), calls=%async_computation.1 | async-start | bytes 327680 | tf_op jit(solution)/shard_map/all_to_all | solution.py:465
  63.3 0.0 copy-start.7
  63.3 0.0 copy-start.4
  63.3 0.0 copy-start.6
  63.4 2.9 %copy.12 = bf16[512,2048]{0,1:T(8,128)(2,1)S(1)} copy(bf16[512,2048]{1,0:T(8,128)(2,1)} %embed.3) | data formatting | bytes 4194304 | tf_op args[0]
  66.9 0.0 copy-done.7
  66.9 0.1 copy.11
  67.0 0.1 reshape.28.pairs
  67.1 4.2 %all-to-all-done.1.got = f32[8,40,128]{2,1,0:T(8,128)S(1)} async-done(((f32[8,40,128]{2,1,0:T(8,128)}), f32[8,40,128]{2,1,0:T(8,128)S(1)}, u32[]{:S(2)}, u32[]{:S(2)}) %all-to-all-start.1) | async-done | bytes 163872 | tf_op jit(solution)/shard_map/all_to_all | solution.py:465
  71.3 0.0 copy-done.4
  71.3 1.0 label.1
  72.3 0.0 collective-permute-done.9.args_3_
  72.3 0.0 collective-permute-done.8.args_2_
  72.3 0.0 collective-permute-done.7.args_1_
  72.3 0.0 copy-done.6
  72.3 4.6 %cost_rows.1 = (f32[24,256,256]{2,1,0:T(8,128)S(1)}, f32[8,16,128]{2,1,0:T(8,128)S(1)}) custom-call(s32[48]{0:T(128)S(1)} %reshape.28.pairs, s32[1]{0:T(128)} %bitcast.11.count, s32[1]{0:T(128)} %bitcast.1.place, bf16[16,2048]{1,0:T(8,128)(2,1)S(1)} %get-tuple-element.17.xa, bf16[2048,512]{1,0:T(8,128)(2,1)S(1)} %bitcast.15, ...), custom_call_target="tpu_custom_call" | custom-call | tf_op jit(solution)/shard_map/cost_rows/pallas_call | solution.py:479
  76.9 10.4 %all_to_all.30.g_ref = f32[8,16,128]{2,1,0:T(8,128)S(1)} all-to-all(f32[8,16,128]{2,1,0:T(8,128)S(1)} %get-tuple-element.20), channel_id=1, replica_groups=mesh['z'=8,'x'=4,'y'=4,'c'=2] {'y','c'}, dimensions={0} | all-to-all | bytes 131072 | tf_op jit(solution)/shard_map/all_to_all | solution.py:524
  87.2 2.0 %columns.2 = (f32[32,16,128]{2,1,0:T(8,128)S(1)}, f32[16,128]{1,0:T(8,128)}) custom-call(s32[48]{0:T(128)S(1)} %reshape.28.pairs, s32[1]{0:T(128)} %bitcast.12.count, f32[24,256,256]{2,1,0:T(8,128)S(1)} %get-tuple-element.19.tiles, f32[8,16,128]{2,1,0:T(8,128)S(1)} %all_to_all.30.g_ref), custom_call_target="tpu_custom_call" | custom-call | tf_op jit(solution)/shard_map/columns/pallas_call | solution.py:503
  89.2 20.2 %all_to_all.31.g_ref = f32[32,16,128]{2,1,0:T(8,128)S(1)} all-to-all(f32[32,16,128]{2,1,0:T(8,128)S(1)} %get-tuple-element.21), channel_id=1, replica_groups=mesh['z'=8,'x'=4,'y'=4,'c'=2] {'z','x'}, dimensions={0} | all-to-all | bytes 524288 | tf_op jit(solution)/shard_map/all_to_all | solution.py:525
  109.5 2.5 %rows.1 = f32[8,16,128]{2,1,0:T(8,128)S(1)} custom-call(s32[48]{0:T(128)S(1)} %reshape.28.pairs, s32[1]{0:T(128)} %bitcast.13.count, f32[24,256,256]{2,1,0:T(8,128)S(1)} %get-tuple-element.19.tiles, f32[32,16,128]{2,1,0:T(8,128)S(1)} %all_to_all.31.g_ref), custom_call_target="tpu_custom_call" | custom-call | tf_op jit(solution)/shard_map/rows/pallas_call | solution.py:514
  112.0 8.5 %all_to_all.32.g_ref = f32[8,16,128]{2,1,0:T(8,128)S(1)} all-to-all(f32[8,16,128]{2,1,0:T(8,128)S(1)} %rows.1), channel_id=1, replica_groups=mesh['z'=8,'x'=4,'y'=4,'c'=2] {'y','c'}, dimensions={0} | all-to-all | bytes 131072 | tf_op jit(solution)/shard_map/all_to_all | solution.py:526
  120.5 2.0 %columns.3 = (f32[32,16,128]{2,1,0:T(8,128)S(1)}, f32[16,128]{1,0:T(8,128)}) custom-call(s32[48]{0:T(128)S(1)} %reshape.28.pairs, s32[1]{0:T(128)} %bitcast.14.count, f32[24,256,256]{2,1,0:T(8,128)S(1)} %get-tuple-element.19.tiles, f32[8,16,128]{2,1,0:T(8,128)S(1)} %all_to_all.32.g_ref), custom_call_target="tpu_custom_call" | custom-call | tf_op jit(solution)/shard_map/columns/pallas_call | solution.py:503
  122.5 18.3 %all_to_all.33.g_ref = f32[32,16,128]{2,1,0:T(8,128)S(1)} all-to-all(f32[32,16,128]{2,1,0:T(8,128)S(1)} %get-tuple-element.23), channel_id=1, replica_groups=mesh['z'=8,'x'=4,'y'=4,'c'=2] {'z','x'}, dimensions={0} | all-to-all | bytes 524288 | tf_op jit(solution)/shard_map/all_to_all | solution.py:534
  140.8 0.7 last.1
  (2 shorter events, 0.1 us)
Async XLA Ops:
  0.6 0.8 copy-start.1
  2.3 24.6 %all-to-all-start = ((bf16[8,16,2048]{2,1,0:T(8,128)(2,1)}), bf16[8,16,2048]{2,1,0:T(8,128)(2,1)S(1)}, u32[]{:S(2)}, u32[]{:S(2)}) async-start(bf16[8,16,2048]{2,1,0:T(8,128)(2,1)} %spread.1), calls=%async_computation | async-start | bytes 1048576 | tf_op jit(solution)/shard_map/all_to_all | solution.py:423
  10.9 0.8 copy-start.2
  11.8 0.7 copy-start.5
  13.0 1.2 collective-permute-start
  14.3 11.6 %collective-permute-start.3 = (f32[16,128]{1,0:T(8,128)S(1)}, f32[16,128]{1,0:T(8,128)S(1)}, u32[]{:S(2)}, u32[]{:S(2)}) collective-permute-start(f32[16,128]{1,0:T(8,128)S(1)} %pair.1.args_0_), channel_id=1, source_target_pairs={{6,0},{0,2},{2,4},{4,6},{7,1},{1,3},{3,5},{5,7},{14,8},{8,10},{10,... | collective-permute-start | bytes 24584 | tf_op jit(solution)/shard_map/ppermute | solution.py:428
  15.9 10.0 %collective-permute-start.2 = (f32[16,128]{1,0:T(8,128)S(1)}, f32[16,128]{1,0:T(8,128)S(1)}, u32[]{:S(2)}, u32[]{:S(2)}) collective-permute-start(f32[16,128]{1,0:T(8,128)S(1)} %pair.1.args_0_), channel_id=1, source_target_pairs={{4,0},{6,2},{0,4},{2,6},{5,1},{7,3},{1,5},{3,7},{12,8},{14,10},{8,... | collective-permute-start | bytes 24584 | tf_op jit(solution)/shard_map/ppermute | solution.py:428
  18.8 7.1 %collective-permute-start.1 = (f32[16,128]{1,0:T(8,128)S(1)}, f32[16,128]{1,0:T(8,128)S(1)}, u32[]{:S(2)}, u32[]{:S(2)}) collective-permute-start(f32[16,128]{1,0:T(8,128)S(1)} %pair.1.args_0_), channel_id=1, source_target_pairs={{2,0},{4,2},{6,4},{0,6},{3,1},{5,3},{7,5},{1,7},{10,8},{12,10},{14... | collective-permute-start | bytes 24584 | tf_op jit(solution)/shard_map/ppermute | solution.py:428
  20.2 1.6 %copy-start = (bf16[512,2048]{1,0:T(8,128)(2,1)S(1)}, bf16[512,2048]{1,0:T(8,128)(2,1)}, u32[]{:S(2)}) copy-start(bf16[512,2048]{1,0:T(8,128)(2,1)} %embed.3) | copy-start | bytes 6291460
  21.8 0.7 copy-start.3
  27.0 45.3 %collective-permute-start.9 = (bf16[8,16,2048]{2,1,0:T(8,128)(2,1)S(1)}, bf16[8,16,2048]{2,1,0:T(8,128)(2,1)S(1)}, u32[]{:S(2)}, u32[]{:S(2)}) collective-permute-start(bf16[8,16,2048]{2,1,0:T(8,128)(2,1)S(1)} %all-to-all-done.args_0_), channel_id=1, source_target_pairs={{24,0},{0,8},{8,16},{16,24},{25,1},{1,9},{9,17},{17,25},{26,2},{2,... | collective-permute-start | bytes 1572872 | tf_op jit(solution)/shard_map/ppermute | solution.py:428
  28.5 43.8 %collective-permute-start.8 = (bf16[8,16,2048]{2,1,0:T(8,128)(2,1)S(1)}, bf16[8,16,2048]{2,1,0:T(8,128)(2,1)}, u32[]{:S(2)}, u32[]{:S(2)}) collective-permute-start(bf16[8,16,2048]{2,1,0:T(8,128)(2,1)S(1)} %all-to-all-done.args_0_), channel_id=1, source_target_pairs={{16,0},{24,8},{0,16},{8,24},{17,1},{25,9},{1,17},{9,25},{18,2},{26... | collective-permute-start | bytes 1572872 | tf_op jit(solution)/shard_map/ppermute | solution.py:428
  31.2 41.1 %collective-permute-start.7 = (bf16[8,16,2048]{2,1,0:T(8,128)(2,1)S(1)}, bf16[8,16,2048]{2,1,0:T(8,128)(2,1)}, u32[]{:S(2)}, u32[]{:S(2)}) collective-permute-start(bf16[8,16,2048]{2,1,0:T(8,128)(2,1)S(1)} %all-to-all-done.args_0_), channel_id=1, source_target_pairs={{8,0},{16,8},{24,16},{0,24},{9,1},{17,9},{25,17},{1,25},{10,2},{18... | collective-permute-start | bytes 1572872 | tf_op jit(solution)/shard_map/ppermute | solution.py:428
  32.6 17.6 %collective-permute-start.6 = (f32[40,128]{1,0:T(8,128)S(1)}, f32[40,128]{1,0:T(8,128)S(1)}, u32[]{:S(2)}, u32[]{:S(2)}) collective-permute-start(f32[40,128]{1,0:T(8,128)S(1)} %near.1.args_0_), channel_id=1, source_target_pairs={{24,0},{0,8},{8,16},{16,24},{25,1},{1,9},{9,17},{17,25},{26,2},{2,... | collective-permute-start | bytes 61448 | tf_op jit(solution)/shard_map/ppermute | solution.py:428
  33.2 20.7 %collective-permute-start.5 = (f32[40,128]{1,0:T(8,128)S(1)}, f32[40,128]{1,0:T(8,128)S(1)}, u32[]{:S(2)}, u32[]{:S(2)}) collective-permute-start(f32[40,128]{1,0:T(8,128)S(1)} %near.1.args_0_), channel_id=1, source_target_pairs={{16,0},{24,8},{0,16},{8,24},{17,1},{25,9},{1,17},{9,25},{18,2},{26... | collective-permute-start | bytes 61448 | tf_op jit(solution)/shard_map/ppermute | solution.py:428
  50.2 5.2 %collective-permute-start.4 = (f32[40,128]{1,0:T(8,128)S(1)}, f32[40,128]{1,0:T(8,128)S(1)}, u32[]{:S(2)}, u32[]{:S(2)}) collective-permute-start(f32[40,128]{1,0:T(8,128)S(1)} %near.1.args_0_), channel_id=1, source_target_pairs={{8,0},{16,8},{24,16},{0,24},{9,1},{17,9},{25,17},{1,25},{10,2},{18... | collective-permute-start | bytes 61448 | tf_op jit(solution)/shard_map/ppermute | solution.py:428
  56.1 15.2 %all-to-all-start.1 = ((f32[8,40,128]{2,1,0:T(8,128)}), f32[8,40,128]{2,1,0:T(8,128)S(1)}, u32[]{:S(2)}, u32[]{:S(2)}) async-start(f32[8,40,128]{2,1,0:T(8,128)} %middle.1), calls=%async_computation.1 | async-start | bytes 327680 | tf_op jit(solution)/shard_map/all_to_all | solution.py:465
  63.3 3.6 %copy-start.7 = (s32[1,1,24,2]{2,3,1,0:T(2,128)S(1)}, s32[1,1,24,2]{2,3,1,0:T(2,128)}, u32[]{:S(2)}) copy-start(s32[1,1,24,2]{2,3,1,0:T(2,128)} %param.10) | copy-start | bytes 580
  63.3 8.0 %copy-start.4 = (s32[2048]{0:T(1024)S(1)}, s32[2048]{0:T(1024)}, u32[]{:S(2)}) copy-start(s32[2048]{0:T(1024)} %param.8) | copy-start | bytes 24580
  63.3 8.9 %copy-start.6 = (s32[2048]{0:T(1024)S(1)}, s32[2048]{0:T(1024)}, u32[]{:S(2)}) copy-start(s32[2048]{0:T(1024)} %param.9) | copy-start | bytes 24580

commit v6 on v5

--- a/solution.py
+++ b/solution.py
@@ -62,22 +62,48 @@
     return jnp.where(part == 0, mean, spread)[:8], wide
 
 
-def target_group_kernel(embed, labels, out_ref):
-    onehot = repeated_onehot(labels[...])
+def first_kernel(embed, labels, near_ref, out_ref, held, held_labels, sems, out_sems):
+    fetch = [
+        pltpu.make_async_copy(embed, held, sems.at[0]),
+        pltpu.make_async_copy(labels, held_labels, sems.at[1]),
+    ]
+    for copy in fetch:
+        copy.start()
+    for copy in fetch:
+        copy.wait()
+    copies = [
+        pltpu.make_async_copy(held, near_ref.at[k], out_sems.at[k])
+        for k in range(near_ref.shape[0])
+    ]
+    for copy in copies:
+        copy.start()
+    onehot = repeated_onehot(held_labels[...])
     counts = jnp.maximum(jnp.sum(onehot, axis=1, keepdims=True), 1.0)
-    group, _ = class_group(embed[...], onehot.astype(jnp.bfloat16), counts)
+    group, _ = class_group(held[...], onehot.astype(jnp.bfloat16), counts)
     out_ref[...] = jnp.zeros(out_ref.shape, jnp.float32)
     out_ref[0:8, 0 : group.shape[1]] = group
     out_ref[8:16, :] = jnp.broadcast_to(counts[:8], (8, LANES))
-
-
-def source_group_kernel(embed, labels, out_ref, sq_ref):
-    onehot = repeated_onehot(labels[...])
+    for copy in copies:
+        copy.wait()
+
+
+def source_group_kernel(embed, labels, out_ref, sq_ref, held, held_labels, sems):
+    chunks = WIDTH // LANES
+    rows = [pl.ds(c * LANES, LANES) for c in range(chunks)]
+    fetch = [pltpu.make_async_copy(labels, held_labels, sems.at[chunks])] + [
+        pltpu.make_async_copy(embed.at[rows[c], :], held.at[rows[c], :], sems.at[c])
+        for c in range(chunks)
+    ]
+    for copy in fetch:
+        copy.start()
+    fetch[0].wait()
+    onehot = repeated_onehot(held_labels[...])
     counts = jnp.maximum(jnp.sum(onehot, axis=1, keepdims=True), 1.0)
     onehot = onehot.astype(jnp.bfloat16)
     sq = jnp.zeros((1, ROWS), jnp.float32)
-    for c in range(WIDTH // LANES):
-        group, wide = class_group(embed[c * LANES : (c + 1) * LANES, :], onehot, counts)
+    for c in range(chunks):
+        fetch[1 + c].wait()
+        group, wide = class_group(held[rows[c], :], onehot, counts)
         out_ref[8 * c : 8 * c + 8, :] = group
         sq = sq + jnp.sum(wide * wide, axis=0, keepdims=True)
     out_ref[32:40, :] = jnp.broadcast_to(counts[:8], (8, LANES))
@@ -201,16 +227,6 @@
     ).astype(jnp.bfloat16)
 
 
-def spread_kernel(x, out_ref, sems):
-    copies = [
-        pltpu.make_async_copy(x, out_ref.at[k], sems.at[k]) for k in range(out_ref.shape[0])
-    ]
-    for copy in copies:
-        copy.start()
-    for copy in copies:
-        copy.wait()
-
-
 def three_parts(v):
     hi = v.astype(jnp.bfloat16).astype(jnp.float32)
     rest = v - hi
@@ -382,6 +398,10 @@
     return pl.BlockSpec(memory_space=pltpu.SMEM)
 
 
+def hbm():
+    return pl.BlockSpec(memory_space=pltpu.HBM)
+
+
 def vmem():
     return pl.BlockSpec(memory_space=pltpu.VMEM)
 
@@ -411,15 +431,23 @@
 
     n_x, n_z = lax.axis_size("x"), lax.axis_size("z")
     part = target_embed.shape[0]
-    near = pl.pallas_call(
-        spread_kernel,
-        out_shape=jax.ShapeDtypeStruct((n_z,) + target_embed.shape, jnp.bfloat16),
-        in_specs=[pl.BlockSpec(memory_space=pl.ANY)],
-        out_specs=pl.BlockSpec(memory_space=pl.ANY),
-        scratch_shapes=[pltpu.SemaphoreType.DMA((n_z,))],
+    near, tgt_group = pl.pallas_call(
+        first_kernel,
+        out_shape=(
+            jax.ShapeDtypeStruct((n_z,) + target_embed.shape, jnp.bfloat16),
+            f32(16, LANES),
+        ),
+        in_specs=[hbm(), hbm()],
+        out_specs=(hbm(), vmem()),
+        scratch_shapes=[
+            pltpu.VMEM(target_embed.shape, jnp.bfloat16),
+            pltpu.VMEM((1, ROWS), jnp.int32),
+            pltpu.SemaphoreType.DMA((2,)),
+            pltpu.SemaphoreType.DMA((n_z,)),
+        ],
         compiler_params=params(),
-        name="spread",
-    )(target_embed)
+        name="first",
+    )(target_embed, target_labels[None])
     near = lax.all_to_all(near, "z", 0, 0)
 
     def around(x, axis):
@@ -428,8 +456,8 @@
             lax.ppermute(x, axis, [((i + far) % n, i) for i in range(n)]) for far in range(1, n)
         ]
 
-    def join_around(kernel, out_shape, x, axis, *more, name):
-        pieces = around(x, axis)
+    def join_around(kernel, out_shape, pieces, axis, *more, name):
+        x = pieces[0]
         return pl.pallas_call(
             kernel,
             out_shape=out_shape,
@@ -440,24 +468,25 @@
             name=name,
         )(lax.axis_index(axis).reshape(1), *pieces, *more)
 
-    tgt_group = call(
-        target_group_kernel,
-        f32(16, LANES),
-        target_embed,
-        target_labels[None],
-        name="target_group",
-    )
-    tgt_group = join_around(pair_kernel, f32(16, LANES), tgt_group, "c", name="pair")
-    src_group, src_sq = call(
+    tgt_group = join_around(pair_kernel, f32(16, LANES), around(tgt_group, "c"), "c", name="pair")
+    src_group, src_sq = pl.pallas_call(
         source_group_kernel,
-        (f32(40, LANES), f32(1, ROWS)),
-        source_embed,
-        source_labels[None],
+        out_shape=(f32(40, LANES), f32(1, ROWS)),
+        in_specs=[hbm(), hbm()],
+        out_specs=(vmem(), vmem()),
+        scratch_shapes=[
+            pltpu.VMEM((WIDTH, ROWS), jnp.bfloat16),
+            pltpu.VMEM((1, ROWS), jnp.int32),
+            pltpu.SemaphoreType.DMA((WIDTH // LANES + 1,)),
+        ],
+        compiler_params=params(),
         name="source_group",
-    )
-    stats = join_around(near_kernel, f32(40, LANES), tgt_group, "y", src_group, name="near")
-    near, stats = lax.optimization_barrier((near, stats))
-
+    )(source_embed, source_labels[None])
+    stats = join_around(
+        near_kernel, f32(40, LANES), around(tgt_group, "y"), "y", src_group, name="near"
+    )
+
+    near, stats = lax.optimization_barrier((near, around(stats, "x")))
     pieces = around(near, "x")
     stats = join_around(
         functools.partial(middle_kernel, part), f32(n_z, 40, LANES), stats, "x", name="middle"

time: 142 us -> 131 us (0.923)
  waiting for transfers between devices: 24 us -> 12 us
  Pallas kernels: 18.4 us -> 24.4 us
  blocking collectives: 57.5 us -> 54 us
    ppermute x10, waiting for transfers between devices: 18.8 us -> 7.77 us  [around(): lax.ppermute(x, axis, [((i + far) % n, i) for i in range(n)])]
    pallas_call x1 -> x2, Pallas kernels: 0.87 us -> 7.71 us  [the longest x1 6.76 us: on_device(): pl.pallas_call(source_group_kernel, out_shape=(f32(40, LANES), f32(1, ROW...]
    pallas_call x3 -> x1, Pallas kernels: 4.98 us -> 0.95 us  [call(): pl.pallas_call(kernel, out_shape=out_shape, in_specs=[vmem()] * len(args)...]
    all_to_all x1, blocking collectives: 10.4 us -> 7.99 us  [on_device(): sent, _ = columns(lax.all_to_all(sent, TGT, 0, 0))]
    pallas_call x1, Pallas kernels: 4.56 us -> 6.11 us  [on_device(): pl.pallas_call(functools.partial(cost_kernel, n_x), out_shape=(f32(MAXP,...]
    unnamed x18 -> x16, local copies, waits for them, and re-layouts: 7.65 us -> 6.81 us
  transfers between devices with their start and end apart: 12 -> 12, of which waited for: 5 -> 5; matrix products, arithmetic and copies ran while one was open for 2% -> 2% of each run, Pallas kernels for 4% -> 7%
where the time goes in v6:
time: 131 us; the launch traced here: 130 us
  blocking collectives  54 us (41%)
  starting transfers between devices  31.6 us (24%)
  Pallas kernels  24.4 us (19%)
  waiting for transfers between devices  12 us (9%)
  local copies, waits for them, and re-layouts  6.9 us (5%)
  between operations  1.37 us (1%)
    all_to_all x1, blocking collectives, on_device(): sent = rows(lax.all_to_all(sent, SRC, 0, 0))  21 us
    all_to_all x1, blocking collectives, on_device(): lax.all_to_all(sent, SRC, 0, 0)  16.9 us
    ppermute x10, starting transfers between devices, around(): lax.ppermute(x, axis, [((i + far) % n, i) for i in range(n)])  15.8 us
    all_to_all x1, starting transfers between devices, on_device(): near = lax.all_to_all(near, 'z', 0, 0)  8.58 us
    all_to_all x1, blocking collectives, on_device(): sent, _ = columns(lax.all_to_all(sent, TGT, 0, 0))  7.99 us
    all_to_all x1, blocking collectives, on_device(): sent, src_pot = columns(lax.all_to_all(sent, TGT, 0, 0))  7.99 us
    ppermute x10, waiting for transfers between devices, around(): lax.ppermute(x, axis, [((i + far) % n, i) for i in range(n)])  7.77 us
    all_to_all x1, starting transfers between devices, on_device(): stats = lax.all_to_all(stats, 'z', 0, 0)  7.21 us
  transfers between devices with their start and end apart: 12, of which 5 were waited for; matrix products, arithmetic and copies ran while one was open for 2% of the time, Pallas kernels for 7%

profile of v6, /device:TPU:32, one launch (start us, length us, event | category | flops | bytes accessed | tf_op | source)
XLA Modules:
  0.0 130.2 jit_solution(13381170596269360453)
XLA Ops:
  0.6 0.0 copy-start.1
  0.6 0.8 copy-done.1
  1.5 0.0 copy-start.4
  1.5 0.7 copy-done.4
  2.2 1.0 first.1
  3.1 8.6 %all-to-all-start = ((bf16[8,16,2048]{2,1,0:T(8,128)(2,1)}), bf16[8,16,2048]{2,1,0:T(8,128)(2,1)S(1)}, u32[]{:S(2)}, u32[]{:S(2)}) async-start(bf16[8,16,2048]{2,1,0:T(8,128)(2,1)} %get-tuple-element.19), calls=%async_computation | async-start | bytes 1048576 | tf_op jit(solution)/shard_map/all_to_all | solution.py:451
  11.7 0.0 collective-permute-start
  11.7 1.2 collective-permute-done.args_1_
  12.9 1.6 %collective-permute-start.3 = (f32[16,128]{1,0:T(8,128)S(1)}, f32[16,128]{1,0:T(8,128)S(1)}, u32[]{:S(2)}, u32[]{:S(2)}) collective-permute-start(f32[16,128]{1,0:T(8,128)S(1)} %pair.1.args_0_), channel_id=1, source_target_pairs={{6,0},{0,2},{2,4},{4,6},{7,1},{1,3},{3,5},{5,7},{14,8},{8,10},{10,... | collective-permute-start | bytes 24584 | tf_op jit(solution)/shard_map/ppermute | solution.py:456
  14.6 2.9 %collective-permute-start.2 = (f32[16,128]{1,0:T(8,128)S(1)}, f32[16,128]{1,0:T(8,128)S(1)}, u32[]{:S(2)}, u32[]{:S(2)}) collective-permute-start(f32[16,128]{1,0:T(8,128)S(1)} %pair.1.args_0_), channel_id=1, source_target_pairs={{4,0},{6,2},{0,4},{2,6},{5,1},{7,3},{1,5},{3,7},{12,8},{14,10},{8,... | collective-permute-start | bytes 24584 | tf_op jit(solution)/shard_map/ppermute | solution.py:456
  17.5 1.3 %collective-permute-start.1 = (f32[16,128]{1,0:T(8,128)S(1)}, f32[16,128]{1,0:T(8,128)S(1)}, u32[]{:S(2)}, u32[]{:S(2)}) collective-permute-start(f32[16,128]{1,0:T(8,128)S(1)} %pair.1.args_0_), channel_id=1, source_target_pairs={{2,0},{4,2},{6,4},{0,6},{3,1},{5,3},{7,5},{1,7},{10,8},{12,10},{14... | collective-permute-start | bytes 24584 | tf_op jit(solution)/shard_map/ppermute | solution.py:456
  18.8 0.0 copy-start
  18.8 1.6 %copy-done = bf16[512,2048]{1,0:T(8,128)(2,1)S(1)} copy-done((bf16[512,2048]{1,0:T(8,128)(2,1)S(1)}, bf16[512,2048]{1,0:T(8,128)(2,1)}, u32[]{:S(2)}) %copy-start) | copy-done | bytes 2097176
  20.4 0.0 copy-start.2
  20.4 0.7 copy-done.2
  21.1 6.8 %source_group.1 = (f32[40,128]{1,0:T(8,128)S(1)}, f32[1,2048]{1,0:T(1,128)S(1)}) custom-call(bf16[512,2048]{1,0:T(8,128)(2,1)S(1)} %copy-done, s32[1,2048]{1,0:T(1,128)S(1)} %bitcast.16), custom_call_target="tpu_custom_call" | custom-call | tf_op jit(solution)/shard_map/source_group/pallas_call | solution.py:472
  27.9 0.0 collective-permute-done.3.args_3_
  27.9 0.0 collective-permute-done.2.args_2_
  27.9 0.0 collective-permute-done.1.args_1_
  27.9 1.6 %collective-permute-start.6 = (f32[40,128]{1,0:T(8,128)S(1)}, f32[40,128]{1,0:T(8,128)S(1)}, u32[]{:S(2)}, u32[]{:S(2)}) collective-permute-start(f32[40,128]{1,0:T(8,128)S(1)} %near.1.args_0_), channel_id=1, source_target_pairs={{24,0},{0,8},{8,16},{16,24},{25,1},{1,9},{9,17},{17,25},{26,2},{2,... | collective-permute-start | bytes 61448 | tf_op jit(solution)/shard_map/ppermute | solution.py:456
  29.5 2.7 %collective-permute-start.5 = (f32[40,128]{1,0:T(8,128)S(1)}, f32[40,128]{1,0:T(8,128)S(1)}, u32[]{:S(2)}, u32[]{:S(2)}) collective-permute-start(f32[40,128]{1,0:T(8,128)S(1)} %near.1.args_0_), channel_id=1, source_target_pairs={{16,0},{24,8},{0,16},{8,24},{17,1},{25,9},{1,17},{9,25},{18,2},{26... | collective-permute-start | bytes 61448 | tf_op jit(solution)/shard_map/ppermute | solution.py:456
  32.2 1.4 %collective-permute-start.4 = (f32[40,128]{1,0:T(8,128)S(1)}, f32[40,128]{1,0:T(8,128)S(1)}, u32[]{:S(2)}, u32[]{:S(2)}) collective-permute-start(f32[40,128]{1,0:T(8,128)S(1)} %near.1.args_0_), channel_id=1, source_target_pairs={{8,0},{16,8},{24,16},{0,24},{9,1},{17,9},{25,17},{1,25},{10,2},{18... | collective-permute-start | bytes 61448 | tf_op jit(solution)/shard_map/ppermute | solution.py:456
  33.7 0.0 collective-permute-done.6.args_3_
  33.7 1.1 collective-permute-done.5.args_2_
  34.8 1.2 collective-permute-done.4.args_1_
  36.0 0.0 all-to-all-done.args_0_
  36.0 0.3 collective-permute-start.9
  36.3 3.8 %collective-permute-start.8 = (bf16[8,16,2048]{2,1,0:T(8,128)(2,1)S(1)}, bf16[8,16,2048]{2,1,0:T(8,128)(2,1)}, u32[]{:S(2)}, u32[]{:S(2)}) collective-permute-start(bf16[8,16,2048]{2,1,0:T(8,128)(2,1)S(1)} %all-to-all-done.args_0_), channel_id=1, source_target_pairs={{16,0},{24,8},{0,16},{8,24},{17,1},{25,9},{1,17},{9,25},{18,2},{26... | collective-permute-start | bytes 1572872 | tf_op jit(solution)/shard_map/ppermute | solution.py:456
  40.1 0.0 collective-permute-start.7
  40.2 0.8 middle.1
  40.9 7.2 %all-to-all-start.1 = ((f32[8,40,128]{2,1,0:T(8,128)}), f32[8,40,128]{2,1,0:T(8,128)S(1)}, u32[]{:S(2)}, u32[]{:S(2)}) async-start(f32[8,40,128]{2,1,0:T(8,128)} %middle.1), calls=%async_computation.1 | async-start | bytes 327680 | tf_op jit(solution)/shard_map/all_to_all | solution.py:494
  48.1 0.0 copy-start.6
  48.1 0.0 copy-start.3
  48.1 0.0 copy-start.5
  48.1 2.9 %copy.12 = bf16[512,2048]{0,1:T(8,128)(2,1)S(1)} copy(bf16[512,2048]{1,0:T(8,128)(2,1)} %embed.3) | data formatting | bytes 4194304 | tf_op args[0]
  51.7 0.0 copy-done.6
  51.7 0.1 copy.11
  51.8 0.1 reshape.28.pairs
  51.9 4.2 %all-to-all-done.1.got = f32[8,40,128]{2,1,0:T(8,128)S(1)} async-done(((f32[8,40,128]{2,1,0:T(8,128)}), f32[8,40,128]{2,1,0:T(8,128)S(1)}, u32[]{:S(2)}, u32[]{:S(2)}) %all-to-all-start.1) | async-done | bytes 163872 | tf_op jit(solution)/shard_map/all_to_all | solution.py:494
  56.1 0.0 copy-done.3
  56.1 1.0 label.1
  57.1 0.0 collective-permute-done.9.args_3_
  57.1 4.2 %collective-permute-done.8.args_2_ = bf16[8,16,2048]{2,1,0:T(8,128)(2,1)} collective-permute-done((bf16[8,16,2048]{2,1,0:T(8,128)(2,1)S(1)}, bf16[8,16,2048]{2,1,0:T(8,128)(2,1)}, u32[]{:S(2)}, u32[]{:S(2)}) %collective-permute-start.8) | collective-permute-done | bytes 524320 | tf_op jit(solution)/shard_map/ppermute | solution.py:456
  61.3 0.0 collective-permute-done.7.args_1_
  61.3 0.0 copy-done.5
  61.3 6.1 %cost_rows.1 = (f32[24,256,256]{2,1,0:T(8,128)S(1)}, f32[8,16,128]{2,1,0:T(8,128)S(1)}) custom-call(s32[48]{0:T(128)S(1)} %reshape.28.pairs, s32[1]{0:T(128)} %bitcast.11.count, s32[1]{0:T(128)} %bitcast.1.place, bf16[16,2048]{1,0:T(8,128)(2,1)S(1)} %get-tuple-element.27.xa, bf16[2048,512]{1,0:T(8,128)(2,1)S(1)} %bitcast.15, ...), custom_call_target="tpu_custom_call" | custom-call | tf_op jit(solution)/shard_map/cost_rows/pallas_call | solution.py:508
  67.4 8.0 %all_to_all.30.g_ref = f32[8,16,128]{2,1,0:T(8,128)S(1)} all-to-all(f32[8,16,128]{2,1,0:T(8,128)S(1)} %get-tuple-element.30), channel_id=1, replica_groups=mesh['z'=8,'x'=4,'y'=4,'c'=2] {'y','c'}, dimensions={0} | all-to-all | bytes 131072 | tf_op jit(solution)/shard_map/all_to_all | solution.py:553
  75.4 2.5 %columns.2 = (f32[32,16,128]{2,1,0:T(8,128)S(1)}, f32[16,128]{1,0:T(8,128)}) custom-call(s32[48]{0:T(128)S(1)} %reshape.28.pairs, s32[1]{0:T(128)} %bitcast.12.count, f32[24,256,256]{2,1,0:T(8,128)S(1)} %get-tuple-element.29.tiles, f32[8,16,128]{2,1,0:T(8,128)S(1)} %all_to_all.30.g_ref), custom_call_target="tpu_custom_call" | custom-call | tf_op jit(solution)/shard_map/columns/pallas_call | solution.py:532
  77.9 21.0 %all_to_all.31.g_ref = f32[32,16,128]{2,1,0:T(8,128)S(1)} all-to-all(f32[32,16,128]{2,1,0:T(8,128)S(1)} %get-tuple-element.31), channel_id=1, replica_groups=mesh['z'=8,'x'=4,'y'=4,'c'=2] {'z','x'}, dimensions={0} | all-to-all | bytes 524288 | tf_op jit(solution)/shard_map/all_to_all | solution.py:554
  99.0 3.2 %rows.1 = f32[8,16,128]{2,1,0:T(8,128)S(1)} custom-call(s32[48]{0:T(128)S(1)} %reshape.28.pairs, s32[1]{0:T(128)} %bitcast.13.count, f32[24,256,256]{2,1,0:T(8,128)S(1)} %get-tuple-element.29.tiles, f32[32,16,128]{2,1,0:T(8,128)S(1)} %all_to_all.31.g_ref), custom_call_target="tpu_custom_call" | custom-call | tf_op jit(solution)/shard_map/rows/pallas_call | solution.py:543
  102.1 8.0 %all_to_all.32.g_ref = f32[8,16,128]{2,1,0:T(8,128)S(1)} all-to-all(f32[8,16,128]{2,1,0:T(8,128)S(1)} %rows.1), channel_id=1, replica_groups=mesh['z'=8,'x'=4,'y'=4,'c'=2] {'y','c'}, dimensions={0} | all-to-all | bytes 131072 | tf_op jit(solution)/shard_map/all_to_all | solution.py:555
  110.1 2.5 %columns.3 = (f32[32,16,128]{2,1,0:T(8,128)S(1)}, f32[16,128]{1,0:T(8,128)}) custom-call(s32[48]{0:T(128)S(1)} %reshape.28.pairs, s32[1]{0:T(128)} %bitcast.14.count, f32[24,256,256]{2,1,0:T(8,128)S(1)} %get-tuple-element.29.tiles, f32[8,16,128]{2,1,0:T(8,128)S(1)} %all_to_all.32.g_ref), custom_call_target="tpu_custom_call" | custom-call | tf_op jit(solution)/shard_map/columns/pallas_call | solution.py:532
  112.6 16.9 %all_to_all.33.g_ref = f32[32,16,128]{2,1,0:T(8,128)S(1)} all-to-all(f32[32,16,128]{2,1,0:T(8,128)S(1)} %get-tuple-element.33), channel_id=1, replica_groups=mesh['z'=8,'x'=4,'y'=4,'c'=2] {'z','x'}, dimensions={0} | all-to-all | bytes 524288 | tf_op jit(solution)/shard_map/all_to_all | solution.py:563
  129.5 0.7 last.1
  (2 shorter events, 0.1 us)
Async XLA Ops:
  0.6 0.8 copy-start.1
  1.5 0.7 copy-start.4
  3.1 32.9 %all-to-all-start = ((bf16[8,16,2048]{2,1,0:T(8,128)(2,1)}), bf16[8,16,2048]{2,1,0:T(8,128)(2,1)S(1)}, u32[]{:S(2)}, u32[]{:S(2)}) async-start(bf16[8,16,2048]{2,1,0:T(8,128)(2,1)} %get-tuple-element.19), calls=%async_computation | async-start | bytes 1048576 | tf_op jit(solution)/shard_map/all_to_all | solution.py:451
  11.7 1.2 collective-permute-start
  12.9 15.0 %collective-permute-start.3 = (f32[16,128]{1,0:T(8,128)S(1)}, f32[16,128]{1,0:T(8,128)S(1)}, u32[]{:S(2)}, u32[]{:S(2)}) collective-permute-start(f32[16,128]{1,0:T(8,128)S(1)} %pair.1.args_0_), channel_id=1, source_target_pairs={{6,0},{0,2},{2,4},{4,6},{7,1},{1,3},{3,5},{5,7},{14,8},{8,10},{10,... | collective-permute-start | bytes 24584 | tf_op jit(solution)/shard_map/ppermute | solution.py:456
  14.6 13.3 %collective-permute-start.2 = (f32[16,128]{1,0:T(8,128)S(1)}, f32[16,128]{1,0:T(8,128)S(1)}, u32[]{:S(2)}, u32[]{:S(2)}) collective-permute-start(f32[16,128]{1,0:T(8,128)S(1)} %pair.1.args_0_), channel_id=1, source_target_pairs={{4,0},{6,2},{0,4},{2,6},{5,1},{7,3},{1,5},{3,7},{12,8},{14,10},{8,... | collective-permute-start | bytes 24584 | tf_op jit(solution)/shard_map/ppermute | solution.py:456
  17.5 10.4 %collective-permute-start.1 = (f32[16,128]{1,0:T(8,128)S(1)}, f32[16,128]{1,0:T(8,128)S(1)}, u32[]{:S(2)}, u32[]{:S(2)}) collective-permute-start(f32[16,128]{1,0:T(8,128)S(1)} %pair.1.args_0_), channel_id=1, source_target_pairs={{2,0},{4,2},{6,4},{0,6},{3,1},{5,3},{7,5},{1,7},{10,8},{12,10},{14... | collective-permute-start | bytes 24584 | tf_op jit(solution)/shard_map/ppermute | solution.py:456
  18.8 1.6 %copy-start = (bf16[512,2048]{1,0:T(8,128)(2,1)S(1)}, bf16[512,2048]{1,0:T(8,128)(2,1)}, u32[]{:S(2)}) copy-start(bf16[512,2048]{1,0:T(8,128)(2,1)} %embed.3) | copy-start | bytes 6291460
  20.4 0.7 copy-start.2
  27.9 5.7 %collective-permute-start.6 = (f32[40,128]{1,0:T(8,128)S(1)}, f32[40,128]{1,0:T(8,128)S(1)}, u32[]{:S(2)}, u32[]{:S(2)}) collective-permute-start(f32[40,128]{1,0:T(8,128)S(1)} %near.1.args_0_), channel_id=1, source_target_pairs={{24,0},{0,8},{8,16},{16,24},{25,1},{1,9},{9,17},{17,25},{26,2},{2,... | collective-permute-start | bytes 61448 | tf_op jit(solution)/shard_map/ppermute | solution.py:456
  29.5 5.3 %collective-permute-start.5 = (f32[40,128]{1,0:T(8,128)S(1)}, f32[40,128]{1,0:T(8,128)S(1)}, u32[]{:S(2)}, u32[]{:S(2)}) collective-permute-start(f32[40,128]{1,0:T(8,128)S(1)} %near.1.args_0_), channel_id=1, source_target_pairs={{16,0},{24,8},{0,16},{8,24},{17,1},{25,9},{1,17},{9,25},{18,2},{26... | collective-permute-start | bytes 61448 | tf_op jit(solution)/shard_map/ppermute | solution.py:456
  32.2 3.8 %collective-permute-start.4 = (f32[40,128]{1,0:T(8,128)S(1)}, f32[40,128]{1,0:T(8,128)S(1)}, u32[]{:S(2)}, u32[]{:S(2)}) collective-permute-start(f32[40,128]{1,0:T(8,128)S(1)} %near.1.args_0_), channel_id=1, source_target_pairs={{8,0},{16,8},{24,16},{0,24},{9,1},{17,9},{25,17},{1,25},{10,2},{18... | collective-permute-start | bytes 61448 | tf_op jit(solution)/shard_map/ppermute | solution.py:456
  36.0 21.1 %collective-permute-start.9 = (bf16[8,16,2048]{2,1,0:T(8,128)(2,1)S(1)}, bf16[8,16,2048]{2,1,0:T(8,128)(2,1)S(1)}, u32[]{:S(2)}, u32[]{:S(2)}) collective-permute-start(bf16[8,16,2048]{2,1,0:T(8,128)(2,1)S(1)} %all-to-all-done.args_0_), channel_id=1, source_target_pairs={{24,0},{0,8},{8,16},{16,24},{25,1},{1,9},{9,17},{17,25},{26,2},{2,... | collective-permute-start | bytes 1572872 | tf_op jit(solution)/shard_map/ppermute | solution.py:456
  36.3 25.0 %collective-permute-start.8 = (bf16[8,16,2048]{2,1,0:T(8,128)(2,1)S(1)}, bf16[8,16,2048]{2,1,0:T(8,128)(2,1)}, u32[]{:S(2)}, u32[]{:S(2)}) collective-permute-start(bf16[8,16,2048]{2,1,0:T(8,128)(2,1)S(1)} %all-to-all-done.args_0_), channel_id=1, source_target_pairs={{16,0},{24,8},{0,16},{8,24},{17,1},{25,9},{1,17},{9,25},{18,2},{26... | collective-permute-start | bytes 1572872 | tf_op jit(solution)/shard_map/ppermute | solution.py:456
  40.1 21.2 %collective-permute-start.7 = (bf16[8,16,2048]{2,1,0:T(8,128)(2,1)S(1)}, bf16[8,16,2048]{2,1,0:T(8,128)(2,1)}, u32[]{:S(2)}, u32[]{:S(2)}) collective-permute-start(bf16[8,16,2048]{2,1,0:T(8,128)(2,1)S(1)} %all-to-all-done.args_0_), channel_id=1, source_target_pairs={{8,0},{16,8},{24,16},{0,24},{9,1},{17,9},{25,17},{1,25},{10,2},{18... | collective-permute-start | bytes 1572872 | tf_op jit(solution)/shard_map/ppermute | solution.py:456
  40.9 15.2 %all-to-all-start.1 = ((f32[8,40,128]{2,1,0:T(8,128)}), f32[8,40,128]{2,1,0:T(8,128)S(1)}, u32[]{:S(2)}, u32[]{:S(2)}) async-start(f32[8,40,128]{2,1,0:T(8,128)} %middle.1), calls=%async_computation.1 | async-start | bytes 327680 | tf_op jit(solution)/shard_map/all_to_all | solution.py:494
  48.1 3.6 %copy-start.6 = (s32[1,1,24,2]{2,3,1,0:T(2,128)S(1)}, s32[1,1,24,2]{2,3,1,0:T(2,128)}, u32[]{:S(2)}) copy-start(s32[1,1,24,2]{2,3,1,0:T(2,128)} %param.10) | copy-start | bytes 580
  48.1 8.0 %copy-start.3 = (s32[2048]{0:T(1024)S(1)}, s32[2048]{0:T(1024)}, u32[]{:S(2)}) copy-start(s32[2048]{0:T(1024)} %param.8) | copy-start | bytes 24580
  48.1 13.2 %copy-start.5 = (s32[2048]{0:T(1024)S(1)}, s32[2048]{0:T(1024)}, u32[]{:S(2)}) copy-start(s32[2048]{0:T(1024)} %param.9) | copy-start | bytes 24580

commit v7 on v4

--- a/solution.py
+++ b/solution.py
@@ -62,13 +62,20 @@
     return jnp.where(part == 0, mean, spread)[:8], wide
 
 
-def target_group_kernel(embed, labels, out_ref):
+def first_kernel(embed, labels, near_ref, out_ref, sems):
+    copies = [
+        pltpu.make_async_copy(embed, near_ref.at[k], sems.at[k]) for k in range(near_ref.shape[0])
+    ]
+    for copy in copies:
+        copy.start()
     onehot = repeated_onehot(labels[...])
     counts = jnp.maximum(jnp.sum(onehot, axis=1, keepdims=True), 1.0)
     group, _ = class_group(embed[...], onehot.astype(jnp.bfloat16), counts)
     out_ref[...] = jnp.zeros(out_ref.shape, jnp.float32)
     out_ref[0:8, 0 : group.shape[1]] = group
     out_ref[8:16, :] = jnp.broadcast_to(counts[:8], (8, LANES))
+    for copy in copies:
+        copy.wait()
 
 
 def source_group_kernel(embed, labels, out_ref, sq_ref):
@@ -190,16 +197,6 @@
     ).astype(jnp.bfloat16)
 
 
-def spread_kernel(x, out_ref, sems):
-    copies = [
-        pltpu.make_async_copy(x, out_ref.at[k], sems.at[k]) for k in range(out_ref.shape[0])
-    ]
-    for copy in copies:
-        copy.start()
-    for copy in copies:
-        copy.wait()
-
-
 def three_parts(v):
     hi = v.astype(jnp.bfloat16).astype(jnp.float32)
     rest = v - hi
@@ -400,15 +397,18 @@
 
     n_x, n_z = lax.axis_size("x"), lax.axis_size("z")
     part = target_embed.shape[0]
-    near = pl.pallas_call(
-        spread_kernel,
-        out_shape=jax.ShapeDtypeStruct((n_z,) + target_embed.shape, jnp.bfloat16),
-        in_specs=[pl.BlockSpec(memory_space=pl.ANY)],
-        out_specs=pl.BlockSpec(memory_space=pl.ANY),
+    near, tgt_group = pl.pallas_call(
+        first_kernel,
+        out_shape=(
+            jax.ShapeDtypeStruct((n_z,) + target_embed.shape, jnp.bfloat16),
+            f32(16, LANES),
+        ),
+        in_specs=[vmem(), vmem()],
+        out_specs=(pl.BlockSpec(memory_space=pl.ANY), vmem()),
         scratch_shapes=[pltpu.SemaphoreType.DMA((n_z,))],
         compiler_params=params(),
-        name="spread",
-    )(target_embed)
+        name="first",
+    )(target_embed, target_labels[None])
     near = lax.all_to_all(near, "z", 0, 0)
 
     def around(x, axis):
@@ -429,13 +429,6 @@
             name=name,
         )(lax.axis_index(axis).reshape(1), *pieces, *more)
 
-    tgt_group = call(
-        target_group_kernel,
-        f32(16, LANES),
-        target_embed,
-        target_labels[None],
-        name="target_group",
-    )
     tgt_group = join_targets(pair_kernel, f32(16, LANES), tgt_group, "c", name="pair")
     src_group, src_sq = call(
         source_group_kernel,
@@ -447,7 +440,7 @@
     stats = join_targets(
         near_kernel, f32(n_z, 48, LANES), tgt_group, "y", src_group, name="near"
     )
-    near, stats, source_tall = lax.optimization_barrier((near, stats, source_embed.T))
+    near, stats = lax.optimization_barrier((near, stats))
 
     pieces = around(near, "x")
     stats = lax.all_to_all(stats, "z", 0, 0)
@@ -486,7 +479,7 @@
         count,
         lax.axis_index("x").reshape(1),
         xa,
-        source_tall,
+        source_embed.T,
         *pieces,
         target_labels[None],
     )

time: 128 us -> 126 us (0.984)
  Pallas kernels: 21.4 us -> 17.6 us
  blocking collectives: 66.7 us -> 69.6 us
    all_to_all x1, blocking collectives: 7.99 us -> 11.2 us  [on_device(): sent, _ = columns(lax.all_to_all(sent, TGT, 0, 0))]
    all_to_all x1, waiting for transfers between devices: 0.01 us -> 3.14 us  [on_device(): near = lax.all_to_all(near, 'z', 0, 0)]
    all_to_all x1, waiting for transfers between devices: 5.18 us -> 2.27 us  [on_device(): stats = lax.all_to_all(stats, 'x', 0, 0)]
    all_to_all x1, blocking collectives: 15.3 us -> 12.5 us  [on_device(): stats = lax.all_to_all(stats, 'z', 0, 0)]
    pallas_call x1, Pallas kernels: 5.94 us -> 4.39 us  [on_device(): pl.pallas_call(functools.partial(cost_kernel, n_x), out_shape=(f32(MAXP,...]
    pallas_call x4 -> x3, Pallas kernels: 5.67 us -> 5.1 us  [call(): pl.pallas_call(kernel, out_shape=out_shape, in_specs=[vmem()] * len(args)...]
  transfers between devices with their start and end apart: 9 -> 9, of which waited for: 2 -> 3; matrix products, arithmetic and copies ran while one was open for 2% -> 2% of each run, Pallas kernels for 5% -> 4%
where the time goes in v7:
time: 126 us
  blocking collectives  69.6 us (55%)
  starting transfers between devices  23.5 us (19%)
  Pallas kernels  17.6 us (14%)
  local copies, waits for them, and re-layouts  6.89 us (5%)
  waiting for transfers between devices  6.59 us (5%)
  between operations  1.39 us (1%)
    all_to_all x1, blocking collectives, on_device(): sent = rows(lax.all_to_all(sent, SRC, 0, 0))  19.4 us
    all_to_all x1, blocking collectives, on_device(): lax.all_to_all(sent, SRC, 0, 0)  17.4 us
    all_to_all x1, blocking collectives, on_device(): stats = lax.all_to_all(stats, 'z', 0, 0)  12.5 us
    ppermute x7, starting transfers between devices, around(): lax.ppermute(x, axis, [((i + far) % n, i) for i in range(n)])  11.6 us
    all_to_all x1, blocking collectives, on_device(): sent, _ = columns(lax.all_to_all(sent, TGT, 0, 0))  11.2 us
    all_to_all x1, blocking collectives, on_device(): sent, src_pot = columns(lax.all_to_all(sent, TGT, 0, 0))  9.11 us
    all_to_all x1, starting transfers between devices, on_device(): near = lax.all_to_all(near, 'z', 0, 0)  8.58 us
    unnamed x16, local copies, waits for them, and re-layouts  6.79 us
  transfers between devices with their start and end apart: 9, of which 3 were waited for; matrix products, arithmetic and copies ran while one was open for 2% of the time, Pallas kernels for 4%

profile of v7, /device:TPU:32, one launch (start us, length us, event | category | flops | bytes accessed | tf_op | source)
XLA Modules:
  0.0 125.6 jit_solution(9521405126566152669)
XLA Ops:
  0.6 0.0 copy-start.1
  0.6 0.8 copy-done.1
  1.5 0.0 copy-start.4
  1.5 0.7 copy-done.4
  2.2 0.9 first.1
  3.1 8.6 %all-to-all-start = ((bf16[8,16,2048]{2,1,0:T(8,128)(2,1)}), bf16[8,16,2048]{2,1,0:T(8,128)(2,1)S(1)}, u32[]{:S(2)}, u32[]{:S(2)}) async-start(bf16[8,16,2048]{2,1,0:T(8,128)(2,1)} %get-tuple-element.16), calls=%async_computation | async-start | bytes 1048576 | tf_op jit(solution)/shard_map/all_to_all | solution.py:412
  11.6 0.0 collective-permute-start
  11.6 1.2 collective-permute-done.args_1_
  12.8 1.6 %collective-permute-start.3 = (f32[16,128]{1,0:T(8,128)S(1)}, f32[16,128]{1,0:T(8,128)S(1)}, u32[]{:S(2)}, u32[]{:S(2)}) collective-permute-start(f32[16,128]{1,0:T(8,128)S(1)} %pair.1.args_0_), channel_id=1, source_target_pairs={{6,0},{0,2},{2,4},{4,6},{7,1},{1,3},{3,5},{5,7},{14,8},{8,10},{10,... | collective-permute-start | bytes 24584 | tf_op jit(solution)/shard_map/ppermute | solution.py:417
  14.5 2.9 %collective-permute-start.2 = (f32[16,128]{1,0:T(8,128)S(1)}, f32[16,128]{1,0:T(8,128)S(1)}, u32[]{:S(2)}, u32[]{:S(2)}) collective-permute-start(f32[16,128]{1,0:T(8,128)S(1)} %pair.1.args_0_), channel_id=1, source_target_pairs={{4,0},{6,2},{0,4},{2,6},{5,1},{7,3},{1,5},{3,7},{12,8},{14,10},{8,... | collective-permute-start | bytes 24584 | tf_op jit(solution)/shard_map/ppermute | solution.py:417
  17.4 1.3 %collective-permute-start.1 = (f32[16,128]{1,0:T(8,128)S(1)}, f32[16,128]{1,0:T(8,128)S(1)}, u32[]{:S(2)}, u32[]{:S(2)}) collective-permute-start(f32[16,128]{1,0:T(8,128)S(1)} %pair.1.args_0_), channel_id=1, source_target_pairs={{2,0},{4,2},{6,4},{0,6},{3,1},{5,3},{7,5},{1,7},{10,8},{12,10},{14... | collective-permute-start | bytes 24584 | tf_op jit(solution)/shard_map/ppermute | solution.py:417
  18.7 0.0 copy-start
  18.7 1.6 %copy-done = bf16[512,2048]{1,0:T(8,128)(2,1)S(1)} copy-done((bf16[512,2048]{1,0:T(8,128)(2,1)S(1)}, bf16[512,2048]{1,0:T(8,128)(2,1)}, u32[]{:S(2)}) %copy-start) | copy-done | bytes 2097176
  20.3 0.0 copy-start.2
  20.3 0.7 copy-done.2
  21.0 3.5 %source_group.1 = (f32[40,128]{1,0:T(8,128)S(1)}, f32[1,2048]{1,0:T(1,128)S(1)}) custom-call(bf16[512,2048]{1,0:T(8,128)(2,1)S(1)} %copy-done, s32[1,2048]{1,0:T(1,128)S(1)} %bitcast.16), custom_call_target="tpu_custom_call" | custom-call | tf_op jit(solution)/shard_map/source_group/pallas_call | solution.py:389
  24.5 0.0 collective-permute-done.3.args_3_
  24.5 0.0 collective-permute-done.2.args_2_
  24.5 0.0 collective-permute-done.1.args_1_
  24.5 3.1 %all-to-all-done.args_0_ = bf16[8,16,2048]{2,1,0:T(8,128)(2,1)S(1)} async-done(((bf16[8,16,2048]{2,1,0:T(8,128)(2,1)}), bf16[8,16,2048]{2,1,0:T(8,128)(2,1)S(1)}, u32[]{:S(2)}, u32[]{:S(2)}) %all-to-all-start) | async-done | bytes 524320 | tf_op jit(solution)/shard_map/all_to_all | solution.py:412
  27.7 1.5 %collective-permute-start.6 = (bf16[8,16,2048]{2,1,0:T(8,128)(2,1)S(1)}, bf16[8,16,2048]{2,1,0:T(8,128)(2,1)S(1)}, u32[]{:S(2)}, u32[]{:S(2)}) collective-permute-start(bf16[8,16,2048]{2,1,0:T(8,128)(2,1)S(1)} %all-to-all-done.args_0_), channel_id=1, source_target_pairs={{24,0},{0,8},{8,16},{16,24},{25,1},{1,9},{9,17},{17,25},{26,2},{2,... | collective-permute-start | bytes 1572872 | tf_op jit(solution)/shard_map/ppermute | solution.py:417
  29.2 2.7 %collective-permute-start.5 = (bf16[8,16,2048]{2,1,0:T(8,128)(2,1)S(1)}, bf16[8,16,2048]{2,1,0:T(8,128)(2,1)}, u32[]{:S(2)}, u32[]{:S(2)}) collective-permute-start(bf16[8,16,2048]{2,1,0:T(8,128)(2,1)S(1)} %all-to-all-done.args_0_), channel_id=1, source_target_pairs={{16,0},{24,8},{0,16},{8,24},{17,1},{25,9},{1,17},{9,25},{18,2},{26... | collective-permute-start | bytes 1572872 | tf_op jit(solution)/shard_map/ppermute | solution.py:417
  31.9 1.4 %collective-permute-start.4 = (bf16[8,16,2048]{2,1,0:T(8,128)(2,1)S(1)}, bf16[8,16,2048]{2,1,0:T(8,128)(2,1)}, u32[]{:S(2)}, u32[]{:S(2)}) collective-permute-start(bf16[8,16,2048]{2,1,0:T(8,128)(2,1)S(1)} %all-to-all-done.args_0_), channel_id=1, source_target_pairs={{8,0},{16,8},{24,16},{0,24},{9,1},{17,9},{25,17},{1,25},{10,2},{18... | collective-permute-start | bytes 1572872 | tf_op jit(solution)/shard_map/ppermute | solution.py:417
  33.3 12.5 %all_to_all.35.got = f32[8,48,128]{2,1,0:T(8,128)S(1)} all-to-all(f32[8,48,128]{2,1,0:T(8,128)S(1)} %near.1), channel_id=1, replica_groups=mesh['z'=8,'x'=4,'y'=4,'c'=2] {'z'}, dimensions={0} | all-to-all | bytes 393216 | tf_op jit(solution)/shard_map/all_to_all | solution.py:446
  45.8 0.7 middle.1
  46.5 3.3 %all-to-all-start.2 = ((f32[4,72,128]{2,1,0:T(8,128)}), f32[4,72,128]{2,1,0:T(8,128)S(1)}, u32[]{:S(2)}, u32[]{:S(2)}) async-start(f32[4,72,128]{2,1,0:T(8,128)} %middle.1), calls=%async_computation.2 | async-start | bytes 294912 | tf_op jit(solution)/shard_map/all_to_all | solution.py:450
  49.9 0.0 copy-start.6
  49.9 0.0 copy-start.3
  49.9 0.0 copy-start.5
  49.9 2.9 %copy.12 = bf16[512,2048]{0,1:T(8,128)(2,1)S(1)} copy(bf16[512,2048]{1,0:T(8,128)(2,1)} %embed.3) | data formatting | bytes 4194304 | tf_op args[0]
  53.5 0.0 copy-done.6
  53.5 0.1 copy.11
  53.6 0.1 reshape.27.pairs
  53.7 2.3 %all-to-all-done.2.got = f32[4,72,128]{2,1,0:T(8,128)S(1)} async-done(((f32[4,72,128]{2,1,0:T(8,128)}), f32[4,72,128]{2,1,0:T(8,128)S(1)}, u32[]{:S(2)}, u32[]{:S(2)}) %all-to-all-start.2) | async-done | bytes 147488 | tf_op jit(solution)/shard_map/all_to_all | solution.py:450
  55.9 0.0 copy-done.3
  55.9 0.9 label.1
  56.8 0.0 collective-permute-done.6.args_3_
  56.8 0.0 collective-permute-done.5.args_2_
  56.8 0.0 collective-permute-done.4.args_1_
  56.8 0.0 copy-done.5
  56.9 4.4 %cost_rows.1 = (f32[24,256,256]{2,1,0:T(8,128)S(1)}, f32[8,16,128]{2,1,0:T(8,128)S(1)}) custom-call(s32[48]{0:T(128)S(1)} %reshape.27.pairs, s32[1]{0:T(128)} %bitcast.11.count, s32[1]{0:T(128)} %bitcast.1.place, bf16[16,2048]{1,0:T(8,128)(2,1)S(1)} %get-tuple-element.21.xa, bf16[2048,512]{1,0:T(8,128)(2,1)S(1)} %bitcast.15, ...), custom_call_target="tpu_custom_call" | custom-call | tf_op jit(solution)/shard_map/cost_rows/pallas_call | solution.py:464
  61.2 11.2 %all_to_all.36.g_ref = f32[8,16,128]{2,1,0:T(8,128)S(1)} all-to-all(f32[8,16,128]{2,1,0:T(8,128)S(1)} %get-tuple-element.24), channel_id=1, replica_groups=mesh['z'=8,'x'=4,'y'=4,'c'=2] {'y','c'}, dimensions={0} | all-to-all | bytes 131072 | tf_op jit(solution)/shard_map/all_to_all | solution.py:509
  72.5 2.0 %columns.2 = (f32[32,16,128]{2,1,0:T(8,128)S(1)}, f32[16,128]{1,0:T(8,128)}) custom-call(s32[48]{0:T(128)S(1)} %reshape.27.pairs, s32[1]{0:T(128)} %bitcast.12.count, f32[24,256,256]{2,1,0:T(8,128)S(1)} %get-tuple-element.23.tiles, f32[8,16,128]{2,1,0:T(8,128)S(1)} %all_to_all.36.g_ref), custom_call_target="tpu_custom_call" | custom-call | tf_op jit(solution)/shard_map/columns/pallas_call | solution.py:488
  74.5 19.4 %all_to_all.37.g_ref = f32[32,16,128]{2,1,0:T(8,128)S(1)} all-to-all(f32[32,16,128]{2,1,0:T(8,128)S(1)} %get-tuple-element.25), channel_id=1, replica_groups=mesh['z'=8,'x'=4,'y'=4,'c'=2] {'z','x'}, dimensions={0} | all-to-all | bytes 524288 | tf_op jit(solution)/shard_map/all_to_all | solution.py:510
  93.9 2.5 %rows.1 = f32[8,16,128]{2,1,0:T(8,128)S(1)} custom-call(s32[48]{0:T(128)S(1)} %reshape.27.pairs, s32[1]{0:T(128)} %bitcast.13.count, f32[24,256,256]{2,1,0:T(8,128)S(1)} %get-tuple-element.23.tiles, f32[32,16,128]{2,1,0:T(8,128)S(1)} %all_to_all.37.g_ref), custom_call_target="tpu_custom_call" | custom-call | tf_op jit(solution)/shard_map/rows/pallas_call | solution.py:499
  96.3 9.1 %all_to_all.38.g_ref = f32[8,16,128]{2,1,0:T(8,128)S(1)} all-to-all(f32[8,16,128]{2,1,0:T(8,128)S(1)} %rows.1), channel_id=1, replica_groups=mesh['z'=8,'x'=4,'y'=4,'c'=2] {'y','c'}, dimensions={0} | all-to-all | bytes 131072 | tf_op jit(solution)/shard_map/all_to_all | solution.py:511
  105.4 2.0 %columns.3 = (f32[32,16,128]{2,1,0:T(8,128)S(1)}, f32[16,128]{1,0:T(8,128)}) custom-call(s32[48]{0:T(128)S(1)} %reshape.27.pairs, s32[1]{0:T(128)} %bitcast.14.count, f32[24,256,256]{2,1,0:T(8,128)S(1)} %get-tuple-element.23.tiles, f32[8,16,128]{2,1,0:T(8,128)S(1)} %all_to_all.38.g_ref), custom_call_target="tpu_custom_call" | custom-call | tf_op jit(solution)/shard_map/columns/pallas_call | solution.py:488
  107.4 17.4 %all_to_all.39.g_ref = f32[32,16,128]{2,1,0:T(8,128)S(1)} all-to-all(f32[32,16,128]{2,1,0:T(8,128)S(1)} %get-tuple-element.27), channel_id=1, replica_groups=mesh['z'=8,'x'=4,'y'=4,'c'=2] {'z','x'}, dimensions={0} | all-to-all | bytes 524288 | tf_op jit(solution)/shard_map/all_to_all | solution.py:519
  124.9 0.7 last.1
  (2 shorter events, 0.1 us)
Async XLA Ops:
  0.6 0.8 copy-start.1
  1.5 0.7 copy-start.4
  3.1 24.6 %all-to-all-start = ((bf16[8,16,2048]{2,1,0:T(8,128)(2,1)}), bf16[8,16,2048]{2,1,0:T(8,128)(2,1)S(1)}, u32[]{:S(2)}, u32[]{:S(2)}) async-start(bf16[8,16,2048]{2,1,0:T(8,128)(2,1)} %get-tuple-element.16), calls=%async_computation | async-start | bytes 1048576 | tf_op jit(solution)/shard_map/all_to_all | solution.py:412
  11.6 1.2 collective-permute-start
  12.8 11.6 %collective-permute-start.3 = (f32[16,128]{1,0:T(8,128)S(1)}, f32[16,128]{1,0:T(8,128)S(1)}, u32[]{:S(2)}, u32[]{:S(2)}) collective-permute-start(f32[16,128]{1,0:T(8,128)S(1)} %pair.1.args_0_), channel_id=1, source_target_pairs={{6,0},{0,2},{2,4},{4,6},{7,1},{1,3},{3,5},{5,7},{14,8},{8,10},{10,... | collective-permute-start | bytes 24584 | tf_op jit(solution)/shard_map/ppermute | solution.py:417
  14.5 10.0 %collective-permute-start.2 = (f32[16,128]{1,0:T(8,128)S(1)}, f32[16,128]{1,0:T(8,128)S(1)}, u32[]{:S(2)}, u32[]{:S(2)}) collective-permute-start(f32[16,128]{1,0:T(8,128)S(1)} %pair.1.args_0_), channel_id=1, source_target_pairs={{4,0},{6,2},{0,4},{2,6},{5,1},{7,3},{1,5},{3,7},{12,8},{14,10},{8,... | collective-permute-start | bytes 24584 | tf_op jit(solution)/shard_map/ppermute | solution.py:417
  17.4 7.1 %collective-permute-start.1 = (f32[16,128]{1,0:T(8,128)S(1)}, f32[16,128]{1,0:T(8,128)S(1)}, u32[]{:S(2)}, u32[]{:S(2)}) collective-permute-start(f32[16,128]{1,0:T(8,128)S(1)} %pair.1.args_0_), channel_id=1, source_target_pairs={{2,0},{4,2},{6,4},{0,6},{3,1},{5,3},{7,5},{1,7},{10,8},{12,10},{14... | collective-permute-start | bytes 24584 | tf_op jit(solution)/shard_map/ppermute | solution.py:417
  18.7 1.6 %copy-start = (bf16[512,2048]{1,0:T(8,128)(2,1)S(1)}, bf16[512,2048]{1,0:T(8,128)(2,1)}, u32[]{:S(2)}) copy-start(bf16[512,2048]{1,0:T(8,128)(2,1)} %embed.3) | copy-start | bytes 6291460
  20.3 0.7 copy-start.2
  27.7 29.2 %collective-permute-start.6 = (bf16[8,16,2048]{2,1,0:T(8,128)(2,1)S(1)}, bf16[8,16,2048]{2,1,0:T(8,128)(2,1)S(1)}, u32[]{:S(2)}, u32[]{:S(2)}) collective-permute-start(bf16[8,16,2048]{2,1,0:T(8,128)(2,1)S(1)} %all-to-all-done.args_0_), channel_id=1, source_target_pairs={{24,0},{0,8},{8,16},{16,24},{25,1},{1,9},{9,17},{17,25},{26,2},{2,... | collective-permute-start | bytes 1572872 | tf_op jit(solution)/shard_map/ppermute | solution.py:417
  29.2 27.7 %collective-permute-start.5 = (bf16[8,16,2048]{2,1,0:T(8,128)(2,1)S(1)}, bf16[8,16,2048]{2,1,0:T(8,128)(2,1)}, u32[]{:S(2)}, u32[]{:S(2)}) collective-permute-start(bf16[8,16,2048]{2,1,0:T(8,128)(2,1)S(1)} %all-to-all-done.args_0_), channel_id=1, source_target_pairs={{16,0},{24,8},{0,16},{8,24},{17,1},{25,9},{1,17},{9,25},{18,2},{26... | collective-permute-start | bytes 1572872 | tf_op jit(solution)/shard_map/ppermute | solution.py:417
  31.9 24.9 %collective-permute-start.4 = (bf16[8,16,2048]{2,1,0:T(8,128)(2,1)S(1)}, bf16[8,16,2048]{2,1,0:T(8,128)(2,1)}, u32[]{:S(2)}, u32[]{:S(2)}) collective-permute-start(bf16[8,16,2048]{2,1,0:T(8,128)(2,1)S(1)} %all-to-all-done.args_0_), channel_id=1, source_target_pairs={{8,0},{16,8},{24,16},{0,24},{9,1},{17,9},{25,17},{1,25},{10,2},{18... | collective-permute-start | bytes 1572872 | tf_op jit(solution)/shard_map/ppermute | solution.py:417
  46.5 9.4 %all-to-all-start.2 = ((f32[4,72,128]{2,1,0:T(8,128)}), f32[4,72,128]{2,1,0:T(8,128)S(1)}, u32[]{:S(2)}, u32[]{:S(2)}) async-start(f32[4,72,128]{2,1,0:T(8,128)} %middle.1), calls=%async_computation.2 | async-start | bytes 294912 | tf_op jit(solution)/shard_map/all_to_all | solution.py:450
  49.9 3.6 %copy-start.6 = (s32[1,1,24,2]{2,3,1,0:T(2,128)S(1)}, s32[1,1,24,2]{2,3,1,0:T(2,128)}, u32[]{:S(2)}) copy-start(s32[1,1,24,2]{2,3,1,0:T(2,128)} %param.10) | copy-start | bytes 580
  49.9 6.0 %copy-start.3 = (s32[2048]{0:T(1024)S(1)}, s32[2048]{0:T(1024)}, u32[]{:S(2)}) copy-start(s32[2048]{0:T(1024)} %param.8) | copy-start | bytes 24580
  49.9 6.9 %copy-start.5 = (s32[2048]{0:T(1024)S(1)}, s32[2048]{0:T(1024)}, u32[]{:S(2)}) copy-start(s32[2048]{0:T(1024)} %param.9) | copy-start | bytes 24580

commit v8 on v7

--- a/solution.py
+++ b/solution.py
@@ -251,7 +251,8 @@
     for far, piece in enumerate(pieces):
         at = lax.rem(place[0] + far, n_x)
         for k in range(piece.shape[0]):
-            y[pl.ds(pl.multiple_of((k * n_x + at) * 16, 16), 16), :] = piece[k]
+            z = k + place[1] * (piece.shape[0] - 1 - 2 * k)
+            y[pl.ds(pl.multiple_of((z * n_x + at) * 16, 16), 16), :] = piece[k]
             v = piece[k].astype(jnp.float32)
             tgt_sq = tgt_sq + v * v
 
@@ -378,6 +379,12 @@
 
 def params():
     return pltpu.CompilerParams(vmem_limit_bytes=VMEM_LIMIT)
+
+
+def both_ways(x, axes):
+    n = x.shape[0]
+    groups = [[2 * k for k in range(n)], [2 * k + 1 for k in reversed(range(n))]]
+    return lax.all_to_all(x, axes + ("c",), 0, 0, axis_index_groups=groups)
 
 
 def on_device(source_embed, target_embed, source_labels, target_labels, pair_blocks, pair_count):
@@ -409,7 +416,7 @@
         compiler_params=params(),
         name="first",
     )(target_embed, target_labels[None])
-    near = lax.all_to_all(near, "z", 0, 0)
+    near = both_ways(near, ("z",))
 
     def around(x, axis):
         n = lax.axis_size(axis)
@@ -477,7 +484,7 @@
     )(
         pairs,
         count,
-        lax.axis_index("x").reshape(1),
+        jnp.stack([lax.axis_index("x"), lax.axis_index("c")]),
         xa,
         source_embed.T,
         *pieces,
@@ -507,7 +514,7 @@
         )(pairs, count, tiles, got)
 
     sent, _ = columns(lax.all_to_all(sent, TGT, 0, 0))
-    sent = rows(lax.all_to_all(sent, SRC, 0, 0))
+    sent = rows(both_ways(sent, SRC))
     sent, src_pot = columns(lax.all_to_all(sent, TGT, 0, 0))
     tgt_pot = pl.pallas_call(
         functools.partial(last_kernel, log_src),
@@ -516,7 +523,7 @@
         out_specs=vmem(),
         compiler_params=params(),
         name="last",
-    )(lax.all_to_all(sent, SRC, 0, 0))
+    )(both_ways(sent, SRC))
     return (src_pot.reshape(-1), tgt_pot.reshape(-1), label_cost)
 
 

time: 126 us -> 126 us (level); the launches traced: 126 us -> 124 us
  blocking collectives: 69.6 us -> 53.1 us
  starting transfers between devices: 23.5 us -> 29.8 us
  waiting for transfers between devices: 6.59 us -> 12.5 us
  Pallas kernels: 17.6 us -> 19.9 us
    all_to_all x3 -> x2, blocking collectives: 49.3 us -> 34.8 us  [both_ways(): return lax.all_to_all(x, axes + ('c',), 0, 0, axis_index_groups=groups)]
    all_to_all x1 -> x2, starting transfers between devices: 8.58 us -> 14.9 us  [the longest x1 8.58 us: both_ways(): return lax.all_to_all(x, axes + ('c',), 0, 0, axis_index_groups=groups)]
    all_to_all x1, waiting for transfers between devices: 2.27 us -> 5.95 us  [on_device(): stats = lax.all_to_all(stats, 'x', 0, 0)]
    all_to_all x1 -> x2, waiting for transfers between devices: 3.14 us -> 5.41 us  [the longest x1 4.53 us: on_device(): stats = lax.all_to_all(stats, 'z', 0, 0)]
    all_to_all x1, blocking collectives: 11.2 us -> 9.47 us  [on_device(): sent, _ = columns(lax.all_to_all(sent, TGT, 0, 0))]
  transfers between devices with their start and end apart: 9 -> 10, of which waited for: 3 -> 4; matrix products, arithmetic and copies ran while one was open for 2% -> 3% of each run, Pallas kernels for 4% -> 5%
where the time goes in v8:
time: 126 us; the launch traced here: 124 us
  blocking collectives  53.1 us (42%)
  starting transfers between devices  29.8 us (24%)
  Pallas kernels  19.9 us (16%)
  waiting for transfers between devices  12.5 us (10%)
  local copies, waits for them, and re-layouts  6.9 us (5%)
  between operations  1.37 us (1%)
    all_to_all x2, blocking collectives, both_ways(): return lax.all_to_all(x, axes + ('c',), 0, 0, axis_index_groups=groups)  34.8 us
    ppermute x7, starting transfers between devices, around(): lax.ppermute(x, axis, [((i + far) % n, i) for i in range(n)])  11.6 us
    all_to_all x1, blocking collectives, on_device(): sent, _ = columns(lax.all_to_all(sent, TGT, 0, 0))  9.47 us
    all_to_all x1, blocking collectives, on_device(): sent, src_pot = columns(lax.all_to_all(sent, TGT, 0, 0))  8.88 us
    all_to_all x1, starting transfers between devices, both_ways(): return lax.all_to_all(x, axes + ('c',), 0, 0, axis_index_groups=groups)  8.58 us
    unnamed x16, local copies, waits for them, and re-layouts  6.81 us
    all_to_all x1, starting transfers between devices, on_device(): stats = lax.all_to_all(stats, 'z', 0, 0)  6.33 us
    all_to_all x1, waiting for transfers between devices, on_device(): stats = lax.all_to_all(stats, 'x', 0, 0)  5.95 us
  transfers between devices with their start and end apart: 10, of which 4 were waited for; matrix products, arithmetic and copies ran while one was open for 3% of the time, Pallas kernels for 5%

profile of v8, /device:TPU:32, one launch (start us, length us, event | category | flops | bytes accessed | tf_op | source)
XLA Modules:
  0.0 123.7 jit_solution(13307550197745627398)
XLA Ops:
  0.6 0.0 copy-start.1
  0.6 0.8 copy-done.1
  1.5 0.0 copy-start.4
  1.5 0.7 copy-done.4
  2.2 0.9 first.1
  3.1 8.6 %all-to-all-start = ((bf16[8,16,2048]{2,1,0:T(8,128)(2,1)}), bf16[8,16,2048]{2,1,0:T(8,128)(2,1)S(1)}, u32[]{:S(2)}, u32[]{:S(2)}) async-start(bf16[8,16,2048]{2,1,0:T(8,128)(2,1)} %get-tuple-element.16), calls=%async_computation | async-start | bytes 1048576 | tf_op jit(solution)/shard_map/all_to_all | solution.py:387
  11.6 0.0 collective-permute-start
  11.6 1.2 collective-permute-done.args_1_
  12.8 1.6 %collective-permute-start.3 = (f32[16,128]{1,0:T(8,128)S(1)}, f32[16,128]{1,0:T(8,128)S(1)}, u32[]{:S(2)}, u32[]{:S(2)}) collective-permute-start(f32[16,128]{1,0:T(8,128)S(1)} %pair.1.args_0_), channel_id=1, source_target_pairs={{6,0},{0,2},{2,4},{4,6},{7,1},{1,3},{3,5},{5,7},{14,8},{8,10},{10,... | collective-permute-start | bytes 24584 | tf_op jit(solution)/shard_map/ppermute | solution.py:424
  14.5 2.9 %collective-permute-start.2 = (f32[16,128]{1,0:T(8,128)S(1)}, f32[16,128]{1,0:T(8,128)S(1)}, u32[]{:S(2)}, u32[]{:S(2)}) collective-permute-start(f32[16,128]{1,0:T(8,128)S(1)} %pair.1.args_0_), channel_id=1, source_target_pairs={{4,0},{6,2},{0,4},{2,6},{5,1},{7,3},{1,5},{3,7},{12,8},{14,10},{8,... | collective-permute-start | bytes 24584 | tf_op jit(solution)/shard_map/ppermute | solution.py:424
  17.4 1.3 %collective-permute-start.1 = (f32[16,128]{1,0:T(8,128)S(1)}, f32[16,128]{1,0:T(8,128)S(1)}, u32[]{:S(2)}, u32[]{:S(2)}) collective-permute-start(f32[16,128]{1,0:T(8,128)S(1)} %pair.1.args_0_), channel_id=1, source_target_pairs={{2,0},{4,2},{6,4},{0,6},{3,1},{5,3},{7,5},{1,7},{10,8},{12,10},{14... | collective-permute-start | bytes 24584 | tf_op jit(solution)/shard_map/ppermute | solution.py:424
  18.7 0.0 copy-start
  18.7 1.6 %copy-done = bf16[512,2048]{1,0:T(8,128)(2,1)S(1)} copy-done((bf16[512,2048]{1,0:T(8,128)(2,1)S(1)}, bf16[512,2048]{1,0:T(8,128)(2,1)}, u32[]{:S(2)}) %copy-start) | copy-done | bytes 2097176
  20.3 0.0 copy-start.2
  20.3 0.7 copy-done.2
  21.0 3.5 %source_group.1 = (f32[40,128]{1,0:T(8,128)S(1)}, f32[1,2048]{1,0:T(1,128)S(1)}) custom-call(bf16[512,2048]{1,0:T(8,128)(2,1)S(1)} %copy-done, s32[1,2048]{1,0:T(1,128)S(1)} %bitcast.16), custom_call_target="tpu_custom_call" | custom-call | tf_op jit(solution)/shard_map/source_group/pallas_call | solution.py:396
  24.5 0.0 collective-permute-done.3.args_3_
  24.5 0.0 collective-permute-done.2.args_2_
  24.5 0.0 collective-permute-done.1.args_1_
  24.5 0.7 near.1
  25.2 0.9 all-to-all-done.args_0_
  26.1 1.5 %collective-permute-start.6 = (bf16[8,16,2048]{2,1,0:T(8,128)(2,1)S(1)}, bf16[8,16,2048]{2,1,0:T(8,128)(2,1)S(1)}, u32[]{:S(2)}, u32[]{:S(2)}) collective-permute-start(bf16[8,16,2048]{2,1,0:T(8,128)(2,1)S(1)} %all-to-all-done.args_0_), channel_id=1, source_target_pairs={{24,0},{0,8},{8,16},{16,24},{25,1},{1,9},{9,17},{17,25},{26,2},{2,... | collective-permute-start | bytes 1572872 | tf_op jit(solution)/shard_map/ppermute | solution.py:424
  27.6 2.7 %collective-permute-start.5 = (bf16[8,16,2048]{2,1,0:T(8,128)(2,1)S(1)}, bf16[8,16,2048]{2,1,0:T(8,128)(2,1)}, u32[]{:S(2)}, u32[]{:S(2)}) collective-permute-start(bf16[8,16,2048]{2,1,0:T(8,128)(2,1)S(1)} %all-to-all-done.args_0_), channel_id=1, source_target_pairs={{16,0},{24,8},{0,16},{8,24},{17,1},{25,9},{1,17},{9,25},{18,2},{26... | collective-permute-start | bytes 1572872 | tf_op jit(solution)/shard_map/ppermute | solution.py:424
  30.3 1.4 %collective-permute-start.4 = (bf16[8,16,2048]{2,1,0:T(8,128)(2,1)S(1)}, bf16[8,16,2048]{2,1,0:T(8,128)(2,1)}, u32[]{:S(2)}, u32[]{:S(2)}) collective-permute-start(bf16[8,16,2048]{2,1,0:T(8,128)(2,1)S(1)} %all-to-all-done.args_0_), channel_id=1, source_target_pairs={{8,0},{16,8},{24,16},{0,24},{9,1},{17,9},{25,17},{1,25},{10,2},{18... | collective-permute-start | bytes 1572872 | tf_op jit(solution)/shard_map/ppermute | solution.py:424
  31.7 6.3 %all-to-all-start.1 = ((f32[8,48,128]{2,1,0:T(8,128)}), f32[8,48,128]{2,1,0:T(8,128)S(1)}, u32[]{:S(2)}, u32[]{:S(2)}) async-start(f32[8,48,128]{2,1,0:T(8,128)} %near.1), calls=%async_computation.1 | async-start | bytes 393216 | tf_op jit(solution)/shard_map/all_to_all | solution.py:453
  38.1 0.0 copy-start.6
  38.1 0.0 copy-start.3
  38.1 0.0 copy-start.5
  38.1 2.9 %copy.12 = bf16[512,2048]{0,1:T(8,128)(2,1)S(1)} copy(bf16[512,2048]{1,0:T(8,128)(2,1)} %embed.3) | data formatting | bytes 4194304 | tf_op args[0]
  41.6 0.0 copy-done.6
  41.6 0.1 copy.11
  41.7 0.1 reshape.22.pairs
  41.8 4.5 %all-to-all-done.1.got = f32[8,48,128]{2,1,0:T(8,128)S(1)} async-done(((f32[8,48,128]{2,1,0:T(8,128)}), f32[8,48,128]{2,1,0:T(8,128)S(1)}, u32[]{:S(2)}, u32[]{:S(2)}) %all-to-all-start.1) | async-done | bytes 196640 | tf_op jit(solution)/shard_map/all_to_all | solution.py:453
  46.4 0.7 middle.1
  47.1 3.3 %all-to-all-start.2 = ((f32[4,72,128]{2,1,0:T(8,128)}), f32[4,72,128]{2,1,0:T(8,128)S(1)}, u32[]{:S(2)}, u32[]{:S(2)}) async-start(f32[4,72,128]{2,1,0:T(8,128)} %middle.1), calls=%async_computation.2 | async-start | bytes 294912 | tf_op jit(solution)/shard_map/all_to_all | solution.py:457
  50.4 0.1 pad_add_fusion.place
  50.5 5.9 %all-to-all-done.2.got = f32[4,72,128]{2,1,0:T(8,128)S(1)} async-done(((f32[4,72,128]{2,1,0:T(8,128)}), f32[4,72,128]{2,1,0:T(8,128)S(1)}, u32[]{:S(2)}, u32[]{:S(2)}) %all-to-all-start.2) | async-done | bytes 147488 | tf_op jit(solution)/shard_map/all_to_all | solution.py:457
  56.5 0.0 copy-done.3
  56.5 0.9 label.1
  57.4 0.0 collective-permute-done.6.args_3_
  57.4 0.0 collective-permute-done.5.args_2_
  57.4 0.0 collective-permute-done.4.args_1_
  57.4 0.0 copy-done.5
  57.4 5.2 %cost_rows.1 = (f32[24,256,256]{2,1,0:T(8,128)S(1)}, f32[8,16,128]{2,1,0:T(8,128)S(1)}) custom-call(s32[48]{0:T(128)S(1)} %reshape.22.pairs, s32[1]{0:T(128)} %bitcast.11.count, s32[2]{0:T(128)S(1)} %pad_add_fusion.place, bf16[16,2048]{1,0:T(8,128)(2,1)S(1)} %get-tuple-element.21.xa, bf16[2048,512]{1,0:T(8,128)(2,1)S(1)} %bitcast.15, ...), custom_call_target="tpu_custom_call" | custom-call | tf_op jit(solution)/shard_map/cost_rows/pallas_call | solution.py:471
  62.6 9.5 %all_to_all.35.g_ref = f32[8,16,128]{2,1,0:T(8,128)S(1)} all-to-all(f32[8,16,128]{2,1,0:T(8,128)S(1)} %get-tuple-element.24), channel_id=1, replica_groups=mesh['z'=8,'x'=4,'y'=4,'c'=2] {'y','c'}, dimensions={0} | all-to-all | bytes 131072 | tf_op jit(solution)/shard_map/all_to_all | solution.py:516
  72.0 2.2 %columns.2 = (f32[32,16,128]{2,1,0:T(8,128)S(1)}, f32[16,128]{1,0:T(8,128)}) custom-call(s32[48]{0:T(128)S(1)} %reshape.22.pairs, s32[1]{0:T(128)} %bitcast.12.count, f32[24,256,256]{2,1,0:T(8,128)S(1)} %get-tuple-element.23.tiles, f32[8,16,128]{2,1,0:T(8,128)S(1)} %all_to_all.35.g_ref), custom_call_target="tpu_custom_call" | custom-call | tf_op jit(solution)/shard_map/columns/pallas_call | solution.py:495
  74.3 18.2 %all_to_all.36.g_ref = f32[32,16,128]{2,1,0:T(8,128)S(1)} all-to-all(f32[32,16,128]{2,1,0:T(8,128)S(1)} %get-tuple-element.25), channel_id=1, replica_groups={{0,8,16,24,32,40,48,56,64,72,80,88,96,104,112,120,128,136,144,152,160,1..., dimensions={0} | all-to-all | bytes 524288 | tf_op jit(solution)/shard_map/all_to_all | solution.py:387
  92.5 2.8 %rows.1 = f32[8,16,128]{2,1,0:T(8,128)S(1)} custom-call(s32[48]{0:T(128)S(1)} %reshape.22.pairs, s32[1]{0:T(128)} %bitcast.13.count, f32[24,256,256]{2,1,0:T(8,128)S(1)} %get-tuple-element.23.tiles, f32[32,16,128]{2,1,0:T(8,128)S(1)} %all_to_all.36.g_ref), custom_call_target="tpu_custom_call" | custom-call | tf_op jit(solution)/shard_map/rows/pallas_call | solution.py:506
  95.3 8.9 %all_to_all.37.g_ref = f32[8,16,128]{2,1,0:T(8,128)S(1)} all-to-all(f32[8,16,128]{2,1,0:T(8,128)S(1)} %rows.1), channel_id=1, replica_groups=mesh['z'=8,'x'=4,'y'=4,'c'=2] {'y','c'}, dimensions={0} | all-to-all | bytes 131072 | tf_op jit(solution)/shard_map/all_to_all | solution.py:518
  104.2 2.2 %columns.3 = (f32[32,16,128]{2,1,0:T(8,128)S(1)}, f32[16,128]{1,0:T(8,128)}) custom-call(s32[48]{0:T(128)S(1)} %reshape.22.pairs, s32[1]{0:T(128)} %bitcast.14.count, f32[24,256,256]{2,1,0:T(8,128)S(1)} %get-tuple-element.23.tiles, f32[8,16,128]{2,1,0:T(8,128)S(1)} %all_to_all.37.g_ref), custom_call_target="tpu_custom_call" | custom-call | tf_op jit(solution)/shard_map/columns/pallas_call | solution.py:495
  106.4 16.6 %all_to_all.38.g_ref = f32[32,16,128]{2,1,0:T(8,128)S(1)} all-to-all(f32[32,16,128]{2,1,0:T(8,128)S(1)} %get-tuple-element.27), channel_id=1, replica_groups={{0,8,16,24,32,40,48,56,64,72,80,88,96,104,112,120,128,136,144,152,160,1..., dimensions={0} | all-to-all | bytes 524288 | tf_op jit(solution)/shard_map/all_to_all | solution.py:387
  123.0 0.7 last.1
  (1 shorter events, 0.0 us)
Async XLA Ops:
  0.6 0.8 copy-start.1
  1.5 0.7 copy-start.4
  3.1 23.0 %all-to-all-start = ((bf16[8,16,2048]{2,1,0:T(8,128)(2,1)}), bf16[8,16,2048]{2,1,0:T(8,128)(2,1)S(1)}, u32[]{:S(2)}, u32[]{:S(2)}) async-start(bf16[8,16,2048]{2,1,0:T(8,128)(2,1)} %get-tuple-element.16), calls=%async_computation | async-start | bytes 1048576 | tf_op jit(solution)/shard_map/all_to_all | solution.py:387
  11.6 1.2 collective-permute-start
  12.8 11.6 %collective-permute-start.3 = (f32[16,128]{1,0:T(8,128)S(1)}, f32[16,128]{1,0:T(8,128)S(1)}, u32[]{:S(2)}, u32[]{:S(2)}) collective-permute-start(f32[16,128]{1,0:T(8,128)S(1)} %pair.1.args_0_), channel_id=1, source_target_pairs={{6,0},{0,2},{2,4},{4,6},{7,1},{1,3},{3,5},{5,7},{14,8},{8,10},{10,... | collective-permute-start | bytes 24584 | tf_op jit(solution)/shard_map/ppermute | solution.py:424
  14.5 10.0 %collective-permute-start.2 = (f32[16,128]{1,0:T(8,128)S(1)}, f32[16,128]{1,0:T(8,128)S(1)}, u32[]{:S(2)}, u32[]{:S(2)}) collective-permute-start(f32[16,128]{1,0:T(8,128)S(1)} %pair.1.args_0_), channel_id=1, source_target_pairs={{4,0},{6,2},{0,4},{2,6},{5,1},{7,3},{1,5},{3,7},{12,8},{14,10},{8,... | collective-permute-start | bytes 24584 | tf_op jit(solution)/shard_map/ppermute | solution.py:424
  17.4 7.1 %collective-permute-start.1 = (f32[16,128]{1,0:T(8,128)S(1)}, f32[16,128]{1,0:T(8,128)S(1)}, u32[]{:S(2)}, u32[]{:S(2)}) collective-permute-start(f32[16,128]{1,0:T(8,128)S(1)} %pair.1.args_0_), channel_id=1, source_target_pairs={{2,0},{4,2},{6,4},{0,6},{3,1},{5,3},{7,5},{1,7},{10,8},{12,10},{14... | collective-permute-start | bytes 24584 | tf_op jit(solution)/shard_map/ppermute | solution.py:424
  18.7 1.6 %copy-start = (bf16[512,2048]{1,0:T(8,128)(2,1)S(1)}, bf16[512,2048]{1,0:T(8,128)(2,1)}, u32[]{:S(2)}) copy-start(bf16[512,2048]{1,0:T(8,128)(2,1)} %embed.3) | copy-start | bytes 6291460
  20.3 0.7 copy-start.2
  26.1 31.3 %collective-permute-start.6 = (bf16[8,16,2048]{2,1,0:T(8,128)(2,1)S(1)}, bf16[8,16,2048]{2,1,0:T(8,128)(2,1)S(1)}, u32[]{:S(2)}, u32[]{:S(2)}) collective-permute-start(bf16[8,16,2048]{2,1,0:T(8,128)(2,1)S(1)} %all-to-all-done.args_0_), channel_id=1, source_target_pairs={{24,0},{0,8},{8,16},{16,24},{25,1},{1,9},{9,17},{17,25},{26,2},{2,... | collective-permute-start | bytes 1572872 | tf_op jit(solution)/shard_map/ppermute | solution.py:424
  27.6 29.8 %collective-permute-start.5 = (bf16[8,16,2048]{2,1,0:T(8,128)(2,1)S(1)}, bf16[8,16,2048]{2,1,0:T(8,128)(2,1)}, u32[]{:S(2)}, u32[]{:S(2)}) collective-permute-start(bf16[8,16,2048]{2,1,0:T(8,128)(2,1)S(1)} %all-to-all-done.args_0_), channel_id=1, source_target_pairs={{16,0},{24,8},{0,16},{8,24},{17,1},{25,9},{1,17},{9,25},{18,2},{26... | collective-permute-start | bytes 1572872 | tf_op jit(solution)/shard_map/ppermute | solution.py:424
  30.3 27.1 %collective-permute-start.4 = (bf16[8,16,2048]{2,1,0:T(8,128)(2,1)S(1)}, bf16[8,16,2048]{2,1,0:T(8,128)(2,1)}, u32[]{:S(2)}, u32[]{:S(2)}) collective-permute-start(bf16[8,16,2048]{2,1,0:T(8,128)(2,1)S(1)} %all-to-all-done.args_0_), channel_id=1, source_target_pairs={{8,0},{16,8},{24,16},{0,24},{9,1},{17,9},{25,17},{1,25},{10,2},{18... | collective-permute-start | bytes 1572872 | tf_op jit(solution)/shard_map/ppermute | solution.py:424
  31.7 14.6 %all-to-all-start.1 = ((f32[8,48,128]{2,1,0:T(8,128)}), f32[8,48,128]{2,1,0:T(8,128)S(1)}, u32[]{:S(2)}, u32[]{:S(2)}) async-start(f32[8,48,128]{2,1,0:T(8,128)} %near.1), calls=%async_computation.1 | async-start | bytes 393216 | tf_op jit(solution)/shard_map/all_to_all | solution.py:453
  38.1 3.6 %copy-start.6 = (s32[1,1,24,2]{2,3,1,0:T(2,128)S(1)}, s32[1,1,24,2]{2,3,1,0:T(2,128)}, u32[]{:S(2)}) copy-start(s32[1,1,24,2]{2,3,1,0:T(2,128)} %param.10) | copy-start | bytes 580
  38.1 18.4 %copy-start.3 = (s32[2048]{0:T(1024)S(1)}, s32[2048]{0:T(1024)}, u32[]{:S(2)}) copy-start(s32[2048]{0:T(1024)} %param.8) | copy-start | bytes 24580
  38.1 19.3 %copy-start.5 = (s32[2048]{0:T(1024)S(1)}, s32[2048]{0:T(1024)}, u32[]{:S(2)}) copy-start(s32[2048]{0:T(1024)} %param.9) | copy-start | bytes 24580
  47.1 9.4 %all-to-all-start.2 = ((f32[4,72,128]{2,1,0:T(8,128)}), f32[4,72,128]{2,1,0:T(8,128)S(1)}, u32[]{:S(2)}, u32[]{:S(2)}) async-start(f32[4,72,128]{2,1,0:T(8,128)} %middle.1), calls=%async_computation.2 | async-start | bytes 294912 | tf_op jit(solution)/shard_map/all_to_all | solution.py:457

commit v9 on v8

--- a/solution.py
+++ b/solution.py
@@ -28,6 +28,7 @@
 SRC = ("z", "x")
 TGT = ("y", "c")
 VMEM_LIMIT = 24 * 1024 * 1024
+FULL_VMEM = 64 * 1024 * 1024 - 32 * 1024
 
 
 def log2(x):
@@ -157,7 +158,7 @@
         out_ref[k, 32:40, :] = total
 
 
-def label_kernel(part, got, src_sq, src_lab, label_ref, xa_ref):
+def label_rows(part, got, src_sq, src_lab, label_ref, xa_ref):
     groups, total = source_joined(got)
     row_id = lax.broadcasted_iota(jnp.int32, (8, LANES), 0)
     lane_id = lax.broadcasted_iota(jnp.int32, (8, LANES), 1)
@@ -241,8 +242,9 @@
     return row, pairs[2 * index + 1]
 
 
-def cost_kernel(n_x, pairs, count, place, xa, xt, *args):
-    pieces, (tgt_lab, tiles, out_ref, y, ya, top, total) = args[:n_x], args[n_x:]
+def cost_kernel(n_x, n_f, pairs, count, place, got, src_sq, src_lab, xt, *args):
+    pieces, (tgt_lab, label_ref, tiles, out_ref, xa, y, ya, top, total) = args[:n_x], args[n_x:]
+    label_rows(n_f, got, src_sq, src_lab, label_ref, xa)
     row_id = lax.broadcasted_iota(jnp.int32, (16, 1), 0)
     part = row_id // CLASSES
     cls = row_id % CLASSES
@@ -377,8 +379,8 @@
     return jax.ShapeDtypeStruct(shape, jnp.float32)
 
 
-def params():
-    return pltpu.CompilerParams(vmem_limit_bytes=VMEM_LIMIT)
+def params(limit=VMEM_LIMIT):
+    return pltpu.CompilerParams(vmem_limit_bytes=limit)
 
 
 def both_ways(x, axes):
@@ -413,7 +415,7 @@
         in_specs=[vmem(), vmem()],
         out_specs=(pl.BlockSpec(memory_space=pl.ANY), vmem()),
         scratch_shapes=[pltpu.SemaphoreType.DMA((n_z,))],
-        compiler_params=params(),
+        compiler_params=params(FULL_VMEM),
         name="first",
     )(target_embed, target_labels[None])
     near = both_ways(near, ("z",))
@@ -455,25 +457,21 @@
         functools.partial(middle_kernel, part * n_x), f32(n_x, 72, LANES), stats, name="middle"
     )
     stats = lax.all_to_all(stats, "x", 0, 0)
-    label_cost, xa = call(
-        functools.partial(label_kernel, part),
-        (f32(CLASSES, CLASSES), jax.ShapeDtypeStruct((16, ROWS), jnp.bfloat16)),
-        stats,
-        src_sq,
-        source_labels[None],
-        name="label",
-    )
-
     tall = pltpu.VMEM((ROWS, LANES), jnp.float32)
     wide = pltpu.VMEM((BLK, 8, BLOCK), jnp.float32)
     log_src = math.log2(ROWS * n_src)
     log_tgt = math.log2(ROWS * n_tgt)
-    tiles, sent = pl.pallas_call(
-        functools.partial(cost_kernel, n_x),
-        out_shape=(f32(MAXP, BLOCK, BLOCK), f32(n_tgt, CHUNKS, LANES)),
-        in_specs=[smem()] * 3 + [vmem()] * (3 + n_x),
-        out_specs=(vmem(), vmem()),
+    label_cost, tiles, sent = pl.pallas_call(
+        functools.partial(cost_kernel, n_x, part),
+        out_shape=(
+            f32(CLASSES, CLASSES),
+            f32(MAXP, BLOCK, BLOCK),
+            f32(n_tgt, CHUNKS, LANES),
+        ),
+        in_specs=[smem()] * 3 + [vmem()] * (5 + n_x),
+        out_specs=(vmem(), vmem(), vmem()),
         scratch_shapes=[
+            pltpu.VMEM((16, ROWS), jnp.bfloat16),
             pltpu.VMEM((WIDTH, ROWS), jnp.bfloat16),
             pltpu.VMEM((16, ROWS), jnp.bfloat16),
             tall,
@@ -485,7 +483,9 @@
         pairs,
         count,
         jnp.stack([lax.axis_index("x"), lax.axis_index("c")]),
-        xa,
+        stats,
+        src_sq,
+        source_labels[None],
         source_embed.T,
         *pieces,
         target_labels[None],

time: 126 us -> 125 us (level)
    all_to_all x2, blocking collectives: 34.8 us -> 33.3 us  [both_ways(): return lax.all_to_all(x, axes + ('c',), 0, 0, axis_index_groups=groups)]
    pallas_call x1, Pallas kernels: 0.88 us -> 2.31 us  [on_device(): pl.pallas_call(first_kernel, out_shape=(jax.ShapeDtypeStruct((n_z,) + tar...]
    pallas_call x3 -> x2, Pallas kernels: 5.08 us -> 4.19 us  [call(): pl.pallas_call(kernel, out_shape=out_shape, in_specs=[vmem()] * len(args)...]
    unnamed x16 -> x14, local copies, waits for them, and re-layouts: 6.81 us -> 5.97 us
  transfers between devices with their start and end apart: 10 -> 10, of which waited for: 4 -> 3; matrix products, arithmetic and copies ran while one was open for 3% -> 3% of each run, Pallas kernels for 5% -> 4%
where the time goes in v9:
time: 125 us; the launch traced here: 123 us
  blocking collectives  52.7 us (42%)
  starting transfers between devices  30.7 us (25%)
  Pallas kernels  20.7 us (17%)
  waiting for transfers between devices  11.9 us (10%)
  local copies, waits for them, and re-layouts  6.07 us (5%)
  between operations  1.37 us (1%)
    all_to_all x2, blocking collectives, both_ways(): return lax.all_to_all(x, axes + ('c',), 0, 0, axis_index_groups=groups)  33.3 us
    ppermute x7, starting transfers between devices, around(): lax.ppermute(x, axis, [((i + far) % n, i) for i in range(n)])  11.6 us
    all_to_all x1, blocking collectives, on_device(): sent, _ = columns(lax.all_to_all(sent, TGT, 0, 0))  10.1 us
    all_to_all x1, blocking collectives, on_device(): sent, src_pot = columns(lax.all_to_all(sent, TGT, 0, 0))  9.4 us
    all_to_all x1, starting transfers between devices, both_ways(): return lax.all_to_all(x, axes + ('c',), 0, 0, axis_index_groups=groups)  8.58 us
    all_to_all x1, starting transfers between devices, on_device(): stats = lax.all_to_all(stats, 'z', 0, 0)  7.21 us
    unnamed x14, local copies, waits for them, and re-layouts  5.97 us
    all_to_all x1, waiting for transfers between devices, on_device(): stats = lax.all_to_all(stats, 'x', 0, 0)  5.95 us
  transfers between devices with their start and end apart: 10, of which 3 were waited for; matrix products, arithmetic and copies ran while one was open for 3% of the time, Pallas kernels for 4%

profile of v9, /device:TPU:32, one launch (start us, length us, event | category | flops | bytes accessed | tf_op | source)
XLA Modules:
  0.0 123.5 jit_solution(7538467059066158886)
XLA Ops:
  0.6 2.3 %first.1 = (bf16[8,16,2048]{2,1,0:T(8,128)(2,1)}, f32[16,128]{1,0:T(8,128)}) custom-call(bf16[16,2048]{1,0:T(8,128)(2,1)} %embed.2, s32[1,2048]{1,0:T(1,128)} %bitcast.18), custom_call_target="tpu_custom_call" | custom-call | tf_op jit(solution)/shard_map/first/pallas_call | solution.py:409
  2.9 8.6 %all-to-all-start = ((bf16[8,16,2048]{2,1,0:T(8,128)(2,1)}), bf16[8,16,2048]{2,1,0:T(8,128)(2,1)S(1)}, u32[]{:S(2)}, u32[]{:S(2)}) async-start(bf16[8,16,2048]{2,1,0:T(8,128)(2,1)} %get-tuple-element.15), calls=%async_computation | async-start | bytes 1048576 | tf_op jit(solution)/shard_map/all_to_all | solution.py:389
  11.5 0.0 collective-permute-start
  11.5 1.4 %collective-permute-done.args_1_ = f32[16,128]{1,0:T(8,128)S(1)} collective-permute-done((f32[16,128]{1,0:T(8,128)}, f32[16,128]{1,0:T(8,128)S(1)}, u32[]{:S(2)}, u32[]{:S(2)}) %collective-permute-start) | collective-permute-done | bytes 8224 | tf_op jit(solution)/shard_map/ppermute | solution.py:426
  12.9 0.0 copy-start.4
  12.9 0.7 copy-done.4
  13.6 1.6 %collective-permute-start.3 = (f32[16,128]{1,0:T(8,128)S(1)}, f32[16,128]{1,0:T(8,128)S(1)}, u32[]{:S(2)}, u32[]{:S(2)}) collective-permute-start(f32[16,128]{1,0:T(8,128)S(1)} %pair.1.args_0_), channel_id=1, source_target_pairs={{6,0},{0,2},{2,4},{4,6},{7,1},{1,3},{3,5},{5,7},{14,8},{8,10},{10,... | collective-permute-start | bytes 24584 | tf_op jit(solution)/shard_map/ppermute | solution.py:426
  15.3 2.9 %collective-permute-start.2 = (f32[16,128]{1,0:T(8,128)S(1)}, f32[16,128]{1,0:T(8,128)S(1)}, u32[]{:S(2)}, u32[]{:S(2)}) collective-permute-start(f32[16,128]{1,0:T(8,128)S(1)} %pair.1.args_0_), channel_id=1, source_target_pairs={{4,0},{6,2},{0,4},{2,6},{5,1},{7,3},{1,5},{3,7},{12,8},{14,10},{8,... | collective-permute-start | bytes 24584 | tf_op jit(solution)/shard_map/ppermute | solution.py:426
  18.2 1.3 %collective-permute-start.1 = (f32[16,128]{1,0:T(8,128)S(1)}, f32[16,128]{1,0:T(8,128)S(1)}, u32[]{:S(2)}, u32[]{:S(2)}) collective-permute-start(f32[16,128]{1,0:T(8,128)S(1)} %pair.1.args_0_), channel_id=1, source_target_pairs={{2,0},{4,2},{6,4},{0,6},{3,1},{5,3},{7,5},{1,7},{10,8},{12,10},{14... | collective-permute-start | bytes 24584 | tf_op jit(solution)/shard_map/ppermute | solution.py:426
  19.5 0.0 copy-start
  19.5 1.6 %copy-done = bf16[512,2048]{1,0:T(8,128)(2,1)S(1)} copy-done((bf16[512,2048]{1,0:T(8,128)(2,1)S(1)}, bf16[512,2048]{1,0:T(8,128)(2,1)}, u32[]{:S(2)}) %copy-start) | copy-done | bytes 2097176
  21.1 0.0 copy-start.1
  21.1 0.7 copy-done.1
  21.8 3.5 %source_group.1 = (f32[40,128]{1,0:T(8,128)S(1)}, f32[1,2048]{1,0:T(1,128)S(1)}) custom-call(bf16[512,2048]{1,0:T(8,128)(2,1)S(1)} %copy-done, s32[1,2048]{1,0:T(1,128)S(1)} %bitcast.16), custom_call_target="tpu_custom_call" | custom-call | tf_op jit(solution)/shard_map/source_group/pallas_call | solution.py:398
  25.3 0.0 collective-permute-done.3.args_3_
  25.3 0.0 collective-permute-done.2.args_2_
  25.3 0.0 collective-permute-done.1.args_1_
  25.3 0.7 near.1
  26.0 0.0 all-to-all-done.args_0_
  26.0 1.5 %collective-permute-start.6 = (bf16[8,16,2048]{2,1,0:T(8,128)(2,1)S(1)}, bf16[8,16,2048]{2,1,0:T(8,128)(2,1)S(1)}, u32[]{:S(2)}, u32[]{:S(2)}) collective-permute-start(bf16[8,16,2048]{2,1,0:T(8,128)(2,1)S(1)} %all-to-all-done.args_0_), channel_id=1, source_target_pairs={{24,0},{0,8},{8,16},{16,24},{25,1},{1,9},{9,17},{17,25},{26,2},{2,... | collective-permute-start | bytes 1572872 | tf_op jit(solution)/shard_map/ppermute | solution.py:426
  27.5 2.7 %collective-permute-start.5 = (bf16[8,16,2048]{2,1,0:T(8,128)(2,1)S(1)}, bf16[8,16,2048]{2,1,0:T(8,128)(2,1)}, u32[]{:S(2)}, u32[]{:S(2)}) collective-permute-start(bf16[8,16,2048]{2,1,0:T(8,128)(2,1)S(1)} %all-to-all-done.args_0_), channel_id=1, source_target_pairs={{16,0},{24,8},{0,16},{8,24},{17,1},{25,9},{1,17},{9,25},{18,2},{26... | collective-permute-start | bytes 1572872 | tf_op jit(solution)/shard_map/ppermute | solution.py:426
  30.3 1.4 %collective-permute-start.4 = (bf16[8,16,2048]{2,1,0:T(8,128)(2,1)S(1)}, bf16[8,16,2048]{2,1,0:T(8,128)(2,1)}, u32[]{:S(2)}, u32[]{:S(2)}) collective-permute-start(bf16[8,16,2048]{2,1,0:T(8,128)(2,1)S(1)} %all-to-all-done.args_0_), channel_id=1, source_target_pairs={{8,0},{16,8},{24,16},{0,24},{9,1},{17,9},{25,17},{1,25},{10,2},{18... | collective-permute-start | bytes 1572872 | tf_op jit(solution)/shard_map/ppermute | solution.py:426
  31.7 7.2 %all-to-all-start.1 = ((f32[8,48,128]{2,1,0:T(8,128)}), f32[8,48,128]{2,1,0:T(8,128)S(1)}, u32[]{:S(2)}, u32[]{:S(2)}) async-start(f32[8,48,128]{2,1,0:T(8,128)} %near.1), calls=%async_computation.1 | async-start | bytes 393216 | tf_op jit(solution)/shard_map/all_to_all | solution.py:455
  38.9 0.0 copy-start.5
  38.9 0.0 copy-start.2
  38.9 0.0 copy-start.3
  38.9 2.9 %copy.12 = bf16[512,2048]{0,1:T(8,128)(2,1)S(1)} copy(bf16[512,2048]{1,0:T(8,128)(2,1)} %embed.3) | data formatting | bytes 4194304 | tf_op args[0]
  42.5 0.0 copy-done.5
  42.5 0.1 copy.11
  42.6 0.1 reshape.22.pairs
  42.7 4.5 %all-to-all-done.1.got = f32[8,48,128]{2,1,0:T(8,128)S(1)} async-done(((f32[8,48,128]{2,1,0:T(8,128)}), f32[8,48,128]{2,1,0:T(8,128)S(1)}, u32[]{:S(2)}, u32[]{:S(2)}) %all-to-all-start.1) | async-done | bytes 196640 | tf_op jit(solution)/shard_map/all_to_all | solution.py:455
  47.2 0.7 middle.1
  47.9 3.3 %all-to-all-start.2 = ((f32[4,72,128]{2,1,0:T(8,128)}), f32[4,72,128]{2,1,0:T(8,128)S(1)}, u32[]{:S(2)}, u32[]{:S(2)}) async-start(f32[4,72,128]{2,1,0:T(8,128)} %middle.1), calls=%async_computation.2 | async-start | bytes 294912 | tf_op jit(solution)/shard_map/all_to_all | solution.py:459
  51.3 0.1 pad_add_fusion.place
  51.3 5.9 %all-to-all-done.2.got = f32[4,72,128]{2,1,0:T(8,128)S(1)} async-done(((f32[4,72,128]{2,1,0:T(8,128)}), f32[4,72,128]{2,1,0:T(8,128)S(1)}, u32[]{:S(2)}, u32[]{:S(2)}) %all-to-all-start.2) | async-done | bytes 147488 | tf_op jit(solution)/shard_map/all_to_all | solution.py:459
  57.3 0.0 collective-permute-done.6.args_3_
  57.3 0.0 collective-permute-done.5.args_2_
  57.3 0.0 collective-permute-done.4.args_1_
  57.3 0.0 copy-done.2
  57.3 0.0 copy-done.3
  57.3 5.4 %cost_rows.1 = (f32[4,4]{1,0:T(4,128)}, f32[24,256,256]{2,1,0:T(8,128)S(1)}, f32[8,16,128]{2,1,0:T(8,128)S(1)}) custom-call(s32[48]{0:T(128)S(1)} %reshape.22.pairs, s32[1]{0:T(128)} %bitcast.11.count, s32[2]{0:T(128)S(1)} %pad_add_fusion.place, f32[4,72,128]{2,1,0:T(8,128)S(1)} %all-to-all-done.2.got, f32[1,2048]{1,0:T(1,128)S(1)} %get-tuple-element.19.src_sq, ...), custom_call_target="tpu_custom_call" | custom-call | tf_op jit(solution)/shard_map/cost_rows/pallas_call | solution.py:464
  62.7 10.1 %all_to_all.35.g_ref = f32[8,16,128]{2,1,0:T(8,128)S(1)} all-to-all(f32[8,16,128]{2,1,0:T(8,128)S(1)} %get-tuple-element.22), channel_id=1, replica_groups=mesh['z'=8,'x'=4,'y'=4,'c'=2] {'y','c'}, dimensions={0} | all-to-all | bytes 131072 | tf_op jit(solution)/shard_map/all_to_all | solution.py:516
  72.8 2.2 %columns.2 = (f32[32,16,128]{2,1,0:T(8,128)S(1)}, f32[16,128]{1,0:T(8,128)}) custom-call(s32[48]{0:T(128)S(1)} %reshape.22.pairs, s32[1]{0:T(128)} %bitcast.12.count, f32[24,256,256]{2,1,0:T(8,128)S(1)} %get-tuple-element.21.tiles, f32[8,16,128]{2,1,0:T(8,128)S(1)} %all_to_all.35.g_ref), custom_call_target="tpu_custom_call" | custom-call | tf_op jit(solution)/shard_map/columns/pallas_call | solution.py:495
  75.1 16.7 %all_to_all.36.g_ref = f32[32,16,128]{2,1,0:T(8,128)S(1)} all-to-all(f32[32,16,128]{2,1,0:T(8,128)S(1)} %get-tuple-element.23), channel_id=1, replica_groups={{0,8,16,24,32,40,48,56,64,72,80,88,96,104,112,120,128,136,144,152,160,1..., dimensions={0} | all-to-all | bytes 524288 | tf_op jit(solution)/shard_map/all_to_all | solution.py:389
  91.7 2.8 %rows.1 = f32[8,16,128]{2,1,0:T(8,128)S(1)} custom-call(s32[48]{0:T(128)S(1)} %reshape.22.pairs, s32[1]{0:T(128)} %bitcast.13.count, f32[24,256,256]{2,1,0:T(8,128)S(1)} %get-tuple-element.21.tiles, f32[32,16,128]{2,1,0:T(8,128)S(1)} %all_to_all.36.g_ref), custom_call_target="tpu_custom_call" | custom-call | tf_op jit(solution)/shard_map/rows/pallas_call | solution.py:506
  94.6 9.4 %all_to_all.37.g_ref = f32[8,16,128]{2,1,0:T(8,128)S(1)} all-to-all(f32[8,16,128]{2,1,0:T(8,128)S(1)} %rows.1), channel_id=1, replica_groups=mesh['z'=8,'x'=4,'y'=4,'c'=2] {'y','c'}, dimensions={0} | all-to-all | bytes 131072 | tf_op jit(solution)/shard_map/all_to_all | solution.py:518
  104.0 2.2 %columns.3 = (f32[32,16,128]{2,1,0:T(8,128)S(1)}, f32[16,128]{1,0:T(8,128)}) custom-call(s32[48]{0:T(128)S(1)} %reshape.22.pairs, s32[1]{0:T(128)} %bitcast.14.count, f32[24,256,256]{2,1,0:T(8,128)S(1)} %get-tuple-element.21.tiles, f32[8,16,128]{2,1,0:T(8,128)S(1)} %all_to_all.37.g_ref), custom_call_target="tpu_custom_call" | custom-call | tf_op jit(solution)/shard_map/columns/pallas_call | solution.py:495
  106.2 16.6 %all_to_all.38.g_ref = f32[32,16,128]{2,1,0:T(8,128)S(1)} all-to-all(f32[32,16,128]{2,1,0:T(8,128)S(1)} %get-tuple-element.25), channel_id=1, replica_groups={{0,8,16,24,32,40,48,56,64,72,80,88,96,104,112,120,128,136,144,152,160,1..., dimensions={0} | all-to-all | bytes 524288 | tf_op jit(solution)/shard_map/all_to_all | solution.py:389
  122.8 0.7 last.1
  (1 shorter events, 0.0 us)
Async XLA Ops:
  2.9 23.1 %all-to-all-start = ((bf16[8,16,2048]{2,1,0:T(8,128)(2,1)}), bf16[8,16,2048]{2,1,0:T(8,128)(2,1)S(1)}, u32[]{:S(2)}, u32[]{:S(2)}) async-start(bf16[8,16,2048]{2,1,0:T(8,128)(2,1)} %get-tuple-element.15), calls=%async_computation | async-start | bytes 1048576 | tf_op jit(solution)/shard_map/all_to_all | solution.py:389
  11.5 1.4 %collective-permute-start = (f32[16,128]{1,0:T(8,128)}, f32[16,128]{1,0:T(8,128)S(1)}, u32[]{:S(2)}, u32[]{:S(2)}) collective-permute-start(f32[16,128]{1,0:T(8,128)} %get-tuple-element.16.args_0_), channel_id=1, source_target_pairs={{1,0},{0,1},{3,2},{2,3},{5,4},{4,5},{7,6},{6,7},{9,8},{8,9},{11,10... | collective-permute-start | bytes 24584 | tf_op jit(solution)/shard_map/ppermute | solution.py:426
  12.9 0.7 copy-start.4
  13.6 11.6 %collective-permute-start.3 = (f32[16,128]{1,0:T(8,128)S(1)}, f32[16,128]{1,0:T(8,128)S(1)}, u32[]{:S(2)}, u32[]{:S(2)}) collective-permute-start(f32[16,128]{1,0:T(8,128)S(1)} %pair.1.args_0_), channel_id=1, source_target_pairs={{6,0},{0,2},{2,4},{4,6},{7,1},{1,3},{3,5},{5,7},{14,8},{8,10},{10,... | collective-permute-start | bytes 24584 | tf_op jit(solution)/shard_map/ppermute | solution.py:426
  15.3 10.0 %collective-permute-start.2 = (f32[16,128]{1,0:T(8,128)S(1)}, f32[16,128]{1,0:T(8,128)S(1)}, u32[]{:S(2)}, u32[]{:S(2)}) collective-permute-start(f32[16,128]{1,0:T(8,128)S(1)} %pair.1.args_0_), channel_id=1, source_target_pairs={{4,0},{6,2},{0,4},{2,6},{5,1},{7,3},{1,5},{3,7},{12,8},{14,10},{8,... | collective-permute-start | bytes 24584 | tf_op jit(solution)/shard_map/ppermute | solution.py:426
  18.2 7.1 %collective-permute-start.1 = (f32[16,128]{1,0:T(8,128)S(1)}, f32[16,128]{1,0:T(8,128)S(1)}, u32[]{:S(2)}, u32[]{:S(2)}) collective-permute-start(f32[16,128]{1,0:T(8,128)S(1)} %pair.1.args_0_), channel_id=1, source_target_pairs={{2,0},{4,2},{6,4},{0,6},{3,1},{5,3},{7,5},{1,7},{10,8},{12,10},{14... | collective-permute-start | bytes 24584 | tf_op jit(solution)/shard_map/ppermute | solution.py:426
  19.5 1.6 %copy-start = (bf16[512,2048]{1,0:T(8,128)(2,1)S(1)}, bf16[512,2048]{1,0:T(8,128)(2,1)}, u32[]{:S(2)}) copy-start(bf16[512,2048]{1,0:T(8,128)(2,1)} %embed.3) | copy-start | bytes 6291460
  21.1 0.7 copy-start.1
  26.0 31.3 %collective-permute-start.6 = (bf16[8,16,2048]{2,1,0:T(8,128)(2,1)S(1)}, bf16[8,16,2048]{2,1,0:T(8,128)(2,1)S(1)}, u32[]{:S(2)}, u32[]{:S(2)}) collective-permute-start(bf16[8,16,2048]{2,1,0:T(8,128)(2,1)S(1)} %all-to-all-done.args_0_), channel_id=1, source_target_pairs={{24,0},{0,8},{8,16},{16,24},{25,1},{1,9},{9,17},{17,25},{26,2},{2,... | collective-permute-start | bytes 1572872 | tf_op jit(solution)/shard_map/ppermute | solution.py:426
  27.5 29.8 %collective-permute-start.5 = (bf16[8,16,2048]{2,1,0:T(8,128)(2,1)S(1)}, bf16[8,16,2048]{2,1,0:T(8,128)(2,1)}, u32[]{:S(2)}, u32[]{:S(2)}) collective-permute-start(bf16[8,16,2048]{2,1,0:T(8,128)(2,1)S(1)} %all-to-all-done.args_0_), channel_id=1, source_target_pairs={{16,0},{24,8},{0,16},{8,24},{17,1},{25,9},{1,17},{9,25},{18,2},{26... | collective-permute-start | bytes 1572872 | tf_op jit(solution)/shard_map/ppermute | solution.py:426
  30.3 27.1 %collective-permute-start.4 = (bf16[8,16,2048]{2,1,0:T(8,128)(2,1)S(1)}, bf16[8,16,2048]{2,1,0:T(8,128)(2,1)}, u32[]{:S(2)}, u32[]{:S(2)}) collective-permute-start(bf16[8,16,2048]{2,1,0:T(8,128)(2,1)S(1)} %all-to-all-done.args_0_), channel_id=1, source_target_pairs={{8,0},{16,8},{24,16},{0,24},{9,1},{17,9},{25,17},{1,25},{10,2},{18... | collective-permute-start | bytes 1572872 | tf_op jit(solution)/shard_map/ppermute | solution.py:426
  31.7 15.5 %all-to-all-start.1 = ((f32[8,48,128]{2,1,0:T(8,128)}), f32[8,48,128]{2,1,0:T(8,128)S(1)}, u32[]{:S(2)}, u32[]{:S(2)}) async-start(f32[8,48,128]{2,1,0:T(8,128)} %near.1), calls=%async_computation.1 | async-start | bytes 393216 | tf_op jit(solution)/shard_map/all_to_all | solution.py:455
  38.9 3.6 %copy-start.5 = (s32[1,1,24,2]{2,3,1,0:T(2,128)S(1)}, s32[1,1,24,2]{2,3,1,0:T(2,128)}, u32[]{:S(2)}) copy-start(s32[1,1,24,2]{2,3,1,0:T(2,128)} %param.10) | copy-start | bytes 580
  38.9 18.4 %copy-start.2 = (s32[2048]{0:T(1024)S(1)}, s32[2048]{0:T(1024)}, u32[]{:S(2)}) copy-start(s32[2048]{0:T(1024)} %param.8) | copy-start | bytes 24580
  38.9 18.4 %copy-start.3 = (s32[2048]{0:T(1024)S(1)}, s32[2048]{0:T(1024)}, u32[]{:S(2)}) copy-start(s32[2048]{0:T(1024)} %param.9) | copy-start | bytes 24580
  47.9 9.4 %all-to-all-start.2 = ((f32[4,72,128]{2,1,0:T(8,128)}), f32[4,72,128]{2,1,0:T(8,128)S(1)}, u32[]{:S(2)}, u32[]{:S(2)}) async-start(f32[4,72,128]{2,1,0:T(8,128)} %middle.1), calls=%async_computation.2 | async-start | bytes 294912 | tf_op jit(solution)/shard_map/all_to_all | solution.py:459

commit v10 on v9

--- a/solution.py
+++ b/solution.py
@@ -79,7 +79,11 @@
         copy.wait()
 
 
-def source_group_kernel(embed, labels, out_ref, sq_ref):
+def lower_lanes():
+    return lax.broadcasted_iota(jnp.int32, (8, LANES), 1) < LANES // 2
+
+
+def source_group_kernel(embed, labels, tgt_group, out_ref, sq_ref):
     onehot = repeated_onehot(labels[...])
     counts = jnp.maximum(jnp.sum(onehot, axis=1, keepdims=True), 1.0)
     onehot = onehot.astype(jnp.bfloat16)
@@ -88,7 +92,7 @@
         group, wide = class_group(embed[c * LANES : (c + 1) * LANES, :], onehot, counts)
         out_ref[8 * c : 8 * c + 8, :] = group
         sq = sq + jnp.sum(wide * wide, axis=0, keepdims=True)
-    out_ref[32:40, :] = jnp.broadcast_to(counts[:8], (8, LANES))
+    out_ref[32:40, :] = jnp.where(lower_lanes(), tgt_group[0:8, :], counts[:8])
     sq_ref[...] = sq
 
 
@@ -107,67 +111,64 @@
     return jnp.where(row_id < CLASSES, mean, spread)
 
 
-def target_joined(place, pieces, slots):
-    n = len(pieces)
-    for far, piece in enumerate(pieces):
-        slots[lax.rem(place[0] + far, n)] = piece[...]
-    counts = [slots[k, 8:16, :] for k in range(n)]
-    total, shares = joined_counts(counts)
-    return joined_group([slots[k, 0:8, :] for k in range(n)], counts, shares), total
-
-
-def pair_kernel(place, *args):
-    pieces, (out_ref, slots) = args[:-2], args[-2:]
-    group, total = target_joined(place, pieces, slots)
-    out_ref[0:8, :] = group
-    out_ref[8:16, :] = total
-
-
-def near_kernel(place, *args):
-    pieces, (src_group, out_ref, slots) = args[:-3], args[-3:]
-    group, total = target_joined(place, pieces, slots)
-    row_id = lax.broadcasted_iota(jnp.int32, (8, LANES), 0)
-    group = jnp.where(row_id < CLASSES, group, group / total)
-    for k in range(out_ref.shape[0]):
-        out_ref[k, 0:40, :] = src_group[...]
-        out_ref[k, 40:48, :] = group
-
-
 def source_joined(got):
     peers = got.shape[0]
-    counts = [got[k, 32:40, :] for k in range(peers)]
+    half = LANES // 2
+    lower = lower_lanes()
+    last = [got[k, 32:40, :] for k in range(peers)]
+    targets = [jnp.where(lower, g, 0.0) for g in last]
+    counts = [jnp.where(lower, pltpu.roll(g, half, 1), g) for g in last]
     total, shares = joined_counts(counts)
     groups = [
         joined_group([got[k, 8 * c : 8 * c + 8, :] for k in range(peers)], counts, shares)
         for c in range(WIDTH // LANES)
     ]
-    return groups, total
-
-
-def middle_kernel(width, got, out_ref):
-    groups, total = source_joined(got)
-    each = LANES // width
-    for c in range(WIDTH // LANES):
-        tgt = got[each * c, 40:48, :]
-        for k in range(1, each):
-            tgt = tgt + pltpu.roll(got[each * c + k, 40:48, :], k * width, 1)
-        for k in range(out_ref.shape[0]):
-            out_ref[k, 8 * c : 8 * c + 8, :] = groups[c]
-            out_ref[k, 40 + 8 * c : 48 + 8 * c, :] = tgt
+    return groups, total, targets
+
+
+def side_by_side(targets, width):
+    out = targets[0]
+    for k, target in enumerate(targets[1:]):
+        out = out + pltpu.roll(target, (k + 1) * width, 1)
+    return out
+
+
+def near_kernel(part, place, *args):
+    pieces, (tgt_group, src_ref, tgt_ref, slots) = args[:-4], args[-4:]
+    for far, piece in enumerate(pieces):
+        slots[lax.rem(place[0] + far, len(pieces))] = piece[...]
+    groups, total, targets = source_joined(slots)
+    for c, group in enumerate(groups):
+        src_ref[8 * c : 8 * c + 8, :] = group
+    src_ref[32:40, :] = total
+    target = jnp.where(lower_lanes(), side_by_side(targets, part), tgt_group[8:16, :])
+    for k in range(tgt_ref.shape[0]):
+        tgt_ref[k] = target
+
+
+def middle_kernel(got, src, out_ref):
+    half = LANES // 2
+    lower = lower_lanes()
+    row_id = lax.broadcasted_iota(jnp.int32, (8, LANES), 0)
+    each = [got[k] for k in range(got.shape[0])]
+    counts = [jnp.where(lower, pltpu.roll(g, half, 1), g) for g in each]
+    total, shares = joined_counts(counts)
+    group = joined_group([jnp.where(lower, g, 0.0) for g in each], counts, shares)
+    group = jnp.where(row_id < CLASSES, group, group / total)
+    last = jnp.where(lower, group, src[32:40, :])
     for k in range(out_ref.shape[0]):
-        out_ref[k, 32:40, :] = total
-
-
-def label_rows(part, got, src_sq, src_lab, label_ref, xa_ref):
-    groups, total = source_joined(got)
+        out_ref[k, 0:32, :] = src[0:32, :]
+        out_ref[k, 32:40, :] = last
+
+
+def label_rows(width, got, src_sq, src_lab, label_ref, xa_ref):
+    groups, total, targets = source_joined(got)
     row_id = lax.broadcasted_iota(jnp.int32, (8, LANES), 0)
     lane_id = lax.broadcasted_iota(jnp.int32, (8, LANES), 1)
+    each = LANES // width
     sides = ([], [])
     for c, group in enumerate(groups):
-        at = slice(40 + 8 * c, 48 + 8 * c)
-        tgt = got[0, at, :]
-        for k in range(1, got.shape[0]):
-            tgt = tgt + pltpu.roll(got[k, at, :], k * part, 1)
+        tgt = side_by_side(targets[each * c : each * c + each], width)
         for side, stat in zip(sides, (jnp.where(row_id < CLASSES, group, group / total), tgt)):
             side.append(jnp.where(row_id < CLASSES, stat, jnp.sqrt(stat + 1e-06)))
 
@@ -426,43 +427,36 @@
             lax.ppermute(x, axis, [((i + far) % n, i) for i in range(n)]) for far in range(1, n)
         ]
 
-    def join_targets(kernel, out_shape, x, axis, *more, name):
-        pieces = around(x, axis)
-        return pl.pallas_call(
-            kernel,
-            out_shape=out_shape,
-            in_specs=[smem()] + [vmem()] * (len(pieces) + len(more)),
-            out_specs=vmem(),
-            scratch_shapes=[pltpu.VMEM((len(pieces), 16, LANES), jnp.float32)],
-            compiler_params=params(),
-            name=name,
-        )(lax.axis_index(axis).reshape(1), *pieces, *more)
-
-    tgt_group = join_targets(pair_kernel, f32(16, LANES), tgt_group, "c", name="pair")
     src_group, src_sq = call(
         source_group_kernel,
         (f32(40, LANES), f32(1, ROWS)),
         source_embed,
         source_labels[None],
+        tgt_group,
         name="source_group",
     )
-    stats = join_targets(
-        near_kernel, f32(n_z, 48, LANES), tgt_group, "y", src_group, name="near"
-    )
-    near, stats = lax.optimization_barrier((near, stats))
-
+
+    near, packets = lax.optimization_barrier((near, around(src_group, "x")))
     pieces = around(near, "x")
+    src_group, tgt_near = pl.pallas_call(
+        functools.partial(near_kernel, part),
+        out_shape=(f32(40, LANES), f32(n_tgt, 8, LANES)),
+        in_specs=[smem()] + [vmem()] * (n_x + 1),
+        out_specs=(vmem(), vmem()),
+        scratch_shapes=[pltpu.VMEM((n_x, 40, LANES), jnp.float32)],
+        compiler_params=params(),
+        name="near",
+    )(lax.axis_index("x").reshape(1), *packets, tgt_group)
+    tgt_near = lax.all_to_all(tgt_near, TGT, 0, 0)
+    stats = call(middle_kernel, f32(n_z, 40, LANES), tgt_near, src_group, name="middle")
     stats = lax.all_to_all(stats, "z", 0, 0)
-    stats = call(
-        functools.partial(middle_kernel, part * n_x), f32(n_x, 72, LANES), stats, name="middle"
-    )
-    stats = lax.all_to_all(stats, "x", 0, 0)
+
     tall = pltpu.VMEM((ROWS, LANES), jnp.float32)
     wide = pltpu.VMEM((BLK, 8, BLOCK), jnp.float32)
     log_src = math.log2(ROWS * n_src)
     log_tgt = math.log2(ROWS * n_tgt)
     label_cost, tiles, sent = pl.pallas_call(
-        functools.partial(cost_kernel, n_x, part),
+        functools.partial(cost_kernel, n_x, part * n_x),
         out_shape=(
             f32(CLASSES, CLASSES),
             f32(MAXP, BLOCK, BLOCK),

time: 125 us -> 124 us (level)
  blocking collectives: 52.7 us -> 58.3 us
  waiting for transfers between devices: 11.9 us -> 6.78 us
  starting transfers between devices: 30.7 us -> 25.6 us
  Pallas kernels: 20.7 us -> 24.9 us
    all_to_all x0 -> x1, blocking collectives: none -> 9.72 us  [on_device(): tgt_near = lax.all_to_all(tgt_near, TGT, 0, 0)]
    all_to_all x1 -> x0, waiting for transfers between devices: 5.95 us -> none  [on_device(): stats = lax.all_to_all(stats, 'x', 0, 0)]
    all_to_all x1 -> x0, starting transfers between devices: 3.33 us -> none  [on_device(): stats = lax.all_to_all(stats, 'x', 0, 0)]
    all_to_all x1, blocking collectives: 10.1 us -> 7.99 us  [on_device(): sent, _ = columns(lax.all_to_all(sent, TGT, 0, 0))]
    pallas_call x3 -> x2, Pallas kernels: 6.17 us -> 7.82 us  [the longest x1 7.71 us: on_device(): pl.pallas_call(functools.partial(cost_kernel, n_x, part * n_x), out_shape...]
    all_to_all x1, starting transfers between devices: 7.21 us -> 5.76 us  [on_device(): stats = lax.all_to_all(stats, 'z', 0, 0)]
    pallas_call x2, Pallas kernels: 4.49 us -> 5.93 us  [columns(): pl.pallas_call(functools.partial(col_kernel, log_tgt), out_shape=(f32(n_s...]
    all_to_all x1, blocking collectives: 9.4 us -> 7.99 us  [on_device(): sent, src_pot = columns(lax.all_to_all(sent, TGT, 0, 0))]
  transfers between devices with their start and end apart: 10 -> 8, of which waited for: 3 -> 3; matrix products, arithmetic and copies ran while one was open for 3% -> 3% of each run, Pallas kernels for 4% -> 4%
where the time goes in v10:
time: 124 us; the launch traced here: 123 us
  blocking collectives  58.3 us (47%)
  starting transfers between devices  25.6 us (21%)
  Pallas kernels  24.9 us (20%)
  waiting for transfers between devices  6.78 us (5%)
  local copies, waits for them, and re-layouts  6.07 us (5%)
  between operations  1.36 us (1%)
    all_to_all x2, blocking collectives, both_ways(): return lax.all_to_all(x, axes + ('c',), 0, 0, axis_index_groups=groups)  32.6 us
    ppermute x6, starting transfers between devices, around(): lax.ppermute(x, axis, [((i + far) % n, i) for i in range(n)])  11.3 us
    all_to_all x1, blocking collectives, on_device(): tgt_near = lax.all_to_all(tgt_near, TGT, 0, 0)  9.72 us
    all_to_all x1, starting transfers between devices, both_ways(): return lax.all_to_all(x, axes + ('c',), 0, 0, axis_index_groups=groups)  8.58 us
    all_to_all x1, blocking collectives, on_device(): sent, _ = columns(lax.all_to_all(sent, TGT, 0, 0))  7.99 us
    all_to_all x1, blocking collectives, on_device(): sent, src_pot = columns(lax.all_to_all(sent, TGT, 0, 0))  7.99 us
    pallas_call x1, Pallas kernels, on_device(): pl.pallas_call(functools.partial(cost_kernel, n_x, part * n_x), out_shape...  7.71 us
    unnamed x16, local copies, waits for them, and re-layouts  5.98 us
  transfers between devices with their start and end apart: 8, of which 3 were waited for; matrix products, arithmetic and copies ran while one was open for 3% of the time, Pallas kernels for 4%

profile of v10, /device:TPU:32, one launch (start us, length us, event | category | flops | bytes accessed | tf_op | source)
XLA Modules:
  0.0 123.1 jit_solution(2682792646795338746)
XLA Ops:
  0.6 2.3 %first.1 = (bf16[8,16,2048]{2,1,0:T(8,128)(2,1)}, f32[16,128]{1,0:T(8,128)}) custom-call(bf16[16,2048]{1,0:T(8,128)(2,1)} %embed.2, s32[1,2048]{1,0:T(1,128)} %bitcast.17), custom_call_target="tpu_custom_call" | custom-call | tf_op jit(solution)/shard_map/first/pallas_call | solution.py:410
  3.0 0.0 copy-start.5
  3.0 8.6 %all-to-all-start = ((bf16[8,16,2048]{2,1,0:T(8,128)(2,1)}), bf16[8,16,2048]{2,1,0:T(8,128)(2,1)S(1)}, u32[]{:S(2)}, u32[]{:S(2)}) async-start(bf16[8,16,2048]{2,1,0:T(8,128)(2,1)} %get-tuple-element.20), calls=%async_computation | async-start | bytes 1048576 | tf_op jit(solution)/shard_map/all_to_all | solution.py:390
  11.5 0.0 copy-start
  11.6 1.6 %copy-done = bf16[512,2048]{1,0:T(8,128)(2,1)S(1)} copy-done((bf16[512,2048]{1,0:T(8,128)(2,1)S(1)}, bf16[512,2048]{1,0:T(8,128)(2,1)}, u32[]{:S(2)}) %copy-start) | copy-done | bytes 2097176
  13.1 0.0 copy-start.1
  13.1 0.7 copy-done.1
  13.8 0.0 copy-start.4
  13.8 0.7 copy-done.4
  14.5 3.5 %source_group.1 = (f32[40,128]{1,0:T(8,128)S(1)}, f32[1,2048]{1,0:T(1,128)S(1)}) custom-call(bf16[512,2048]{1,0:T(8,128)(2,1)S(1)} %copy-done, s32[1,2048]{1,0:T(1,128)S(1)} %bitcast.15, f32[16,128]{1,0:T(8,128)S(1)} %copy-done.4), custom_call_target="tpu_custom_call" | custom-call | tf_op jit(solution)/shard_map/source_group/pallas_call | solution.py:399
  18.0 1.6 %collective-permute-start.2 = (f32[40,128]{1,0:T(8,128)S(1)}, f32[40,128]{1,0:T(8,128)S(1)}, u32[]{:S(2)}, u32[]{:S(2)}) collective-permute-start(f32[40,128]{1,0:T(8,128)S(1)} %get-tuple-element.23.args_0_), channel_id=1, source_target_pairs={{24,0},{0,8},{8,16},{16,24},{25,1},{1,9},{9,17},{17,25},{26,2},{2,... | collective-permute-start | bytes 61448 | tf_op jit(solution)/shard_map/ppermute | solution.py:427
  19.5 2.7 %collective-permute-start.1 = (f32[40,128]{1,0:T(8,128)S(1)}, f32[40,128]{1,0:T(8,128)S(1)}, u32[]{:S(2)}, u32[]{:S(2)}) collective-permute-start(f32[40,128]{1,0:T(8,128)S(1)} %get-tuple-element.23.args_0_), channel_id=1, source_target_pairs={{16,0},{24,8},{0,16},{8,24},{17,1},{25,9},{1,17},{9,25},{18,2},{26... | collective-permute-start | bytes 61448 | tf_op jit(solution)/shard_map/ppermute | solution.py:427
  22.3 1.4 %collective-permute-start = (f32[40,128]{1,0:T(8,128)S(1)}, f32[40,128]{1,0:T(8,128)S(1)}, u32[]{:S(2)}, u32[]{:S(2)}) collective-permute-start(f32[40,128]{1,0:T(8,128)S(1)} %get-tuple-element.23.args_0_), channel_id=1, source_target_pairs={{8,0},{16,8},{24,16},{0,24},{9,1},{17,9},{25,17},{1,25},{10,2},{18... | collective-permute-start | bytes 61448 | tf_op jit(solution)/shard_map/ppermute | solution.py:427
  23.7 0.0 collective-permute-done.2.args_3_
  23.7 1.1 collective-permute-done.1.args_2_
  24.8 1.2 collective-permute-done.args_1_
  26.1 0.0 all-to-all-done.args_0_
  26.1 1.4 %collective-permute-start.5 = (bf16[8,16,2048]{2,1,0:T(8,128)(2,1)S(1)}, bf16[8,16,2048]{2,1,0:T(8,128)(2,1)S(1)}, u32[]{:S(2)}, u32[]{:S(2)}) collective-permute-start(bf16[8,16,2048]{2,1,0:T(8,128)(2,1)S(1)} %all-to-all-done.args_0_), channel_id=1, source_target_pairs={{24,0},{0,8},{8,16},{16,24},{25,1},{1,9},{9,17},{17,25},{26,2},{2,... | collective-permute-start | bytes 1572872 | tf_op jit(solution)/shard_map/ppermute | solution.py:427
  27.5 2.7 %collective-permute-start.4 = (bf16[8,16,2048]{2,1,0:T(8,128)(2,1)S(1)}, bf16[8,16,2048]{2,1,0:T(8,128)(2,1)}, u32[]{:S(2)}, u32[]{:S(2)}) collective-permute-start(bf16[8,16,2048]{2,1,0:T(8,128)(2,1)S(1)} %all-to-all-done.args_0_), channel_id=1, source_target_pairs={{16,0},{24,8},{0,16},{8,24},{17,1},{25,9},{1,17},{9,25},{18,2},{26... | collective-permute-start | bytes 1572872 | tf_op jit(solution)/shard_map/ppermute | solution.py:427
  30.2 1.4 %collective-permute-start.3 = (bf16[8,16,2048]{2,1,0:T(8,128)(2,1)S(1)}, bf16[8,16,2048]{2,1,0:T(8,128)(2,1)}, u32[]{:S(2)}, u32[]{:S(2)}) collective-permute-start(bf16[8,16,2048]{2,1,0:T(8,128)(2,1)S(1)} %all-to-all-done.args_0_), channel_id=1, source_target_pairs={{8,0},{16,8},{24,16},{0,24},{9,1},{17,9},{25,17},{1,25},{10,2},{18... | collective-permute-start | bytes 1572872 | tf_op jit(solution)/shard_map/ppermute | solution.py:427
  31.7 0.0 copy-done.5
  31.7 0.1 near.1
  31.8 9.7 %all_to_all.35.got = f32[8,8,128]{2,1,0:T(8,128)S(1)} all-to-all(f32[8,8,128]{2,1,0:T(8,128)S(1)} %get-tuple-element.27), channel_id=1, replica_groups=mesh['z'=8,'x'=4,'y'=4,'c'=2] {'y','c'}, dimensions={0} | all-to-all | bytes 65536 | tf_op jit(solution)/shard_map/all_to_all | solution.py:450
  41.5 0.8 middle.1
  42.3 5.8 %all-to-all-start.2 = ((f32[8,40,128]{2,1,0:T(8,128)}), f32[8,40,128]{2,1,0:T(8,128)S(1)}, u32[]{:S(2)}, u32[]{:S(2)}) async-start(f32[8,40,128]{2,1,0:T(8,128)} %middle.1), calls=%async_computation.2 | async-start | bytes 327680 | tf_op jit(solution)/shard_map/all_to_all | solution.py:452
  48.0 0.0 copy-start.6
  48.0 0.0 copy-start.2
  48.0 0.0 copy-start.3
  48.0 2.9 %copy.12 = bf16[512,2048]{0,1:T(8,128)(2,1)S(1)} copy(bf16[512,2048]{1,0:T(8,128)(2,1)} %embed.3) | data formatting | bytes 4194304 | tf_op args[0]
  51.6 0.0 copy-done.6
  51.6 0.1 copy.11
  51.7 0.1 reshape.19.pairs
  51.8 0.1 pad_add_fusion.place
  51.9 4.4 %all-to-all-done.2.got = f32[8,40,128]{2,1,0:T(8,128)S(1)} async-done(((f32[8,40,128]{2,1,0:T(8,128)}), f32[8,40,128]{2,1,0:T(8,128)S(1)}, u32[]{:S(2)}, u32[]{:S(2)}) %all-to-all-start.2) | async-done | bytes 163872 | tf_op jit(solution)/shard_map/all_to_all | solution.py:452
  56.3 0.0 collective-permute-done.5.args_3_
  56.3 0.0 collective-permute-done.4.args_2_
  56.3 0.0 collective-permute-done.3.args_1_
  56.3 0.0 copy-done.2
  56.3 0.0 copy-done.3
  56.3 7.7 %cost_rows.1 = (f32[4,4]{1,0:T(4,128)}, f32[24,256,256]{2,1,0:T(8,128)S(1)}, f32[8,16,128]{2,1,0:T(8,128)S(1)}) custom-call(s32[48]{0:T(128)S(1)} %reshape.19.pairs, s32[1]{0:T(128)} %bitcast.10.count, s32[2]{0:T(128)S(1)} %pad_add_fusion.place, f32[8,40,128]{2,1,0:T(8,128)S(1)} %all-to-all-done.2.got, f32[1,2048]{1,0:T(1,128)S(1)} %get-tuple-element.29.src_sq, ...), custom_call_target="tpu_custom_call" | custom-call | tf_op jit(solution)/shard_map/cost_rows/pallas_call | solution.py:458
  64.0 8.0 %all_to_all.36.g_ref = f32[8,16,128]{2,1,0:T(8,128)S(1)} all-to-all(f32[8,16,128]{2,1,0:T(8,128)S(1)} %get-tuple-element.32), channel_id=1, replica_groups=mesh['z'=8,'x'=4,'y'=4,'c'=2] {'y','c'}, dimensions={0} | all-to-all | bytes 131072 | tf_op jit(solution)/shard_map/all_to_all | solution.py:510
  72.0 3.0 %columns.2 = (f32[32,16,128]{2,1,0:T(8,128)S(1)}, f32[16,128]{1,0:T(8,128)}) custom-call(s32[48]{0:T(128)S(1)} %reshape.19.pairs, s32[1]{0:T(128)} %bitcast.11.count, f32[24,256,256]{2,1,0:T(8,128)S(1)} %get-tuple-element.31.tiles, f32[8,16,128]{2,1,0:T(8,128)S(1)} %all_to_all.36.g_ref), custom_call_target="tpu_custom_call" | custom-call | tf_op jit(solution)/shard_map/columns/pallas_call | solution.py:489
  75.0 16.6 %all_to_all.37.g_ref = f32[32,16,128]{2,1,0:T(8,128)S(1)} all-to-all(f32[32,16,128]{2,1,0:T(8,128)S(1)} %get-tuple-element.33), channel_id=1, replica_groups={{0,8,16,24,32,40,48,56,64,72,80,88,96,104,112,120,128,136,144,152,160,1..., dimensions={0} | all-to-all | bytes 524288 | tf_op jit(solution)/shard_map/all_to_all | solution.py:390
  91.6 3.9 %rows.1 = f32[8,16,128]{2,1,0:T(8,128)S(1)} custom-call(s32[48]{0:T(128)S(1)} %reshape.19.pairs, s32[1]{0:T(128)} %bitcast.12.count, f32[24,256,256]{2,1,0:T(8,128)S(1)} %get-tuple-element.31.tiles, f32[32,16,128]{2,1,0:T(8,128)S(1)} %all_to_all.37.g_ref), custom_call_target="tpu_custom_call" | custom-call | tf_op jit(solution)/shard_map/rows/pallas_call | solution.py:500
  95.5 8.0 %all_to_all.38.g_ref = f32[8,16,128]{2,1,0:T(8,128)S(1)} all-to-all(f32[8,16,128]{2,1,0:T(8,128)S(1)} %rows.1), channel_id=1, replica_groups=mesh['z'=8,'x'=4,'y'=4,'c'=2] {'y','c'}, dimensions={0} | all-to-all | bytes 131072 | tf_op jit(solution)/shard_map/all_to_all | solution.py:512
  103.5 3.0 %columns.3 = (f32[32,16,128]{2,1,0:T(8,128)S(1)}, f32[16,128]{1,0:T(8,128)}) custom-call(s32[48]{0:T(128)S(1)} %reshape.19.pairs, s32[1]{0:T(128)} %bitcast.13.count, f32[24,256,256]{2,1,0:T(8,128)S(1)} %get-tuple-element.31.tiles, f32[8,16,128]{2,1,0:T(8,128)S(1)} %all_to_all.38.g_ref), custom_call_target="tpu_custom_call" | custom-call | tf_op jit(solution)/shard_map/columns/pallas_call | solution.py:489
  106.5 16.0 %all_to_all.39.g_ref = f32[32,16,128]{2,1,0:T(8,128)S(1)} all-to-all(f32[32,16,128]{2,1,0:T(8,128)S(1)} %get-tuple-element.35), channel_id=1, replica_groups={{0,8,16,24,32,40,48,56,64,72,80,88,96,104,112,120,128,136,144,152,160,1..., dimensions={0} | all-to-all | bytes 524288 | tf_op jit(solution)/shard_map/all_to_all | solution.py:390
  122.4 0.7 last.1
Async XLA Ops:
  3.0 28.7 %copy-start.5 = (f32[16,128]{1,0:T(8,128)S(1)}, f32[16,128]{1,0:T(8,128)}, u32[]{:S(2)}) copy-start(f32[16,128]{1,0:T(8,128)} %get-tuple-element.21.tgt_group.args_4_) | copy-start | bytes 24580
  3.0 23.1 %all-to-all-start = ((bf16[8,16,2048]{2,1,0:T(8,128)(2,1)}), bf16[8,16,2048]{2,1,0:T(8,128)(2,1)S(1)}, u32[]{:S(2)}, u32[]{:S(2)}) async-start(bf16[8,16,2048]{2,1,0:T(8,128)(2,1)} %get-tuple-element.20), calls=%async_computation | async-start | bytes 1048576 | tf_op jit(solution)/shard_map/all_to_all | solution.py:390
  11.5 1.6 %copy-start = (bf16[512,2048]{1,0:T(8,128)(2,1)S(1)}, bf16[512,2048]{1,0:T(8,128)(2,1)}, u32[]{:S(2)}) copy-start(bf16[512,2048]{1,0:T(8,128)(2,1)} %embed.3) | copy-start | bytes 6291460
  13.1 0.7 copy-start.1
  13.8 0.7 copy-start.4
  18.0 5.7 %collective-permute-start.2 = (f32[40,128]{1,0:T(8,128)S(1)}, f32[40,128]{1,0:T(8,128)S(1)}, u32[]{:S(2)}, u32[]{:S(2)}) collective-permute-start(f32[40,128]{1,0:T(8,128)S(1)} %get-tuple-element.23.args_0_), channel_id=1, source_target_pairs={{24,0},{0,8},{8,16},{16,24},{25,1},{1,9},{9,17},{17,25},{26,2},{2,... | collective-permute-start | bytes 61448 | tf_op jit(solution)/shard_map/ppermute | solution.py:427
  19.5 5.3 %collective-permute-start.1 = (f32[40,128]{1,0:T(8,128)S(1)}, f32[40,128]{1,0:T(8,128)S(1)}, u32[]{:S(2)}, u32[]{:S(2)}) collective-permute-start(f32[40,128]{1,0:T(8,128)S(1)} %get-tuple-element.23.args_0_), channel_id=1, source_target_pairs={{16,0},{24,8},{0,16},{8,24},{17,1},{25,9},{1,17},{9,25},{18,2},{26... | collective-permute-start | bytes 61448 | tf_op jit(solution)/shard_map/ppermute | solution.py:427
  22.3 3.8 %collective-permute-start = (f32[40,128]{1,0:T(8,128)S(1)}, f32[40,128]{1,0:T(8,128)S(1)}, u32[]{:S(2)}, u32[]{:S(2)}) collective-permute-start(f32[40,128]{1,0:T(8,128)S(1)} %get-tuple-element.23.args_0_), channel_id=1, source_target_pairs={{8,0},{16,8},{24,16},{0,24},{9,1},{17,9},{25,17},{1,25},{10,2},{18... | collective-permute-start | bytes 61448 | tf_op jit(solution)/shard_map/ppermute | solution.py:427
  26.1 30.2 %collective-permute-start.5 = (bf16[8,16,2048]{2,1,0:T(8,128)(2,1)S(1)}, bf16[8,16,2048]{2,1,0:T(8,128)(2,1)S(1)}, u32[]{:S(2)}, u32[]{:S(2)}) collective-permute-start(bf16[8,16,2048]{2,1,0:T(8,128)(2,1)S(1)} %all-to-all-done.args_0_), channel_id=1, source_target_pairs={{24,0},{0,8},{8,16},{16,24},{25,1},{1,9},{9,17},{17,25},{26,2},{2,... | collective-permute-start | bytes 1572872 | tf_op jit(solution)/shard_map/ppermute | solution.py:427
  27.5 28.8 %collective-permute-start.4 = (bf16[8,16,2048]{2,1,0:T(8,128)(2,1)S(1)}, bf16[8,16,2048]{2,1,0:T(8,128)(2,1)}, u32[]{:S(2)}, u32[]{:S(2)}) collective-permute-start(bf16[8,16,2048]{2,1,0:T(8,128)(2,1)S(1)} %all-to-all-done.args_0_), channel_id=1, source_target_pairs={{16,0},{24,8},{0,16},{8,24},{17,1},{25,9},{1,17},{9,25},{18,2},{26... | collective-permute-start | bytes 1572872 | tf_op jit(solution)/shard_map/ppermute | solution.py:427
  30.2 26.1 %collective-permute-start.3 = (bf16[8,16,2048]{2,1,0:T(8,128)(2,1)S(1)}, bf16[8,16,2048]{2,1,0:T(8,128)(2,1)}, u32[]{:S(2)}, u32[]{:S(2)}) collective-permute-start(bf16[8,16,2048]{2,1,0:T(8,128)(2,1)S(1)} %all-to-all-done.args_0_), channel_id=1, source_target_pairs={{8,0},{16,8},{24,16},{0,24},{9,1},{17,9},{25,17},{1,25},{10,2},{18... | collective-permute-start | bytes 1572872 | tf_op jit(solution)/shard_map/ppermute | solution.py:427
  42.3 14.0 %all-to-all-start.2 = ((f32[8,40,128]{2,1,0:T(8,128)}), f32[8,40,128]{2,1,0:T(8,128)S(1)}, u32[]{:S(2)}, u32[]{:S(2)}) async-start(f32[8,40,128]{2,1,0:T(8,128)} %middle.1), calls=%async_computation.2 | async-start | bytes 327680 | tf_op jit(solution)/shard_map/all_to_all | solution.py:452
  48.0 3.6 %copy-start.6 = (s32[1,1,24,2]{2,3,1,0:T(2,128)S(1)}, s32[1,1,24,2]{2,3,1,0:T(2,128)}, u32[]{:S(2)}) copy-start(s32[1,1,24,2]{2,3,1,0:T(2,128)} %param.10) | copy-start | bytes 580
  48.0 8.3 %copy-start.2 = (s32[2048]{0:T(1024)S(1)}, s32[2048]{0:T(1024)}, u32[]{:S(2)}) copy-start(s32[2048]{0:T(1024)} %param.8) | copy-start | bytes 24580
  48.0 8.3 %copy-start.3 = (s32[2048]{0:T(1024)S(1)}, s32[2048]{0:T(1024)}, u32[]{:S(2)}) copy-start(s32[2048]{0:T(1024)} %param.9) | copy-start | bytes 24580

commit v11 on v10

--- a/solution.py
+++ b/solution.py
@@ -111,16 +111,17 @@
     return jnp.where(row_id < CLASSES, mean, spread)
 
 
-def source_joined(got):
+def source_joined(got, order=None):
     peers = got.shape[0]
+    order = range(peers) if order is None else order
     half = LANES // 2
     lower = lower_lanes()
-    last = [got[k, 32:40, :] for k in range(peers)]
+    last = [got[k, 32:40, :] for k in order]
     targets = [jnp.where(lower, g, 0.0) for g in last]
     counts = [jnp.where(lower, pltpu.roll(g, half, 1), g) for g in last]
     total, shares = joined_counts(counts)
     groups = [
-        joined_group([got[k, 8 * c : 8 * c + 8, :] for k in range(peers)], counts, shares)
+        joined_group([got[k, 8 * c : 8 * c + 8, :] for k in order], counts, shares)
         for c in range(WIDTH // LANES)
     ]
     return groups, total, targets
@@ -161,8 +162,11 @@
         out_ref[k, 32:40, :] = last
 
 
-def label_rows(width, got, src_sq, src_lab, label_ref, xa_ref):
-    groups, total, targets = source_joined(got)
+def label_rows(width, core, got, src_sq, src_lab, label_ref, xa_ref):
+    peers = got.shape[0]
+    groups, total, targets = source_joined(
+        got, [k + core * (peers - 1 - 2 * k) for k in range(peers)]
+    )
     row_id = lax.broadcasted_iota(jnp.int32, (8, LANES), 0)
     lane_id = lax.broadcasted_iota(jnp.int32, (8, LANES), 1)
     each = LANES // width
@@ -245,7 +249,7 @@
 
 def cost_kernel(n_x, n_f, pairs, count, place, got, src_sq, src_lab, xt, *args):
     pieces, (tgt_lab, label_ref, tiles, out_ref, xa, y, ya, top, total) = args[:n_x], args[n_x:]
-    label_rows(n_f, got, src_sq, src_lab, label_ref, xa)
+    label_rows(n_f, place[1], got, src_sq, src_lab, label_ref, xa)
     row_id = lax.broadcasted_iota(jnp.int32, (16, 1), 0)
     part = row_id // CLASSES
     cls = row_id % CLASSES
@@ -448,8 +452,9 @@
         name="near",
     )(lax.axis_index("x").reshape(1), *packets, tgt_group)
     tgt_near = lax.all_to_all(tgt_near, TGT, 0, 0)
+    tgt_near, source_tall = lax.optimization_barrier((tgt_near, source_embed.T))
     stats = call(middle_kernel, f32(n_z, 40, LANES), tgt_near, src_group, name="middle")
-    stats = lax.all_to_all(stats, "z", 0, 0)
+    stats = both_ways(stats, ("z",))
 
     tall = pltpu.VMEM((ROWS, LANES), jnp.float32)
     wide = pltpu.VMEM((BLK, 8, BLOCK), jnp.float32)
@@ -480,7 +485,7 @@
         stats,
         src_sq,
         source_labels[None],
-        source_embed.T,
+        source_tall,
         *pieces,
         target_labels[None],
     )

time: 124 us -> 125 us (level)
  blocking collectives: 58.3 us -> 52.3 us
  waiting for transfers between devices: 6.78 us -> 11.6 us
  starting transfers between devices: 25.6 us -> 30.1 us
  Pallas kernels: 24.9 us -> 22.3 us
    all_to_all x1 -> x0, blocking collectives: 9.72 us -> none  [on_device(): tgt_near = lax.all_to_all(tgt_near, TGT, 0, 0)]
    all_to_all x1 -> x2, waiting for transfers between devices: 0.01 us -> 6.66 us  [both_ways(): return lax.all_to_all(x, axes + ('c',), 0, 0, axis_index_groups=groups)]
    all_to_all x1 -> x2, starting transfers between devices: 8.58 us -> 14.3 us  [both_ways(): return lax.all_to_all(x, axes + ('c',), 0, 0, axis_index_groups=groups)]
    all_to_all x2, blocking collectives: 32.6 us -> 35.4 us  [both_ways(): return lax.all_to_all(x, axes + ('c',), 0, 0, axis_index_groups=groups)]
    all_to_all x1, waiting for transfers between devices: 4.42 us -> 2.53 us  [on_device(): tgt_near = lax.all_to_all(tgt_near, TGT, 0, 0)]
    pallas_call x1, Pallas kernels: 7.71 us -> 6.2 us  [on_device(): pl.pallas_call(functools.partial(cost_kernel, n_x, part * n_x), out_shape...]
    all_to_all x1, starting transfers between devices: 5.76 us -> 4.47 us  [on_device(): tgt_near = lax.all_to_all(tgt_near, TGT, 0, 0)]
  transfers between devices with their start and end apart: 8 -> 9, of which waited for: 3 -> 4; matrix products, arithmetic and copies ran while one was open for 3% -> 3% of each run, Pallas kernels for 4% -> 4%
where the time goes in v11:
time: 125 us; the launch traced here: 124 us
  blocking collectives  52.3 us (42%)
  starting transfers between devices  30.1 us (24%)
  Pallas kernels  22.3 us (18%)
  waiting for transfers between devices  11.6 us (9%)
  local copies, waits for them, and re-layouts  6.06 us (5%)
  between operations  1.37 us (1%)
    all_to_all x2, blocking collectives, both_ways(): return lax.all_to_all(x, axes + ('c',), 0, 0, axis_index_groups=groups)  35.4 us
    all_to_all x2, starting transfers between devices, both_ways(): return lax.all_to_all(x, axes + ('c',), 0, 0, axis_index_groups=groups)  14.3 us
    ppermute x6, starting transfers between devices, around(): lax.ppermute(x, axis, [((i + far) % n, i) for i in range(n)])  11.3 us
    all_to_all x1, blocking collectives, on_device(): sent, _ = columns(lax.all_to_all(sent, TGT, 0, 0))  8.91 us
    all_to_all x1, blocking collectives, on_device(): sent, src_pot = columns(lax.all_to_all(sent, TGT, 0, 0))  7.99 us
    all_to_all x2, waiting for transfers between devices, both_ways(): return lax.all_to_all(x, axes + ('c',), 0, 0, axis_index_groups=groups)  6.66 us
    pallas_call x1, Pallas kernels, on_device(): pl.pallas_call(functools.partial(cost_kernel, n_x, part * n_x), out_shape...  6.2 us
    unnamed x16, local copies, waits for them, and re-layouts  5.97 us
  transfers between devices with their start and end apart: 9, of which 4 were waited for; matrix products, arithmetic and copies ran while one was open for 3% of the time, Pallas kernels for 4%

profile of v11, /device:TPU:32, one launch (start us, length us, event | category | flops | bytes accessed | tf_op | source)
XLA Modules:
  0.0 123.7 jit_solution(9437663659471545820)
XLA Ops:
  0.6 2.3 %first.1 = (bf16[8,16,2048]{2,1,0:T(8,128)(2,1)}, f32[16,128]{1,0:T(8,128)}) custom-call(bf16[16,2048]{1,0:T(8,128)(2,1)} %embed.2, s32[1,2048]{1,0:T(1,128)} %bitcast.17), custom_call_target="tpu_custom_call" | custom-call | tf_op jit(solution)/shard_map/first/pallas_call | solution.py:414
  3.0 0.0 copy-start.5
  3.0 8.6 %all-to-all-start = ((bf16[8,16,2048]{2,1,0:T(8,128)(2,1)}), bf16[8,16,2048]{2,1,0:T(8,128)(2,1)S(1)}, u32[]{:S(2)}, u32[]{:S(2)}) async-start(bf16[8,16,2048]{2,1,0:T(8,128)(2,1)} %get-tuple-element.22), calls=%async_computation | async-start | bytes 1048576 | tf_op jit(solution)/shard_map/all_to_all | solution.py:394
  11.5 0.0 copy-start
  11.6 1.6 %copy-done = bf16[512,2048]{1,0:T(8,128)(2,1)S(1)} copy-done((bf16[512,2048]{1,0:T(8,128)(2,1)S(1)}, bf16[512,2048]{1,0:T(8,128)(2,1)}, u32[]{:S(2)}) %copy-start) | copy-done | bytes 2097176
  13.1 0.0 copy-start.1
  13.1 0.7 copy-done.1
  13.8 0.0 copy-start.4
  13.8 0.7 copy-done.4
  14.5 3.5 %source_group.1 = (f32[40,128]{1,0:T(8,128)S(1)}, f32[1,2048]{1,0:T(1,128)S(1)}) custom-call(bf16[512,2048]{1,0:T(8,128)(2,1)S(1)} %copy-done, s32[1,2048]{1,0:T(1,128)S(1)} %bitcast.15, f32[16,128]{1,0:T(8,128)S(1)} %copy-done.4), custom_call_target="tpu_custom_call" | custom-call | tf_op jit(solution)/shard_map/source_group/pallas_call | solution.py:403
  18.0 1.6 %collective-permute-start.2 = (f32[40,128]{1,0:T(8,128)S(1)}, f32[40,128]{1,0:T(8,128)S(1)}, u32[]{:S(2)}, u32[]{:S(2)}) collective-permute-start(f32[40,128]{1,0:T(8,128)S(1)} %get-tuple-element.25.args_0_), channel_id=1, source_target_pairs={{24,0},{0,8},{8,16},{16,24},{25,1},{1,9},{9,17},{17,25},{26,2},{2,... | collective-permute-start | bytes 61448 | tf_op jit(solution)/shard_map/ppermute | solution.py:431
  19.5 2.7 %collective-permute-start.1 = (f32[40,128]{1,0:T(8,128)S(1)}, f32[40,128]{1,0:T(8,128)S(1)}, u32[]{:S(2)}, u32[]{:S(2)}) collective-permute-start(f32[40,128]{1,0:T(8,128)S(1)} %get-tuple-element.25.args_0_), channel_id=1, source_target_pairs={{16,0},{24,8},{0,16},{8,24},{17,1},{25,9},{1,17},{9,25},{18,2},{26... | collective-permute-start | bytes 61448 | tf_op jit(solution)/shard_map/ppermute | solution.py:431
  22.3 1.4 %collective-permute-start = (f32[40,128]{1,0:T(8,128)S(1)}, f32[40,128]{1,0:T(8,128)S(1)}, u32[]{:S(2)}, u32[]{:S(2)}) collective-permute-start(f32[40,128]{1,0:T(8,128)S(1)} %get-tuple-element.25.args_0_), channel_id=1, source_target_pairs={{8,0},{16,8},{24,16},{0,24},{9,1},{17,9},{25,17},{1,25},{10,2},{18... | collective-permute-start | bytes 61448 | tf_op jit(solution)/shard_map/ppermute | solution.py:431
  23.7 0.0 collective-permute-done.2.args_3_
  23.7 1.1 collective-permute-done.1.args_2_
  24.8 1.2 collective-permute-done.args_1_
  26.1 0.0 all-to-all-done.args_0_
  26.1 1.4 %collective-permute-start.5 = (bf16[8,16,2048]{2,1,0:T(8,128)(2,1)S(1)}, bf16[8,16,2048]{2,1,0:T(8,128)(2,1)S(1)}, u32[]{:S(2)}, u32[]{:S(2)}) collective-permute-start(bf16[8,16,2048]{2,1,0:T(8,128)(2,1)S(1)} %all-to-all-done.args_0_), channel_id=1, source_target_pairs={{24,0},{0,8},{8,16},{16,24},{25,1},{1,9},{9,17},{17,25},{26,2},{2,... | collective-permute-start | bytes 1572872 | tf_op jit(solution)/shard_map/ppermute | solution.py:431
  27.5 2.7 %collective-permute-start.4 = (bf16[8,16,2048]{2,1,0:T(8,128)(2,1)S(1)}, bf16[8,16,2048]{2,1,0:T(8,128)(2,1)}, u32[]{:S(2)}, u32[]{:S(2)}) collective-permute-start(bf16[8,16,2048]{2,1,0:T(8,128)(2,1)S(1)} %all-to-all-done.args_0_), channel_id=1, source_target_pairs={{16,0},{24,8},{0,16},{8,24},{17,1},{25,9},{1,17},{9,25},{18,2},{26... | collective-permute-start | bytes 1572872 | tf_op jit(solution)/shard_map/ppermute | solution.py:431
  30.2 1.4 %collective-permute-start.3 = (bf16[8,16,2048]{2,1,0:T(8,128)(2,1)S(1)}, bf16[8,16,2048]{2,1,0:T(8,128)(2,1)}, u32[]{:S(2)}, u32[]{:S(2)}) collective-permute-start(bf16[8,16,2048]{2,1,0:T(8,128)(2,1)S(1)} %all-to-all-done.args_0_), channel_id=1, source_target_pairs={{8,0},{16,8},{24,16},{0,24},{9,1},{17,9},{25,17},{1,25},{10,2},{18... | collective-permute-start | bytes 1572872 | tf_op jit(solution)/shard_map/ppermute | solution.py:431
  31.7 0.0 copy-done.5
  31.7 0.7 near.1
  32.4 4.5 %all-to-all-start.1 = ((f32[8,8,128]{2,1,0:T(8,128)}), f32[8,8,128]{2,1,0:T(8,128)S(1)}, u32[]{:S(2)}, u32[]{:S(2)}) async-start(f32[8,8,128]{2,1,0:T(8,128)} %get-tuple-element.29), calls=%async_computation.1 | async-start | bytes 65536 | tf_op jit(solution)/shard_map/all_to_all | solution.py:454
  36.8 0.0 copy-start.6
  36.8 0.0 copy-start.2
  36.8 0.0 copy-start.3
  36.9 2.9 %copy.12 = bf16[512,2048]{0,1:T(8,128)(2,1)S(1)} copy(bf16[512,2048]{1,0:T(8,128)(2,1)} %embed.3) | data formatting | bytes 4194304 | tf_op args[0]
  39.7 2.5 %all-to-all-done.1.got = f32[8,8,128]{2,1,0:T(8,128)S(1)} async-done(((f32[8,8,128]{2,1,0:T(8,128)}), f32[8,8,128]{2,1,0:T(8,128)S(1)}, u32[]{:S(2)}, u32[]{:S(2)}) %all-to-all-start.1) | async-done | bytes 32800 | tf_op jit(solution)/shard_map/all_to_all | solution.py:454
  42.3 0.8 middle.1
  43.1 5.8 %all-to-all-start.2 = ((f32[8,40,128]{2,1,0:T(8,128)}), f32[8,40,128]{2,1,0:T(8,128)S(1)}, u32[]{:S(2)}, u32[]{:S(2)}) async-start(f32[8,40,128]{2,1,0:T(8,128)} %middle.1), calls=%async_computation.2 | async-start | bytes 327680 | tf_op jit(solution)/shard_map/all_to_all | solution.py:394
  49.5 0.0 copy-done.6
  49.5 0.1 copy.11
  49.6 0.1 reshape.19.pairs
  49.7 0.1 pad_add_fusion.place
  49.7 6.7 %all-to-all-done.2.got = f32[8,40,128]{2,1,0:T(8,128)S(1)} async-done(((f32[8,40,128]{2,1,0:T(8,128)}), f32[8,40,128]{2,1,0:T(8,128)S(1)}, u32[]{:S(2)}, u32[]{:S(2)}) %all-to-all-start.2) | async-done | bytes 163872 | tf_op jit(solution)/shard_map/all_to_all | solution.py:394
  56.4 0.0 collective-permute-done.5.args_3_
  56.4 0.0 collective-permute-done.4.args_2_
  56.4 0.0 collective-permute-done.3.args_1_
  56.4 0.0 copy-done.2
  56.4 0.0 copy-done.3
  56.4 6.2 %cost_rows.1 = (f32[4,4]{1,0:T(4,128)}, f32[24,256,256]{2,1,0:T(8,128)S(1)}, f32[8,16,128]{2,1,0:T(8,128)S(1)}) custom-call(s32[48]{0:T(128)S(1)} %reshape.19.pairs, s32[1]{0:T(128)} %bitcast.10.count, s32[2]{0:T(128)S(1)} %pad_add_fusion.place, f32[8,40,128]{2,1,0:T(8,128)S(1)} %all-to-all-done.2.got, f32[1,2048]{1,0:T(1,128)S(1)} %get-tuple-element.32.src_sq, ...), custom_call_target="tpu_custom_call" | custom-call | tf_op jit(solution)/shard_map/cost_rows/pallas_call | solution.py:463
  62.6 8.9 %all_to_all.35.g_ref = f32[8,16,128]{2,1,0:T(8,128)S(1)} all-to-all(f32[8,16,128]{2,1,0:T(8,128)S(1)} %get-tuple-element.36), channel_id=1, replica_groups=mesh['z'=8,'x'=4,'y'=4,'c'=2] {'y','c'}, dimensions={0} | all-to-all | bytes 131072 | tf_op jit(solution)/shard_map/all_to_all | solution.py:515
  71.5 2.5 %columns.2 = (f32[32,16,128]{2,1,0:T(8,128)S(1)}, f32[16,128]{1,0:T(8,128)}) custom-call(s32[48]{0:T(128)S(1)} %reshape.19.pairs, s32[1]{0:T(128)} %bitcast.11.count, f32[24,256,256]{2,1,0:T(8,128)S(1)} %get-tuple-element.35.tiles, f32[8,16,128]{2,1,0:T(8,128)S(1)} %all_to_all.35.g_ref), custom_call_target="tpu_custom_call" | custom-call | tf_op jit(solution)/shard_map/columns/pallas_call | solution.py:494
  74.0 18.4 %all_to_all.36.g_ref = f32[32,16,128]{2,1,0:T(8,128)S(1)} all-to-all(f32[32,16,128]{2,1,0:T(8,128)S(1)} %get-tuple-element.37), channel_id=1, replica_groups={{0,8,16,24,32,40,48,56,64,72,80,88,96,104,112,120,128,136,144,152,160,1..., dimensions={0} | all-to-all | bytes 524288 | tf_op jit(solution)/shard_map/all_to_all | solution.py:394
  92.4 3.2 %rows.1 = f32[8,16,128]{2,1,0:T(8,128)S(1)} custom-call(s32[48]{0:T(128)S(1)} %reshape.19.pairs, s32[1]{0:T(128)} %bitcast.12.count, f32[24,256,256]{2,1,0:T(8,128)S(1)} %get-tuple-element.35.tiles, f32[32,16,128]{2,1,0:T(8,128)S(1)} %all_to_all.36.g_ref), custom_call_target="tpu_custom_call" | custom-call | tf_op jit(solution)/shard_map/rows/pallas_call | solution.py:505
  95.6 8.0 %all_to_all.37.g_ref = f32[8,16,128]{2,1,0:T(8,128)S(1)} all-to-all(f32[8,16,128]{2,1,0:T(8,128)S(1)} %rows.1), channel_id=1, replica_groups=mesh['z'=8,'x'=4,'y'=4,'c'=2] {'y','c'}, dimensions={0} | all-to-all | bytes 131072 | tf_op jit(solution)/shard_map/all_to_all | solution.py:517
  103.6 2.5 %columns.3 = (f32[32,16,128]{2,1,0:T(8,128)S(1)}, f32[16,128]{1,0:T(8,128)}) custom-call(s32[48]{0:T(128)S(1)} %reshape.19.pairs, s32[1]{0:T(128)} %bitcast.13.count, f32[24,256,256]{2,1,0:T(8,128)S(1)} %get-tuple-element.35.tiles, f32[8,16,128]{2,1,0:T(8,128)S(1)} %all_to_all.37.g_ref), custom_call_target="tpu_custom_call" | custom-call | tf_op jit(solution)/shard_map/columns/pallas_call | solution.py:494
  106.1 17.0 %all_to_all.38.g_ref = f32[32,16,128]{2,1,0:T(8,128)S(1)} all-to-all(f32[32,16,128]{2,1,0:T(8,128)S(1)} %get-tuple-element.39), channel_id=1, replica_groups={{0,8,16,24,32,40,48,56,64,72,80,88,96,104,112,120,128,136,144,152,160,1..., dimensions={0} | all-to-all | bytes 524288 | tf_op jit(solution)/shard_map/all_to_all | solution.py:394
  123.0 0.7 last.1
Async XLA Ops:
  3.0 28.7 %copy-start.5 = (f32[16,128]{1,0:T(8,128)S(1)}, f32[16,128]{1,0:T(8,128)}, u32[]{:S(2)}) copy-start(f32[16,128]{1,0:T(8,128)} %get-tuple-element.23.tgt_group.args_4_) | copy-start | bytes 24580
  3.0 23.1 %all-to-all-start = ((bf16[8,16,2048]{2,1,0:T(8,128)(2,1)}), bf16[8,16,2048]{2,1,0:T(8,128)(2,1)S(1)}, u32[]{:S(2)}, u32[]{:S(2)}) async-start(bf16[8,16,2048]{2,1,0:T(8,128)(2,1)} %get-tuple-element.22), calls=%async_computation | async-start | bytes 1048576 | tf_op jit(solution)/shard_map/all_to_all | solution.py:394
  11.5 1.6 %copy-start = (bf16[512,2048]{1,0:T(8,128)(2,1)S(1)}, bf16[512,2048]{1,0:T(8,128)(2,1)}, u32[]{:S(2)}) copy-start(bf16[512,2048]{1,0:T(8,128)(2,1)} %embed.3) | copy-start | bytes 6291460
  13.1 0.7 copy-start.1
  13.8 0.7 copy-start.4
  18.0 5.7 %collective-permute-start.2 = (f32[40,128]{1,0:T(8,128)S(1)}, f32[40,128]{1,0:T(8,128)S(1)}, u32[]{:S(2)}, u32[]{:S(2)}) collective-permute-start(f32[40,128]{1,0:T(8,128)S(1)} %get-tuple-element.25.args_0_), channel_id=1, source_target_pairs={{24,0},{0,8},{8,16},{16,24},{25,1},{1,9},{9,17},{17,25},{26,2},{2,... | collective-permute-start | bytes 61448 | tf_op jit(solution)/shard_map/ppermute | solution.py:431
  19.5 5.3 %collective-permute-start.1 = (f32[40,128]{1,0:T(8,128)S(1)}, f32[40,128]{1,0:T(8,128)S(1)}, u32[]{:S(2)}, u32[]{:S(2)}) collective-permute-start(f32[40,128]{1,0:T(8,128)S(1)} %get-tuple-element.25.args_0_), channel_id=1, source_target_pairs={{16,0},{24,8},{0,16},{8,24},{17,1},{25,9},{1,17},{9,25},{18,2},{26... | collective-permute-start | bytes 61448 | tf_op jit(solution)/shard_map/ppermute | solution.py:431
  22.3 3.8 %collective-permute-start = (f32[40,128]{1,0:T(8,128)S(1)}, f32[40,128]{1,0:T(8,128)S(1)}, u32[]{:S(2)}, u32[]{:S(2)}) collective-permute-start(f32[40,128]{1,0:T(8,128)S(1)} %get-tuple-element.25.args_0_), channel_id=1, source_target_pairs={{8,0},{16,8},{24,16},{0,24},{9,1},{17,9},{25,17},{1,25},{10,2},{18... | collective-permute-start | bytes 61448 | tf_op jit(solution)/shard_map/ppermute | solution.py:431
  26.1 30.3 %collective-permute-start.5 = (bf16[8,16,2048]{2,1,0:T(8,128)(2,1)S(1)}, bf16[8,16,2048]{2,1,0:T(8,128)(2,1)S(1)}, u32[]{:S(2)}, u32[]{:S(2)}) collective-permute-start(bf16[8,16,2048]{2,1,0:T(8,128)(2,1)S(1)} %all-to-all-done.args_0_), channel_id=1, source_target_pairs={{24,0},{0,8},{8,16},{16,24},{25,1},{1,9},{9,17},{17,25},{26,2},{2,... | collective-permute-start | bytes 1572872 | tf_op jit(solution)/shard_map/ppermute | solution.py:431
  27.5 28.9 %collective-permute-start.4 = (bf16[8,16,2048]{2,1,0:T(8,128)(2,1)S(1)}, bf16[8,16,2048]{2,1,0:T(8,128)(2,1)}, u32[]{:S(2)}, u32[]{:S(2)}) collective-permute-start(bf16[8,16,2048]{2,1,0:T(8,128)(2,1)S(1)} %all-to-all-done.args_0_), channel_id=1, source_target_pairs={{16,0},{24,8},{0,16},{8,24},{17,1},{25,9},{1,17},{9,25},{18,2},{26... | collective-permute-start | bytes 1572872 | tf_op jit(solution)/shard_map/ppermute | solution.py:431
  30.2 26.2 %collective-permute-start.3 = (bf16[8,16,2048]{2,1,0:T(8,128)(2,1)S(1)}, bf16[8,16,2048]{2,1,0:T(8,128)(2,1)}, u32[]{:S(2)}, u32[]{:S(2)}) collective-permute-start(bf16[8,16,2048]{2,1,0:T(8,128)(2,1)S(1)} %all-to-all-done.args_0_), channel_id=1, source_target_pairs={{8,0},{16,8},{24,16},{0,24},{9,1},{17,9},{25,17},{1,25},{10,2},{18... | collective-permute-start | bytes 1572872 | tf_op jit(solution)/shard_map/ppermute | solution.py:431
  32.4 9.9 %all-to-all-start.1 = ((f32[8,8,128]{2,1,0:T(8,128)}), f32[8,8,128]{2,1,0:T(8,128)S(1)}, u32[]{:S(2)}, u32[]{:S(2)}) async-start(f32[8,8,128]{2,1,0:T(8,128)} %get-tuple-element.29), calls=%async_computation.1 | async-start | bytes 65536 | tf_op jit(solution)/shard_map/all_to_all | solution.py:454
  36.8 12.6 %copy-start.6 = (s32[1,1,24,2]{2,3,1,0:T(2,128)S(1)}, s32[1,1,24,2]{2,3,1,0:T(2,128)}, u32[]{:S(2)}) copy-start(s32[1,1,24,2]{2,3,1,0:T(2,128)} %param.10) | copy-start | bytes 580
  36.8 19.6 %copy-start.2 = (s32[2048]{0:T(1024)S(1)}, s32[2048]{0:T(1024)}, u32[]{:S(2)}) copy-start(s32[2048]{0:T(1024)} %param.8) | copy-start | bytes 24580
  36.8 19.6 %copy-start.3 = (s32[2048]{0:T(1024)S(1)}, s32[2048]{0:T(1024)}, u32[]{:S(2)}) copy-start(s32[2048]{0:T(1024)} %param.9) | copy-start | bytes 24580
  43.1 13.3 %all-to-all-start.2 = ((f32[8,40,128]{2,1,0:T(8,128)}), f32[8,40,128]{2,1,0:T(8,128)S(1)}, u32[]{:S(2)}, u32[]{:S(2)}) async-start(f32[8,40,128]{2,1,0:T(8,128)} %middle.1), calls=%async_computation.2 | async-start | bytes 327680 | tf_op jit(solution)/shard_map/all_to_all | solution.py:394

commit v12 on v11

--- a/solution.py
+++ b/solution.py
@@ -26,6 +26,8 @@
 TO_POT = EPSILON / LOG2E
 
 SRC = ("z", "x")
+Z_ORDER = (0, 4, 2, 6, 1, 5, 3, 7)
+X_ORDER = (0, 2, 1, 3)
 TGT = ("y", "c")
 VMEM_LIMIT = 24 * 1024 * 1024
 FULL_VMEM = 64 * 1024 * 1024 - 32 * 1024
@@ -163,10 +165,11 @@
 
 
 def label_rows(width, core, got, src_sq, src_lab, label_ref, xa_ref):
-    peers = got.shape[0]
-    groups, total, targets = source_joined(
-        got, [k + core * (peers - 1 - 2 * k) for k in range(peers)]
-    )
+    order = []
+    for z in range(got.shape[0]):
+        first, second = (peer_order(("z",), c).index(z) for c in range(2))
+        order.append(first + core * (second - first))
+    groups, total, targets = source_joined(got, order)
     row_id = lax.broadcasted_iota(jnp.int32, (8, LANES), 0)
     lane_id = lax.broadcasted_iota(jnp.int32, (8, LANES), 1)
     each = LANES // width
@@ -258,7 +261,8 @@
     for far, piece in enumerate(pieces):
         at = lax.rem(place[0] + far, n_x)
         for k in range(piece.shape[0]):
-            z = k + place[1] * (piece.shape[0] - 1 - 2 * k)
+            first, second = (peer_order(("z",), core)[k] for core in range(2))
+            z = first + place[1] * (second - first)
             y[pl.ds(pl.multiple_of((z * n_x + at) * 16, 16), 16), :] = piece[k]
             v = piece[k].astype(jnp.float32)
             tgt_sq = tgt_sq + v * v
@@ -388,9 +392,15 @@
     return pltpu.CompilerParams(vmem_limit_bytes=limit)
 
 
-def both_ways(x, axes):
-    n = x.shape[0]
-    groups = [[2 * k for k in range(n)], [2 * k + 1 for k in reversed(range(n))]]
+def peer_order(axes, core):
+    rows = [(z + 2 * core) % 8 for z in Z_ORDER]
+    if axes == ("z",):
+        return rows
+    return [rows[k % 8] * 4 + (X_ORDER[(k // 8 + k) % 4] + 2 * core) % 4 for k in range(32)]
+
+
+def exchange(x, axes):
+    groups = [[2 * k + core for k in peer_order(axes, core)] for core in range(2)]
     return lax.all_to_all(x, axes + ("c",), 0, 0, axis_index_groups=groups)
 
 
@@ -423,7 +433,7 @@
         compiler_params=params(FULL_VMEM),
         name="first",
     )(target_embed, target_labels[None])
-    near = both_ways(near, ("z",))
+    near = exchange(near, ("z",))
 
     def around(x, axis):
         n = lax.axis_size(axis)
@@ -454,7 +464,7 @@
     tgt_near = lax.all_to_all(tgt_near, TGT, 0, 0)
     tgt_near, source_tall = lax.optimization_barrier((tgt_near, source_embed.T))
     stats = call(middle_kernel, f32(n_z, 40, LANES), tgt_near, src_group, name="middle")
-    stats = both_ways(stats, ("z",))
+    stats = exchange(stats, ("z",))
 
     tall = pltpu.VMEM((ROWS, LANES), jnp.float32)
     wide = pltpu.VMEM((BLK, 8, BLOCK), jnp.float32)
@@ -513,7 +523,7 @@
         )(pairs, count, tiles, got)
 
     sent, _ = columns(lax.all_to_all(sent, TGT, 0, 0))
-    sent = rows(both_ways(sent, SRC))
+    sent = rows(exchange(sent, SRC))
     sent, src_pot = columns(lax.all_to_all(sent, TGT, 0, 0))
     tgt_pot = pl.pallas_call(
         functools.partial(last_kernel, log_src),
@@ -522,7 +532,7 @@
         out_specs=vmem(),
         compiler_params=params(),
         name="last",
-    )(both_ways(sent, SRC))
+    )(exchange(sent, SRC))
     return (src_pot.reshape(-1), tgt_pot.reshape(-1), label_cost)
 
 

time: 125 us -> 125 us (level)
  blocking collectives: 52.3 us -> 54.7 us
  Pallas kernels: 22.3 us -> 20.7 us
    all_to_all x2, blocking collectives: 35.4 us -> 37.8 us  [exchange(): return lax.all_to_all(x, axes + ('c',), 0, 0, axis_index_groups=groups)]
where the time goes in v12:
time: 125 us; the launch traced here: 124 us
  blocking collectives  54.7 us (44%)
  starting transfers between devices  30.1 us (24%)
  Pallas kernels  20.7 us (17%)
  waiting for transfers between devices  11.1 us (9%)
  local copies, waits for them, and re-layouts  6.06 us (5%)
  between operations  1.37 us (1%)
    all_to_all x2, blocking collectives, exchange(): return lax.all_to_all(x, axes + ('c',), 0, 0, axis_index_groups=groups)  37.8 us
    all_to_all x2, starting transfers between devices, exchange(): return lax.all_to_all(x, axes + ('c',), 0, 0, axis_index_groups=groups)  14.8 us
    ppermute x6, starting transfers between devices, around(): lax.ppermute(x, axis, [((i + far) % n, i) for i in range(n)])  10.8 us
    all_to_all x1, blocking collectives, on_device(): sent, _ = columns(lax.all_to_all(sent, TGT, 0, 0))  8.63 us
    all_to_all x1, blocking collectives, on_device(): sent, src_pot = columns(lax.all_to_all(sent, TGT, 0, 0))  8.22 us
    all_to_all x2, waiting for transfers between devices, exchange(): return lax.all_to_all(x, axes + ('c',), 0, 0, axis_index_groups=groups)  6.18 us
    unnamed x16, local copies, waits for them, and re-layouts  5.97 us
    pallas_call x1, Pallas kernels, on_device(): pl.pallas_call(functools.partial(cost_kernel, n_x, part * n_x), out_shape...  5.43 us
  transfers between devices with their start and end apart: 9, of which 4 were waited for; matrix products, arithmetic and copies ran while one was open for 3% of the time, Pallas kernels for 4%

profile of v12, /device:TPU:32, one launch (start us, length us, event | category | flops | bytes accessed | tf_op | source)
XLA Modules:
  0.0 124.1 jit_solution(12583658735828835038)
XLA Ops:
  0.6 2.3 %first.1 = (bf16[8,16,2048]{2,1,0:T(8,128)(2,1)}, f32[16,128]{1,0:T(8,128)}) custom-call(bf16[16,2048]{1,0:T(8,128)(2,1)} %embed.2, s32[1,2048]{1,0:T(1,128)} %bitcast.17), custom_call_target="tpu_custom_call" | custom-call | tf_op jit(solution)/shard_map/first/pallas_call | solution.py:424
  3.0 0.0 copy-start.5
  3.0 8.6 %all-to-all-start = ((bf16[8,16,2048]{2,1,0:T(8,128)(2,1)}), bf16[8,16,2048]{2,1,0:T(8,128)(2,1)S(1)}, u32[]{:S(2)}, u32[]{:S(2)}) async-start(bf16[8,16,2048]{2,1,0:T(8,128)(2,1)} %get-tuple-element.22), calls=%async_computation | async-start | bytes 1048576 | tf_op jit(solution)/shard_map/all_to_all | solution.py:404
  11.6 0.0 copy-start
  11.6 1.6 %copy-done = bf16[512,2048]{1,0:T(8,128)(2,1)S(1)} copy-done((bf16[512,2048]{1,0:T(8,128)(2,1)S(1)}, bf16[512,2048]{1,0:T(8,128)(2,1)}, u32[]{:S(2)}) %copy-start) | copy-done | bytes 2097176
  13.1 0.0 copy-start.1
  13.1 0.7 copy-done.1
  13.8 0.0 copy-start.4
  13.8 0.7 copy-done.4
  14.5 3.5 %source_group.1 = (f32[40,128]{1,0:T(8,128)S(1)}, f32[1,2048]{1,0:T(1,128)S(1)}) custom-call(bf16[512,2048]{1,0:T(8,128)(2,1)S(1)} %copy-done, s32[1,2048]{1,0:T(1,128)S(1)} %bitcast.15, f32[16,128]{1,0:T(8,128)S(1)} %copy-done.4), custom_call_target="tpu_custom_call" | custom-call | tf_op jit(solution)/shard_map/source_group/pallas_call | solution.py:413
  18.0 1.6 %collective-permute-start.2 = (f32[40,128]{1,0:T(8,128)S(1)}, f32[40,128]{1,0:T(8,128)S(1)}, u32[]{:S(2)}, u32[]{:S(2)}) collective-permute-start(f32[40,128]{1,0:T(8,128)S(1)} %get-tuple-element.25.args_0_), channel_id=1, source_target_pairs={{24,0},{0,8},{8,16},{16,24},{25,1},{1,9},{9,17},{17,25},{26,2},{2,... | collective-permute-start | bytes 61448 | tf_op jit(solution)/shard_map/ppermute | solution.py:441
  19.5 2.7 %collective-permute-start.1 = (f32[40,128]{1,0:T(8,128)S(1)}, f32[40,128]{1,0:T(8,128)S(1)}, u32[]{:S(2)}, u32[]{:S(2)}) collective-permute-start(f32[40,128]{1,0:T(8,128)S(1)} %get-tuple-element.25.args_0_), channel_id=1, source_target_pairs={{16,0},{24,8},{0,16},{8,24},{17,1},{25,9},{1,17},{9,25},{18,2},{26... | collective-permute-start | bytes 61448 | tf_op jit(solution)/shard_map/ppermute | solution.py:441
  22.3 1.4 %collective-permute-start = (f32[40,128]{1,0:T(8,128)S(1)}, f32[40,128]{1,0:T(8,128)S(1)}, u32[]{:S(2)}, u32[]{:S(2)}) collective-permute-start(f32[40,128]{1,0:T(8,128)S(1)} %get-tuple-element.25.args_0_), channel_id=1, source_target_pairs={{8,0},{16,8},{24,16},{0,24},{9,1},{17,9},{25,17},{1,25},{10,2},{18... | collective-permute-start | bytes 61448 | tf_op jit(solution)/shard_map/ppermute | solution.py:441
  23.7 0.0 collective-permute-done.2.args_3_
  23.7 1.1 collective-permute-done.1.args_2_
  24.8 1.2 collective-permute-done.args_1_
  26.1 0.0 all-to-all-done.args_0_
  26.1 1.0 collective-permute-start.5
  27.0 3.2 %collective-permute-start.4 = (bf16[8,16,2048]{2,1,0:T(8,128)(2,1)S(1)}, bf16[8,16,2048]{2,1,0:T(8,128)(2,1)}, u32[]{:S(2)}, u32[]{:S(2)}) collective-permute-start(bf16[8,16,2048]{2,1,0:T(8,128)(2,1)S(1)} %all-to-all-done.args_0_), channel_id=1, source_target_pairs={{16,0},{24,8},{0,16},{8,24},{17,1},{25,9},{1,17},{9,25},{18,2},{26... | collective-permute-start | bytes 1572872 | tf_op jit(solution)/shard_map/ppermute | solution.py:441
  30.2 1.0 collective-permute-start.3
  31.2 0.0 copy-done.5
  31.2 0.7 near.1
  31.9 4.5 %all-to-all-start.1 = ((f32[8,8,128]{2,1,0:T(8,128)}), f32[8,8,128]{2,1,0:T(8,128)S(1)}, u32[]{:S(2)}, u32[]{:S(2)}) async-start(f32[8,8,128]{2,1,0:T(8,128)} %get-tuple-element.29), calls=%async_computation.1 | async-start | bytes 65536 | tf_op jit(solution)/shard_map/all_to_all | solution.py:464
  36.4 0.0 copy-start.6
  36.4 0.0 copy-start.2
  36.4 0.0 copy-start.3
  36.4 2.9 %copy.12 = bf16[512,2048]{0,1:T(8,128)(2,1)S(1)} copy(bf16[512,2048]{1,0:T(8,128)(2,1)} %embed.3) | data formatting | bytes 4194304 | tf_op args[0]
  39.3 2.5 %all-to-all-done.1.got = f32[8,8,128]{2,1,0:T(8,128)S(1)} async-done(((f32[8,8,128]{2,1,0:T(8,128)}), f32[8,8,128]{2,1,0:T(8,128)S(1)}, u32[]{:S(2)}, u32[]{:S(2)}) %all-to-all-start.1) | async-done | bytes 32800 | tf_op jit(solution)/shard_map/all_to_all | solution.py:464
  41.8 0.8 middle.1
  42.6 6.2 %all-to-all-start.2 = ((f32[8,40,128]{2,1,0:T(8,128)}), f32[8,40,128]{2,1,0:T(8,128)S(1)}, u32[]{:S(2)}, u32[]{:S(2)}) async-start(f32[8,40,128]{2,1,0:T(8,128)} %middle.1), calls=%async_computation.2 | async-start | bytes 327680 | tf_op jit(solution)/shard_map/all_to_all | solution.py:404
  49.5 0.0 copy-done.6
  49.5 0.1 copy.11
  49.6 0.1 reshape.19.pairs
  49.7 0.1 pad_add_fusion.place
  49.7 6.2 %all-to-all-done.2.got = f32[8,40,128]{2,1,0:T(8,128)S(1)} async-done(((f32[8,40,128]{2,1,0:T(8,128)}), f32[8,40,128]{2,1,0:T(8,128)S(1)}, u32[]{:S(2)}, u32[]{:S(2)}) %all-to-all-start.2) | async-done | bytes 163872 | tf_op jit(solution)/shard_map/all_to_all | solution.py:404
  55.9 0.0 collective-permute-done.5.args_3_
  55.9 0.0 collective-permute-done.4.args_2_
  55.9 0.0 collective-permute-done.3.args_1_
  55.9 0.0 copy-done.2
  55.9 0.0 copy-done.3
  55.9 5.4 %cost_rows.1 = (f32[4,4]{1,0:T(4,128)}, f32[24,256,256]{2,1,0:T(8,128)S(1)}, f32[8,16,128]{2,1,0:T(8,128)S(1)}) custom-call(s32[48]{0:T(128)S(1)} %reshape.19.pairs, s32[1]{0:T(128)} %bitcast.10.count, s32[2]{0:T(128)S(1)} %pad_add_fusion.place, f32[8,40,128]{2,1,0:T(8,128)S(1)} %all-to-all-done.2.got, f32[1,2048]{1,0:T(1,128)S(1)} %get-tuple-element.32.src_sq, ...), custom_call_target="tpu_custom_call" | custom-call | tf_op jit(solution)/shard_map/cost_rows/pallas_call | solution.py:473
  61.4 8.6 %all_to_all.35.g_ref = f32[8,16,128]{2,1,0:T(8,128)S(1)} all-to-all(f32[8,16,128]{2,1,0:T(8,128)S(1)} %get-tuple-element.36), channel_id=1, replica_groups=mesh['z'=8,'x'=4,'y'=4,'c'=2] {'y','c'}, dimensions={0} | all-to-all | bytes 131072 | tf_op jit(solution)/shard_map/all_to_all | solution.py:525
  70.0 2.2 %columns.2 = (f32[32,16,128]{2,1,0:T(8,128)S(1)}, f32[16,128]{1,0:T(8,128)}) custom-call(s32[48]{0:T(128)S(1)} %reshape.19.pairs, s32[1]{0:T(128)} %bitcast.11.count, f32[24,256,256]{2,1,0:T(8,128)S(1)} %get-tuple-element.35.tiles, f32[8,16,128]{2,1,0:T(8,128)S(1)} %all_to_all.35.g_ref), custom_call_target="tpu_custom_call" | custom-call | tf_op jit(solution)/shard_map/columns/pallas_call | solution.py:504
  72.3 19.5 %all_to_all.36.g_ref = f32[32,16,128]{2,1,0:T(8,128)S(1)} all-to-all(f32[32,16,128]{2,1,0:T(8,128)S(1)} %get-tuple-element.37), channel_id=1, replica_groups={{0,144,72,216,32,176,104,248,16,136,88,192,48,168,120,224,8,152,64,208,..., dimensions={0} | all-to-all | bytes 524288 | tf_op jit(solution)/shard_map/all_to_all | solution.py:404
  91.7 2.8 %rows.1 = f32[8,16,128]{2,1,0:T(8,128)S(1)} custom-call(s32[48]{0:T(128)S(1)} %reshape.19.pairs, s32[1]{0:T(128)} %bitcast.12.count, f32[24,256,256]{2,1,0:T(8,128)S(1)} %get-tuple-element.35.tiles, f32[32,16,128]{2,1,0:T(8,128)S(1)} %all_to_all.36.g_ref), custom_call_target="tpu_custom_call" | custom-call | tf_op jit(solution)/shard_map/rows/pallas_call | solution.py:515
  94.5 8.2 %all_to_all.37.g_ref = f32[8,16,128]{2,1,0:T(8,128)S(1)} all-to-all(f32[8,16,128]{2,1,0:T(8,128)S(1)} %rows.1), channel_id=1, replica_groups=mesh['z'=8,'x'=4,'y'=4,'c'=2] {'y','c'}, dimensions={0} | all-to-all | bytes 131072 | tf_op jit(solution)/shard_map/all_to_all | solution.py:527
  102.8 2.2 %columns.3 = (f32[32,16,128]{2,1,0:T(8,128)S(1)}, f32[16,128]{1,0:T(8,128)}) custom-call(s32[48]{0:T(128)S(1)} %reshape.19.pairs, s32[1]{0:T(128)} %bitcast.13.count, f32[24,256,256]{2,1,0:T(8,128)S(1)} %get-tuple-element.35.tiles, f32[8,16,128]{2,1,0:T(8,128)S(1)} %all_to_all.37.g_ref), custom_call_target="tpu_custom_call" | custom-call | tf_op jit(solution)/shard_map/columns/pallas_call | solution.py:504
  105.0 18.4 %all_to_all.38.g_ref = f32[32,16,128]{2,1,0:T(8,128)S(1)} all-to-all(f32[32,16,128]{2,1,0:T(8,128)S(1)} %get-tuple-element.39), channel_id=1, replica_groups={{0,144,72,216,32,176,104,248,16,136,88,192,48,168,120,224,8,152,64,208,..., dimensions={0} | all-to-all | bytes 524288 | tf_op jit(solution)/shard_map/all_to_all | solution.py:404
  123.4 0.7 last.1
Async XLA Ops:
  3.0 28.2 %copy-start.5 = (f32[16,128]{1,0:T(8,128)S(1)}, f32[16,128]{1,0:T(8,128)}, u32[]{:S(2)}) copy-start(f32[16,128]{1,0:T(8,128)} %get-tuple-element.23.tgt_group.args_4_) | copy-start | bytes 24580
  3.0 23.1 %all-to-all-start = ((bf16[8,16,2048]{2,1,0:T(8,128)(2,1)}), bf16[8,16,2048]{2,1,0:T(8,128)(2,1)S(1)}, u32[]{:S(2)}, u32[]{:S(2)}) async-start(bf16[8,16,2048]{2,1,0:T(8,128)(2,1)} %get-tuple-element.22), calls=%async_computation | async-start | bytes 1048576 | tf_op jit(solution)/shard_map/all_to_all | solution.py:404
  11.6 1.6 %copy-start = (bf16[512,2048]{1,0:T(8,128)(2,1)S(1)}, bf16[512,2048]{1,0:T(8,128)(2,1)}, u32[]{:S(2)}) copy-start(bf16[512,2048]{1,0:T(8,128)(2,1)} %embed.3) | copy-start | bytes 6291460
  13.1 0.7 copy-start.1
  13.8 0.7 copy-start.4
  18.0 5.7 %collective-permute-start.2 = (f32[40,128]{1,0:T(8,128)S(1)}, f32[40,128]{1,0:T(8,128)S(1)}, u32[]{:S(2)}, u32[]{:S(2)}) collective-permute-start(f32[40,128]{1,0:T(8,128)S(1)} %get-tuple-element.25.args_0_), channel_id=1, source_target_pairs={{24,0},{0,8},{8,16},{16,24},{25,1},{1,9},{9,17},{17,25},{26,2},{2,... | collective-permute-start | bytes 61448 | tf_op jit(solution)/shard_map/ppermute | solution.py:441
  19.5 5.3 %collective-permute-start.1 = (f32[40,128]{1,0:T(8,128)S(1)}, f32[40,128]{1,0:T(8,128)S(1)}, u32[]{:S(2)}, u32[]{:S(2)}) collective-permute-start(f32[40,128]{1,0:T(8,128)S(1)} %get-tuple-element.25.args_0_), channel_id=1, source_target_pairs={{16,0},{24,8},{0,16},{8,24},{17,1},{25,9},{1,17},{9,25},{18,2},{26... | collective-permute-start | bytes 61448 | tf_op jit(solution)/shard_map/ppermute | solution.py:441
  22.3 3.8 %collective-permute-start = (f32[40,128]{1,0:T(8,128)S(1)}, f32[40,128]{1,0:T(8,128)S(1)}, u32[]{:S(2)}, u32[]{:S(2)}) collective-permute-start(f32[40,128]{1,0:T(8,128)S(1)} %get-tuple-element.25.args_0_), channel_id=1, source_target_pairs={{8,0},{16,8},{24,16},{0,24},{9,1},{17,9},{25,17},{1,25},{10,2},{18... | collective-permute-start | bytes 61448 | tf_op jit(solution)/shard_map/ppermute | solution.py:441
  26.1 29.9 %collective-permute-start.5 = (bf16[8,16,2048]{2,1,0:T(8,128)(2,1)S(1)}, bf16[8,16,2048]{2,1,0:T(8,128)(2,1)S(1)}, u32[]{:S(2)}, u32[]{:S(2)}) collective-permute-start(bf16[8,16,2048]{2,1,0:T(8,128)(2,1)S(1)} %all-to-all-done.args_0_), channel_id=1, source_target_pairs={{24,0},{0,8},{8,16},{16,24},{25,1},{1,9},{9,17},{17,25},{26,2},{2,... | collective-permute-start | bytes 1572872 | tf_op jit(solution)/shard_map/ppermute | solution.py:441
  27.0 28.9 %collective-permute-start.4 = (bf16[8,16,2048]{2,1,0:T(8,128)(2,1)S(1)}, bf16[8,16,2048]{2,1,0:T(8,128)(2,1)}, u32[]{:S(2)}, u32[]{:S(2)}) collective-permute-start(bf16[8,16,2048]{2,1,0:T(8,128)(2,1)S(1)} %all-to-all-done.args_0_), channel_id=1, source_target_pairs={{16,0},{24,8},{0,16},{8,24},{17,1},{25,9},{1,17},{9,25},{18,2},{26... | collective-permute-start | bytes 1572872 | tf_op jit(solution)/shard_map/ppermute | solution.py:441
  30.2 25.8 %collective-permute-start.3 = (bf16[8,16,2048]{2,1,0:T(8,128)(2,1)S(1)}, bf16[8,16,2048]{2,1,0:T(8,128)(2,1)}, u32[]{:S(2)}, u32[]{:S(2)}) collective-permute-start(bf16[8,16,2048]{2,1,0:T(8,128)(2,1)S(1)} %all-to-all-done.args_0_), channel_id=1, source_target_pairs={{8,0},{16,8},{24,16},{0,24},{9,1},{17,9},{25,17},{1,25},{10,2},{18... | collective-permute-start | bytes 1572872 | tf_op jit(solution)/shard_map/ppermute | solution.py:441
  31.9 9.9 %all-to-all-start.1 = ((f32[8,8,128]{2,1,0:T(8,128)}), f32[8,8,128]{2,1,0:T(8,128)S(1)}, u32[]{:S(2)}, u32[]{:S(2)}) async-start(f32[8,8,128]{2,1,0:T(8,128)} %get-tuple-element.29), calls=%async_computation.1 | async-start | bytes 65536 | tf_op jit(solution)/shard_map/all_to_all | solution.py:464
  36.4 13.1 %copy-start.6 = (s32[1,1,24,2]{2,3,1,0:T(2,128)S(1)}, s32[1,1,24,2]{2,3,1,0:T(2,128)}, u32[]{:S(2)}) copy-start(s32[1,1,24,2]{2,3,1,0:T(2,128)} %param.10) | copy-start | bytes 580
  36.4 19.6 %copy-start.2 = (s32[2048]{0:T(1024)S(1)}, s32[2048]{0:T(1024)}, u32[]{:S(2)}) copy-start(s32[2048]{0:T(1024)} %param.8) | copy-start | bytes 24580
  36.4 19.6 %copy-start.3 = (s32[2048]{0:T(1024)S(1)}, s32[2048]{0:T(1024)}, u32[]{:S(2)}) copy-start(s32[2048]{0:T(1024)} %param.9) | copy-start | bytes 24580
  42.6 13.3 %all-to-all-start.2 = ((f32[8,40,128]{2,1,0:T(8,128)}), f32[8,40,128]{2,1,0:T(8,128)S(1)}, u32[]{:S(2)}, u32[]{:S(2)}) async-start(f32[8,40,128]{2,1,0:T(8,128)} %middle.1), calls=%async_computation.2 | async-start | bytes 327680 | tf_op jit(solution)/shard_map/all_to_all | solution.py:404

commit v13 on v11

--- a/solution.py
+++ b/solution.py
@@ -28,7 +28,6 @@
 SRC = ("z", "x")
 TGT = ("y", "c")
 VMEM_LIMIT = 24 * 1024 * 1024
-FULL_VMEM = 64 * 1024 * 1024 - 32 * 1024
 
 
 def log2(x):
@@ -384,8 +383,8 @@
     return jax.ShapeDtypeStruct(shape, jnp.float32)
 
 
-def params(limit=VMEM_LIMIT):
-    return pltpu.CompilerParams(vmem_limit_bytes=limit)
+def params():
+    return pltpu.CompilerParams(vmem_limit_bytes=VMEM_LIMIT)
 
 
 def both_ways(x, axes):
@@ -420,7 +419,7 @@
         in_specs=[vmem(), vmem()],
         out_specs=(pl.BlockSpec(memory_space=pl.ANY), vmem()),
         scratch_shapes=[pltpu.SemaphoreType.DMA((n_z,))],
-        compiler_params=params(FULL_VMEM),
+        compiler_params=params(),
         name="first",
     )(target_embed, target_labels[None])
     near = both_ways(near, ("z",))

time: 125 us -> 124 us (level)
  Pallas kernels: 22.3 us -> 20.8 us
    pallas_call x1, Pallas kernels: 2.32 us -> 0.88 us  [on_device(): pl.pallas_call(first_kernel, out_shape=(jax.ShapeDtypeStruct((n_z,) + tar...]
  transfers between devices with their start and end apart: 9 -> 9, of which waited for: 4 -> 5; matrix products, arithmetic and copies ran while one was open for 3% -> 3% of each run, Pallas kernels for 4% -> 4%
where the time goes in v13:
time: 124 us; the launch traced here: 123 us
  blocking collectives  51.9 us (42%)
  starting transfers between devices  29.8 us (24%)
  Pallas kernels  20.8 us (17%)
  waiting for transfers between devices  12.3 us (10%)
  local copies, waits for them, and re-layouts  6.89 us (6%)
  between operations  1.37 us (1%)
    all_to_all x2, blocking collectives, both_ways(): return lax.all_to_all(x, axes + ('c',), 0, 0, axis_index_groups=groups)  35.9 us
    all_to_all x2, starting transfers between devices, both_ways(): return lax.all_to_all(x, axes + ('c',), 0, 0, axis_index_groups=groups)  14 us
    ppermute x6, starting transfers between devices, around(): lax.ppermute(x, axis, [((i + far) % n, i) for i in range(n)])  11.4 us
    all_to_all x1, blocking collectives, on_device(): sent, _ = columns(lax.all_to_all(sent, TGT, 0, 0))  8.02 us
    all_to_all x1, blocking collectives, on_device(): sent, src_pot = columns(lax.all_to_all(sent, TGT, 0, 0))  7.99 us
    all_to_all x2, waiting for transfers between devices, both_ways(): return lax.all_to_all(x, axes + ('c',), 0, 0, axis_index_groups=groups)  7.44 us
    unnamed x16, local copies, waits for them, and re-layouts  6.79 us
    pallas_call x1, Pallas kernels, on_device(): pl.pallas_call(functools.partial(cost_kernel, n_x, part * n_x), out_shape...  6.2 us
  transfers between devices with their start and end apart: 9, of which 5 were waited for; matrix products, arithmetic and copies ran while one was open for 3% of the time, Pallas kernels for 4%

profile of v13, /device:TPU:32, one launch (start us, length us, event | category | flops | bytes accessed | tf_op | source)
XLA Modules:
  0.0 123.2 jit_solution(2361438235769018027)
XLA Ops:
  0.6 0.0 copy-start.1
  0.6 0.8 copy-done.1
  1.5 0.0 copy-start.4
  1.5 0.7 copy-done.4
  2.2 0.9 first.1
  3.1 8.6 %all-to-all-start = ((bf16[8,16,2048]{2,1,0:T(8,128)(2,1)}), bf16[8,16,2048]{2,1,0:T(8,128)(2,1)S(1)}, u32[]{:S(2)}, u32[]{:S(2)}) async-start(bf16[8,16,2048]{2,1,0:T(8,128)(2,1)} %get-tuple-element.22), calls=%async_computation | async-start | bytes 1048576 | tf_op jit(solution)/shard_map/all_to_all | solution.py:393
  11.6 0.0 copy-start
  11.6 1.6 %copy-done = bf16[512,2048]{1,0:T(8,128)(2,1)S(1)} copy-done((bf16[512,2048]{1,0:T(8,128)(2,1)S(1)}, bf16[512,2048]{1,0:T(8,128)(2,1)}, u32[]{:S(2)}) %copy-start) | copy-done | bytes 2097176
  13.2 0.0 copy-start.2
  13.2 0.7 copy-done.2
  13.9 3.5 %source_group.1 = (f32[40,128]{1,0:T(8,128)S(1)}, f32[1,2048]{1,0:T(1,128)S(1)}) custom-call(bf16[512,2048]{1,0:T(8,128)(2,1)S(1)} %copy-done, s32[1,2048]{1,0:T(1,128)S(1)} %bitcast.15, f32[16,128]{1,0:T(8,128)S(1)} %get-tuple-element.23.tgt_group.args_4_), custom_call_target="tpu_custom_call" | custom-call | tf_op jit(solution)/shard_map/source_group/pallas_call | solution.py:402
  17.4 1.6 %collective-permute-start.2 = (f32[40,128]{1,0:T(8,128)S(1)}, f32[40,128]{1,0:T(8,128)S(1)}, u32[]{:S(2)}, u32[]{:S(2)}) collective-permute-start(f32[40,128]{1,0:T(8,128)S(1)} %get-tuple-element.25.args_0_), channel_id=1, source_target_pairs={{24,0},{0,8},{8,16},{16,24},{25,1},{1,9},{9,17},{17,25},{26,2},{2,... | collective-permute-start | bytes 61448 | tf_op jit(solution)/shard_map/ppermute | solution.py:430
  18.9 2.7 %collective-permute-start.1 = (f32[40,128]{1,0:T(8,128)S(1)}, f32[40,128]{1,0:T(8,128)S(1)}, u32[]{:S(2)}, u32[]{:S(2)}) collective-permute-start(f32[40,128]{1,0:T(8,128)S(1)} %get-tuple-element.25.args_0_), channel_id=1, source_target_pairs={{16,0},{24,8},{0,16},{8,24},{17,1},{25,9},{1,17},{9,25},{18,2},{26... | collective-permute-start | bytes 61448 | tf_op jit(solution)/shard_map/ppermute | solution.py:430
  21.7 1.4 %collective-permute-start = (f32[40,128]{1,0:T(8,128)S(1)}, f32[40,128]{1,0:T(8,128)S(1)}, u32[]{:S(2)}, u32[]{:S(2)}) collective-permute-start(f32[40,128]{1,0:T(8,128)S(1)} %get-tuple-element.25.args_0_), channel_id=1, source_target_pairs={{8,0},{16,8},{24,16},{0,24},{9,1},{17,9},{25,17},{1,25},{10,2},{18... | collective-permute-start | bytes 61448 | tf_op jit(solution)/shard_map/ppermute | solution.py:430
  23.1 0.0 collective-permute-done.2.args_3_
  23.1 1.1 collective-permute-done.1.args_2_
  24.2 1.2 collective-permute-done.args_1_
  25.4 0.6 all-to-all-done.args_0_
  26.1 1.5 %collective-permute-start.5 = (bf16[8,16,2048]{2,1,0:T(8,128)(2,1)S(1)}, bf16[8,16,2048]{2,1,0:T(8,128)(2,1)S(1)}, u32[]{:S(2)}, u32[]{:S(2)}) collective-permute-start(bf16[8,16,2048]{2,1,0:T(8,128)(2,1)S(1)} %all-to-all-done.args_0_), channel_id=1, source_target_pairs={{24,0},{0,8},{8,16},{16,24},{25,1},{1,9},{9,17},{17,25},{26,2},{2,... | collective-permute-start | bytes 1572872 | tf_op jit(solution)/shard_map/ppermute | solution.py:430
  27.6 2.7 %collective-permute-start.4 = (bf16[8,16,2048]{2,1,0:T(8,128)(2,1)S(1)}, bf16[8,16,2048]{2,1,0:T(8,128)(2,1)}, u32[]{:S(2)}, u32[]{:S(2)}) collective-permute-start(bf16[8,16,2048]{2,1,0:T(8,128)(2,1)S(1)} %all-to-all-done.args_0_), channel_id=1, source_target_pairs={{16,0},{24,8},{0,16},{8,24},{17,1},{25,9},{1,17},{9,25},{18,2},{26... | collective-permute-start | bytes 1572872 | tf_op jit(solution)/shard_map/ppermute | solution.py:430
  30.3 1.4 %collective-permute-start.3 = (bf16[8,16,2048]{2,1,0:T(8,128)(2,1)S(1)}, bf16[8,16,2048]{2,1,0:T(8,128)(2,1)}, u32[]{:S(2)}, u32[]{:S(2)}) collective-permute-start(bf16[8,16,2048]{2,1,0:T(8,128)(2,1)S(1)} %all-to-all-done.args_0_), channel_id=1, source_target_pairs={{8,0},{16,8},{24,16},{0,24},{9,1},{17,9},{25,17},{1,25},{10,2},{18... | collective-permute-start | bytes 1572872 | tf_op jit(solution)/shard_map/ppermute | solution.py:430
  31.7 0.7 near.1
  32.4 4.5 %all-to-all-start.1 = ((f32[8,8,128]{2,1,0:T(8,128)}), f32[8,8,128]{2,1,0:T(8,128)S(1)}, u32[]{:S(2)}, u32[]{:S(2)}) async-start(f32[8,8,128]{2,1,0:T(8,128)} %get-tuple-element.29), calls=%async_computation.1 | async-start | bytes 65536 | tf_op jit(solution)/shard_map/all_to_all | solution.py:453
  36.9 0.0 copy-start.6
  36.9 0.0 copy-start.3
  36.9 0.0 copy-start.5
  36.9 2.9 %copy.12 = bf16[512,2048]{0,1:T(8,128)(2,1)S(1)} copy(bf16[512,2048]{1,0:T(8,128)(2,1)} %embed.3) | data formatting | bytes 4194304 | tf_op args[0]
  39.8 2.5 %all-to-all-done.1.got = f32[8,8,128]{2,1,0:T(8,128)S(1)} async-done(((f32[8,8,128]{2,1,0:T(8,128)}), f32[8,8,128]{2,1,0:T(8,128)S(1)}, u32[]{:S(2)}, u32[]{:S(2)}) %all-to-all-start.1) | async-done | bytes 32800 | tf_op jit(solution)/shard_map/all_to_all | solution.py:453
  42.4 0.8 middle.1
  43.1 5.4 %all-to-all-start.2 = ((f32[8,40,128]{2,1,0:T(8,128)}), f32[8,40,128]{2,1,0:T(8,128)S(1)}, u32[]{:S(2)}, u32[]{:S(2)}) async-start(f32[8,40,128]{2,1,0:T(8,128)} %middle.1), calls=%async_computation.2 | async-start | bytes 327680 | tf_op jit(solution)/shard_map/all_to_all | solution.py:393
  49.2 0.0 copy-done.6
  49.2 0.1 copy.11
  49.3 0.1 reshape.19.pairs
  49.4 0.1 pad_add_fusion.place
  49.5 6.8 %all-to-all-done.2.got = f32[8,40,128]{2,1,0:T(8,128)S(1)} async-done(((f32[8,40,128]{2,1,0:T(8,128)}), f32[8,40,128]{2,1,0:T(8,128)S(1)}, u32[]{:S(2)}, u32[]{:S(2)}) %all-to-all-start.2) | async-done | bytes 163872 | tf_op jit(solution)/shard_map/all_to_all | solution.py:393
  56.3 0.0 collective-permute-done.5.args_3_
  56.3 0.0 collective-permute-done.4.args_2_
  56.3 0.0 collective-permute-done.3.args_1_
  56.3 0.0 copy-done.3
  56.3 0.0 copy-done.5
  56.3 6.2 %cost_rows.1 = (f32[4,4]{1,0:T(4,128)}, f32[24,256,256]{2,1,0:T(8,128)S(1)}, f32[8,16,128]{2,1,0:T(8,128)S(1)}) custom-call(s32[48]{0:T(128)S(1)} %reshape.19.pairs, s32[1]{0:T(128)} %bitcast.10.count, s32[2]{0:T(128)S(1)} %pad_add_fusion.place, f32[8,40,128]{2,1,0:T(8,128)S(1)} %all-to-all-done.2.got, f32[1,2048]{1,0:T(1,128)S(1)} %get-tuple-element.32.src_sq, ...), custom_call_target="tpu_custom_call" | custom-call | tf_op jit(solution)/shard_map/cost_rows/pallas_call | solution.py:462
  62.5 8.0 %all_to_all.35.g_ref = f32[8,16,128]{2,1,0:T(8,128)S(1)} all-to-all(f32[8,16,128]{2,1,0:T(8,128)S(1)} %get-tuple-element.36), channel_id=1, replica_groups=mesh['z'=8,'x'=4,'y'=4,'c'=2] {'y','c'}, dimensions={0} | all-to-all | bytes 131072 | tf_op jit(solution)/shard_map/all_to_all | solution.py:514
  70.5 2.5 %columns.2 = (f32[32,16,128]{2,1,0:T(8,128)S(1)}, f32[16,128]{1,0:T(8,128)}) custom-call(s32[48]{0:T(128)S(1)} %reshape.19.pairs, s32[1]{0:T(128)} %bitcast.11.count, f32[24,256,256]{2,1,0:T(8,128)S(1)} %get-tuple-element.35.tiles, f32[8,16,128]{2,1,0:T(8,128)S(1)} %all_to_all.35.g_ref), custom_call_target="tpu_custom_call" | custom-call | tf_op jit(solution)/shard_map/columns/pallas_call | solution.py:493
  73.0 18.0 %all_to_all.36.g_ref = f32[32,16,128]{2,1,0:T(8,128)S(1)} all-to-all(f32[32,16,128]{2,1,0:T(8,128)S(1)} %get-tuple-element.37), channel_id=1, replica_groups={{0,8,16,24,32,40,48,56,64,72,80,88,96,104,112,120,128,136,144,152,160,1..., dimensions={0} | all-to-all | bytes 524288 | tf_op jit(solution)/shard_map/all_to_all | solution.py:393
  91.0 3.2 %rows.1 = f32[8,16,128]{2,1,0:T(8,128)S(1)} custom-call(s32[48]{0:T(128)S(1)} %reshape.19.pairs, s32[1]{0:T(128)} %bitcast.12.count, f32[24,256,256]{2,1,0:T(8,128)S(1)} %get-tuple-element.35.tiles, f32[32,16,128]{2,1,0:T(8,128)S(1)} %all_to_all.36.g_ref), custom_call_target="tpu_custom_call" | custom-call | tf_op jit(solution)/shard_map/rows/pallas_call | solution.py:504
  94.2 8.0 %all_to_all.37.g_ref = f32[8,16,128]{2,1,0:T(8,128)S(1)} all-to-all(f32[8,16,128]{2,1,0:T(8,128)S(1)} %rows.1), channel_id=1, replica_groups=mesh['z'=8,'x'=4,'y'=4,'c'=2] {'y','c'}, dimensions={0} | all-to-all | bytes 131072 | tf_op jit(solution)/shard_map/all_to_all | solution.py:516
  102.2 2.5 %columns.3 = (f32[32,16,128]{2,1,0:T(8,128)S(1)}, f32[16,128]{1,0:T(8,128)}) custom-call(s32[48]{0:T(128)S(1)} %reshape.19.pairs, s32[1]{0:T(128)} %bitcast.13.count, f32[24,256,256]{2,1,0:T(8,128)S(1)} %get-tuple-element.35.tiles, f32[8,16,128]{2,1,0:T(8,128)S(1)} %all_to_all.37.g_ref), custom_call_target="tpu_custom_call" | custom-call | tf_op jit(solution)/shard_map/columns/pallas_call | solution.py:493
  104.7 17.9 %all_to_all.38.g_ref = f32[32,16,128]{2,1,0:T(8,128)S(1)} all-to-all(f32[32,16,128]{2,1,0:T(8,128)S(1)} %get-tuple-element.39), channel_id=1, replica_groups={{0,8,16,24,32,40,48,56,64,72,80,88,96,104,112,120,128,136,144,152,160,1..., dimensions={0} | all-to-all | bytes 524288 | tf_op jit(solution)/shard_map/all_to_all | solution.py:393
  122.6 0.7 last.1
Async XLA Ops:
  0.6 0.8 copy-start.1
  1.5 0.7 copy-start.4
  3.1 23.0 %all-to-all-start = ((bf16[8,16,2048]{2,1,0:T(8,128)(2,1)}), bf16[8,16,2048]{2,1,0:T(8,128)(2,1)S(1)}, u32[]{:S(2)}, u32[]{:S(2)}) async-start(bf16[8,16,2048]{2,1,0:T(8,128)(2,1)} %get-tuple-element.22), calls=%async_computation | async-start | bytes 1048576 | tf_op jit(solution)/shard_map/all_to_all | solution.py:393
  11.6 1.6 %copy-start = (bf16[512,2048]{1,0:T(8,128)(2,1)S(1)}, bf16[512,2048]{1,0:T(8,128)(2,1)}, u32[]{:S(2)}) copy-start(bf16[512,2048]{1,0:T(8,128)(2,1)} %embed.3) | copy-start | bytes 6291460
  13.2 0.7 copy-start.2
  17.4 5.7 %collective-permute-start.2 = (f32[40,128]{1,0:T(8,128)S(1)}, f32[40,128]{1,0:T(8,128)S(1)}, u32[]{:S(2)}, u32[]{:S(2)}) collective-permute-start(f32[40,128]{1,0:T(8,128)S(1)} %get-tuple-element.25.args_0_), channel_id=1, source_target_pairs={{24,0},{0,8},{8,16},{16,24},{25,1},{1,9},{9,17},{17,25},{26,2},{2,... | collective-permute-start | bytes 61448 | tf_op jit(solution)/shard_map/ppermute | solution.py:430
  18.9 5.3 %collective-permute-start.1 = (f32[40,128]{1,0:T(8,128)S(1)}, f32[40,128]{1,0:T(8,128)S(1)}, u32[]{:S(2)}, u32[]{:S(2)}) collective-permute-start(f32[40,128]{1,0:T(8,128)S(1)} %get-tuple-element.25.args_0_), channel_id=1, source_target_pairs={{16,0},{24,8},{0,16},{8,24},{17,1},{25,9},{1,17},{9,25},{18,2},{26... | collective-permute-start | bytes 61448 | tf_op jit(solution)/shard_map/ppermute | solution.py:430
  21.7 3.8 %collective-permute-start = (f32[40,128]{1,0:T(8,128)S(1)}, f32[40,128]{1,0:T(8,128)S(1)}, u32[]{:S(2)}, u32[]{:S(2)}) collective-permute-start(f32[40,128]{1,0:T(8,128)S(1)} %get-tuple-element.25.args_0_), channel_id=1, source_target_pairs={{8,0},{16,8},{24,16},{0,24},{9,1},{17,9},{25,17},{1,25},{10,2},{18... | collective-permute-start | bytes 61448 | tf_op jit(solution)/shard_map/ppermute | solution.py:430
  26.1 30.2 %collective-permute-start.5 = (bf16[8,16,2048]{2,1,0:T(8,128)(2,1)S(1)}, bf16[8,16,2048]{2,1,0:T(8,128)(2,1)S(1)}, u32[]{:S(2)}, u32[]{:S(2)}) collective-permute-start(bf16[8,16,2048]{2,1,0:T(8,128)(2,1)S(1)} %all-to-all-done.args_0_), channel_id=1, source_target_pairs={{24,0},{0,8},{8,16},{16,24},{25,1},{1,9},{9,17},{17,25},{26,2},{2,... | collective-permute-start | bytes 1572872 | tf_op jit(solution)/shard_map/ppermute | solution.py:430
  27.6 28.7 %collective-permute-start.4 = (bf16[8,16,2048]{2,1,0:T(8,128)(2,1)S(1)}, bf16[8,16,2048]{2,1,0:T(8,128)(2,1)}, u32[]{:S(2)}, u32[]{:S(2)}) collective-permute-start(bf16[8,16,2048]{2,1,0:T(8,128)(2,1)S(1)} %all-to-all-done.args_0_), channel_id=1, source_target_pairs={{16,0},{24,8},{0,16},{8,24},{17,1},{25,9},{1,17},{9,25},{18,2},{26... | collective-permute-start | bytes 1572872 | tf_op jit(solution)/shard_map/ppermute | solution.py:430
  30.3 26.0 %collective-permute-start.3 = (bf16[8,16,2048]{2,1,0:T(8,128)(2,1)S(1)}, bf16[8,16,2048]{2,1,0:T(8,128)(2,1)}, u32[]{:S(2)}, u32[]{:S(2)}) collective-permute-start(bf16[8,16,2048]{2,1,0:T(8,128)(2,1)S(1)} %all-to-all-done.args_0_), channel_id=1, source_target_pairs={{8,0},{16,8},{24,16},{0,24},{9,1},{17,9},{25,17},{1,25},{10,2},{18... | collective-permute-start | bytes 1572872 | tf_op jit(solution)/shard_map/ppermute | solution.py:430
  32.4 9.9 %all-to-all-start.1 = ((f32[8,8,128]{2,1,0:T(8,128)}), f32[8,8,128]{2,1,0:T(8,128)S(1)}, u32[]{:S(2)}, u32[]{:S(2)}) async-start(f32[8,8,128]{2,1,0:T(8,128)} %get-tuple-element.29), calls=%async_computation.1 | async-start | bytes 65536 | tf_op jit(solution)/shard_map/all_to_all | solution.py:453
  36.9 12.3 %copy-start.6 = (s32[1,1,24,2]{2,3,1,0:T(2,128)S(1)}, s32[1,1,24,2]{2,3,1,0:T(2,128)}, u32[]{:S(2)}) copy-start(s32[1,1,24,2]{2,3,1,0:T(2,128)} %param.10) | copy-start | bytes 580
  36.9 19.4 %copy-start.3 = (s32[2048]{0:T(1024)S(1)}, s32[2048]{0:T(1024)}, u32[]{:S(2)}) copy-start(s32[2048]{0:T(1024)} %param.8) | copy-start | bytes 24580
  36.9 19.4 %copy-start.5 = (s32[2048]{0:T(1024)S(1)}, s32[2048]{0:T(1024)}, u32[]{:S(2)}) copy-start(s32[2048]{0:T(1024)} %param.9) | copy-start | bytes 24580
  43.1 13.1 %all-to-all-start.2 = ((f32[8,40,128]{2,1,0:T(8,128)}), f32[8,40,128]{2,1,0:T(8,128)S(1)}, u32[]{:S(2)}, u32[]{:S(2)}) async-start(f32[8,40,128]{2,1,0:T(8,128)} %middle.1), calls=%async_computation.2 | async-start | bytes 327680 | tf_op jit(solution)/shard_map/all_to_all | solution.py:393

commit v14 on v13

--- a/solution.py
+++ b/solution.py
@@ -512,7 +512,7 @@
         )(pairs, count, tiles, got)
 
     sent, _ = columns(lax.all_to_all(sent, TGT, 0, 0))
-    sent = rows(both_ways(sent, SRC))
+    sent = rows(lax.all_to_all(sent, SRC, 0, 0))
     sent, src_pot = columns(lax.all_to_all(sent, TGT, 0, 0))
     tgt_pot = pl.pallas_call(
         functools.partial(last_kernel, log_src),
@@ -521,7 +521,7 @@
         out_specs=vmem(),
         compiler_params=params(),
         name="last",
-    )(both_ways(sent, SRC))
+    )(lax.all_to_all(sent, SRC, 0, 0))
     return (src_pot.reshape(-1), tgt_pot.reshape(-1), label_cost)
 
 

time: 124 us -> 124 us (level); the launches traced: 123 us -> 125 us
  blocking collectives: 51.9 us -> 54.9 us
  Pallas kernels: 20.8 us -> 19.2 us
    all_to_all x1, blocking collectives: 8.02 us -> 10.3 us  [on_device(): sent, _ = columns(lax.all_to_all(sent, TGT, 0, 0))]
where the time goes in v14:
time: 124 us; the launch traced here: 125 us
  blocking collectives  54.9 us (44%)
  starting transfers between devices  29.8 us (24%)
  Pallas kernels  19.2 us (15%)
  waiting for transfers between devices  12.3 us (10%)
  local copies, waits for them, and re-layouts  6.89 us (6%)
  between operations  1.37 us (1%)
    all_to_all x1, blocking collectives, on_device(): sent = rows(lax.all_to_all(sent, SRC, 0, 0))  18.3 us
    all_to_all x1, blocking collectives, on_device(): lax.all_to_all(sent, SRC, 0, 0)  18.3 us
    all_to_all x2, starting transfers between devices, both_ways(): return lax.all_to_all(x, axes + ('c',), 0, 0, axis_index_groups=groups)  14 us
    ppermute x6, starting transfers between devices, around(): lax.ppermute(x, axis, [((i + far) % n, i) for i in range(n)])  11.4 us
    all_to_all x1, blocking collectives, on_device(): sent, _ = columns(lax.all_to_all(sent, TGT, 0, 0))  10.3 us
    all_to_all x1, blocking collectives, on_device(): sent, src_pot = columns(lax.all_to_all(sent, TGT, 0, 0))  7.99 us
    all_to_all x2, waiting for transfers between devices, both_ways(): return lax.all_to_all(x, axes + ('c',), 0, 0, axis_index_groups=groups)  7.44 us
    unnamed x16, local copies, waits for them, and re-layouts  6.79 us
  transfers between devices with their start and end apart: 9, of which 5 were waited for; matrix products, arithmetic and copies ran while one was open for 3% of the time, Pallas kernels for 4%

profile of v14, /device:TPU:32, one launch (start us, length us, event | category | flops | bytes accessed | tf_op | source)
XLA Modules:
  0.0 124.7 jit_solution(7393465447016649472)
XLA Ops:
  0.6 0.0 copy-start.1
  0.6 0.8 copy-done.1
  1.5 0.0 copy-start.4
  1.5 0.7 copy-done.4
  2.2 0.9 first.1
  3.1 8.6 %all-to-all-start = ((bf16[8,16,2048]{2,1,0:T(8,128)(2,1)}), bf16[8,16,2048]{2,1,0:T(8,128)(2,1)S(1)}, u32[]{:S(2)}, u32[]{:S(2)}) async-start(bf16[8,16,2048]{2,1,0:T(8,128)(2,1)} %get-tuple-element.22), calls=%async_computation | async-start | bytes 1048576 | tf_op jit(solution)/shard_map/all_to_all | solution.py:393
  11.6 0.0 copy-start
  11.6 1.6 %copy-done = bf16[512,2048]{1,0:T(8,128)(2,1)S(1)} copy-done((bf16[512,2048]{1,0:T(8,128)(2,1)S(1)}, bf16[512,2048]{1,0:T(8,128)(2,1)}, u32[]{:S(2)}) %copy-start) | copy-done | bytes 2097176
  13.2 0.0 copy-start.2
  13.2 0.7 copy-done.2
  13.9 3.5 %source_group.1 = (f32[40,128]{1,0:T(8,128)S(1)}, f32[1,2048]{1,0:T(1,128)S(1)}) custom-call(bf16[512,2048]{1,0:T(8,128)(2,1)S(1)} %copy-done, s32[1,2048]{1,0:T(1,128)S(1)} %bitcast.15, f32[16,128]{1,0:T(8,128)S(1)} %get-tuple-element.23.tgt_group.args_4_), custom_call_target="tpu_custom_call" | custom-call | tf_op jit(solution)/shard_map/source_group/pallas_call | solution.py:402
  17.4 1.6 %collective-permute-start.2 = (f32[40,128]{1,0:T(8,128)S(1)}, f32[40,128]{1,0:T(8,128)S(1)}, u32[]{:S(2)}, u32[]{:S(2)}) collective-permute-start(f32[40,128]{1,0:T(8,128)S(1)} %get-tuple-element.25.args_0_), channel_id=1, source_target_pairs={{24,0},{0,8},{8,16},{16,24},{25,1},{1,9},{9,17},{17,25},{26,2},{2,... | collective-permute-start | bytes 61448 | tf_op jit(solution)/shard_map/ppermute | solution.py:430
  18.9 2.7 %collective-permute-start.1 = (f32[40,128]{1,0:T(8,128)S(1)}, f32[40,128]{1,0:T(8,128)S(1)}, u32[]{:S(2)}, u32[]{:S(2)}) collective-permute-start(f32[40,128]{1,0:T(8,128)S(1)} %get-tuple-element.25.args_0_), channel_id=1, source_target_pairs={{16,0},{24,8},{0,16},{8,24},{17,1},{25,9},{1,17},{9,25},{18,2},{26... | collective-permute-start | bytes 61448 | tf_op jit(solution)/shard_map/ppermute | solution.py:430
  21.7 1.4 %collective-permute-start = (f32[40,128]{1,0:T(8,128)S(1)}, f32[40,128]{1,0:T(8,128)S(1)}, u32[]{:S(2)}, u32[]{:S(2)}) collective-permute-start(f32[40,128]{1,0:T(8,128)S(1)} %get-tuple-element.25.args_0_), channel_id=1, source_target_pairs={{8,0},{16,8},{24,16},{0,24},{9,1},{17,9},{25,17},{1,25},{10,2},{18... | collective-permute-start | bytes 61448 | tf_op jit(solution)/shard_map/ppermute | solution.py:430
  23.1 0.0 collective-permute-done.2.args_3_
  23.1 1.1 collective-permute-done.1.args_2_
  24.2 1.2 collective-permute-done.args_1_
  25.4 0.6 all-to-all-done.args_0_
  26.1 1.5 %collective-permute-start.5 = (bf16[8,16,2048]{2,1,0:T(8,128)(2,1)S(1)}, bf16[8,16,2048]{2,1,0:T(8,128)(2,1)S(1)}, u32[]{:S(2)}, u32[]{:S(2)}) collective-permute-start(bf16[8,16,2048]{2,1,0:T(8,128)(2,1)S(1)} %all-to-all-done.args_0_), channel_id=1, source_target_pairs={{24,0},{0,8},{8,16},{16,24},{25,1},{1,9},{9,17},{17,25},{26,2},{2,... | collective-permute-start | bytes 1572872 | tf_op jit(solution)/shard_map/ppermute | solution.py:430
  27.6 2.7 %collective-permute-start.4 = (bf16[8,16,2048]{2,1,0:T(8,128)(2,1)S(1)}, bf16[8,16,2048]{2,1,0:T(8,128)(2,1)}, u32[]{:S(2)}, u32[]{:S(2)}) collective-permute-start(bf16[8,16,2048]{2,1,0:T(8,128)(2,1)S(1)} %all-to-all-done.args_0_), channel_id=1, source_target_pairs={{16,0},{24,8},{0,16},{8,24},{17,1},{25,9},{1,17},{9,25},{18,2},{26... | collective-permute-start | bytes 1572872 | tf_op jit(solution)/shard_map/ppermute | solution.py:430
  30.3 1.4 %collective-permute-start.3 = (bf16[8,16,2048]{2,1,0:T(8,128)(2,1)S(1)}, bf16[8,16,2048]{2,1,0:T(8,128)(2,1)}, u32[]{:S(2)}, u32[]{:S(2)}) collective-permute-start(bf16[8,16,2048]{2,1,0:T(8,128)(2,1)S(1)} %all-to-all-done.args_0_), channel_id=1, source_target_pairs={{8,0},{16,8},{24,16},{0,24},{9,1},{17,9},{25,17},{1,25},{10,2},{18... | collective-permute-start | bytes 1572872 | tf_op jit(solution)/shard_map/ppermute | solution.py:430
  31.7 0.7 near.1
  32.4 4.5 %all-to-all-start.1 = ((f32[8,8,128]{2,1,0:T(8,128)}), f32[8,8,128]{2,1,0:T(8,128)S(1)}, u32[]{:S(2)}, u32[]{:S(2)}) async-start(f32[8,8,128]{2,1,0:T(8,128)} %get-tuple-element.29), calls=%async_computation.1 | async-start | bytes 65536 | tf_op jit(solution)/shard_map/all_to_all | solution.py:453
  36.9 0.0 copy-start.6
  36.9 0.0 copy-start.3
  36.9 0.0 copy-start.5
  36.9 2.9 %copy.12 = bf16[512,2048]{0,1:T(8,128)(2,1)S(1)} copy(bf16[512,2048]{1,0:T(8,128)(2,1)} %embed.3) | data formatting | bytes 4194304 | tf_op args[0]
  39.8 2.5 %all-to-all-done.1.got = f32[8,8,128]{2,1,0:T(8,128)S(1)} async-done(((f32[8,8,128]{2,1,0:T(8,128)}), f32[8,8,128]{2,1,0:T(8,128)S(1)}, u32[]{:S(2)}, u32[]{:S(2)}) %all-to-all-start.1) | async-done | bytes 32800 | tf_op jit(solution)/shard_map/all_to_all | solution.py:453
  42.4 0.8 middle.1
  43.1 5.4 %all-to-all-start.2 = ((f32[8,40,128]{2,1,0:T(8,128)}), f32[8,40,128]{2,1,0:T(8,128)S(1)}, u32[]{:S(2)}, u32[]{:S(2)}) async-start(f32[8,40,128]{2,1,0:T(8,128)} %middle.1), calls=%async_computation.2 | async-start | bytes 327680 | tf_op jit(solution)/shard_map/all_to_all | solution.py:393
  49.2 0.0 copy-done.6
  49.2 0.1 copy.11
  49.3 0.1 reshape.19.pairs
  49.4 0.1 pad_add_fusion.place
  49.5 6.8 %all-to-all-done.2.got = f32[8,40,128]{2,1,0:T(8,128)S(1)} async-done(((f32[8,40,128]{2,1,0:T(8,128)}), f32[8,40,128]{2,1,0:T(8,128)S(1)}, u32[]{:S(2)}, u32[]{:S(2)}) %all-to-all-start.2) | async-done | bytes 163872 | tf_op jit(solution)/shard_map/all_to_all | solution.py:393
  56.3 0.0 collective-permute-done.5.args_3_
  56.3 0.0 collective-permute-done.4.args_2_
  56.3 0.0 collective-permute-done.3.args_1_
  56.3 0.0 copy-done.3
  56.3 0.0 copy-done.5
  56.3 5.4 %cost_rows.1 = (f32[4,4]{1,0:T(4,128)}, f32[24,256,256]{2,1,0:T(8,128)S(1)}, f32[8,16,128]{2,1,0:T(8,128)S(1)}) custom-call(s32[48]{0:T(128)S(1)} %reshape.19.pairs, s32[1]{0:T(128)} %bitcast.10.count, s32[2]{0:T(128)S(1)} %pad_add_fusion.place, f32[8,40,128]{2,1,0:T(8,128)S(1)} %all-to-all-done.2.got, f32[1,2048]{1,0:T(1,128)S(1)} %get-tuple-element.32.src_sq, ...), custom_call_target="tpu_custom_call" | custom-call | tf_op jit(solution)/shard_map/cost_rows/pallas_call | solution.py:462
  61.7 10.3 %all_to_all.35.g_ref = f32[8,16,128]{2,1,0:T(8,128)S(1)} all-to-all(f32[8,16,128]{2,1,0:T(8,128)S(1)} %get-tuple-element.36), channel_id=1, replica_groups=mesh['z'=8,'x'=4,'y'=4,'c'=2] {'y','c'}, dimensions={0} | all-to-all | bytes 131072 | tf_op jit(solution)/shard_map/all_to_all | solution.py:514
  72.1 2.2 %columns.2 = (f32[32,16,128]{2,1,0:T(8,128)S(1)}, f32[16,128]{1,0:T(8,128)}) custom-call(s32[48]{0:T(128)S(1)} %reshape.19.pairs, s32[1]{0:T(128)} %bitcast.11.count, f32[24,256,256]{2,1,0:T(8,128)S(1)} %get-tuple-element.35.tiles, f32[8,16,128]{2,1,0:T(8,128)S(1)} %all_to_all.35.g_ref), custom_call_target="tpu_custom_call" | custom-call | tf_op jit(solution)/shard_map/columns/pallas_call | solution.py:493
  74.3 18.3 %all_to_all.36.g_ref = f32[32,16,128]{2,1,0:T(8,128)S(1)} all-to-all(f32[32,16,128]{2,1,0:T(8,128)S(1)} %get-tuple-element.37), channel_id=1, replica_groups=mesh['z'=8,'x'=4,'y'=4,'c'=2] {'z','x'}, dimensions={0} | all-to-all | bytes 524288 | tf_op jit(solution)/shard_map/all_to_all | solution.py:515
  92.7 2.8 %rows.1 = f32[8,16,128]{2,1,0:T(8,128)S(1)} custom-call(s32[48]{0:T(128)S(1)} %reshape.19.pairs, s32[1]{0:T(128)} %bitcast.12.count, f32[24,256,256]{2,1,0:T(8,128)S(1)} %get-tuple-element.35.tiles, f32[32,16,128]{2,1,0:T(8,128)S(1)} %all_to_all.36.g_ref), custom_call_target="tpu_custom_call" | custom-call | tf_op jit(solution)/shard_map/rows/pallas_call | solution.py:504
  95.5 8.0 %all_to_all.37.g_ref = f32[8,16,128]{2,1,0:T(8,128)S(1)} all-to-all(f32[8,16,128]{2,1,0:T(8,128)S(1)} %rows.1), channel_id=1, replica_groups=mesh['z'=8,'x'=4,'y'=4,'c'=2] {'y','c'}, dimensions={0} | all-to-all | bytes 131072 | tf_op jit(solution)/shard_map/all_to_all | solution.py:516
  103.5 2.2 %columns.3 = (f32[32,16,128]{2,1,0:T(8,128)S(1)}, f32[16,128]{1,0:T(8,128)}) custom-call(s32[48]{0:T(128)S(1)} %reshape.19.pairs, s32[1]{0:T(128)} %bitcast.13.count, f32[24,256,256]{2,1,0:T(8,128)S(1)} %get-tuple-element.35.tiles, f32[8,16,128]{2,1,0:T(8,128)S(1)} %all_to_all.37.g_ref), custom_call_target="tpu_custom_call" | custom-call | tf_op jit(solution)/shard_map/columns/pallas_call | solution.py:493
  105.7 18.3 %all_to_all.38.g_ref = f32[32,16,128]{2,1,0:T(8,128)S(1)} all-to-all(f32[32,16,128]{2,1,0:T(8,128)S(1)} %get-tuple-element.39), channel_id=1, replica_groups=mesh['z'=8,'x'=4,'y'=4,'c'=2] {'z','x'}, dimensions={0} | all-to-all | bytes 524288 | tf_op jit(solution)/shard_map/all_to_all | solution.py:524
  124.0 0.7 last.1
Async XLA Ops:
  0.6 0.8 copy-start.1
  1.5 0.7 copy-start.4
  3.1 23.0 %all-to-all-start = ((bf16[8,16,2048]{2,1,0:T(8,128)(2,1)}), bf16[8,16,2048]{2,1,0:T(8,128)(2,1)S(1)}, u32[]{:S(2)}, u32[]{:S(2)}) async-start(bf16[8,16,2048]{2,1,0:T(8,128)(2,1)} %get-tuple-element.22), calls=%async_computation | async-start | bytes 1048576 | tf_op jit(solution)/shard_map/all_to_all | solution.py:393
  11.6 1.6 %copy-start = (bf16[512,2048]{1,0:T(8,128)(2,1)S(1)}, bf16[512,2048]{1,0:T(8,128)(2,1)}, u32[]{:S(2)}) copy-start(bf16[512,2048]{1,0:T(8,128)(2,1)} %embed.3) | copy-start | bytes 6291460
  13.2 0.7 copy-start.2
  17.4 5.7 %collective-permute-start.2 = (f32[40,128]{1,0:T(8,128)S(1)}, f32[40,128]{1,0:T(8,128)S(1)}, u32[]{:S(2)}, u32[]{:S(2)}) collective-permute-start(f32[40,128]{1,0:T(8,128)S(1)} %get-tuple-element.25.args_0_), channel_id=1, source_target_pairs={{24,0},{0,8},{8,16},{16,24},{25,1},{1,9},{9,17},{17,25},{26,2},{2,... | collective-permute-start | bytes 61448 | tf_op jit(solution)/shard_map/ppermute | solution.py:430
  18.9 5.3 %collective-permute-start.1 = (f32[40,128]{1,0:T(8,128)S(1)}, f32[40,128]{1,0:T(8,128)S(1)}, u32[]{:S(2)}, u32[]{:S(2)}) collective-permute-start(f32[40,128]{1,0:T(8,128)S(1)} %get-tuple-element.25.args_0_), channel_id=1, source_target_pairs={{16,0},{24,8},{0,16},{8,24},{17,1},{25,9},{1,17},{9,25},{18,2},{26... | collective-permute-start | bytes 61448 | tf_op jit(solution)/shard_map/ppermute | solution.py:430
  21.7 3.8 %collective-permute-start = (f32[40,128]{1,0:T(8,128)S(1)}, f32[40,128]{1,0:T(8,128)S(1)}, u32[]{:S(2)}, u32[]{:S(2)}) collective-permute-start(f32[40,128]{1,0:T(8,128)S(1)} %get-tuple-element.25.args_0_), channel_id=1, source_target_pairs={{8,0},{16,8},{24,16},{0,24},{9,1},{17,9},{25,17},{1,25},{10,2},{18... | collective-permute-start | bytes 61448 | tf_op jit(solution)/shard_map/ppermute | solution.py:430
  26.1 30.2 %collective-permute-start.5 = (bf16[8,16,2048]{2,1,0:T(8,128)(2,1)S(1)}, bf16[8,16,2048]{2,1,0:T(8,128)(2,1)S(1)}, u32[]{:S(2)}, u32[]{:S(2)}) collective-permute-start(bf16[8,16,2048]{2,1,0:T(8,128)(2,1)S(1)} %all-to-all-done.args_0_), channel_id=1, source_target_pairs={{24,0},{0,8},{8,16},{16,24},{25,1},{1,9},{9,17},{17,25},{26,2},{2,... | collective-permute-start | bytes 1572872 | tf_op jit(solution)/shard_map/ppermute | solution.py:430
  27.6 28.7 %collective-permute-start.4 = (bf16[8,16,2048]{2,1,0:T(8,128)(2,1)S(1)}, bf16[8,16,2048]{2,1,0:T(8,128)(2,1)}, u32[]{:S(2)}, u32[]{:S(2)}) collective-permute-start(bf16[8,16,2048]{2,1,0:T(8,128)(2,1)S(1)} %all-to-all-done.args_0_), channel_id=1, source_target_pairs={{16,0},{24,8},{0,16},{8,24},{17,1},{25,9},{1,17},{9,25},{18,2},{26... | collective-permute-start | bytes 1572872 | tf_op jit(solution)/shard_map/ppermute | solution.py:430
  30.3 26.0 %collective-permute-start.3 = (bf16[8,16,2048]{2,1,0:T(8,128)(2,1)S(1)}, bf16[8,16,2048]{2,1,0:T(8,128)(2,1)}, u32[]{:S(2)}, u32[]{:S(2)}) collective-permute-start(bf16[8,16,2048]{2,1,0:T(8,128)(2,1)S(1)} %all-to-all-done.args_0_), channel_id=1, source_target_pairs={{8,0},{16,8},{24,16},{0,24},{9,1},{17,9},{25,17},{1,25},{10,2},{18... | collective-permute-start | bytes 1572872 | tf_op jit(solution)/shard_map/ppermute | solution.py:430
  32.4 9.9 %all-to-all-start.1 = ((f32[8,8,128]{2,1,0:T(8,128)}), f32[8,8,128]{2,1,0:T(8,128)S(1)}, u32[]{:S(2)}, u32[]{:S(2)}) async-start(f32[8,8,128]{2,1,0:T(8,128)} %get-tuple-element.29), calls=%async_computation.1 | async-start | bytes 65536 | tf_op jit(solution)/shard_map/all_to_all | solution.py:453
  36.9 12.3 %copy-start.6 = (s32[1,1,24,2]{2,3,1,0:T(2,128)S(1)}, s32[1,1,24,2]{2,3,1,0:T(2,128)}, u32[]{:S(2)}) copy-start(s32[1,1,24,2]{2,3,1,0:T(2,128)} %param.10) | copy-start | bytes 580
  36.9 19.4 %copy-start.3 = (s32[2048]{0:T(1024)S(1)}, s32[2048]{0:T(1024)}, u32[]{:S(2)}) copy-start(s32[2048]{0:T(1024)} %param.8) | copy-start | bytes 24580
  36.9 19.4 %copy-start.5 = (s32[2048]{0:T(1024)S(1)}, s32[2048]{0:T(1024)}, u32[]{:S(2)}) copy-start(s32[2048]{0:T(1024)} %param.9) | copy-start | bytes 24580
  43.1 13.1 %all-to-all-start.2 = ((f32[8,40,128]{2,1,0:T(8,128)}), f32[8,40,128]{2,1,0:T(8,128)S(1)}, u32[]{:S(2)}, u32[]{:S(2)}) async-start(f32[8,40,128]{2,1,0:T(8,128)} %middle.1), calls=%async_computation.2 | async-start | bytes 327680 | tf_op jit(solution)/shard_map/all_to_all | solution.py:393

commit v15 on v14

--- a/solution.py
+++ b/solution.py
@@ -16,7 +16,7 @@
 LANES = 128
 CHUNKS = ROWS // LANES
 MAXP = 24
-UNROLL = 4
+UNROLL = 8
 WIDTH = 512
 
 EPSILON = 0.05
@@ -285,7 +285,7 @@
         tiles[index] = tile
         top[rows, :] = jnp.maximum(top[rows, :], jnp.maximum(tile[:, :LANES], tile[:, LANES:]))
 
-    over_pairs(count, build, 4)
+    over_pairs(count, build, 8)
     widen_top(top)
 
     def add(index):

time: 124 us -> 123 us (level)
  blocking collectives: 54.9 us -> 51.9 us
  Pallas kernels: 19.2 us -> 20.5 us
    all_to_all x1, blocking collectives: 10.3 us -> 8.02 us  [on_device(): sent, _ = columns(lax.all_to_all(sent, TGT, 0, 0))]
where the time goes in v15:
time: 123 us
  blocking collectives  51.9 us (42%)
  starting transfers between devices  29.8 us (24%)
  Pallas kernels  20.5 us (17%)
  waiting for transfers between devices  12.3 us (10%)
  local copies, waits for them, and re-layouts  6.89 us (6%)
  between operations  1.37 us (1%)
    all_to_all x1, blocking collectives, on_device(): sent = rows(lax.all_to_all(sent, SRC, 0, 0))  18.4 us
    all_to_all x1, blocking collectives, on_device(): lax.all_to_all(sent, SRC, 0, 0)  17.5 us
    all_to_all x2, starting transfers between devices, both_ways(): return lax.all_to_all(x, axes + ('c',), 0, 0, axis_index_groups=groups)  14 us
    ppermute x6, starting transfers between devices, around(): lax.ppermute(x, axis, [((i + far) % n, i) for i in range(n)])  11.4 us
    all_to_all x1, blocking collectives, on_device(): sent, _ = columns(lax.all_to_all(sent, TGT, 0, 0))  8.02 us
    all_to_all x1, blocking collectives, on_device(): sent, src_pot = columns(lax.all_to_all(sent, TGT, 0, 0))  7.99 us
    all_to_all x2, waiting for transfers between devices, both_ways(): return lax.all_to_all(x, axes + ('c',), 0, 0, axis_index_groups=groups)  7.44 us
    unnamed x16, local copies, waits for them, and re-layouts  6.79 us
  transfers between devices with their start and end apart: 9, of which 5 were waited for; matrix products, arithmetic and copies ran while one was open for 3% of the time, Pallas kernels for 4%

profile of v15, /device:TPU:32, one launch (start us, length us, event | category | flops | bytes accessed | tf_op | source)
XLA Modules:
  0.0 122.9 jit_solution(1889457799027984045)
XLA Ops:
  0.6 0.0 copy-start.1
  0.6 0.8 copy-done.1
  1.5 0.0 copy-start.4
  1.5 0.7 copy-done.4
  2.2 0.9 first.1
  3.1 8.6 %all-to-all-start = ((bf16[8,16,2048]{2,1,0:T(8,128)(2,1)}), bf16[8,16,2048]{2,1,0:T(8,128)(2,1)S(1)}, u32[]{:S(2)}, u32[]{:S(2)}) async-start(bf16[8,16,2048]{2,1,0:T(8,128)(2,1)} %get-tuple-element.22), calls=%async_computation | async-start | bytes 1048576 | tf_op jit(solution)/shard_map/all_to_all | solution.py:393
  11.6 0.0 copy-start
  11.6 1.6 %copy-done = bf16[512,2048]{1,0:T(8,128)(2,1)S(1)} copy-done((bf16[512,2048]{1,0:T(8,128)(2,1)S(1)}, bf16[512,2048]{1,0:T(8,128)(2,1)}, u32[]{:S(2)}) %copy-start) | copy-done | bytes 2097176
  13.2 0.0 copy-start.2
  13.2 0.7 copy-done.2
  13.9 3.5 %source_group.1 = (f32[40,128]{1,0:T(8,128)S(1)}, f32[1,2048]{1,0:T(1,128)S(1)}) custom-call(bf16[512,2048]{1,0:T(8,128)(2,1)S(1)} %copy-done, s32[1,2048]{1,0:T(1,128)S(1)} %bitcast.15, f32[16,128]{1,0:T(8,128)S(1)} %get-tuple-element.23.tgt_group.args_4_), custom_call_target="tpu_custom_call" | custom-call | tf_op jit(solution)/shard_map/source_group/pallas_call | solution.py:402
  17.4 1.6 %collective-permute-start.2 = (f32[40,128]{1,0:T(8,128)S(1)}, f32[40,128]{1,0:T(8,128)S(1)}, u32[]{:S(2)}, u32[]{:S(2)}) collective-permute-start(f32[40,128]{1,0:T(8,128)S(1)} %get-tuple-element.25.args_0_), channel_id=1, source_target_pairs={{24,0},{0,8},{8,16},{16,24},{25,1},{1,9},{9,17},{17,25},{26,2},{2,... | collective-permute-start | bytes 61448 | tf_op jit(solution)/shard_map/ppermute | solution.py:430
  18.9 2.7 %collective-permute-start.1 = (f32[40,128]{1,0:T(8,128)S(1)}, f32[40,128]{1,0:T(8,128)S(1)}, u32[]{:S(2)}, u32[]{:S(2)}) collective-permute-start(f32[40,128]{1,0:T(8,128)S(1)} %get-tuple-element.25.args_0_), channel_id=1, source_target_pairs={{16,0},{24,8},{0,16},{8,24},{17,1},{25,9},{1,17},{9,25},{18,2},{26... | collective-permute-start | bytes 61448 | tf_op jit(solution)/shard_map/ppermute | solution.py:430
  21.7 1.4 %collective-permute-start = (f32[40,128]{1,0:T(8,128)S(1)}, f32[40,128]{1,0:T(8,128)S(1)}, u32[]{:S(2)}, u32[]{:S(2)}) collective-permute-start(f32[40,128]{1,0:T(8,128)S(1)} %get-tuple-element.25.args_0_), channel_id=1, source_target_pairs={{8,0},{16,8},{24,16},{0,24},{9,1},{17,9},{25,17},{1,25},{10,2},{18... | collective-permute-start | bytes 61448 | tf_op jit(solution)/shard_map/ppermute | solution.py:430
  23.1 0.0 collective-permute-done.2.args_3_
  23.1 1.1 collective-permute-done.1.args_2_
  24.2 1.2 collective-permute-done.args_1_
  25.4 0.6 all-to-all-done.args_0_
  26.1 1.5 %collective-permute-start.5 = (bf16[8,16,2048]{2,1,0:T(8,128)(2,1)S(1)}, bf16[8,16,2048]{2,1,0:T(8,128)(2,1)S(1)}, u32[]{:S(2)}, u32[]{:S(2)}) collective-permute-start(bf16[8,16,2048]{2,1,0:T(8,128)(2,1)S(1)} %all-to-all-done.args_0_), channel_id=1, source_target_pairs={{24,0},{0,8},{8,16},{16,24},{25,1},{1,9},{9,17},{17,25},{26,2},{2,... | collective-permute-start | bytes 1572872 | tf_op jit(solution)/shard_map/ppermute | solution.py:430
  27.6 2.7 %collective-permute-start.4 = (bf16[8,16,2048]{2,1,0:T(8,128)(2,1)S(1)}, bf16[8,16,2048]{2,1,0:T(8,128)(2,1)}, u32[]{:S(2)}, u32[]{:S(2)}) collective-permute-start(bf16[8,16,2048]{2,1,0:T(8,128)(2,1)S(1)} %all-to-all-done.args_0_), channel_id=1, source_target_pairs={{16,0},{24,8},{0,16},{8,24},{17,1},{25,9},{1,17},{9,25},{18,2},{26... | collective-permute-start | bytes 1572872 | tf_op jit(solution)/shard_map/ppermute | solution.py:430
  30.3 1.4 %collective-permute-start.3 = (bf16[8,16,2048]{2,1,0:T(8,128)(2,1)S(1)}, bf16[8,16,2048]{2,1,0:T(8,128)(2,1)}, u32[]{:S(2)}, u32[]{:S(2)}) collective-permute-start(bf16[8,16,2048]{2,1,0:T(8,128)(2,1)S(1)} %all-to-all-done.args_0_), channel_id=1, source_target_pairs={{8,0},{16,8},{24,16},{0,24},{9,1},{17,9},{25,17},{1,25},{10,2},{18... | collective-permute-start | bytes 1572872 | tf_op jit(solution)/shard_map/ppermute | solution.py:430
  31.7 0.7 near.1
  32.4 4.5 %all-to-all-start.1 = ((f32[8,8,128]{2,1,0:T(8,128)}), f32[8,8,128]{2,1,0:T(8,128)S(1)}, u32[]{:S(2)}, u32[]{:S(2)}) async-start(f32[8,8,128]{2,1,0:T(8,128)} %get-tuple-element.29), calls=%async_computation.1 | async-start | bytes 65536 | tf_op jit(solution)/shard_map/all_to_all | solution.py:453
  36.9 0.0 copy-start.6
  36.9 0.0 copy-start.3
  36.9 0.0 copy-start.5
  36.9 2.9 %copy.12 = bf16[512,2048]{0,1:T(8,128)(2,1)S(1)} copy(bf16[512,2048]{1,0:T(8,128)(2,1)} %embed.3) | data formatting | bytes 4194304 | tf_op args[0]
  39.8 2.5 %all-to-all-done.1.got = f32[8,8,128]{2,1,0:T(8,128)S(1)} async-done(((f32[8,8,128]{2,1,0:T(8,128)}), f32[8,8,128]{2,1,0:T(8,128)S(1)}, u32[]{:S(2)}, u32[]{:S(2)}) %all-to-all-start.1) | async-done | bytes 32800 | tf_op jit(solution)/shard_map/all_to_all | solution.py:453
  42.4 0.8 middle.1
  43.1 5.4 %all-to-all-start.2 = ((f32[8,40,128]{2,1,0:T(8,128)}), f32[8,40,128]{2,1,0:T(8,128)S(1)}, u32[]{:S(2)}, u32[]{:S(2)}) async-start(f32[8,40,128]{2,1,0:T(8,128)} %middle.1), calls=%async_computation.2 | async-start | bytes 327680 | tf_op jit(solution)/shard_map/all_to_all | solution.py:393
  49.2 0.0 copy-done.6
  49.2 0.1 copy.11
  49.3 0.1 reshape.19.pairs
  49.4 0.1 pad_add_fusion.place
  49.5 6.8 %all-to-all-done.2.got = f32[8,40,128]{2,1,0:T(8,128)S(1)} async-done(((f32[8,40,128]{2,1,0:T(8,128)}), f32[8,40,128]{2,1,0:T(8,128)S(1)}, u32[]{:S(2)}, u32[]{:S(2)}) %all-to-all-start.2) | async-done | bytes 163872 | tf_op jit(solution)/shard_map/all_to_all | solution.py:393
  56.3 0.0 collective-permute-done.5.args_3_
  56.3 0.0 collective-permute-done.4.args_2_
  56.3 0.0 collective-permute-done.3.args_1_
  56.3 0.0 copy-done.3
  56.3 0.0 copy-done.5
  56.3 5.8 %cost_rows.1 = (f32[4,4]{1,0:T(4,128)}, f32[24,256,256]{2,1,0:T(8,128)S(1)}, f32[8,16,128]{2,1,0:T(8,128)S(1)}) custom-call(s32[48]{0:T(128)S(1)} %reshape.19.pairs, s32[1]{0:T(128)} %bitcast.10.count, s32[2]{0:T(128)S(1)} %pad_add_fusion.place, f32[8,40,128]{2,1,0:T(8,128)S(1)} %all-to-all-done.2.got, f32[1,2048]{1,0:T(1,128)S(1)} %get-tuple-element.32.src_sq, ...), custom_call_target="tpu_custom_call" | custom-call | tf_op jit(solution)/shard_map/cost_rows/pallas_call | solution.py:462
  62.1 8.0 %all_to_all.35.g_ref = f32[8,16,128]{2,1,0:T(8,128)S(1)} all-to-all(f32[8,16,128]{2,1,0:T(8,128)S(1)} %get-tuple-element.36), channel_id=1, replica_groups=mesh['z'=8,'x'=4,'y'=4,'c'=2] {'y','c'}, dimensions={0} | all-to-all | bytes 131072 | tf_op jit(solution)/shard_map/all_to_all | solution.py:514
  70.1 2.5 %columns.2 = (f32[32,16,128]{2,1,0:T(8,128)S(1)}, f32[16,128]{1,0:T(8,128)}) custom-call(s32[48]{0:T(128)S(1)} %reshape.19.pairs, s32[1]{0:T(128)} %bitcast.11.count, f32[24,256,256]{2,1,0:T(8,128)S(1)} %get-tuple-element.35.tiles, f32[8,16,128]{2,1,0:T(8,128)S(1)} %all_to_all.35.g_ref), custom_call_target="tpu_custom_call" | custom-call | tf_op jit(solution)/shard_map/columns/pallas_call | solution.py:493
  72.6 18.4 %all_to_all.36.g_ref = f32[32,16,128]{2,1,0:T(8,128)S(1)} all-to-all(f32[32,16,128]{2,1,0:T(8,128)S(1)} %get-tuple-element.37), channel_id=1, replica_groups=mesh['z'=8,'x'=4,'y'=4,'c'=2] {'z','x'}, dimensions={0} | all-to-all | bytes 524288 | tf_op jit(solution)/shard_map/all_to_all | solution.py:515
  91.1 3.2 %rows.1 = f32[8,16,128]{2,1,0:T(8,128)S(1)} custom-call(s32[48]{0:T(128)S(1)} %reshape.19.pairs, s32[1]{0:T(128)} %bitcast.12.count, f32[24,256,256]{2,1,0:T(8,128)S(1)} %get-tuple-element.35.tiles, f32[32,16,128]{2,1,0:T(8,128)S(1)} %all_to_all.36.g_ref), custom_call_target="tpu_custom_call" | custom-call | tf_op jit(solution)/shard_map/rows/pallas_call | solution.py:504
  94.2 8.0 %all_to_all.37.g_ref = f32[8,16,128]{2,1,0:T(8,128)S(1)} all-to-all(f32[8,16,128]{2,1,0:T(8,128)S(1)} %rows.1), channel_id=1, replica_groups=mesh['z'=8,'x'=4,'y'=4,'c'=2] {'y','c'}, dimensions={0} | all-to-all | bytes 131072 | tf_op jit(solution)/shard_map/all_to_all | solution.py:516
  102.2 2.5 %columns.3 = (f32[32,16,128]{2,1,0:T(8,128)S(1)}, f32[16,128]{1,0:T(8,128)}) custom-call(s32[48]{0:T(128)S(1)} %reshape.19.pairs, s32[1]{0:T(128)} %bitcast.13.count, f32[24,256,256]{2,1,0:T(8,128)S(1)} %get-tuple-element.35.tiles, f32[8,16,128]{2,1,0:T(8,128)S(1)} %all_to_all.37.g_ref), custom_call_target="tpu_custom_call" | custom-call | tf_op jit(solution)/shard_map/columns/pallas_call | solution.py:493
  104.7 17.5 %all_to_all.38.g_ref = f32[32,16,128]{2,1,0:T(8,128)S(1)} all-to-all(f32[32,16,128]{2,1,0:T(8,128)S(1)} %get-tuple-element.39), channel_id=1, replica_groups=mesh['z'=8,'x'=4,'y'=4,'c'=2] {'z','x'}, dimensions={0} | all-to-all | bytes 524288 | tf_op jit(solution)/shard_map/all_to_all | solution.py:524
  122.2 0.7 last.1
Async XLA Ops:
  0.6 0.8 copy-start.1
  1.5 0.7 copy-start.4
  3.1 23.0 %all-to-all-start = ((bf16[8,16,2048]{2,1,0:T(8,128)(2,1)}), bf16[8,16,2048]{2,1,0:T(8,128)(2,1)S(1)}, u32[]{:S(2)}, u32[]{:S(2)}) async-start(bf16[8,16,2048]{2,1,0:T(8,128)(2,1)} %get-tuple-element.22), calls=%async_computation | async-start | bytes 1048576 | tf_op jit(solution)/shard_map/all_to_all | solution.py:393
  11.6 1.6 %copy-start = (bf16[512,2048]{1,0:T(8,128)(2,1)S(1)}, bf16[512,2048]{1,0:T(8,128)(2,1)}, u32[]{:S(2)}) copy-start(bf16[512,2048]{1,0:T(8,128)(2,1)} %embed.3) | copy-start | bytes 6291460
  13.2 0.7 copy-start.2
  17.4 5.7 %collective-permute-start.2 = (f32[40,128]{1,0:T(8,128)S(1)}, f32[40,128]{1,0:T(8,128)S(1)}, u32[]{:S(2)}, u32[]{:S(2)}) collective-permute-start(f32[40,128]{1,0:T(8,128)S(1)} %get-tuple-element.25.args_0_), channel_id=1, source_target_pairs={{24,0},{0,8},{8,16},{16,24},{25,1},{1,9},{9,17},{17,25},{26,2},{2,... | collective-permute-start | bytes 61448 | tf_op jit(solution)/shard_map/ppermute | solution.py:430
  18.9 5.3 %collective-permute-start.1 = (f32[40,128]{1,0:T(8,128)S(1)}, f32[40,128]{1,0:T(8,128)S(1)}, u32[]{:S(2)}, u32[]{:S(2)}) collective-permute-start(f32[40,128]{1,0:T(8,128)S(1)} %get-tuple-element.25.args_0_), channel_id=1, source_target_pairs={{16,0},{24,8},{0,16},{8,24},{17,1},{25,9},{1,17},{9,25},{18,2},{26... | collective-permute-start | bytes 61448 | tf_op jit(solution)/shard_map/ppermute | solution.py:430
  21.7 3.8 %collective-permute-start = (f32[40,128]{1,0:T(8,128)S(1)}, f32[40,128]{1,0:T(8,128)S(1)}, u32[]{:S(2)}, u32[]{:S(2)}) collective-permute-start(f32[40,128]{1,0:T(8,128)S(1)} %get-tuple-element.25.args_0_), channel_id=1, source_target_pairs={{8,0},{16,8},{24,16},{0,24},{9,1},{17,9},{25,17},{1,25},{10,2},{18... | collective-permute-start | bytes 61448 | tf_op jit(solution)/shard_map/ppermute | solution.py:430
  26.1 30.2 %collective-permute-start.5 = (bf16[8,16,2048]{2,1,0:T(8,128)(2,1)S(1)}, bf16[8,16,2048]{2,1,0:T(8,128)(2,1)S(1)}, u32[]{:S(2)}, u32[]{:S(2)}) collective-permute-start(bf16[8,16,2048]{2,1,0:T(8,128)(2,1)S(1)} %all-to-all-done.args_0_), channel_id=1, source_target_pairs={{24,0},{0,8},{8,16},{16,24},{25,1},{1,9},{9,17},{17,25},{26,2},{2,... | collective-permute-start | bytes 1572872 | tf_op jit(solution)/shard_map/ppermute | solution.py:430
  27.6 28.7 %collective-permute-start.4 = (bf16[8,16,2048]{2,1,0:T(8,128)(2,1)S(1)}, bf16[8,16,2048]{2,1,0:T(8,128)(2,1)}, u32[]{:S(2)}, u32[]{:S(2)}) collective-permute-start(bf16[8,16,2048]{2,1,0:T(8,128)(2,1)S(1)} %all-to-all-done.args_0_), channel_id=1, source_target_pairs={{16,0},{24,8},{0,16},{8,24},{17,1},{25,9},{1,17},{9,25},{18,2},{26... | collective-permute-start | bytes 1572872 | tf_op jit(solution)/shard_map/ppermute | solution.py:430
  30.3 26.0 %collective-permute-start.3 = (bf16[8,16,2048]{2,1,0:T(8,128)(2,1)S(1)}, bf16[8,16,2048]{2,1,0:T(8,128)(2,1)}, u32[]{:S(2)}, u32[]{:S(2)}) collective-permute-start(bf16[8,16,2048]{2,1,0:T(8,128)(2,1)S(1)} %all-to-all-done.args_0_), channel_id=1, source_target_pairs={{8,0},{16,8},{24,16},{0,24},{9,1},{17,9},{25,17},{1,25},{10,2},{18... | collective-permute-start | bytes 1572872 | tf_op jit(solution)/shard_map/ppermute | solution.py:430
  32.4 9.9 %all-to-all-start.1 = ((f32[8,8,128]{2,1,0:T(8,128)}), f32[8,8,128]{2,1,0:T(8,128)S(1)}, u32[]{:S(2)}, u32[]{:S(2)}) async-start(f32[8,8,128]{2,1,0:T(8,128)} %get-tuple-element.29), calls=%async_computation.1 | async-start | bytes 65536 | tf_op jit(solution)/shard_map/all_to_all | solution.py:453
  36.9 12.3 %copy-start.6 = (s32[1,1,24,2]{2,3,1,0:T(2,128)S(1)}, s32[1,1,24,2]{2,3,1,0:T(2,128)}, u32[]{:S(2)}) copy-start(s32[1,1,24,2]{2,3,1,0:T(2,128)} %param.10) | copy-start | bytes 580
  36.9 19.4 %copy-start.3 = (s32[2048]{0:T(1024)S(1)}, s32[2048]{0:T(1024)}, u32[]{:S(2)}) copy-start(s32[2048]{0:T(1024)} %param.8) | copy-start | bytes 24580
  36.9 19.4 %copy-start.5 = (s32[2048]{0:T(1024)S(1)}, s32[2048]{0:T(1024)}, u32[]{:S(2)}) copy-start(s32[2048]{0:T(1024)} %param.9) | copy-start | bytes 24580
  43.1 13.1 %all-to-all-start.2 = ((f32[8,40,128]{2,1,0:T(8,128)}), f32[8,40,128]{2,1,0:T(8,128)S(1)}, u32[]{:S(2)}, u32[]{:S(2)}) async-start(f32[8,40,128]{2,1,0:T(8,128)} %middle.1), calls=%async_computation.2 | async-start | bytes 327680 | tf_op jit(solution)/shard_map/all_to_all | solution.py:393

commit v16 on v15

--- a/solution.py
+++ b/solution.py
@@ -16,7 +16,7 @@
 LANES = 128
 CHUNKS = ROWS // LANES
 MAXP = 24
-UNROLL = 8
+UNROLL = 12
 WIDTH = 512
 
 EPSILON = 0.05
@@ -285,7 +285,7 @@
         tiles[index] = tile
         top[rows, :] = jnp.maximum(top[rows, :], jnp.maximum(tile[:, :LANES], tile[:, LANES:]))
 
-    over_pairs(count, build, 8)
+    over_pairs(count, build, 12)
     widen_top(top)
 
     def add(index):

time: 123 us -> 124 us (level)
  blocking collectives: 51.9 us -> 54.4 us
  Pallas kernels: 20.5 us -> 18.8 us
    all_to_all x1, blocking collectives: 8.02 us -> 9.78 us  [on_device(): sent, _ = columns(lax.all_to_all(sent, TGT, 0, 0))]
where the time goes in v16:
time: 124 us
  blocking collectives  54.4 us (44%)
  starting transfers between devices  29.8 us (24%)
  Pallas kernels  18.8 us (15%)
  waiting for transfers between devices  12.3 us (10%)
  local copies, waits for them, and re-layouts  6.89 us (6%)
  between operations  1.37 us (1%)
    all_to_all x1, blocking collectives, on_device(): sent = rows(lax.all_to_all(sent, SRC, 0, 0))  18.3 us
    all_to_all x1, blocking collectives, on_device(): lax.all_to_all(sent, SRC, 0, 0)  17.3 us
    all_to_all x2, starting transfers between devices, both_ways(): return lax.all_to_all(x, axes + ('c',), 0, 0, axis_index_groups=groups)  14 us
    ppermute x6, starting transfers between devices, around(): lax.ppermute(x, axis, [((i + far) % n, i) for i in range(n)])  11.4 us
    all_to_all x1, blocking collectives, on_device(): sent, _ = columns(lax.all_to_all(sent, TGT, 0, 0))  9.78 us
    all_to_all x1, blocking collectives, on_device(): sent, src_pot = columns(lax.all_to_all(sent, TGT, 0, 0))  8.92 us
    all_to_all x2, waiting for transfers between devices, both_ways(): return lax.all_to_all(x, axes + ('c',), 0, 0, axis_index_groups=groups)  7.44 us
    unnamed x16, local copies, waits for them, and re-layouts  6.79 us
  transfers between devices with their start and end apart: 9, of which 5 were waited for; matrix products, arithmetic and copies ran while one was open for 3% of the time, Pallas kernels for 4%

profile of v16, /device:TPU:32, one launch (start us, length us, event | category | flops | bytes accessed | tf_op | source)
XLA Modules:
  0.0 123.7 jit_solution(8348811770879599446)
XLA Ops:
  0.6 0.0 copy-start.1
  0.6 0.8 copy-done.1
  1.5 0.0 copy-start.4
  1.5 0.7 copy-done.4
  2.2 0.9 first.1
  3.1 8.6 %all-to-all-start = ((bf16[8,16,2048]{2,1,0:T(8,128)(2,1)}), bf16[8,16,2048]{2,1,0:T(8,128)(2,1)S(1)}, u32[]{:S(2)}, u32[]{:S(2)}) async-start(bf16[8,16,2048]{2,1,0:T(8,128)(2,1)} %get-tuple-element.22), calls=%async_computation | async-start | bytes 1048576 | tf_op jit(solution)/shard_map/all_to_all | solution.py:393
  11.6 0.0 copy-start
  11.6 1.6 %copy-done = bf16[512,2048]{1,0:T(8,128)(2,1)S(1)} copy-done((bf16[512,2048]{1,0:T(8,128)(2,1)S(1)}, bf16[512,2048]{1,0:T(8,128)(2,1)}, u32[]{:S(2)}) %copy-start) | copy-done | bytes 2097176
  13.2 0.0 copy-start.2
  13.2 0.7 copy-done.2
  13.9 3.5 %source_group.1 = (f32[40,128]{1,0:T(8,128)S(1)}, f32[1,2048]{1,0:T(1,128)S(1)}) custom-call(bf16[512,2048]{1,0:T(8,128)(2,1)S(1)} %copy-done, s32[1,2048]{1,0:T(1,128)S(1)} %bitcast.15, f32[16,128]{1,0:T(8,128)S(1)} %get-tuple-element.23.tgt_group.args_4_), custom_call_target="tpu_custom_call" | custom-call | tf_op jit(solution)/shard_map/source_group/pallas_call | solution.py:402
  17.4 1.6 %collective-permute-start.2 = (f32[40,128]{1,0:T(8,128)S(1)}, f32[40,128]{1,0:T(8,128)S(1)}, u32[]{:S(2)}, u32[]{:S(2)}) collective-permute-start(f32[40,128]{1,0:T(8,128)S(1)} %get-tuple-element.25.args_0_), channel_id=1, source_target_pairs={{24,0},{0,8},{8,16},{16,24},{25,1},{1,9},{9,17},{17,25},{26,2},{2,... | collective-permute-start | bytes 61448 | tf_op jit(solution)/shard_map/ppermute | solution.py:430
  18.9 2.7 %collective-permute-start.1 = (f32[40,128]{1,0:T(8,128)S(1)}, f32[40,128]{1,0:T(8,128)S(1)}, u32[]{:S(2)}, u32[]{:S(2)}) collective-permute-start(f32[40,128]{1,0:T(8,128)S(1)} %get-tuple-element.25.args_0_), channel_id=1, source_target_pairs={{16,0},{24,8},{0,16},{8,24},{17,1},{25,9},{1,17},{9,25},{18,2},{26... | collective-permute-start | bytes 61448 | tf_op jit(solution)/shard_map/ppermute | solution.py:430
  21.7 1.4 %collective-permute-start = (f32[40,128]{1,0:T(8,128)S(1)}, f32[40,128]{1,0:T(8,128)S(1)}, u32[]{:S(2)}, u32[]{:S(2)}) collective-permute-start(f32[40,128]{1,0:T(8,128)S(1)} %get-tuple-element.25.args_0_), channel_id=1, source_target_pairs={{8,0},{16,8},{24,16},{0,24},{9,1},{17,9},{25,17},{1,25},{10,2},{18... | collective-permute-start | bytes 61448 | tf_op jit(solution)/shard_map/ppermute | solution.py:430
  23.1 0.0 collective-permute-done.2.args_3_
  23.1 1.1 collective-permute-done.1.args_2_
  24.2 1.2 collective-permute-done.args_1_
  25.4 0.6 all-to-all-done.args_0_
  26.1 1.5 %collective-permute-start.5 = (bf16[8,16,2048]{2,1,0:T(8,128)(2,1)S(1)}, bf16[8,16,2048]{2,1,0:T(8,128)(2,1)S(1)}, u32[]{:S(2)}, u32[]{:S(2)}) collective-permute-start(bf16[8,16,2048]{2,1,0:T(8,128)(2,1)S(1)} %all-to-all-done.args_0_), channel_id=1, source_target_pairs={{24,0},{0,8},{8,16},{16,24},{25,1},{1,9},{9,17},{17,25},{26,2},{2,... | collective-permute-start | bytes 1572872 | tf_op jit(solution)/shard_map/ppermute | solution.py:430
  27.6 2.7 %collective-permute-start.4 = (bf16[8,16,2048]{2,1,0:T(8,128)(2,1)S(1)}, bf16[8,16,2048]{2,1,0:T(8,128)(2,1)}, u32[]{:S(2)}, u32[]{:S(2)}) collective-permute-start(bf16[8,16,2048]{2,1,0:T(8,128)(2,1)S(1)} %all-to-all-done.args_0_), channel_id=1, source_target_pairs={{16,0},{24,8},{0,16},{8,24},{17,1},{25,9},{1,17},{9,25},{18,2},{26... | collective-permute-start | bytes 1572872 | tf_op jit(solution)/shard_map/ppermute | solution.py:430
  30.3 1.4 %collective-permute-start.3 = (bf16[8,16,2048]{2,1,0:T(8,128)(2,1)S(1)}, bf16[8,16,2048]{2,1,0:T(8,128)(2,1)}, u32[]{:S(2)}, u32[]{:S(2)}) collective-permute-start(bf16[8,16,2048]{2,1,0:T(8,128)(2,1)S(1)} %all-to-all-done.args_0_), channel_id=1, source_target_pairs={{8,0},{16,8},{24,16},{0,24},{9,1},{17,9},{25,17},{1,25},{10,2},{18... | collective-permute-start | bytes 1572872 | tf_op jit(solution)/shard_map/ppermute | solution.py:430
  31.7 0.7 near.1
  32.4 4.5 %all-to-all-start.1 = ((f32[8,8,128]{2,1,0:T(8,128)}), f32[8,8,128]{2,1,0:T(8,128)S(1)}, u32[]{:S(2)}, u32[]{:S(2)}) async-start(f32[8,8,128]{2,1,0:T(8,128)} %get-tuple-element.29), calls=%async_computation.1 | async-start | bytes 65536 | tf_op jit(solution)/shard_map/all_to_all | solution.py:453
  36.9 0.0 copy-start.6
  36.9 0.0 copy-start.3
  36.9 0.0 copy-start.5
  36.9 2.9 %copy.12 = bf16[512,2048]{0,1:T(8,128)(2,1)S(1)} copy(bf16[512,2048]{1,0:T(8,128)(2,1)} %embed.3) | data formatting | bytes 4194304 | tf_op args[0]
  39.8 2.5 %all-to-all-done.1.got = f32[8,8,128]{2,1,0:T(8,128)S(1)} async-done(((f32[8,8,128]{2,1,0:T(8,128)}), f32[8,8,128]{2,1,0:T(8,128)S(1)}, u32[]{:S(2)}, u32[]{:S(2)}) %all-to-all-start.1) | async-done | bytes 32800 | tf_op jit(solution)/shard_map/all_to_all | solution.py:453
  42.4 0.8 middle.1
  43.1 5.4 %all-to-all-start.2 = ((f32[8,40,128]{2,1,0:T(8,128)}), f32[8,40,128]{2,1,0:T(8,128)S(1)}, u32[]{:S(2)}, u32[]{:S(2)}) async-start(f32[8,40,128]{2,1,0:T(8,128)} %middle.1), calls=%async_computation.2 | async-start | bytes 327680 | tf_op jit(solution)/shard_map/all_to_all | solution.py:393
  49.2 0.0 copy-done.6
  49.2 0.1 copy.11
  49.3 0.1 reshape.19.pairs
  49.4 0.1 pad_add_fusion.place
  49.5 6.8 %all-to-all-done.2.got = f32[8,40,128]{2,1,0:T(8,128)S(1)} async-done(((f32[8,40,128]{2,1,0:T(8,128)}), f32[8,40,128]{2,1,0:T(8,128)S(1)}, u32[]{:S(2)}, u32[]{:S(2)}) %all-to-all-start.2) | async-done | bytes 163872 | tf_op jit(solution)/shard_map/all_to_all | solution.py:393
  56.3 0.0 collective-permute-done.5.args_3_
  56.3 0.0 collective-permute-done.4.args_2_
  56.3 0.0 collective-permute-done.3.args_1_
  56.3 0.0 copy-done.3
  56.3 0.0 copy-done.5
  56.3 5.0 %cost_rows.1 = (f32[4,4]{1,0:T(4,128)}, f32[24,256,256]{2,1,0:T(8,128)S(1)}, f32[8,16,128]{2,1,0:T(8,128)S(1)}) custom-call(s32[48]{0:T(128)S(1)} %reshape.19.pairs, s32[1]{0:T(128)} %bitcast.10.count, s32[2]{0:T(128)S(1)} %pad_add_fusion.place, f32[8,40,128]{2,1,0:T(8,128)S(1)} %all-to-all-done.2.got, f32[1,2048]{1,0:T(1,128)S(1)} %get-tuple-element.32.src_sq, ...), custom_call_target="tpu_custom_call" | custom-call | tf_op jit(solution)/shard_map/cost_rows/pallas_call | solution.py:462
  61.4 9.8 %all_to_all.35.g_ref = f32[8,16,128]{2,1,0:T(8,128)S(1)} all-to-all(f32[8,16,128]{2,1,0:T(8,128)S(1)} %get-tuple-element.36), channel_id=1, replica_groups=mesh['z'=8,'x'=4,'y'=4,'c'=2] {'y','c'}, dimensions={0} | all-to-all | bytes 131072 | tf_op jit(solution)/shard_map/all_to_all | solution.py:514
  71.1 2.2 %columns.2 = (f32[32,16,128]{2,1,0:T(8,128)S(1)}, f32[16,128]{1,0:T(8,128)}) custom-call(s32[48]{0:T(128)S(1)} %reshape.19.pairs, s32[1]{0:T(128)} %bitcast.11.count, f32[24,256,256]{2,1,0:T(8,128)S(1)} %get-tuple-element.35.tiles, f32[8,16,128]{2,1,0:T(8,128)S(1)} %all_to_all.35.g_ref), custom_call_target="tpu_custom_call" | custom-call | tf_op jit(solution)/shard_map/columns/pallas_call | solution.py:493
  73.4 18.3 %all_to_all.36.g_ref = f32[32,16,128]{2,1,0:T(8,128)S(1)} all-to-all(f32[32,16,128]{2,1,0:T(8,128)S(1)} %get-tuple-element.37), channel_id=1, replica_groups=mesh['z'=8,'x'=4,'y'=4,'c'=2] {'z','x'}, dimensions={0} | all-to-all | bytes 524288 | tf_op jit(solution)/shard_map/all_to_all | solution.py:515
  91.7 2.8 %rows.1 = f32[8,16,128]{2,1,0:T(8,128)S(1)} custom-call(s32[48]{0:T(128)S(1)} %reshape.19.pairs, s32[1]{0:T(128)} %bitcast.12.count, f32[24,256,256]{2,1,0:T(8,128)S(1)} %get-tuple-element.35.tiles, f32[32,16,128]{2,1,0:T(8,128)S(1)} %all_to_all.36.g_ref), custom_call_target="tpu_custom_call" | custom-call | tf_op jit(solution)/shard_map/rows/pallas_call | solution.py:504
  94.5 8.9 %all_to_all.37.g_ref = f32[8,16,128]{2,1,0:T(8,128)S(1)} all-to-all(f32[8,16,128]{2,1,0:T(8,128)S(1)} %rows.1), channel_id=1, replica_groups=mesh['z'=8,'x'=4,'y'=4,'c'=2] {'y','c'}, dimensions={0} | all-to-all | bytes 131072 | tf_op jit(solution)/shard_map/all_to_all | solution.py:516
  103.5 2.2 %columns.3 = (f32[32,16,128]{2,1,0:T(8,128)S(1)}, f32[16,128]{1,0:T(8,128)}) custom-call(s32[48]{0:T(128)S(1)} %reshape.19.pairs, s32[1]{0:T(128)} %bitcast.13.count, f32[24,256,256]{2,1,0:T(8,128)S(1)} %get-tuple-element.35.tiles, f32[8,16,128]{2,1,0:T(8,128)S(1)} %all_to_all.37.g_ref), custom_call_target="tpu_custom_call" | custom-call | tf_op jit(solution)/shard_map/columns/pallas_call | solution.py:493
  105.7 17.3 %all_to_all.38.g_ref = f32[32,16,128]{2,1,0:T(8,128)S(1)} all-to-all(f32[32,16,128]{2,1,0:T(8,128)S(1)} %get-tuple-element.39), channel_id=1, replica_groups=mesh['z'=8,'x'=4,'y'=4,'c'=2] {'z','x'}, dimensions={0} | all-to-all | bytes 524288 | tf_op jit(solution)/shard_map/all_to_all | solution.py:524
  123.0 0.7 last.1
Async XLA Ops:
  0.6 0.8 copy-start.1
  1.5 0.7 copy-start.4
  3.1 23.0 %all-to-all-start = ((bf16[8,16,2048]{2,1,0:T(8,128)(2,1)}), bf16[8,16,2048]{2,1,0:T(8,128)(2,1)S(1)}, u32[]{:S(2)}, u32[]{:S(2)}) async-start(bf16[8,16,2048]{2,1,0:T(8,128)(2,1)} %get-tuple-element.22), calls=%async_computation | async-start | bytes 1048576 | tf_op jit(solution)/shard_map/all_to_all | solution.py:393
  11.6 1.6 %copy-start = (bf16[512,2048]{1,0:T(8,128)(2,1)S(1)}, bf16[512,2048]{1,0:T(8,128)(2,1)}, u32[]{:S(2)}) copy-start(bf16[512,2048]{1,0:T(8,128)(2,1)} %embed.3) | copy-start | bytes 6291460
  13.2 0.7 copy-start.2
  17.4 5.7 %collective-permute-start.2 = (f32[40,128]{1,0:T(8,128)S(1)}, f32[40,128]{1,0:T(8,128)S(1)}, u32[]{:S(2)}, u32[]{:S(2)}) collective-permute-start(f32[40,128]{1,0:T(8,128)S(1)} %get-tuple-element.25.args_0_), channel_id=1, source_target_pairs={{24,0},{0,8},{8,16},{16,24},{25,1},{1,9},{9,17},{17,25},{26,2},{2,... | collective-permute-start | bytes 61448 | tf_op jit(solution)/shard_map/ppermute | solution.py:430
  18.9 5.3 %collective-permute-start.1 = (f32[40,128]{1,0:T(8,128)S(1)}, f32[40,128]{1,0:T(8,128)S(1)}, u32[]{:S(2)}, u32[]{:S(2)}) collective-permute-start(f32[40,128]{1,0:T(8,128)S(1)} %get-tuple-element.25.args_0_), channel_id=1, source_target_pairs={{16,0},{24,8},{0,16},{8,24},{17,1},{25,9},{1,17},{9,25},{18,2},{26... | collective-permute-start | bytes 61448 | tf_op jit(solution)/shard_map/ppermute | solution.py:430
  21.7 3.8 %collective-permute-start = (f32[40,128]{1,0:T(8,128)S(1)}, f32[40,128]{1,0:T(8,128)S(1)}, u32[]{:S(2)}, u32[]{:S(2)}) collective-permute-start(f32[40,128]{1,0:T(8,128)S(1)} %get-tuple-element.25.args_0_), channel_id=1, source_target_pairs={{8,0},{16,8},{24,16},{0,24},{9,1},{17,9},{25,17},{1,25},{10,2},{18... | collective-permute-start | bytes 61448 | tf_op jit(solution)/shard_map/ppermute | solution.py:430
  26.1 30.2 %collective-permute-start.5 = (bf16[8,16,2048]{2,1,0:T(8,128)(2,1)S(1)}, bf16[8,16,2048]{2,1,0:T(8,128)(2,1)S(1)}, u32[]{:S(2)}, u32[]{:S(2)}) collective-permute-start(bf16[8,16,2048]{2,1,0:T(8,128)(2,1)S(1)} %all-to-all-done.args_0_), channel_id=1, source_target_pairs={{24,0},{0,8},{8,16},{16,24},{25,1},{1,9},{9,17},{17,25},{26,2},{2,... | collective-permute-start | bytes 1572872 | tf_op jit(solution)/shard_map/ppermute | solution.py:430
  27.6 28.7 %collective-permute-start.4 = (bf16[8,16,2048]{2,1,0:T(8,128)(2,1)S(1)}, bf16[8,16,2048]{2,1,0:T(8,128)(2,1)}, u32[]{:S(2)}, u32[]{:S(2)}) collective-permute-start(bf16[8,16,2048]{2,1,0:T(8,128)(2,1)S(1)} %all-to-all-done.args_0_), channel_id=1, source_target_pairs={{16,0},{24,8},{0,16},{8,24},{17,1},{25,9},{1,17},{9,25},{18,2},{26... | collective-permute-start | bytes 1572872 | tf_op jit(solution)/shard_map/ppermute | solution.py:430
  30.3 26.0 %collective-permute-start.3 = (bf16[8,16,2048]{2,1,0:T(8,128)(2,1)S(1)}, bf16[8,16,2048]{2,1,0:T(8,128)(2,1)}, u32[]{:S(2)}, u32[]{:S(2)}) collective-permute-start(bf16[8,16,2048]{2,1,0:T(8,128)(2,1)S(1)} %all-to-all-done.args_0_), channel_id=1, source_target_pairs={{8,0},{16,8},{24,16},{0,24},{9,1},{17,9},{25,17},{1,25},{10,2},{18... | collective-permute-start | bytes 1572872 | tf_op jit(solution)/shard_map/ppermute | solution.py:430
  32.4 9.9 %all-to-all-start.1 = ((f32[8,8,128]{2,1,0:T(8,128)}), f32[8,8,128]{2,1,0:T(8,128)S(1)}, u32[]{:S(2)}, u32[]{:S(2)}) async-start(f32[8,8,128]{2,1,0:T(8,128)} %get-tuple-element.29), calls=%async_computation.1 | async-start | bytes 65536 | tf_op jit(solution)/shard_map/all_to_all | solution.py:453
  36.9 12.3 %copy-start.6 = (s32[1,1,24,2]{2,3,1,0:T(2,128)S(1)}, s32[1,1,24,2]{2,3,1,0:T(2,128)}, u32[]{:S(2)}) copy-start(s32[1,1,24,2]{2,3,1,0:T(2,128)} %param.10) | copy-start | bytes 580
  36.9 19.4 %copy-start.3 = (s32[2048]{0:T(1024)S(1)}, s32[2048]{0:T(1024)}, u32[]{:S(2)}) copy-start(s32[2048]{0:T(1024)} %param.8) | copy-start | bytes 24580
  36.9 19.4 %copy-start.5 = (s32[2048]{0:T(1024)S(1)}, s32[2048]{0:T(1024)}, u32[]{:S(2)}) copy-start(s32[2048]{0:T(1024)} %param.9) | copy-start | bytes 24580
  43.1 13.1 %all-to-all-start.2 = ((f32[8,40,128]{2,1,0:T(8,128)}), f32[8,40,128]{2,1,0:T(8,128)S(1)}, u32[]{:S(2)}, u32[]{:S(2)}) async-start(f32[8,40,128]{2,1,0:T(8,128)} %middle.1), calls=%async_computation.2 | async-start | bytes 327680 | tf_op jit(solution)/shard_map/all_to_all | solution.py:393

commit v17 on v15

--- a/solution.py
+++ b/solution.py
@@ -161,11 +161,8 @@
         out_ref[k, 32:40, :] = last
 
 
-def label_rows(width, core, got, src_sq, src_lab, label_ref, xa_ref):
-    peers = got.shape[0]
-    groups, total, targets = source_joined(
-        got, [k + core * (peers - 1 - 2 * k) for k in range(peers)]
-    )
+def label_rows(width, got, src_sq, src_lab, label_ref, xa_ref):
+    groups, total, targets = source_joined(got)
     row_id = lax.broadcasted_iota(jnp.int32, (8, LANES), 0)
     lane_id = lax.broadcasted_iota(jnp.int32, (8, LANES), 1)
     each = LANES // width
@@ -248,7 +245,7 @@
 
 def cost_kernel(n_x, n_f, pairs, count, place, got, src_sq, src_lab, xt, *args):
     pieces, (tgt_lab, label_ref, tiles, out_ref, xa, y, ya, top, total) = args[:n_x], args[n_x:]
-    label_rows(n_f, place[1], got, src_sq, src_lab, label_ref, xa)
+    label_rows(n_f, got, src_sq, src_lab, label_ref, xa)
     row_id = lax.broadcasted_iota(jnp.int32, (16, 1), 0)
     part = row_id // CLASSES
     cls = row_id % CLASSES
@@ -453,7 +450,7 @@
     tgt_near = lax.all_to_all(tgt_near, TGT, 0, 0)
     tgt_near, source_tall = lax.optimization_barrier((tgt_near, source_embed.T))
     stats = call(middle_kernel, f32(n_z, 40, LANES), tgt_near, src_group, name="middle")
-    stats = both_ways(stats, ("z",))
+    stats = lax.all_to_all(stats, "z", 0, 0)
 
     tall = pltpu.VMEM((ROWS, LANES), jnp.float32)
     wide = pltpu.VMEM((BLK, 8, BLOCK), jnp.float32)

time: 123 us -> 124 us (level); the launches traced: 123 us -> 123 us
    all_to_all x0 -> x1, waiting for transfers between devices: none -> 7.33 us  [on_device(): stats = lax.all_to_all(stats, 'z', 0, 0)]
    all_to_all x2 -> x1, waiting for transfers between devices: 7.44 us -> 0.64 us  [both_ways(): return lax.all_to_all(x, axes + ('c',), 0, 0, axis_index_groups=groups)]
    all_to_all x0 -> x1, starting transfers between devices: none -> 5.42 us  [on_device(): stats = lax.all_to_all(stats, 'z', 0, 0)]
    all_to_all x2 -> x1, starting transfers between devices: 14 us -> 8.58 us  [both_ways(): return lax.all_to_all(x, axes + ('c',), 0, 0, axis_index_groups=groups)]
where the time goes in v17:
time: 124 us; the launch traced here: 123 us
  blocking collectives  51.1 us (41%)
  starting transfers between devices  29.8 us (24%)
  Pallas kernels  20.4 us (16%)
  waiting for transfers between devices  12.9 us (10%)
  local copies, waits for them, and re-layouts  6.89 us (6%)
  between operations  1.37 us (1%)
    all_to_all x1, blocking collectives, on_device(): sent = rows(lax.all_to_all(sent, SRC, 0, 0))  17.6 us
    all_to_all x1, blocking collectives, on_device(): lax.all_to_all(sent, SRC, 0, 0)  16.8 us
    ppermute x6, starting transfers between devices, around(): lax.ppermute(x, axis, [((i + far) % n, i) for i in range(n)])  11.4 us
    all_to_all x1, blocking collectives, on_device(): sent, _ = columns(lax.all_to_all(sent, TGT, 0, 0))  8.77 us
    all_to_all x1, starting transfers between devices, both_ways(): return lax.all_to_all(x, axes + ('c',), 0, 0, axis_index_groups=groups)  8.58 us
    all_to_all x1, blocking collectives, on_device(): sent, src_pot = columns(lax.all_to_all(sent, TGT, 0, 0))  7.99 us
    all_to_all x1, waiting for transfers between devices, on_device(): stats = lax.all_to_all(stats, 'z', 0, 0)  7.33 us
    unnamed x16, local copies, waits for them, and re-layouts  6.79 us
  transfers between devices with their start and end apart: 9, of which 5 were waited for; matrix products, arithmetic and copies ran while one was open for 3% of the time, Pallas kernels for 4%

profile of v17, /device:TPU:32, one launch (start us, length us, event | category | flops | bytes accessed | tf_op | source)
XLA Modules:
  0.0 122.6 jit_solution(8381739882919348457)
XLA Ops:
  0.6 0.0 copy-start.1
  0.6 0.8 copy-done.1
  1.5 0.0 copy-start.4
  1.5 0.7 copy-done.4
  2.2 0.9 first.1
  3.1 8.6 %all-to-all-start = ((bf16[8,16,2048]{2,1,0:T(8,128)(2,1)}), bf16[8,16,2048]{2,1,0:T(8,128)(2,1)S(1)}, u32[]{:S(2)}, u32[]{:S(2)}) async-start(bf16[8,16,2048]{2,1,0:T(8,128)(2,1)} %get-tuple-element.22), calls=%async_computation | async-start | bytes 1048576 | tf_op jit(solution)/shard_map/all_to_all | solution.py:390
  11.6 0.0 copy-start
  11.6 1.6 %copy-done = bf16[512,2048]{1,0:T(8,128)(2,1)S(1)} copy-done((bf16[512,2048]{1,0:T(8,128)(2,1)S(1)}, bf16[512,2048]{1,0:T(8,128)(2,1)}, u32[]{:S(2)}) %copy-start) | copy-done | bytes 2097176
  13.2 0.0 copy-start.2
  13.2 0.7 copy-done.2
  13.9 3.5 %source_group.1 = (f32[40,128]{1,0:T(8,128)S(1)}, f32[1,2048]{1,0:T(1,128)S(1)}) custom-call(bf16[512,2048]{1,0:T(8,128)(2,1)S(1)} %copy-done, s32[1,2048]{1,0:T(1,128)S(1)} %bitcast.15, f32[16,128]{1,0:T(8,128)S(1)} %get-tuple-element.23.tgt_group.args_4_), custom_call_target="tpu_custom_call" | custom-call | tf_op jit(solution)/shard_map/source_group/pallas_call | solution.py:399
  17.4 1.6 %collective-permute-start.2 = (f32[40,128]{1,0:T(8,128)S(1)}, f32[40,128]{1,0:T(8,128)S(1)}, u32[]{:S(2)}, u32[]{:S(2)}) collective-permute-start(f32[40,128]{1,0:T(8,128)S(1)} %get-tuple-element.25.args_0_), channel_id=1, source_target_pairs={{24,0},{0,8},{8,16},{16,24},{25,1},{1,9},{9,17},{17,25},{26,2},{2,... | collective-permute-start | bytes 61448 | tf_op jit(solution)/shard_map/ppermute | solution.py:427
  18.9 2.7 %collective-permute-start.1 = (f32[40,128]{1,0:T(8,128)S(1)}, f32[40,128]{1,0:T(8,128)S(1)}, u32[]{:S(2)}, u32[]{:S(2)}) collective-permute-start(f32[40,128]{1,0:T(8,128)S(1)} %get-tuple-element.25.args_0_), channel_id=1, source_target_pairs={{16,0},{24,8},{0,16},{8,24},{17,1},{25,9},{1,17},{9,25},{18,2},{26... | collective-permute-start | bytes 61448 | tf_op jit(solution)/shard_map/ppermute | solution.py:427
  21.7 1.4 %collective-permute-start = (f32[40,128]{1,0:T(8,128)S(1)}, f32[40,128]{1,0:T(8,128)S(1)}, u32[]{:S(2)}, u32[]{:S(2)}) collective-permute-start(f32[40,128]{1,0:T(8,128)S(1)} %get-tuple-element.25.args_0_), channel_id=1, source_target_pairs={{8,0},{16,8},{24,16},{0,24},{9,1},{17,9},{25,17},{1,25},{10,2},{18... | collective-permute-start | bytes 61448 | tf_op jit(solution)/shard_map/ppermute | solution.py:427
  23.1 0.0 collective-permute-done.2.args_3_
  23.1 1.1 collective-permute-done.1.args_2_
  24.2 1.2 %collective-permute-done.args_1_ = f32[40,128]{1,0:T(8,128)S(1)} collective-permute-done((f32[40,128]{1,0:T(8,128)S(1)}, f32[40,128]{1,0:T(8,128)S(1)}, u32[]{:S(2)}, u32[]{:S(2)}) %collective-permute-start) | collective-permute-done | bytes 20512 | tf_op jit(solution)/shard_map/ppermute | solution.py:427
  25.4 0.6 all-to-all-done.args_0_
  26.1 1.5 %collective-permute-start.5 = (bf16[8,16,2048]{2,1,0:T(8,128)(2,1)S(1)}, bf16[8,16,2048]{2,1,0:T(8,128)(2,1)S(1)}, u32[]{:S(2)}, u32[]{:S(2)}) collective-permute-start(bf16[8,16,2048]{2,1,0:T(8,128)(2,1)S(1)} %all-to-all-done.args_0_), channel_id=1, source_target_pairs={{24,0},{0,8},{8,16},{16,24},{25,1},{1,9},{9,17},{17,25},{26,2},{2,... | collective-permute-start | bytes 1572872 | tf_op jit(solution)/shard_map/ppermute | solution.py:427
  27.6 2.7 %collective-permute-start.4 = (bf16[8,16,2048]{2,1,0:T(8,128)(2,1)S(1)}, bf16[8,16,2048]{2,1,0:T(8,128)(2,1)}, u32[]{:S(2)}, u32[]{:S(2)}) collective-permute-start(bf16[8,16,2048]{2,1,0:T(8,128)(2,1)S(1)} %all-to-all-done.args_0_), channel_id=1, source_target_pairs={{16,0},{24,8},{0,16},{8,24},{17,1},{25,9},{1,17},{9,25},{18,2},{26... | collective-permute-start | bytes 1572872 | tf_op jit(solution)/shard_map/ppermute | solution.py:427
  30.3 1.4 %collective-permute-start.3 = (bf16[8,16,2048]{2,1,0:T(8,128)(2,1)S(1)}, bf16[8,16,2048]{2,1,0:T(8,128)(2,1)}, u32[]{:S(2)}, u32[]{:S(2)}) collective-permute-start(bf16[8,16,2048]{2,1,0:T(8,128)(2,1)S(1)} %all-to-all-done.args_0_), channel_id=1, source_target_pairs={{8,0},{16,8},{24,16},{0,24},{9,1},{17,9},{25,17},{1,25},{10,2},{18... | collective-permute-start | bytes 1572872 | tf_op jit(solution)/shard_map/ppermute | solution.py:427
  31.7 0.7 near.1
  32.4 4.5 %all-to-all-start.1 = ((f32[8,8,128]{2,1,0:T(8,128)}), f32[8,8,128]{2,1,0:T(8,128)S(1)}, u32[]{:S(2)}, u32[]{:S(2)}) async-start(f32[8,8,128]{2,1,0:T(8,128)} %get-tuple-element.29), calls=%async_computation.1 | async-start | bytes 65536 | tf_op jit(solution)/shard_map/all_to_all | solution.py:450
  36.9 0.0 copy-start.6
  36.9 0.0 copy-start.3
  36.9 0.0 copy-start.5
  36.9 2.9 %copy.12 = bf16[512,2048]{0,1:T(8,128)(2,1)S(1)} copy(bf16[512,2048]{1,0:T(8,128)(2,1)} %embed.3) | data formatting | bytes 4194304 | tf_op args[0]
  39.8 2.5 %all-to-all-done.1.got = f32[8,8,128]{2,1,0:T(8,128)S(1)} async-done(((f32[8,8,128]{2,1,0:T(8,128)}), f32[8,8,128]{2,1,0:T(8,128)S(1)}, u32[]{:S(2)}, u32[]{:S(2)}) %all-to-all-start.1) | async-done | bytes 32800 | tf_op jit(solution)/shard_map/all_to_all | solution.py:450
  42.4 0.8 middle.1
  43.1 5.4 %all-to-all-start.2 = ((f32[8,40,128]{2,1,0:T(8,128)}), f32[8,40,128]{2,1,0:T(8,128)S(1)}, u32[]{:S(2)}, u32[]{:S(2)}) async-start(f32[8,40,128]{2,1,0:T(8,128)} %middle.1), calls=%async_computation.2 | async-start | bytes 327680 | tf_op jit(solution)/shard_map/all_to_all | solution.py:453
  49.2 0.0 copy-done.6
  49.2 0.1 copy.11
  49.3 0.1 reshape.19.pairs
  49.4 0.1 pad_add_fusion.place
  49.5 7.3 %all-to-all-done.2.got = f32[8,40,128]{2,1,0:T(8,128)S(1)} async-done(((f32[8,40,128]{2,1,0:T(8,128)}), f32[8,40,128]{2,1,0:T(8,128)S(1)}, u32[]{:S(2)}, u32[]{:S(2)}) %all-to-all-start.2) | async-done | bytes 163872 | tf_op jit(solution)/shard_map/all_to_all | solution.py:453
  56.8 0.0 collective-permute-done.5.args_3_
  56.8 0.0 collective-permute-done.4.args_2_
  56.8 0.0 collective-permute-done.3.args_1_
  56.8 0.0 copy-done.3
  56.8 0.0 copy-done.5
  56.8 5.8 %cost_rows.1 = (f32[4,4]{1,0:T(4,128)}, f32[24,256,256]{2,1,0:T(8,128)S(1)}, f32[8,16,128]{2,1,0:T(8,128)S(1)}) custom-call(s32[48]{0:T(128)S(1)} %reshape.19.pairs, s32[1]{0:T(128)} %bitcast.10.count, s32[2]{0:T(128)S(1)} %pad_add_fusion.place, f32[8,40,128]{2,1,0:T(8,128)S(1)} %all-to-all-done.2.got, f32[1,2048]{1,0:T(1,128)S(1)} %get-tuple-element.32.src_sq, ...), custom_call_target="tpu_custom_call" | custom-call | tf_op jit(solution)/shard_map/cost_rows/pallas_call | solution.py:459
  62.6 8.8 %all_to_all.35.g_ref = f32[8,16,128]{2,1,0:T(8,128)S(1)} all-to-all(f32[8,16,128]{2,1,0:T(8,128)S(1)} %get-tuple-element.36), channel_id=1, replica_groups=mesh['z'=8,'x'=4,'y'=4,'c'=2] {'y','c'}, dimensions={0} | all-to-all | bytes 131072 | tf_op jit(solution)/shard_map/all_to_all | solution.py:511
  71.4 2.5 %columns.2 = (f32[32,16,128]{2,1,0:T(8,128)S(1)}, f32[16,128]{1,0:T(8,128)}) custom-call(s32[48]{0:T(128)S(1)} %reshape.19.pairs, s32[1]{0:T(128)} %bitcast.11.count, f32[24,256,256]{2,1,0:T(8,128)S(1)} %get-tuple-element.35.tiles, f32[8,16,128]{2,1,0:T(8,128)S(1)} %all_to_all.35.g_ref), custom_call_target="tpu_custom_call" | custom-call | tf_op jit(solution)/shard_map/columns/pallas_call | solution.py:490
  73.9 17.6 %all_to_all.36.g_ref = f32[32,16,128]{2,1,0:T(8,128)S(1)} all-to-all(f32[32,16,128]{2,1,0:T(8,128)S(1)} %get-tuple-element.37), channel_id=1, replica_groups=mesh['z'=8,'x'=4,'y'=4,'c'=2] {'z','x'}, dimensions={0} | all-to-all | bytes 524288 | tf_op jit(solution)/shard_map/all_to_all | solution.py:512
  91.5 3.2 %rows.1 = f32[8,16,128]{2,1,0:T(8,128)S(1)} custom-call(s32[48]{0:T(128)S(1)} %reshape.19.pairs, s32[1]{0:T(128)} %bitcast.12.count, f32[24,256,256]{2,1,0:T(8,128)S(1)} %get-tuple-element.35.tiles, f32[32,16,128]{2,1,0:T(8,128)S(1)} %all_to_all.36.g_ref), custom_call_target="tpu_custom_call" | custom-call | tf_op jit(solution)/shard_map/rows/pallas_call | solution.py:501
  94.7 8.0 %all_to_all.37.g_ref = f32[8,16,128]{2,1,0:T(8,128)S(1)} all-to-all(f32[8,16,128]{2,1,0:T(8,128)S(1)} %rows.1), channel_id=1, replica_groups=mesh['z'=8,'x'=4,'y'=4,'c'=2] {'y','c'}, dimensions={0} | all-to-all | bytes 131072 | tf_op jit(solution)/shard_map/all_to_all | solution.py:513
  102.7 2.5 %columns.3 = (f32[32,16,128]{2,1,0:T(8,128)S(1)}, f32[16,128]{1,0:T(8,128)}) custom-call(s32[48]{0:T(128)S(1)} %reshape.19.pairs, s32[1]{0:T(128)} %bitcast.13.count, f32[24,256,256]{2,1,0:T(8,128)S(1)} %get-tuple-element.35.tiles, f32[8,16,128]{2,1,0:T(8,128)S(1)} %all_to_all.37.g_ref), custom_call_target="tpu_custom_call" | custom-call | tf_op jit(solution)/shard_map/columns/pallas_call | solution.py:490
  105.2 16.8 %all_to_all.38.g_ref = f32[32,16,128]{2,1,0:T(8,128)S(1)} all-to-all(f32[32,16,128]{2,1,0:T(8,128)S(1)} %get-tuple-element.39), channel_id=1, replica_groups=mesh['z'=8,'x'=4,'y'=4,'c'=2] {'z','x'}, dimensions={0} | all-to-all | bytes 524288 | tf_op jit(solution)/shard_map/all_to_all | solution.py:521
  121.9 0.7 last.1
Async XLA Ops:
  0.6 0.8 copy-start.1
  1.5 0.7 copy-start.4
  3.1 23.0 %all-to-all-start = ((bf16[8,16,2048]{2,1,0:T(8,128)(2,1)}), bf16[8,16,2048]{2,1,0:T(8,128)(2,1)S(1)}, u32[]{:S(2)}, u32[]{:S(2)}) async-start(bf16[8,16,2048]{2,1,0:T(8,128)(2,1)} %get-tuple-element.22), calls=%async_computation | async-start | bytes 1048576 | tf_op jit(solution)/shard_map/all_to_all | solution.py:390
  11.6 1.6 %copy-start = (bf16[512,2048]{1,0:T(8,128)(2,1)S(1)}, bf16[512,2048]{1,0:T(8,128)(2,1)}, u32[]{:S(2)}) copy-start(bf16[512,2048]{1,0:T(8,128)(2,1)} %embed.3) | copy-start | bytes 6291460
  13.2 0.7 copy-start.2
  17.4 5.7 %collective-permute-start.2 = (f32[40,128]{1,0:T(8,128)S(1)}, f32[40,128]{1,0:T(8,128)S(1)}, u32[]{:S(2)}, u32[]{:S(2)}) collective-permute-start(f32[40,128]{1,0:T(8,128)S(1)} %get-tuple-element.25.args_0_), channel_id=1, source_target_pairs={{24,0},{0,8},{8,16},{16,24},{25,1},{1,9},{9,17},{17,25},{26,2},{2,... | collective-permute-start | bytes 61448 | tf_op jit(solution)/shard_map/ppermute | solution.py:427
  18.9 5.3 %collective-permute-start.1 = (f32[40,128]{1,0:T(8,128)S(1)}, f32[40,128]{1,0:T(8,128)S(1)}, u32[]{:S(2)}, u32[]{:S(2)}) collective-permute-start(f32[40,128]{1,0:T(8,128)S(1)} %get-tuple-element.25.args_0_), channel_id=1, source_target_pairs={{16,0},{24,8},{0,16},{8,24},{17,1},{25,9},{1,17},{9,25},{18,2},{26... | collective-permute-start | bytes 61448 | tf_op jit(solution)/shard_map/ppermute | solution.py:427
  21.7 3.8 %collective-permute-start = (f32[40,128]{1,0:T(8,128)S(1)}, f32[40,128]{1,0:T(8,128)S(1)}, u32[]{:S(2)}, u32[]{:S(2)}) collective-permute-start(f32[40,128]{1,0:T(8,128)S(1)} %get-tuple-element.25.args_0_), channel_id=1, source_target_pairs={{8,0},{16,8},{24,16},{0,24},{9,1},{17,9},{25,17},{1,25},{10,2},{18... | collective-permute-start | bytes 61448 | tf_op jit(solution)/shard_map/ppermute | solution.py:427
  26.1 30.7 %collective-permute-start.5 = (bf16[8,16,2048]{2,1,0:T(8,128)(2,1)S(1)}, bf16[8,16,2048]{2,1,0:T(8,128)(2,1)S(1)}, u32[]{:S(2)}, u32[]{:S(2)}) collective-permute-start(bf16[8,16,2048]{2,1,0:T(8,128)(2,1)S(1)} %all-to-all-done.args_0_), channel_id=1, source_target_pairs={{24,0},{0,8},{8,16},{16,24},{25,1},{1,9},{9,17},{17,25},{26,2},{2,... | collective-permute-start | bytes 1572872 | tf_op jit(solution)/shard_map/ppermute | solution.py:427
  27.6 29.2 %collective-permute-start.4 = (bf16[8,16,2048]{2,1,0:T(8,128)(2,1)S(1)}, bf16[8,16,2048]{2,1,0:T(8,128)(2,1)}, u32[]{:S(2)}, u32[]{:S(2)}) collective-permute-start(bf16[8,16,2048]{2,1,0:T(8,128)(2,1)S(1)} %all-to-all-done.args_0_), channel_id=1, source_target_pairs={{16,0},{24,8},{0,16},{8,24},{17,1},{25,9},{1,17},{9,25},{18,2},{26... | collective-permute-start | bytes 1572872 | tf_op jit(solution)/shard_map/ppermute | solution.py:427
  30.3 26.5 %collective-permute-start.3 = (bf16[8,16,2048]{2,1,0:T(8,128)(2,1)S(1)}, bf16[8,16,2048]{2,1,0:T(8,128)(2,1)}, u32[]{:S(2)}, u32[]{:S(2)}) collective-permute-start(bf16[8,16,2048]{2,1,0:T(8,128)(2,1)S(1)} %all-to-all-done.args_0_), channel_id=1, source_target_pairs={{8,0},{16,8},{24,16},{0,24},{9,1},{17,9},{25,17},{1,25},{10,2},{18... | collective-permute-start | bytes 1572872 | tf_op jit(solution)/shard_map/ppermute | solution.py:427
  32.4 9.9 %all-to-all-start.1 = ((f32[8,8,128]{2,1,0:T(8,128)}), f32[8,8,128]{2,1,0:T(8,128)S(1)}, u32[]{:S(2)}, u32[]{:S(2)}) async-start(f32[8,8,128]{2,1,0:T(8,128)} %get-tuple-element.29), calls=%async_computation.1 | async-start | bytes 65536 | tf_op jit(solution)/shard_map/all_to_all | solution.py:450
  36.9 12.3 %copy-start.6 = (s32[1,1,24,2]{2,3,1,0:T(2,128)S(1)}, s32[1,1,24,2]{2,3,1,0:T(2,128)}, u32[]{:S(2)}) copy-start(s32[1,1,24,2]{2,3,1,0:T(2,128)} %param.10) | copy-start | bytes 580
  36.9 19.9 %copy-start.3 = (s32[2048]{0:T(1024)S(1)}, s32[2048]{0:T(1024)}, u32[]{:S(2)}) copy-start(s32[2048]{0:T(1024)} %param.8) | copy-start | bytes 24580
  36.9 19.9 %copy-start.5 = (s32[2048]{0:T(1024)S(1)}, s32[2048]{0:T(1024)}, u32[]{:S(2)}) copy-start(s32[2048]{0:T(1024)} %param.9) | copy-start | bytes 24580
  43.1 13.7 %all-to-all-start.2 = ((f32[8,40,128]{2,1,0:T(8,128)}), f32[8,40,128]{2,1,0:T(8,128)S(1)}, u32[]{:S(2)}, u32[]{:S(2)}) async-start(f32[8,40,128]{2,1,0:T(8,128)} %middle.1), calls=%async_computation.2 | async-start | bytes 327680 | tf_op jit(solution)/shard_map/all_to_all | solution.py:453
